TPU v7x, 32 devices: a whole 2x2x4 slice. The times are simulated.
32 devices in a mesh: ep: 8 (over z, y), tp: 4 (over x, core).
Axes of the slice: x: 2, y: 2, z: 4, core: 2. Of those that a mesh axis runs over, the one named last changes fastest.
Arguments:
- layer_input: bfloat16 [4096, 2048], P('ep'), may hold values from -6 to 6
- attention_gain: float32 [2048], replicated, may hold values from 0.5 to 1.5
- attention_in: bfloat16 [3, 2048, 2048], P(None, 'ep', 'tp'), may hold values from -0.125 to 0.125
- attention_bias: float32 [3, 2048], P(None, 'tp'), may hold values from -1.75 to 1.75
- attention_out: bfloat16 [2048, 2048], P('tp', 'ep'), may hold values from -1 to 1
- feedforward_gain: float32 [2048], replicated, may hold values from 0.5 to 1.5
- shared_in: bfloat16 [2, 2048, 5632], P(None, 'ep', 'tp'), may hold values from -0.125 to 0.125
- shared_down: bfloat16 [5632, 2048], P('tp', 'ep'), may hold values from -0.15625 to 0.15625
- shared_gate: float32 [2048], replicated, may hold values from -0.125 to 0.125
- router: float32 [2048, 16], replicated, may hold values from -0.0625 to 0.0625
- expert_in: bfloat16 [16, 2, 2048, 1408], P('ep', None, None, 'tp'), may hold values from -0.125 to 0.125
- expert_down: bfloat16 [16, 1408, 2048], P('ep', 'tp'), may hold values from -0.3125 to 0.3125
- routes: int32 [4096, 4], P('ep'), may hold values from 0 to 15, all different within a row
- document_lengths: int32 [8], replicated, may hold values from 1 to 3871, as said below
- cotangent: bfloat16 [4096, 2048], P('ep'), may hold values from -6 to 6
Outputs:
- layer_output: bfloat16 [4096, 2048], P('ep')
- grad_input: bfloat16 [4096, 2048], P('ep')
- grad_attention_gain: float32 [2048], replicated
- grad_attention_in: float32 [3, 2048, 2048], P(None, 'ep', 'tp')
- grad_attention_bias: float32 [3, 2048], P(None, 'tp')
- grad_attention_out: float32 [2048, 2048], P('tp', 'ep')
- grad_feedforward_gain: float32 [2048], replicated
- grad_shared_in: float32 [2, 2048, 5632], P(None, 'ep', 'tp')
- grad_shared_down: float32 [5632, 2048], P('tp', 'ep')
- grad_shared_gate: float32 [2048], replicated
- grad_router: float32 [2048, 16], replicated
- grad_expert_in: float32 [16, 2, 2048, 1408], P('ep', None, None, 'tp')
- grad_expert_down: float32 [16, 1408, 2048], P('ep', 'tp')
Inputs may be any that keep to these rules, and one draw needn't show every extreme that they name: `document_lengths`: 8 document lengths in order, followed by a padded tail of one or more positions; one document, at a place drawn from the seed, has the largest length, begins within the first 512 positions and ends within the last 512; some document has length 1.
All inputs are finite; a program needn't handle non-finite values.
Results may differ from a plain program's by a relative error of at most 0.02.
Values may be sent and summed in bfloat16 or wider, within the bound.
A program may use at most 320 MiB of HBM per device.

v0:
```python
import math

import jax
import jax.numpy as jnp
from jax import lax
from jax.sharding import PartitionSpec as P

HD = 128
WINDOW = 1024


HIGHEST = lax.Precision.HIGHEST
EPSILON = 1e-06
ROPE_BASE = 1000000.0
MASKED = -1000000000.0


def shifted(value, axis, steps):
    count = lax.axis_size(axis)
    leading, last = (max(0, -steps), min(count, count - steps))
    return lax.ppermute(value, axis, [(source, source + steps) for source in range(leading, last)])


def tensor_total(partial_sum):
    return lax.psum(partial_sum, "tp")


def rms_parts(values):
    inverse = lax.rsqrt(jnp.mean(values * values, axis=-1, keepdims=True) + EPSILON)
    return (inverse, values * inverse)


def norm_back(grad_rows, gain_vec, inverse, normed):
    scaled = grad_rows * gain_vec
    grad_in = inverse * (scaled - normed * jnp.mean(scaled * normed, axis=-1, keepdims=True))
    return (grad_in, jnp.sum(grad_rows * normed, axis=0))


def doc_table(document_lengths, positions):
    doc_ends = jnp.cumsum(document_lengths)
    starts_all = jnp.concatenate([doc_ends - document_lengths, doc_ends[-1:]])
    doc_ids = jnp.sum((positions[:, None] >= doc_ends[None, :]).astype(jnp.int32), axis=1)
    matches = (
        doc_ids[:, None] == jnp.arange(document_lengths.shape[0] + 1, dtype=jnp.int32)[None, :]
    )
    doc_begin = jnp.sum(jnp.where(matches, starts_all[None, :], 0), axis=1)
    rope_pos = positions - doc_begin
    valid_mask = positions < doc_ends[-1]
    doc_ids = jnp.where(positions < 0, -1, doc_ids)
    return (doc_ids, rope_pos, valid_mask)


def rope_angles(rope_pos, head_dim):
    half_width = head_dim // 2
    freqs = jnp.power(ROPE_BASE, -2.0 * jnp.arange(half_width, dtype=jnp.float32) / head_dim)
    angles = rope_pos.astype(jnp.float32)[:, None] * freqs[None, :]
    return (jnp.cos(angles)[:, None, :], jnp.sin(angles)[:, None, :])


def rotate(values, cosine, sine_part, turn_sign):
    half_width = values.shape[-1] // 2
    first_part = values[..., :half_width]
    second_part = values[..., half_width:]
    return jnp.concatenate(
        [
            first_part * cosine - turn_sign * second_part * sine_part,
            second_part * cosine + turn_sign * first_part * sine_part,
        ],
        axis=-1,
    )


def silu_parts(gate_pre):
    sig_gate = jax.nn.sigmoid(gate_pre)
    return (gate_pre * sig_gate, sig_gate * (1.0 + gate_pre * (1.0 - sig_gate)))


def per_device(
    layer_input,
    attention_gain,
    attention_in,
    attention_bias,
    attention_out,
    feedforward_gain,
    shared_in,
    shared_down,
    shared_gate,
    router,
    expert_in,
    expert_down,
    routes,
    document_lengths,
    cotangent,
):
    bf16 = jnp.bfloat16
    f32 = jnp.float32
    tok_count = layer_input.shape[0]
    model_width = layer_input.shape[1]
    expert_count = router.shape[1]
    top_count = routes.shape[1]
    ep_size = lax.axis_size("ep")
    tp_size = lax.axis_size("tp")
    capacity = tp_size * (
        (5 * tok_count * top_count + 4 * expert_count * tp_size - 1) // (4 * expert_count * tp_size)
    )
    reach_back = min((WINDOW + tok_count - 2) // tok_count, ep_size - 1)
    head_dim = HD
    local_heads = attention_in.shape[2] // head_dim
    score_scale = 1.0 / math.sqrt(head_dim)
    in_full, out_full, shared_in_full, shared_down_full = (
        lax.all_gather(attention_in, "ep", axis=1, tiled=True),
        lax.all_gather(attention_out, "ep", axis=1, tiled=True),
        lax.all_gather(shared_in, "ep", axis=1, tiled=True),
        lax.all_gather(shared_down, "ep", axis=1, tiled=True),
    )
    ep_index = lax.axis_index("ep")
    positions = ep_index * tok_count + jnp.arange(tok_count, dtype=jnp.int32)
    key_count = (reach_back + 1) * tok_count
    key_positions = (ep_index - reach_back) * tok_count + jnp.arange(key_count, dtype=jnp.int32)
    query_doc, rope_pos, valid_mask = doc_table(document_lengths, positions)
    key_doc = doc_table(document_lengths, key_positions)[0]
    distance = positions[:, None] - key_positions[None, :]
    allowed = (query_doc[:, None] == key_doc[None, :]) & (distance >= 0) & (distance < WINDOW)
    valid_rows = valid_mask.astype(f32)[:, None]
    cosine, sine_part = rope_angles(rope_pos, head_dim)
    input_rows = layer_input.astype(f32)
    inverse_one, normed_one = rms_parts(input_rows)
    normed_attention = (normed_one * attention_gain).astype(bf16)
    raw_proj = (
        jnp.einsum("td,sde->ste", normed_attention, in_full, preferred_element_type=f32)
        + attention_bias[:, None, :]
    )
    queries = rotate(
        raw_proj[0].reshape(tok_count, local_heads, head_dim), cosine, sine_part, 1.0
    ).astype(bf16)
    keys_own = rotate(
        raw_proj[1].reshape(tok_count, local_heads, head_dim), cosine, sine_part, 1.0
    ).astype(bf16)
    values_own = raw_proj[2].reshape(tok_count, local_heads, head_dim).astype(bf16)
    key_value = jnp.stack([keys_own, values_own])
    earlier = []
    for hop_count in range(reach_back, 0, -1):
        earlier.append(shifted(key_value, "ep", hop_count))
    all_kv = jnp.concatenate(earlier + [key_value], axis=1)
    all_keys = all_kv[0]
    all_values = all_kv[1]
    scores = jnp.einsum("qhe,khe->hqk", queries, all_keys, preferred_element_type=f32) * score_scale
    scores = jnp.where(allowed[None], scores, MASKED)
    row_max = jnp.max(scores, axis=-1, keepdims=True)
    exp_terms = jnp.exp(scores - row_max)
    row_total = jnp.sum(exp_terms, axis=-1, keepdims=True)
    log_total = row_max + jnp.log(row_total)
    weights = (exp_terms / row_total).astype(bf16)
    heads_out = jnp.einsum("hqk,khe->qhe", weights, all_values, preferred_element_type=f32).reshape(
        tok_count, -1
    )
    heads_low = (heads_out * valid_rows).astype(bf16)
    attention_sum = tensor_total(jnp.dot(heads_low, out_full, preferred_element_type=f32))
    residual = input_rows + attention_sum
    inverse_two, normed_two = rms_parts(residual)
    normed_ffn = normed_two * feedforward_gain
    normed_low = normed_ffn.astype(bf16)
    shared_pre = jnp.einsum("td,sdf->stf", normed_low, shared_in_full, preferred_element_type=f32)
    shared_silu, shared_slope = silu_parts(shared_pre[0])
    shared_hidden = (shared_silu * shared_pre[1]).astype(bf16)
    shared_out = tensor_total(jnp.dot(shared_hidden, shared_down_full, preferred_element_type=f32))
    shared_scale = jax.nn.sigmoid(jnp.dot(normed_ffn, shared_gate, precision=HIGHEST))
    router_probs = jax.nn.softmax(jnp.dot(normed_ffn, router, precision=HIGHEST), axis=-1)
    chosen = jnp.take_along_axis(router_probs, routes, axis=1)
    chosen_total = jnp.sum(chosen, axis=1, keepdims=True)
    gate_values = chosen / chosen_total
    assign_count = tok_count * top_count
    flat_routes = routes.reshape(-1)
    expert_ids = jnp.arange(expert_count, dtype=jnp.int32)
    one_hot = (flat_routes[:, None] == expert_ids[None, :]).astype(jnp.int32)
    arrival_rank = jnp.sum((jnp.cumsum(one_hot, axis=0) - one_hot) * one_hot, axis=1)
    slot_count = expert_count * capacity
    slot_index = jnp.where(
        arrival_rank < capacity, flat_routes * capacity + arrival_rank, slot_count
    )
    slot_assign = (
        jnp.full((slot_count + 1,), assign_count, jnp.int32)
        .at[slot_index]
        .set(jnp.arange(assign_count, dtype=jnp.int32))[:slot_count]
    )
    slot_token = slot_assign // top_count
    padded_rows = jnp.concatenate([normed_low, jnp.zeros((1, model_width), bf16)])
    send_rows = padded_rows[slot_token].reshape(expert_count, capacity, model_width)

    def expert_trip(outgoing, work):
        row_block = lax.all_to_all(outgoing, "ep", split_axis=0, concat_axis=1, tiled=True)
        partial_rows, extras = work(row_block)
        share_rows = lax.psum_scatter(partial_rows, "tp", scatter_dimension=1, tiled=True).astype(
            bf16
        )
        whole_rows = lax.all_gather(share_rows, "tp", axis=1, tiled=True)
        return (lax.all_to_all(whole_rows, "ep", split_axis=1, concat_axis=0, tiled=True), extras)

    def expert_forward(row_block):
        pre_acts = jnp.einsum("erd,esdf->serf", row_block, expert_in, preferred_element_type=f32)
        gate_silu, gate_slope = silu_parts(pre_acts[0])
        hidden = (gate_silu * pre_acts[1]).astype(bf16)
        partial_rows = jnp.einsum("erf,efd->erd", hidden, expert_down, preferred_element_type=f32)
        return (partial_rows, (row_block, pre_acts, hidden, gate_silu, gate_slope))

    returned_rows, kept_state = expert_trip(send_rows, expert_forward)
    expert_rows, expert_pre, expert_hidden, expert_silu, expert_slope = kept_state
    padded_back = jnp.concatenate(
        [returned_rows.reshape(slot_count, model_width), jnp.zeros((1, model_width), bf16)]
    )
    picked = padded_back[slot_index].reshape(tok_count, top_count, model_width).astype(f32)
    moe_sum = jnp.sum(gate_values[:, :, None] * picked, axis=1)
    layer_output = (residual + shared_scale[:, None] * shared_out + moe_sum).astype(bf16)
    grad_rows = cotangent.astype(f32)
    padded_grad = jnp.concatenate([grad_rows, jnp.zeros((1, model_width), f32)])
    padded_gates = jnp.concatenate([gate_values.reshape(-1), jnp.zeros((1,), f32)])
    grad_send = (padded_gates[slot_assign][:, None] * padded_grad[slot_token]).astype(bf16)
    grad_send = grad_send.reshape(expert_count, capacity, model_width)

    def expert_backward(grad_block):
        grad_down = jnp.einsum(
            "erf,erd->efd", expert_hidden, grad_block, preferred_element_type=f32
        )
        grad_hidden = jnp.einsum(
            "erd,efd->erf", grad_block, expert_down, preferred_element_type=f32
        )
        grad_pre = jnp.stack(
            [grad_hidden * expert_pre[1] * expert_slope, grad_hidden * expert_silu]
        ).astype(bf16)
        grad_weights_in = jnp.einsum(
            "erd,serf->esdf", expert_rows, grad_pre, preferred_element_type=f32
        )
        grad_back_rows = jnp.einsum(
            "serf,esdf->erd", grad_pre, expert_in, preferred_element_type=f32
        )
        return (grad_back_rows, (grad_weights_in, grad_down))

    grad_returned, expert_grads = expert_trip(grad_send, expert_backward)
    grad_expert_in, grad_expert_down = expert_grads
    grad_gate_values = jnp.sum(picked * grad_rows[:, None, :], axis=2)
    grad_chosen = (
        grad_gate_values - jnp.sum(grad_gate_values * gate_values, axis=1, keepdims=True)
    ) / chosen_total
    grad_probs = jnp.sum(
        jnp.where(routes[:, :, None] == expert_ids[None, None, :], grad_chosen[:, :, None], 0.0),
        axis=1,
    )
    grad_logits = router_probs * (
        grad_probs - jnp.sum(grad_probs * router_probs, axis=1, keepdims=True)
    )
    grad_router = jnp.einsum("td,te->de", normed_ffn, grad_logits, precision=HIGHEST)
    grad_shared_out = (shared_scale[:, None] * grad_rows).astype(bf16)
    grad_shared_down = jnp.einsum(
        "tf,td->fd", shared_hidden, grad_shared_out, preferred_element_type=f32
    )
    grad_shared_hidden = jnp.einsum(
        "td,fd->tf", grad_shared_out, shared_down_full, preferred_element_type=f32
    )
    grad_shared_pre = jnp.stack(
        [grad_shared_hidden * shared_pre[1] * shared_slope, grad_shared_hidden * shared_silu]
    ).astype(bf16)
    grad_shared_in = jnp.einsum(
        "td,stf->sdf", normed_low, grad_shared_pre, preferred_element_type=f32
    )
    shared_back = jnp.einsum(
        "stf,sdf->td", grad_shared_pre, shared_in_full, preferred_element_type=f32
    )
    grad_scale_pre = jnp.sum(grad_rows * shared_out, axis=1) * shared_scale * (1.0 - shared_scale)
    grad_shared_gate = jnp.dot(grad_scale_pre, normed_ffn, precision=HIGHEST)
    padded_return = jnp.concatenate(
        [grad_returned.reshape(slot_count, model_width), jnp.zeros((1, model_width), bf16)]
    )
    moe_back = jnp.sum(
        padded_return[slot_index].reshape(tok_count, top_count, model_width).astype(f32), axis=1
    )
    grad_normed = (
        tensor_total(shared_back)
        + moe_back
        + jnp.einsum("te,de->td", grad_logits, router, precision=HIGHEST)
        + grad_scale_pre[:, None] * shared_gate[None, :]
    )
    grad_mid_norm, grad_feedforward_gain = norm_back(
        grad_normed, feedforward_gain, inverse_two, normed_two
    )
    grad_residual = grad_rows + grad_mid_norm
    grad_attention = grad_residual.astype(bf16)
    grad_attention_out = jnp.einsum(
        "tf,td->fd", heads_low, grad_attention, preferred_element_type=f32
    )
    grad_heads = jnp.einsum(
        "td,fd->tf", grad_attention, out_full, preferred_element_type=f32
    ).astype(bf16)
    grad_heads = (grad_heads * valid_rows.astype(bf16)).reshape(tok_count, local_heads, head_dim)
    scores_again = (
        jnp.einsum("qhe,khe->hqk", queries, all_keys, preferred_element_type=f32) * score_scale
    )
    scores_again = jnp.where(allowed[None], scores_again, MASKED)
    softmax_out = jnp.exp(scores_again - log_total)
    weights_again = softmax_out.astype(bf16)
    grad_weights = jnp.einsum("qhe,khe->hqk", grad_heads, all_values, preferred_element_type=f32)
    grad_scores = (
        softmax_out * (grad_weights - jnp.sum(softmax_out * grad_weights, axis=-1, keepdims=True))
    ).astype(bf16)
    grad_queries = (
        jnp.einsum("hqk,khe->qhe", grad_scores, all_keys, preferred_element_type=f32) * score_scale
    )
    grad_keys = (
        jnp.einsum("hqk,qhe->khe", grad_scores, queries, preferred_element_type=f32) * score_scale
    )
    grad_values = jnp.einsum("hqk,qhe->khe", weights_again, grad_heads, preferred_element_type=f32)
    grad_kv = jnp.stack([grad_keys, grad_values])
    own_part = grad_kv[:, reach_back * tok_count :]
    for hop_count in range(1, reach_back + 1):
        segment_start = (reach_back - hop_count) * tok_count
        segment = grad_kv[:, segment_start : segment_start + tok_count]
        own_part = own_part + shifted(segment, "ep", -hop_count)
    grad_raw = (
        jnp.stack(
            [
                rotate(grad_queries, cosine, sine_part, -1.0),
                rotate(own_part[0], cosine, sine_part, -1.0),
                own_part[1],
            ]
        )
        .reshape(3, tok_count, -1)
        .astype(bf16)
    )
    grad_attention_bias = jnp.sum(grad_raw.astype(f32), axis=1)
    grad_attention_in = jnp.einsum(
        "td,ste->sde", normed_attention, grad_raw, preferred_element_type=f32
    )
    grad_normed_attention = tensor_total(
        jnp.einsum("ste,sde->td", grad_raw, in_full, preferred_element_type=f32)
    )
    grad_in_norm, grad_attention_gain = norm_back(
        grad_normed_attention, attention_gain, inverse_one, normed_one
    )
    grad_input = (grad_residual + grad_in_norm).astype(bf16)
    grad_attention_in, grad_attention_out, grad_shared_in, grad_shared_down = (
        lax.psum_scatter(
            grad_attention_in.astype(jnp.bfloat16), "ep", scatter_dimension=1, tiled=True
        ).astype(jnp.float32),
        lax.psum_scatter(
            grad_attention_out.astype(jnp.bfloat16), "ep", scatter_dimension=1, tiled=True
        ).astype(jnp.float32),
        lax.psum_scatter(
            grad_shared_in.astype(jnp.bfloat16), "ep", scatter_dimension=1, tiled=True
        ).astype(jnp.float32),
        lax.psum_scatter(
            grad_shared_down.astype(jnp.bfloat16), "ep", scatter_dimension=1, tiled=True
        ).astype(jnp.float32),
    )
    (
        grad_attention_gain,
        grad_attention_bias,
        grad_feedforward_gain,
        grad_shared_gate,
        grad_router,
    ) = (
        lax.psum(grad_attention_gain.astype(jnp.bfloat16), "ep").astype(jnp.float32),
        lax.psum(grad_attention_bias.astype(jnp.bfloat16), "ep").astype(jnp.float32),
        lax.psum(grad_feedforward_gain.astype(jnp.bfloat16), "ep").astype(jnp.float32),
        lax.psum(grad_shared_gate.astype(jnp.bfloat16), "ep").astype(jnp.float32),
        lax.psum(grad_router.astype(jnp.bfloat16), "ep").astype(jnp.float32),
    )
    return (
        layer_output,
        grad_input,
        grad_attention_gain,
        grad_attention_in,
        grad_attention_bias,
        grad_attention_out,
        grad_feedforward_gain,
        grad_shared_in,
        grad_shared_down,
        grad_shared_gate,
        grad_router,
        grad_expert_in,
        grad_expert_down,
    )


def solution(mesh):
    return jax.shard_map(
        per_device,
        mesh=mesh,
        in_specs=(
            P("ep", None),
            P(),
            P(None, "ep", "tp"),
            P(None, "tp"),
            P("tp", "ep"),
            P(),
            P(None, "ep", "tp"),
            P("tp", "ep"),
            P(),
            P(),
            P("ep", None, None, "tp"),
            P("ep", "tp", None),
            P("ep", None),
            P(),
            P("ep", None),
        ),
        out_specs=(
            P("ep", None),
            P("ep", None),
            P(),
            P(None, "ep", "tp"),
            P(None, "tp"),
            P("tp", "ep"),
            P(),
            P(None, "ep", "tp"),
            P("tp", "ep"),
            P(),
            P(),
            P("ep", None, None, "tp"),
            P("ep", "tp", None),
        ),
        check_vma=False,
    )
```

profile of v0, /device:TPU:0, one launch (start us, length us, event | category | flops | bytes accessed | tf_op | source)
XLA Modules:
  0.0 2718.1 jit_solution(63898564316468237)
XLA Ops:
  17.6 95.7 %all-gather.7.cloned.1.call-done = bf16[3,2048,512]{1,2,0:T(8,128)(2,1)} async-done(((bf16[3,256,512]{1,2,0:T(8,128)(2,1)}), bf16[3,2048,512]{1,2,0:T(8,128)(2,1)}) %all-gather.7.cloned.1.call-update) | async-done | bytes 6291472 | tf_op jit(solution)/shard_map/all_gather | solution.py:111
  143.3 33.7 %collective-permute-done = bf16[2,512,4,128]{3,1,2,0:T(8,128)(2,1)S(1)} collective-permute-done((bf16[2,512,4,128]{3,1,2,0:T(8,128)(2,1)S(1)}, bf16[2,512,4,128]{3,1,2,0:T(8,128)(2,1)S(1)}, u32[]{:S(2)}, u32[]{:S(2)}) %collective-permute-start) | collective-permute-done | bytes 1048608 | tf_op jit(solution)/shard_map/ppermute | solution.py:21
  215.4 21.9 gather_fusion.3
  237.3 68.1 %all-reduce.11.cloned.1.call-done = f32[512,2048]{1,0:T(8,128)} async-done(((f32[512,2048]{1,0:T(8,128)}), f32[512,2048]{1,0:T(8,128)}) %all-reduce.11.cloned.1.call-update) | async-done | bytes 4194320 | tf_op jit(solution)/shard_map/psum | solution.py:25
  313.5 16.8 gather_fusion.5
  332.3 13.6 gather_fusion.2
  346.0 12.2 multiply_convert_fusion
  369.2 22.0 gather_fusion
  391.2 200.5 %all-to-all-done.2 = bf16[16,160,2048]{2,1,0:T(8,128)(2,1)} async-done(((bf16[16,160,2048]{2,1,0:T(8,128)(2,1)}), bf16[16,160,2048]{2,1,0:T(8,128)(2,1)}, u32[]{:S(2)}, u32[]{:S(2)}) %all-to-all-start.2) | async-done | bytes 10485792 | tf_op jit(solution)/shard_map/all_to_all | solution.py:191
  597.4 10.1 copy.236
  607.5 216.4 %all-to-all-done = bf16[16,160,2048]{2,1,0:T(8,128)(2,1)} async-done(((bf16[16,160,2048]{2,1,0:T(8,128)(2,1)}), bf16[16,160,2048]{2,1,0:T(8,128)(2,1)}, u32[]{:S(2)}, u32[]{:S(2)}) %all-to-all-start) | async-done | bytes 10485792 | tf_op jit(solution)/shard_map/all_to_all | solution.py:191
  823.9 10.1 copy.231
  834.0 14.5 convolution_bitcast_fusion.2
  848.5 14.4 fusion.48
  862.9 11.4 fusion.92
  875.8 19.9 convolution_bitcast_fusion
  895.8 130.8 %reduce-scatter.7.cloned.1.call-done = f32[2,320,2048]{2,1,0:T(8,128)} async-done(((f32[2,1280,2048]{2,1,0:T(8,128)}), f32[2,320,2048]{2,1,0:T(8,128)}) %reduce-scatter.7.cloned.1.call-update) | async-done | bytes 5242896 | tf_op jit(solution)/shard_map/reduce_scatter | solution.py:193
  1032.5 149.7 %reduce-scatter.9.cloned.1.call-done = f32[2,320,2048]{2,1,0:T(8,128)} async-done(((f32[2,1280,2048]{2,1,0:T(8,128)}), f32[2,320,2048]{2,1,0:T(8,128)}) %reduce-scatter.9.cloned.1.call-update) | async-done | bytes 5242896 | tf_op jit(solution)/shard_map/reduce_scatter | solution.py:193
  1186.5 67.9 %all-gather.15.cloned.1.call-done = bf16[2,1280,2048]{2,1,0:T(8,128)(2,1)} async-done(((bf16[2,320,2048]{2,1,0:T(8,128)(2,1)}), bf16[2,1280,2048]{2,1,0:T(8,128)(2,1)}) %all-gather.15.cloned.1.call-update) | async-done | bytes 10485776 | tf_op jit(solution)/shard_map/all_gather | solution.py:196
  1254.4 20.0 copy.233
  1286.3 335.2 %all-gather.11.cloned.1.call-done = bf16[2,2048,1408]{2,1,0:T(8,128)(2,1)} async-done(((bf16[2,256,1408]{2,1,0:T(8,128)(2,1)}), bf16[2,2048,1408]{2,1,0:T(8,128)(2,1)}) %all-gather.11.cloned.1.call-update) | async-done | bytes 11534352 | tf_op jit(solution)/shard_map/all_gather | solution.py:113
  1621.5 12.5 convolution_bitcast_fusion.3
  1634.0 80.6 %all-gather.13.cloned.1.call-done = bf16[1408,2048]{1,0:T(8,128)(2,1)} async-done(((bf16[1408,256]{1,0:T(8,128)(2,1)}), bf16[1408,2048]{1,0:T(8,128)(2,1)}) %all-gather.13.cloned.1.call-update) | async-done | bytes 5767184 | tf_op jit(solution)/shard_map/all_gather | solution.py:114
  1747.2 37.5 %all-gather.17.cloned.1.call-done = bf16[2,1280,2048]{2,1,0:T(8,128)(2,1)} async-done(((bf16[2,320,2048]{2,1,0:T(8,128)(2,1)}), bf16[2,1280,2048]{2,1,0:T(8,128)(2,1)}) %all-gather.17.cloned.1.call-update) | async-done | bytes 10485776 | tf_op jit(solution)/shard_map/all_gather | solution.py:196
  1784.7 20.0 copy.238
  1810.3 11.1 convert_bitcast_fusion
  1824.7 115.9 %all-reduce.17.cloned.1.call-done = (f32[512,2048]{1,0:T(8,128)}, f32[512,2048]{1,0:T(8,128)}) async-done(((f32[512,2048]{1,0:T(8,128)}, f32[512,2048]{1,0:T(8,128)}), (f32[512,2048]{1,0:T(8,128)}, f32[512,2048]{1,0:T(8,128)})) %all-reduce.17.cloned.1.call-update) | async-done | bytes 8388624 | tf_op jit(solution)/shard_map/psum | solution.py:25
  1943.3 12.8 copy.234
  1956.1 10.2 concatenate.57
  1966.3 21.7 gather_fusion.1
  1988.0 15.5 reshape.446
  2003.5 20.2 multiply_reduce_fusion
  2023.8 61.6 %all-to-all-done.3 = bf16[2,1280,2048]{2,0,1:T(2,128)(2,1)} async-done(((bf16[2,1280,2048]{2,0,1:T(2,128)(2,1)}), bf16[2,1280,2048]{2,0,1:T(2,128)(2,1)}, u32[]{:S(2)}, u32[]{:S(2)}) %all-to-all-start.3) | async-done | bytes 10485792 | tf_op jit(solution)/shard_map/all_to_all | solution.py:197
  2085.4 12.9 copy.239
  2098.3 10.5 concatenate.60
  2108.8 21.7 gather_fusion.4
  2130.5 15.5 reshape.447
  2146.1 15.2 reduce_sum.214
  2161.6 9.5 multiply_reduce_fusion.3
  2224.3 46.3 %collective-permute-done.2 = f32[2,512,4,128]{3,1,2,0:T(8,128)} collective-permute-done((f32[2,512,4,128]{3,1,2,0:T(8,128)}, f32[2,512,4,128]{3,1,2,0:T(8,128)}, u32[]{:S(2)}, u32[]{:S(2)}) %collective-permute-start.2) | collective-permute-done | bytes 2097184 | tf_op jit(solution)/shard_map/ppermute | solution.py:21
  2270.6 52.2 %collective-permute-done.3 = f32[2,512,4,128]{3,1,2,0:T(8,128)} collective-permute-done((f32[2,512,4,128]{3,1,2,0:T(8,128)}, f32[2,512,4,128]{3,1,2,0:T(8,128)}, u32[]{:S(2)}, u32[]{:S(2)}) %collective-permute-start.3) | collective-permute-done | bytes 2097184 | tf_op jit(solution)/shard_map/ppermute | solution.py:21
  2358.1 11.1 fusion.93
  2369.2 12.8 convolution_bitcast_fusion.1
  2385.0 42.8 %all-reduce.15.cloned.1.call-done = bf16[2048,16]{0,1:T(8,128)(2,1)} async-done(((bf16[2048,16]{0,1:T(8,128)(2,1)}), bf16[2048,16]{0,1:T(8,128)(2,1)}) %all-reduce.15.cloned.1.call-update) | async-done | bytes 65552 | tf_op jit(solution)/shard_map/psum | solution.py:364
  2430.7 84.9 %all-reduce.13.cloned.1.call-done = f32[512,2048]{1,0:T(8,128)} async-done(((f32[512,2048]{1,0:T(8,128)}), f32[512,2048]{1,0:T(8,128)}) %all-reduce.13.cloned.1.call-update) | async-done | bytes 4194320 | tf_op jit(solution)/shard_map/psum | solution.py:25
  2518.9 37.4 %all-reduce.5 = (bf16[2048]{0:T(1024)(128)(2,1)S(1)}, bf16[3,512]{1,0:T(4,128)(2,1)S(1)}, bf16[2048]{0:T(1024)(128)(2,1)S(1)}, bf16[2048]{0:T(1024)(128)(2,1)S(1)}) all-reduce(bf16[2048]{0:T(1024)(128)(2,1)S(1)} %get-tuple-element.95, bf16[3,512]{1,0:T(4,128)(2,1)S(1)} %fusion.84, ...), channel_id=1, replica_groups=mesh['ep'=8,'tp'=4] {'ep'}, use_global_device_ids=true, to_apply=%region_32.33 | all-reduce | flops 7680 | bytes 30720 | tf_op jit(solution)/shard_map/psum | solution.py:360
  2558.7 29.3 %reduce-scatter.13.cloned.1.call-done = bf16[512,256]{1,0:T(8,128)(2,1)} async-done(((bf16[512,2048]{1,0:T(8,128)(2,1)}), bf16[512,256]{1,0:T(8,128)(2,1)}) %reduce-scatter.13.cloned.1.call-update) | async-done | bytes 262160 | tf_op jit(solution)/shard_map/reduce_scatter | solution.py:343
  2596.4 112.4 %reduce-scatter.11.cloned.1.call-done = bf16[3,256,512]{1,2,0:T(8,128)(2,1)} async-done(((bf16[3,2048,512]{1,2,0:T(8,128)(2,1)}), bf16[3,256,512]{1,2,0:T(8,128)(2,1)}) %reduce-scatter.11.cloned.1.call-update) | async-done | bytes 786448 | tf_op jit(solution)/shard_map/reduce_scatter | solution.py:340
  (316 shorter events, 283.6 us)
Async XLA Ops:
  7.2 841.3 %copy-start = (bf16[2,352,2048]{2,1,0:T(8,128)(2,1)S(1)}, bf16[2,352,2048]{2,1,0:T(8,128)(2,1)}, u32[]{:S(2)}) copy-start(bf16[2,352,2048]{2,1,0:T(8,128)(2,1)} %param.26) | copy-start | bytes 8650756
  7.2 106.1 %copy-start.46 = (f32[2048]{0:T(1024)S(1)}, f32[2048]{0:T(1024)}, u32[]{:S(2)}) copy-start(f32[2048]{0:T(1024)} %param.16) | copy-start | bytes 24580
  7.2 106.1 %copy-start.60 = (f32[3,512]{1,0:T(4,128)S(1)}, f32[3,512]{1,0:T(4,128)}, u32[]{:S(2)}) copy-start(f32[3,512]{1,0:T(4,128)} %param.18) | copy-start | bytes 18436
  7.2 106.1 %all-gather.7.cloned.1.call-start = ((), (), s32[]{:S(2)}) async-start(), calls=%async_computation.10 | async-start | bytes 7077888 | tf_op jit(solution)/shard_map/all_gather | solution.py:111
  9.7 180.9 %all-gather.9.cloned.1.call-start = ((), (), s32[]{:S(2)}) async-start(), calls=%async_computation.11 | async-start | bytes 2359296 | tf_op jit(solution)/shard_map/all_gather | solution.py:112
  10.5 294.8 %all-reduce.11.cloned.1.call-start = ((), (), s32[]{:S(2)}) async-start(), calls=%async_computation.12 | async-start | bytes 8388608 | tf_op jit(solution)/shard_map/psum | solution.py:25
  15.6 104.1 %copy-start.52 = (f32[512]{0:T(512)}, f32[512]{0:T(512)S(1)}, u32[]{:S(2)}) copy-start(f32[512]{0:T(512)S(1)} %add_rsqrt_fusion.1) | copy-start | bytes 6148
  136.3 41.6 %copy-start.16 = (bf16[512,4,64]{2,0,1:T(8,128)(2,1)}, bf16[512,4,64]{2,0,1:T(8,128)(2,1)S(1)}, u32[]{:S(2)}) copy-start(bf16[512,4,64]{2,0,1:T(8,128)(2,1)S(1)} %get-tuple-element.117) | copy-start | bytes 786436
  136.3 41.6 %copy-start.18 = (bf16[512,4,64]{2,0,1:T(8,128)(2,1)}, bf16[512,4,64]{2,0,1:T(8,128)(2,1)S(1)}, u32[]{:S(2)}) copy-start(bf16[512,4,64]{2,0,1:T(8,128)(2,1)S(1)} %get-tuple-element.118) | copy-start | bytes 786436
  136.6 40.4 %collective-permute-start = (bf16[2,512,4,128]{3,1,2,0:T(8,128)(2,1)S(1)}, bf16[2,512,4,128]{3,1,2,0:T(8,128)(2,1)S(1)}, u32[]{:S(2)}, u32[]{:S(2)}) collective-permute-start(bf16[2,512,4,128]{3,1,2,0:T(8,128)(2,1)S(1)} %pad_maximum_fusion.6), channel_id=1, source_target_pairs={{0,8},{4,12},{8,16},{12,20},{16,24},{20,28},{1,9},{5,13},{9,17},{1... | collective-permute-start | bytes 3145736 | tf_op jit(solution)/shard_map/ppermute | solution.py:21
  138.2 38.8 %collective-permute-start.1 = (bf16[2,512,4,128]{3,1,2,0:T(8,128)(2,1)S(1)}, bf16[2,512,4,128]{3,1,2,0:T(8,128)(2,1)S(1)}, u32[]{:S(2)}, u32[]{:S(2)}) collective-permute-start(bf16[2,512,4,128]{3,1,2,0:T(8,128)(2,1)S(1)} %pad_maximum_fusion.6), channel_id=1, source_target_pairs={{0,4},{4,8},{8,12},{12,16},{16,20},{20,24},{24,28},{1,5},{5,9},{9,... | collective-permute-start | bytes 3145736 | tf_op jit(solution)/shard_map/ppermute | solution.py:21
  237.3 71.6 %copy-start.28 = (f32[2048,16]{0,1:T(8,128)S(1)}, f32[2048,16]{0,1:T(8,128)}, u32[]{:S(2)}) copy-start(f32[2048,16]{0,1:T(8,128)} %param.24) | copy-start | bytes 393220
  237.3 71.6 %copy-start.32 = (f32[2048]{0:T(1024)S(1)}, f32[2048]{0:T(1024)}, u32[]{:S(2)}) copy-start(f32[2048]{0:T(1024)} %param.20) | copy-start | bytes 24580
  308.8 971.3 %copy-start.36 = (f32[512]{0:T(512)}, f32[512]{0:T(512)S(1)}, u32[]{:S(2)}) copy-start(f32[512]{0:T(512)S(1)} %add_rsqrt_fusion) | copy-start | bytes 6148
  312.8 17.4 copy-start.44
  313.4 16.8 copy-start.54
  313.5 16.8 copy-start.2
  358.3 233.5 %all-to-all-start.2 = ((bf16[16,160,2048]{2,1,0:T(8,128)(2,1)}), bf16[16,160,2048]{2,1,0:T(8,128)(2,1)}, u32[]{:S(2)}, u32[]{:S(2)}) async-start(bf16[16,160,2048]{2,1,0:T(8,128)(2,1)} %multiply_convert_fusion), calls=%async_computation.3 | async-start | bytes 20971520 | tf_op jit(solution)/shard_map/all_to_all | solution.py:191
  591.8 232.1 %all-to-all-start = ((bf16[16,160,2048]{2,1,0:T(8,128)(2,1)}), bf16[16,160,2048]{2,1,0:T(8,128)(2,1)}, u32[]{:S(2)}, u32[]{:S(2)}) async-start(bf16[16,160,2048]{2,1,0:T(8,128)(2,1)} %bitcast.211), calls=%async_computation | async-start | bytes 20971520 | tf_op jit(solution)/shard_map/all_to_all | solution.py:191
  596.9 429.6 %reduce-scatter.7.cloned.1.call-start = ((), (), s32[]{:S(2)}) async-start(), calls=%async_computation.15 | async-start | bytes 26214400 | tf_op jit(solution)/shard_map/reduce_scatter | solution.py:193
  874.4 307.8 %reduce-scatter.9.cloned.1.call-start = ((), (), s32[]{:S(2)}) async-start(), calls=%async_computation.17 | async-start | bytes 26214400 | tf_op jit(solution)/shard_map/reduce_scatter | solution.py:193
  895.7 358.7 %all-gather.15.cloned.1.call-start = ((), (), s32[]{:S(2)}) async-start(), calls=%async_computation.16 | async-start | bytes 13107200 | tf_op jit(solution)/shard_map/all_gather | solution.py:196
  1030.9 590.6 %all-gather.11.cloned.1.call-start = ((), (), s32[]{:S(2)}) async-start(), calls=%async_computation.13 | async-start | bytes 12976128 | tf_op jit(solution)/shard_map/all_gather | solution.py:113
  1031.7 683.0 %all-gather.13.cloned.1.call-start = ((), (), s32[]{:S(2)}) async-start(), calls=%async_computation.14 | async-start | bytes 6488064 | tf_op jit(solution)/shard_map/all_gather | solution.py:114
  1032.4 752.3 %all-gather.17.cloned.1.call-start = ((), (), s32[]{:S(2)}) async-start(), calls=%async_computation.18 | async-start | bytes 13107200 | tf_op jit(solution)/shard_map/all_gather | solution.py:196
  1274.4 530.3 %all-to-all-start.1 = ((bf16[2,1280,2048]{2,0,1:T(2,128)(2,1)}), bf16[2,1280,2048]{2,0,1:T(2,128)(2,1)}, u32[]{:S(2)}, u32[]{:S(2)}) async-start(bf16[2,1280,2048]{2,0,1:T(2,128)(2,1)} %copy.233), calls=%async_computation.2 | async-start | bytes 20971520 | tf_op jit(solution)/shard_map/all_to_all | solution.py:197
  1280.1 660.5 %all-reduce.17.cloned.1.call-start = ((), (), s32[]{:S(2)}) async-start(), calls=%async_computation.25 | async-start | bytes 16777216 | tf_op jit(solution)/shard_map/psum | solution.py:25
  1286.3 428.4 %copy-start.7 = (bf16[512,2048]{1,0:T(8,128)(2,1)S(1)}, bf16[512,2048]{1,0:T(8,128)(2,1)}, u32[]{:S(2)}) copy-start(bf16[512,2048]{1,0:T(8,128)(2,1)} %param.29) | copy-start | bytes 6291460
  1740.2 615.6 %reduce-scatter.17.cloned.1.call-start = ((), (), s32[]{:S(2)}) async-start(), calls=%async_computation.23 | async-start | bytes 6488064 | tf_op jit(solution)/shard_map/reduce_scatter | solution.py:349
  1804.7 280.7 %all-to-all-start.3 = ((bf16[2,1280,2048]{2,0,1:T(2,128)(2,1)}), bf16[2,1280,2048]{2,0,1:T(2,128)(2,1)}, u32[]{:S(2)}, u32[]{:S(2)}) async-start(bf16[2,1280,2048]{2,0,1:T(2,128)(2,1)} %copy.238), calls=%async_computation.5 | async-start | bytes 20971520 | tf_op jit(solution)/shard_map/all_to_all | solution.py:197
  1810.3 571.8 %reduce-scatter.15.cloned.1.call-start = ((), (), s32[]{:S(2)}) async-start(), calls=%async_computation.22 | async-start | bytes 12976128 | tf_op jit(solution)/shard_map/reduce_scatter | solution.py:346
  1821.5 606.3 %all-reduce.15.cloned.1.call-start = ((), (), s32[]{:S(2)}) async-start(), calls=%async_computation.24 | async-start | bytes 131072 | tf_op jit(solution)/shard_map/psum | solution.py:364
  1988.0 15.5 copy-start.21
  2146.1 15.4 copy-start.3
  2146.1 15.4 copy-start.29
  2146.1 15.4 copy-start.33
  2146.1 15.4 copy-start.37
  2146.1 15.4 copy-start.43
  2213.0 57.6 %collective-permute-start.2 = (f32[2,512,4,128]{3,1,2,0:T(8,128)}, f32[2,512,4,128]{3,1,2,0:T(8,128)}, u32[]{:S(2)}, u32[]{:S(2)}) collective-permute-start(f32[2,512,4,128]{3,1,2,0:T(8,128)} %get-tuple-element.110), channel_id=1, source_target_pairs={{4,0},{8,4},{12,8},{16,12},{20,16},{24,20},{28,24},{5,1},{9,5},{13... | collective-permute-start | bytes 6291464 | tf_op jit(solution)/shard_map/ppermute | solution.py:21
  2214.2 108.5 %collective-permute-start.3 = (f32[2,512,4,128]{3,1,2,0:T(8,128)}, f32[2,512,4,128]{3,1,2,0:T(8,128)}, u32[]{:S(2)}, u32[]{:S(2)}) collective-permute-start(f32[2,512,4,128]{3,1,2,0:T(8,128)} %get-tuple-element.111), channel_id=1, source_target_pairs={{8,0},{12,4},{16,8},{20,12},{24,16},{28,20},{9,1},{13,5},{17,9},{2... | collective-permute-start | bytes 6291464 | tf_op jit(solution)/shard_map/ppermute | solution.py:21
  2218.8 296.8 %all-reduce.13.cloned.1.call-start = ((), (), s32[]{:S(2)}) async-start(), calls=%async_computation.19 | async-start | bytes 8388608 | tf_op jit(solution)/shard_map/psum | solution.py:25
  2218.9 103.9 %copy-start.10 = (f32[1,1536,4,128]{3,1,2,0:T(8,128)S(1)}, f32[1,1536,4,128]{3,1,2,0:T(8,128)}, u32[]{:S(2)}) copy-start(f32[1,1536,4,128]{3,1,2,0:T(8,128)} %copy-done.9) | copy-start | bytes 9437188
  2218.9 103.9 %copy-start.11 = (f32[1,1536,4,128]{3,1,2,0:T(8,128)S(1)}, f32[1,1536,4,128]{3,1,2,0:T(8,128)}, u32[]{:S(2)}) copy-start(f32[1,1536,4,128]{3,1,2,0:T(8,128)} %fusion.21) | copy-start | bytes 9437188
  2224.3 102.0 %copy-start.22 = (f32[512,64]{1,0:T(8,128)S(1)}, f32[512,64]{1,0:T(8,128)}, u32[]{:S(2)}) copy-start(f32[512,64]{1,0:T(8,128)} %get-tuple-element.137) | copy-start | bytes 393220
  2224.3 102.0 %copy-start.27 = (f32[512,64]{1,0:T(8,128)S(1)}, f32[512,64]{1,0:T(8,128)}, u32[]{:S(2)}) copy-start(f32[512,64]{1,0:T(8,128)} %get-tuple-element.135) | copy-start | bytes 393220
  2338.9 249.1 %reduce-scatter.13.cloned.1.call-start = ((), (), s32[]{:S(2)}) async-start(), calls=%async_computation.21 | async-start | bytes 2359296 | tf_op jit(solution)/shard_map/reduce_scatter | solution.py:343
  2344.1 364.8 %reduce-scatter.11.cloned.1.call-start = ((), (), s32[]{:S(2)}) async-start(), calls=%async_computation.20 | async-start | bytes 7077888 | tf_op jit(solution)/shard_map/reduce_scatter | solution.py:340
  2589.8 121.6 %copy-start.1 = (bf16[2,352,2048]{2,1,0:T(8,128)(2,1)S(1)}, bf16[2,352,2048]{2,1,0:T(8,128)(2,1)}, u32[]{:S(2)}) copy-start(bf16[2,352,2048]{2,1,0:T(8,128)(2,1)} %param.26) | copy-start | bytes 8650756
  (45 other events, 314.7 us)
Sparse Core Ops, SparseCore 0:
  10.7 102.6 all-gather.6
  115.4 60.2 all-gather.8
  195.9 109.4 all-reduce.10
  874.5 151.9 reduce-scatter.6
  1029.0 153.1 reduce-scatter.8
  1184.2 70.1 all-gather.14
  1256.8 364.6 all-gather.10
  1623.8 90.8 all-gather.12
  1716.3 68.3 all-gather.16
  1787.3 153.2 all-reduce.16
  1945.3 165.8 reduce-scatter.16
  2115.0 241.5 reduce-scatter.14
  2361.0 66.7 all-reduce.14
  2430.2 85.4 all-reduce.12
  2519.6 68.3 reduce-scatter.12
  2591.5 117.3 reduce-scatter.10
where the time goes:
time: 2730 us; the launch traced here: 2720 us
  waiting for transfers between devices  1960 us (72%)
  local copies, waits for them, and re-layouts  313 us (11%)
  matrix products  226 us (8%)
  other arithmetic  131 us (5%)
  blocking collectives  37.4 us (1%)
  starting transfers between devices  31.1 us (1%)
    all_to_all x2, waiting for transfers between devices, expert_trip(): lax.all_to_all(outgoing, 'ep', split_axis=0, concat_axis=1, tiled=True)  417 us
    all_gather x1, waiting for transfers between devices, per_device(): lax.all_gather(shared_in, 'ep', axis=1, tiled=True)  335 us
    reduce_scatter x2, waiting for transfers between devices, expert_trip(): lax.psum_scatter(partial_rows, 'tp', scatter_dimension=1, tiled=True)  280 us
    psum x3, waiting for transfers between devices, tensor_total(): return lax.psum(partial_sum, 'tp')  269 us
    ppermute x4, waiting for transfers between devices, shifted(): lax.ppermute(value, axis, [(source, source + steps) for source in range(l...  132 us
    reduce_scatter x1, waiting for transfers between devices, per_device(): lax.psum_scatter(grad_attention_in.astype(jnp.bfloat16), 'ep', scatter_di...  112 us
    all_gather x2, waiting for transfers between devices, expert_trip(): whole_rows = lax.all_gather(share_rows, 'tp', axis=1, tiled=True)  105 us
    all_gather x1, waiting for transfers between devices, per_device(): lax.all_gather(attention_in, 'ep', axis=1, tiled=True)  95.7 us
  transfers between devices with their start and end apart: 24, of which 19 were waited for; matrix products, arithmetic and copies ran while one was open for 20% of the time, Pallas kernels for 0%

commit v1 on v0

--- a/solution.py
+++ b/solution.py
@@ -1,10 +1,14 @@
+import functools
 import math
 
 import jax
 import jax.numpy as jnp
 from jax import lax
+from jax.experimental import pallas as pl
+from jax.experimental.pallas import tpu as pltpu
 from jax.sharding import PartitionSpec as P
 
+EP, TP = "ep", "tp"
 HD = 128
 WINDOW = 1024
 
@@ -22,7 +26,7 @@
 
 
 def tensor_total(partial_sum):
-    return lax.psum(partial_sum, "tp")
+    return lax.psum(partial_sum, TP)
 
 
 def rms_parts(values):
@@ -75,7 +79,1391 @@
     return (gate_pre * sig_gate, sig_gate * (1.0 + gate_pre * (1.0 - sig_gate)))
 
 
-def per_device(
+NN = (((1,), (0,)), ((), ()))
+NT = (((1,), (1,)), ((), ()))
+TN = (((0,), (0,)), ((), ()))
+
+
+def product(left, right, dims=NN):
+    return lax.dot_general(left, right, dims, preferred_element_type=jnp.float32)
+
+
+def feed_kernel(
+    rank_row, rank_column, gate_row, scale_column, rows, cotangent,
+    expert_in, expert_down, shared,
+    out_part, back_part, slot_rows, slot_cotangent, grad_pre, gated,
+    grad_shared_pre, scaled, token_grad, scale_grad, out_terms, back_terms,
+):
+    bf16, f32 = jnp.bfloat16, jnp.float32
+    experts, _, slots, _ = slot_rows.shape
+    tokens = rows.shape[1]
+    hidden_count = gated.shape[3]
+    all_slots = experts * slots
+    token_rows, token_cotangent = rows[0], cotangent[0]
+    shared_count = scaled.shape[2]
+
+    @pl.when(pl.program_id(0) == 0)
+    def _():
+        out_terms[all_slots:, :] = shared[2]
+        back_terms[all_slots : all_slots + shared_count, :] = shared[0]
+        back_terms[all_slots + shared_count :, :] = shared[1]
+
+    silu, slope = silu_parts(product(token_rows, shared[0], NT))
+    up = product(token_rows, shared[1], NT)
+    hidden = (silu * up).astype(bf16).astype(f32)
+    scale = scale_column[0]
+    scaled_hidden = (scale * hidden).astype(bf16)
+    scaled[0] = scaled_hidden
+    back = product(token_cotangent, shared[2], NT)
+    scale_grad[0] = jnp.sum(hidden * back, axis=1, keepdims=True)
+    back = scale * back
+    gate_grad = (back * up * slope).astype(bf16)
+    up_grad = (back * silu).astype(bf16)
+    grad_shared_pre[0, 0] = gate_grad
+    grad_shared_pre[1, 0] = up_grad
+    order = lax.broadcasted_iota(jnp.int32, (all_slots, tokens), 0)
+    spread_order = lax.broadcasted_iota(jnp.int32, (tokens, all_slots), 1)
+    hits, spread = None, None
+    for expert in range(experts):
+        row_hits = order == rank_row[0, expert : expert + 1, :] + expert * slots
+        column_hits = spread_order == rank_column[0, :, expert : expert + 1] + expert * slots
+        hits = row_hits if hits is None else hits | row_hits
+        spread = column_hits if spread is None else spread | column_hits
+    place = hits.astype(bf16)
+    taken = product(place, token_rows).astype(bf16)
+    taken_cotangent = product(place, token_cotangent).astype(bf16)
+    for expert in range(experts):
+        mine = slice(expert * slots, (expert + 1) * slots)
+        slot_rows[expert, 0] = taken[mine]
+        slot_cotangent[expert, 0] = taken_cotangent[mine]
+        gate = jnp.sum(
+            jnp.where(hits[mine], gate_row[0, expert : expert + 1, :], 0.0), axis=1, keepdims=True
+        )
+        pre = product(taken[mine], expert_in[expert])
+        silu, slope = silu_parts(pre[:, :hidden_count])
+        up = pre[:, hidden_count:]
+        hidden = (silu * up).astype(bf16).astype(f32)
+        gated_hidden = (gate * hidden).astype(bf16)
+        gated[expert, 0] = gated_hidden
+        back = product(taken_cotangent[mine], expert_down[expert], NT)
+        slot_grad = jnp.sum(hidden * back, axis=1, keepdims=True)
+        token_grad[0, expert : expert + 1, :] = jnp.sum(
+            jnp.where(hits[mine], slot_grad, 0.0), axis=0, keepdims=True
+        )
+        back = gate * back
+        gate_grad_e = (back * up * slope).astype(bf16)
+        up_grad_e = (back * silu).astype(bf16)
+        grad_pre[0, expert, 0] = gate_grad_e
+        grad_pre[1, expert, 0] = up_grad_e
+        out_terms[mine, :] = product(gated_hidden, expert_down[expert]).astype(bf16)
+        both_grads = jnp.concatenate([gate_grad_e, up_grad_e], axis=1)
+        back_terms[mine, :] = product(both_grads, expert_in[expert], NT).astype(bf16)
+    spread = spread.astype(bf16)
+    out_part[0] = product(
+        jnp.concatenate([spread, scaled_hidden], axis=1), out_terms[...]
+    ).astype(bf16)
+    back_part[0] = product(
+        jnp.concatenate([spread, gate_grad, up_grad], axis=1), back_terms[...]
+    ).astype(bf16)
+
+
+def feed(rank, gates, scale, rows, cotangent, expert_in, expert_down, shared, capacity):
+    bf16, f32 = jnp.bfloat16, jnp.float32
+    blocks, experts, tokens = rank.shape
+    width = rows.shape[2]
+    hidden = expert_in.shape[2] // 2
+    slice_hidden = shared.shape[1]
+    once = pl.Buffered(1)
+
+    def whole(array):
+        return pl.BlockSpec(array.shape, lambda b: (0,) * array.ndim, pipeline_mode=once)
+
+    row_spec = pl.BlockSpec((1, experts, tokens), lambda b: (b, 0, 0))
+    token_spec = pl.BlockSpec((1, tokens, width), lambda b: (b, 0, 0))
+    slot_spec = pl.BlockSpec((experts, 1, capacity, width), lambda b: (0, b, 0, 0))
+    shape = jax.ShapeDtypeStruct
+    return pl.pallas_call(
+        feed_kernel,
+        grid=(blocks,),
+        in_specs=[
+            row_spec,
+            pl.BlockSpec((1, tokens, experts), lambda b: (b, 0, 0)),
+            row_spec,
+            pl.BlockSpec((1, tokens, 1), lambda b: (b, 0, 0)),
+            token_spec,
+            token_spec,
+            whole(expert_in),
+            whole(expert_down),
+            whole(shared),
+        ],
+        out_specs=(
+            token_spec,
+            token_spec,
+            slot_spec,
+            slot_spec,
+            pl.BlockSpec((2, experts, 1, capacity, hidden), lambda b: (0, 0, b, 0, 0)),
+            pl.BlockSpec((experts, 1, capacity, hidden), lambda b: (0, b, 0, 0)),
+            pl.BlockSpec((2, 1, tokens, slice_hidden), lambda b: (0, b, 0, 0)),
+            pl.BlockSpec((1, tokens, slice_hidden), lambda b: (b, 0, 0)),
+            row_spec,
+            pl.BlockSpec((1, tokens, 1), lambda b: (b, 0, 0)),
+        ),
+        out_shape=(
+            shape((blocks, tokens, width), bf16),
+            shape((blocks, tokens, width), bf16),
+            shape((experts, blocks, capacity, width), bf16),
+            shape((experts, blocks, capacity, width), bf16),
+            shape((2, experts, blocks, capacity, hidden), bf16),
+            shape((experts, blocks, capacity, hidden), bf16),
+            shape((2, blocks, tokens, slice_hidden), bf16),
+            shape((blocks, tokens, slice_hidden), bf16),
+            shape((blocks, experts, tokens), f32),
+            shape((blocks, tokens, 1), f32),
+        ),
+        scratch_shapes=[
+            pltpu.VMEM((experts * capacity + slice_hidden, width), bf16),
+            pltpu.VMEM((experts * capacity + 2 * slice_hidden, width), bf16),
+        ],
+        compiler_params=pltpu.CompilerParams(vmem_limit_bytes=60 * 2**20),
+        name="feed",
+    )(rank, jnp.swapaxes(rank, 1, 2), gates, scale, rows, cotangent, expert_in, expert_down, shared)
+
+
+def turned(values, cosine, sine):
+    half = values.shape[1] // 2
+    swapped = jnp.concatenate([values[:, half:], values[:, :half]], axis=1)
+    return values * cosine + swapped * sine
+
+
+def project_kernel(rows, gain, weights, bias, cosine, sine, normed, queries, keys_values):
+    bf16, f32 = jnp.bfloat16, jnp.float32
+
+    @pl.when(pl.program_id(0) == 0)
+    def _():
+        _, scaled = rms_parts(rows[...].astype(f32))
+        normed[...] = (scaled * gain[...]).astype(bf16)
+
+    columns = queries.shape[1]
+    for kind in range(3):
+        raw = product(normed[...], weights[kind]) + bias[kind : kind + 1, :]
+        for start in range(0, columns, HD):
+            head = slice(start, start + HD)
+            part = raw[:, head]
+            if kind < 2:
+                part = turned(part, cosine[...], sine[...])
+            if kind == 0:
+                queries[:, head] = part.astype(bf16)
+            else:
+                keys_values[kind - 1, :, head] = part.astype(bf16)
+
+
+def project(rows, gain, weights, bias, cosine, sine):
+    tokens, width = rows.shape
+    columns = weights.shape[2]
+    step = min(2 * HD, columns)
+    shape = jax.ShapeDtypeStruct
+    bf16 = jnp.bfloat16
+
+    def whole(*dims):
+        return pl.BlockSpec(dims, lambda h: (0,) * len(dims))
+
+    return pl.pallas_call(
+        project_kernel,
+        grid=(columns // step,),
+        in_specs=[
+            whole(tokens, width),
+            whole(1, width),
+            pl.BlockSpec((3, width, step), lambda h: (0, 0, h)),
+            pl.BlockSpec((3, step), lambda h: (0, h)),
+            whole(tokens, HD),
+            whole(tokens, HD),
+        ],
+        out_specs=(
+            whole(tokens, width),
+            pl.BlockSpec((tokens, step), lambda h: (0, h)),
+            pl.BlockSpec((2, tokens, step), lambda h: (0, 0, h)),
+        ),
+        out_shape=(
+            shape((tokens, width), bf16),
+            shape((tokens, columns), bf16),
+            shape((2, tokens, columns), bf16),
+        ),
+        compiler_params=pltpu.CompilerParams(vmem_limit_bytes=40 * 2**20),
+        name="project",
+    )(rows, gain[None], weights, bias, cosine, sine)
+
+
+def masked_scores(queries, keys, query_doc, key_doc):
+    tokens, count = queries.shape[0], keys.shape[0]
+    scores = product(queries, keys, NT) * (1.0 / math.sqrt(HD))
+    ahead = lax.broadcasted_iota(jnp.int32, (tokens, count), 0) + (count - tokens)
+    distance = ahead - lax.broadcasted_iota(jnp.int32, (tokens, count), 1)
+    allowed = (query_doc == key_doc) & (distance >= 0) & (distance < WINDOW)
+    return jnp.where(allowed, scores, MASKED)
+
+
+def attend_kernel(queries, keys, values, query_doc, key_doc, valid, heads, log_totals):
+    count = keys.shape[1] * keys.shape[2]
+    keys, values = keys[0].reshape(count, HD), values[0].reshape(count, HD)
+    scores = masked_scores(queries[...], keys, query_doc[...], key_doc[...])
+    row_max = jnp.max(scores, axis=1, keepdims=True)
+    terms = jnp.exp(scores - row_max)
+    total = jnp.sum(terms, axis=1, keepdims=True)
+    weights = (terms / total).astype(jnp.bfloat16)
+    heads[...] = (product(weights, values) * valid[...]).astype(jnp.bfloat16)
+    log_totals[0] = row_max + jnp.log(total)
+
+
+def attention_specs(tokens, blocks):
+    def column(*dims):
+        return pl.BlockSpec(dims, lambda h: (0,) * len(dims))
+
+    head = pl.BlockSpec((tokens, HD), lambda h: (0, h))
+    keys = pl.BlockSpec((1, blocks, tokens, HD), lambda h: (0, 0, 0, h))
+    values = pl.BlockSpec((1, blocks, tokens, HD), lambda h: (1, 0, 0, h))
+    logs = pl.BlockSpec((1, tokens, 1), lambda h: (h, 0, 0))
+    return head, keys, values, column(tokens, 1), column(1, blocks * tokens), logs
+
+
+def attend(queries, keys_values, query_doc, key_doc, valid):
+    tokens, columns = queries.shape
+    blocks = keys_values.shape[1]
+    head, keys, values, column, row, logs = attention_specs(tokens, blocks)
+    shape = jax.ShapeDtypeStruct
+    return pl.pallas_call(
+        attend_kernel,
+        grid=(columns // HD,),
+        in_specs=[head, keys, values, column, row, column],
+        out_specs=(head, logs),
+        out_shape=(
+            shape((tokens, columns), jnp.bfloat16),
+            shape((columns // HD, tokens, 1), jnp.float32),
+        ),
+        compiler_params=pltpu.CompilerParams(vmem_limit_bytes=40 * 2**20),
+        name="attend",
+    )(queries, keys_values, keys_values, query_doc, key_doc, valid)
+
+
+def attend_back_kernel(
+    queries, keys, values, query_doc, key_doc, log_totals, grad_heads, cosine, sine,
+    grad_queries, grad_keys_values,
+):
+    bf16 = jnp.bfloat16
+    scale = 1.0 / math.sqrt(HD)
+    blocks, tokens = keys.shape[1], keys.shape[2]
+    keys, values = (ref[0].reshape(blocks * tokens, HD) for ref in (keys, values))
+    scores = masked_scores(queries[...], keys, query_doc[...], key_doc[...])
+    probs = jnp.exp(scores - log_totals[0])
+    grads = grad_heads[...]
+    slopes = product(grads, values, NT)
+    slopes = probs * (slopes - jnp.sum(probs * slopes, axis=1, keepdims=True))
+    grad_scores = slopes.astype(bf16)
+    turned_back = turned(product(grad_scores, keys) * scale, cosine[...], -sine[...])
+    grad_queries[...] = turned_back.astype(bf16)
+    grad_keys = product(grad_scores, queries[...], TN) * scale
+    grad_keys_values[0] = grad_keys.astype(bf16).reshape(blocks, tokens, HD)
+    grad_values = product(probs.astype(bf16), grads, TN)
+    grad_keys_values[1] = grad_values.astype(bf16).reshape(blocks, tokens, HD)
+
+
+def attend_back(queries, keys_values, query_doc, key_doc, log_totals, grad_heads, cosine, sine):
+    tokens, columns = queries.shape
+    blocks = keys_values.shape[1]
+    head, keys, values, column, row, logs = attention_specs(tokens, blocks)
+    angle = pl.BlockSpec((tokens, HD), lambda h: (0, 0))
+    shape = jax.ShapeDtypeStruct
+    return pl.pallas_call(
+        attend_back_kernel,
+        grid=(columns // HD,),
+        in_specs=[head, keys, values, column, row, logs, head, angle, angle],
+        out_specs=(head, pl.BlockSpec((2, blocks, tokens, HD), lambda h: (0, 0, 0, h))),
+        out_shape=(
+            shape((tokens, columns), jnp.bfloat16),
+            shape(keys_values.shape, jnp.bfloat16),
+        ),
+        compiler_params=pltpu.CompilerParams(vmem_limit_bytes=48 * 2**20),
+        name="attend_back",
+    )(queries, keys_values, keys_values, query_doc, key_doc, log_totals, grad_heads, cosine, sine)
+
+
+RING = 8
+NO_SLOT = 1 << 20
+RIGHT, LEFT, OVER_X, OVER_CORE, OVER_FAR, OVER_Y, OVER_Z, LOCAL = range(8)
+MESH_ID = pl.DeviceIdType.MESH
+
+
+def ring_place(ep):
+    z, y = ep // 2, ep % 2
+    return z + y * (7 - 2 * z)
+
+
+def ring_member(place):
+    upper = place // 4
+    return 2 * place + upper * (15 - 4 * place)
+
+
+class Peers:
+    def __init__(self):
+        self.ep, self.tp = lax.axis_index(EP), lax.axis_index(TP)
+        self.x, self.core = self.tp // 2, self.tp % 2
+        self.z, self.y = self.ep // 2, self.ep % 2
+        self.place = ring_place(self.ep)
+        self.right = (self.block(1), self.tp)
+        self.left = (self.block(RING - 1), self.tp)
+        self.quarter = self.tp
+        self.x_quarter = (1 - self.x) * 2 + self.core
+        self.core_quarter = self.x * 2 + 1 - self.core
+        self.far_quarter = (1 - self.x) * 2 + 1 - self.core
+        self.x_peer = (self.ep, self.x_quarter)
+        self.core_peer = (self.ep, self.core_quarter)
+        self.far_peer = (self.ep, self.far_quarter)
+        self.y_peer = (self.z * 2 + 1 - self.y, self.tp)
+
+    def block(self, step):
+        return ring_member((self.place + step + RING) % RING)
+
+
+def greet(peers):
+    barrier = pltpu.get_barrier_semaphore()
+    for peer in peers:
+        pl.semaphore_signal(barrier, inc=1, device_id=peer, device_id_type=MESH_ID)
+    pl.semaphore_wait(barrier, len(peers))
+
+
+class Copies:
+    def __init__(self, send_sems, recv_sems):
+        self.send_sems, self.recv_sems = send_sems, recv_sems
+        self.count = 0
+        self.sent = []
+        self.landing = {}
+
+    def describe(self, source, target, peer, index):
+        return pltpu.make_async_remote_copy(
+            src_ref=source,
+            dst_ref=target,
+            send_sem=self.send_sems.at[index],
+            recv_sem=self.recv_sems.at[index],
+            device_id=peer,
+            device_id_type=MESH_ID,
+        )
+
+    def send(self, key, source, target, landing, peer):
+        index = self.count
+        self.count += 1
+        copy = self.describe(source, target, peer, index)
+        copy.start()
+        self.sent.append(copy)
+        self.landing[key] = self.describe(landing, landing, peer, index).wait_recv
+
+    def local(self, key, source, target):
+        index = self.count
+        self.count += 1
+        copy = pltpu.make_async_copy(source, target, self.send_sems.at[index])
+        copy.start()
+        self.landing[key] = copy.wait
+
+    def arrive(self, *key):
+        self.landing.pop(key)()
+
+    def finish(self):
+        for wait in self.landing.values():
+            wait()
+        for copy in self.sent:
+            copy.wait_send()
+
+
+def remote_params(collective_id, vmem=48):
+    return pltpu.CompilerParams(
+        collective_id=collective_id, has_side_effects=True, vmem_limit_bytes=vmem * 2**20
+    )
+
+
+def semaphores(count):
+    return [pltpu.SemaphoreType.DMA((count,))] * 2
+
+
+IN_PLACE = pl.BlockSpec(memory_space=pl.ANY)
+IN_VMEM = pl.BlockSpec(memory_space=pltpu.VMEM)
+
+
+def gather_kernel(rows, scales, out, out_scales, send_sems, recv_sems):
+    me = Peers()
+    copies = Copies(send_sems, recv_sems)
+    count = rows.shape[0]
+    half, part = count // 2, count // 4
+    q, qx, qc, qd = me.quarter, me.x_quarter, me.core_quarter, me.far_quarter
+    here = me.block(0)
+    low, high, whole = pl.ds(0, half), pl.ds(half, half), pl.ds(0, count)
+    own, other, scale = range(3)
+    sides = ((RIGHT, me.right, -1, 0), (LEFT, me.left, 1, 1))
+    greet([me.right, me.left, me.x_peer, me.core_peer, me.far_peer])
+
+    def cells(step, quarter, which):
+        return out.at[me.block(step), quarter, which]
+
+    def push(key, step, quarter, which, peer, landing_step, landing_quarter, source=None):
+        cell = cells(step, quarter, which)
+        copies.send(
+            key,
+            cell if source is None else source,
+            cell,
+            cells(landing_step, landing_quarter, which),
+            peer,
+        )
+
+    push((OVER_X, other, 0), 0, q, low, me.x_peer, 0, qx, rows.at[low])
+    push((RIGHT, own, 1), 0, q, whole, me.right, -1, q, rows)
+    push((LEFT, own, 1), 0, q, whole, me.left, 1, q, rows)
+    push((OVER_X, own, 0), 0, q, high, me.x_peer, 0, qx, rows.at[high])
+    push((OVER_CORE, own, 0), 0, q, whole, me.core_peer, 0, qc, rows)
+    copies.local((LOCAL, own), rows, out.at[here, q])
+    for way, peer, quarter in (
+        (OVER_X, me.x_peer, qx),
+        (OVER_CORE, me.core_peer, qc),
+        (OVER_FAR, me.far_peer, qd),
+    ):
+        copies.send(
+            (way, scale, 0), scales, out_scales.at[here, q], out_scales.at[here, quarter], peer
+        )
+    copies.local((LOCAL, scale), scales, out_scales.at[here, q])
+    copies.arrive(OVER_X, other, 0)
+    for side, peer, sign, keep in sides:
+        push((side, other, 1), 0, qx, low, peer, sign, qx)
+    for way in (OVER_X, OVER_CORE, OVER_FAR):
+        copies.arrive(way, scale, 0)
+    copies.arrive(LOCAL, scale)
+
+    def push_scales(step, side, peer, sign):
+        blocks = out_scales.at[me.block(step)]
+        copies.send(
+            (side, scale, abs(step) + 1), blocks, blocks, out_scales.at[me.block(step + sign)], peer
+        )
+
+    for side, peer, sign, keep in sides:
+        push_scales(0, side, peer, sign)
+    copies.arrive(OVER_X, own, 0)
+    push((OVER_CORE, other, 0), 0, qx, whole, me.core_peer, 0, qd)
+    waiting = []
+    for hop in (1, 2, 3):
+        for side, peer, sign, keep in sides:
+            step = sign * hop
+            copies.arrive(side, own, hop)
+            which = whole if hop < 3 else pl.ds(keep * half, half)
+            push((side, own, hop + 1), step, q, which, peer, step + sign, q)
+            push((OVER_X, own, step), step, q, high, me.x_peer, step, qx)
+            push((OVER_CORE, own, step), step, q, whole, me.core_peer, step, qc)
+        for side, peer, sign, keep in sides:
+            step = sign * hop
+            copies.arrive(side, other, hop)
+            which = low if hop < 3 else pl.ds(keep * part, part)
+            push((side, other, hop + 1), step, qx, which, peer, step + sign, qx)
+            push((OVER_CORE, other, step), step, qx, low, me.core_peer, step, qd)
+            copies.arrive(side, scale, hop)
+            if hop < 3 or side == RIGHT:
+                push_scales(step, side, peer, sign)
+        for step in waiting:
+            copies.arrive(OVER_X, own, step)
+            push((OVER_CORE, scale, step), step, qx, high, me.core_peer, step, qd)
+        waiting = [-hop, hop]
+    copies.arrive(LEFT, own, 4)
+    push((OVER_X, own, 4), 4, q, high, me.x_peer, 4, qx)
+    copies.arrive(RIGHT, own, 4)
+    push((OVER_CORE, own, 4), 4, q, whole, me.core_peer, 4, qc)
+    copies.arrive(LEFT, other, 4)
+    copies.arrive(RIGHT, other, 4)
+    push((OVER_CORE, other, 4), 4, qx, low, me.core_peer, 4, qd)
+    for step in waiting + [4]:
+        copies.arrive(OVER_X, own, step)
+        push((OVER_CORE, scale, step), step, qx, high, me.core_peer, step, qd)
+    copies.finish()
+
+
+def gather_rows(rows, scales, collective_id):
+    return pl.pallas_call(
+        gather_kernel,
+        out_shape=(
+            jax.ShapeDtypeStruct((RING, 4) + rows.shape, rows.dtype),
+            jax.ShapeDtypeStruct((RING, 4) + scales.shape, scales.dtype),
+        ),
+        in_specs=[IN_PLACE] * 2,
+        out_specs=(IN_PLACE,) * 2,
+        scratch_shapes=semaphores(80),
+        compiler_params=remote_params(collective_id),
+        name="gather_rows",
+    )(rows, scales)
+
+
+def add_into(total, term, rows, tile=32):
+    tile = min(tile, rows)
+
+    def step(index, carry):
+        here = pl.ds(pl.multiple_of(index * tile, tile), tile)
+        summed = total[here, :].astype(jnp.float32) + term[here, :].astype(jnp.float32)
+        total[here, :] = summed.astype(total.dtype)
+        return carry
+
+    lax.fori_loop(0, rows // tile, step, 0)
+
+
+def scatter_kernel(
+    part, scalars, out, out_scalars,
+    held, core_in, x_in, ring_q, ring_x, last_in,
+    s_held, s_core, s_x, s_ring,
+    send_sems, recv_sems,
+):
+    me = Peers()
+    copies = Copies(send_sems, recv_sems)
+    count = part.shape[2]
+    half, piece = count // 2, count // 4
+    q, qx, qc, qd = me.quarter, me.x_quarter, me.core_quarter, me.far_quarter
+    own, other, scale, last = range(4)
+    peers = {RIGHT: me.right, LEFT: me.left}
+    greet([me.right, me.left, me.x_peer, me.core_peer])
+    order = (4, 3, 5, 2, 6, 1, 7, 0)
+    for k in order:
+        for slot, mine, theirs in ((0, q, qc), (1, qx, qd)):
+            copies.local((LOCAL, k, slot), part.at[me.block(k), mine], held.at[k, slot])
+            target = core_in.at[k, slot]
+            copies.send(
+                (OVER_CORE, k, slot), part.at[me.block(k), theirs], target, target, me.core_peer
+            )
+    for k in range(RING):
+        for slot, mine, theirs in ((0, q, qc), (1, qx, qd)):
+            copies.local((LOCAL, scale, k, slot), scalars.at[me.block(k), mine], s_held.at[slot, k])
+            target = s_core.at[slot, k]
+            copies.send(
+                (OVER_CORE, scale, k, slot),
+                scalars.at[me.block(k), theirs],
+                target,
+                target,
+                me.core_peer,
+            )
+
+    def prepare(k):
+        for slot in (1, 0):
+            copies.arrive(LOCAL, k, slot)
+            copies.arrive(OVER_CORE, k, slot)
+            add_into(held.at[k, slot], core_in.at[k, slot], count)
+            if slot == 1:
+                source = held.at[k, 1, pl.ds(half, half)]
+                copies.send((OVER_X, k), source, x_in.at[k], x_in.at[k], me.x_peer)
+
+    def over_x(k):
+        copies.arrive(OVER_X, k)
+        add_into(held.at[k, 0, pl.ds(half, half)], x_in.at[k], half)
+
+    def pass_on(side, hop, k):
+        if hop == 0:
+            rows_q, rows_x = pl.ds(side * half, half), pl.ds(side * piece, piece)
+        else:
+            rows_q, rows_x = pl.ds(0, count), pl.ds(0, half)
+        for kind, landing, rows in ((own, ring_q, rows_q), (other, ring_x, rows_x)):
+            target = landing.at[side, hop, rows]
+            copies.send((side, kind, hop), held.at[k, kind].at[rows], target, target, peers[side])
+
+    def take_in(side, hop, k):
+        if hop == 0:
+            span_q, span_x, at_q, at_x = half, piece, side * half, side * piece
+        else:
+            span_q, span_x, at_q, at_x = count, half, 0, 0
+        for kind, landing, span, at in ((own, ring_q, span_q, at_q), (other, ring_x, span_x, at_x)):
+            copies.arrive(side, kind, hop)
+            rows = pl.ds(at, span)
+            add_into(held.at[k, kind, rows], landing.at[side, hop, rows], span)
+
+    def pass_scalars(side, hop, k):
+        target = s_ring.at[side, hop]
+        copies.send((side, scale, hop), s_held.at[0, k], target, target, peers[side])
+
+    def take_scalars(side, hop, k):
+        copies.arrive(side, scale, hop)
+        s_held[0, k] += s_ring[side, hop]
+
+    prepare(4)
+    prepare(3)
+    prepare(5)
+    over_x(4)
+    pass_on(RIGHT, 0, 4)
+    pass_on(LEFT, 0, 4)
+    prepare(2)
+    prepare(6)
+    for k in range(RING):
+        for slot in (0, 1):
+            copies.arrive(LOCAL, scale, k, slot)
+            copies.arrive(OVER_CORE, scale, k, slot)
+    s_held[...] += s_core[...]
+    copies.send((OVER_X, scale, scale), s_held.at[1], s_x, s_x, me.x_peer)
+    over_x(3)
+    over_x(5)
+    for hop, right_block, left_block, later in ((1, 3, 5, (1, 7)), (2, 2, 6, (0,)), (3, 1, 7, ())):
+        take_in(RIGHT, hop - 1, right_block)
+        pass_on(RIGHT, hop, right_block)
+        take_in(LEFT, hop - 1, left_block)
+        pass_on(LEFT, hop, left_block)
+        if hop == 1:
+            copies.arrive(OVER_X, scale, scale)
+            s_held[0] += s_x[...]
+            pass_scalars(RIGHT, 0, 4)
+        else:
+            take_scalars(RIGHT, hop - 2, right_block + 1)
+            if hop == 3:
+                take_scalars(LEFT, hop - 2, left_block - 1)
+            pass_scalars(RIGHT, hop - 1, right_block + 1)
+            pass_scalars(LEFT, hop - 1, left_block - 1)
+        for k in later:
+            prepare(k)
+        if hop == 1:
+            over_x(2)
+            over_x(6)
+        elif hop == 2:
+            over_x(1)
+            over_x(7)
+    over_x(0)
+    take_in(RIGHT, 3, 0)
+    for side, k in ((RIGHT, 1), (LEFT, 7)):
+        take_scalars(side, 2, k)
+        pass_scalars(side, 3, k)
+    take_in(LEFT, 3, 0)
+    copies.send((OVER_X, last, last), held.at[0, 1, pl.ds(0, half)], last_in, last_in, me.x_peer)
+    take_scalars(RIGHT, 3, 0)
+    take_scalars(LEFT, 3, 0)
+    out_scalars[...] = s_held[0, 0]
+    out[pl.ds(half, half), :] = held[0, 0, pl.ds(half, half), :].astype(out.dtype)
+    copies.arrive(OVER_X, last, last)
+    out[pl.ds(0, half), :] = (
+        held[0, 0, pl.ds(0, half), :].astype(jnp.float32) + last_in[...].astype(jnp.float32)
+    ).astype(out.dtype)
+    copies.finish()
+
+
+def scatter_rows(part, scalars, collective_id):
+    ring, quarters, count, width = part.shape
+    half = count // 2
+    dtype = part.dtype
+    s_shape = scalars.shape[2:]
+    return pl.pallas_call(
+        scatter_kernel,
+        out_shape=(
+            jax.ShapeDtypeStruct((count, width), jnp.float32),
+            jax.ShapeDtypeStruct(s_shape, jnp.float32),
+        ),
+        in_specs=[IN_PLACE] * 2,
+        out_specs=(IN_VMEM,) * 2,
+        scratch_shapes=[
+            pltpu.VMEM((RING, 2, count, width), dtype),
+            pltpu.VMEM((RING, 2, count, width), dtype),
+            pltpu.VMEM((RING, half, width), dtype),
+            pltpu.VMEM((2, 4, count, width), dtype),
+            pltpu.VMEM((2, 4, half, width), dtype),
+            pltpu.VMEM((half, width), dtype),
+            pltpu.VMEM((2, RING) + s_shape, jnp.float32),
+            pltpu.VMEM((2, RING) + s_shape, jnp.float32),
+            pltpu.VMEM((RING,) + s_shape, jnp.float32),
+            pltpu.VMEM((2, 4) + s_shape, jnp.float32),
+        ]
+        + semaphores(112),
+        compiler_params=remote_params(collective_id),
+        name="scatter_rows",
+    )(part, scalars)
+
+
+def spread_kernel(shard_in, shard_out, full_in, full_out, send_sems, recv_sems):
+    me = Peers()
+    copies = Copies(send_sems, recv_sems)
+    kinds, depth, _ = shard_in.shape
+    rows, columns = shard_out.shape
+    sides = ((RIGHT, me.right, -1), (LEFT, me.left, 1))
+    greet([me.right, me.left])
+
+    def cell(kind, step, part, parts):
+        block = me.block(step)
+        if kind < kinds:
+            return full_in.at[kind, block, pl.ds(part * (depth // parts), depth // parts)]
+        across = pl.ds(pl.multiple_of(block * columns, columns), columns)
+        return full_out.at[pl.ds(part * (rows // parts), rows // parts), across]
+
+    def pass_on(side, peer, sign, kind, hop, source=None):
+        parts = 2 if hop == 3 else 1
+        part = side if hop == 3 else 0
+        step = sign * hop
+        here = cell(kind, step, part, parts)
+        copies.send(
+            (side, kind, hop + 1),
+            here if source is None else source,
+            here,
+            cell(kind, step + sign, part, parts),
+            peer,
+        )
+
+    order = tuple(range(kinds - 1, -1, -1)) + (kinds,)
+    for kind in order:
+        source = shard_in.at[kind] if kind < kinds else shard_out
+        for side, peer, sign in sides:
+            pass_on(side, peer, sign, kind, 0, source)
+        copies.local((LOCAL, kind), source, cell(kind, 0, 0, 1))
+    for hop in (1, 2, 3):
+        for kind in order:
+            for side, peer, sign in sides:
+                copies.arrive(side, kind, hop)
+                pass_on(side, peer, sign, kind, hop)
+    copies.finish()
+
+
+def spread_weights(shard_in, shard_out, collective_id):
+    kinds, depth, width = shard_in.shape
+    rows, columns = shard_out.shape
+    return pl.pallas_call(
+        spread_kernel,
+        out_shape=(
+            jax.ShapeDtypeStruct((kinds, RING, depth, width), shard_in.dtype),
+            jax.ShapeDtypeStruct((rows, RING * columns), shard_out.dtype),
+        ),
+        in_specs=[IN_PLACE] * 2,
+        out_specs=(IN_PLACE,) * 2,
+        scratch_shapes=semaphores(9 * (kinds + 1)),
+        compiler_params=remote_params(collective_id),
+        name="spread_weights",
+    )(shard_in, shard_out)
+
+
+def collect_kernel(
+    grad_in, grad_out, tail, sum_in, sum_out, sum_tail,
+    held_in, held_out, ring_in, ring_out, tails, tail_sums,
+    send_sems, recv_sems,
+):
+    me = Peers()
+    copies = Copies(send_sems, recv_sems)
+    kinds, _, depth, width = grad_in.shape
+    rows, columns = sum_out.shape
+    peers = {RIGHT: me.right, LEFT: me.left}
+    tail_kind = kinds + 1
+    greet([me.right, me.left, me.x_peer, me.core_peer, me.far_peer])
+    order = (4, 3, 5, 2, 6, 1, 7, 0)
+
+    def held(kind, k):
+        return held_in.at[k, kind] if kind < kinds else held_out.at[k]
+
+    def ring(kind, side, hop):
+        return ring_in.at[side, hop, kind] if kind < kinds else ring_out.at[side, hop]
+
+    def span(kind, side, hop):
+        whole = depth if kind < kinds else rows
+        return (side * (whole // 2), whole // 2) if hop == 0 else (0, whole)
+
+    def pass_on(side, hop, k, kind):
+        at = pl.ds(*span(kind, side, hop))
+        target = ring(kind, side, hop).at[at]
+        copies.send((side, kind, hop), held(kind, k).at[at], target, target, peers[side])
+
+    def take_in(side, hop, k, kind):
+        copies.arrive(side, kind, hop)
+        start, size = span(kind, side, hop)
+        at = pl.ds(start, size)
+        add_into(held(kind, k).at[at], ring(kind, side, hop).at[at], size)
+
+    tails[0] = tail[...]
+    for side, place in ((RIGHT, 7), (LEFT, 1)):
+        copies.send((side, tail_kind, 0), tail, tails.at[place], tails.at[place], peers[side])
+    for k in order:
+        block = me.block(k)
+        for kind in range(kinds):
+            copies.local((LOCAL, kind, k), grad_in.at[kind, block], held(kind, k))
+        across = pl.ds(pl.multiple_of(block * columns, columns), columns)
+        copies.local((LOCAL, kinds, k), grad_out.at[:, across], held(kinds, k))
+
+    def ready(*blocks):
+        for k in blocks:
+            for kind in range(kinds + 1):
+                copies.arrive(LOCAL, kind, k)
+
+    ready(4)
+    for kind in range(kinds + 1):
+        for side in (RIGHT, LEFT):
+            pass_on(side, 0, 4, kind)
+    for hop, right_block, left_block in ((1, 3, 5), (2, 2, 6), (3, 1, 7)):
+        ready(right_block, left_block)
+        for kind in range(kinds + 1):
+            for side, k in ((RIGHT, right_block), (LEFT, left_block)):
+                take_in(side, hop - 1, k, kind)
+                pass_on(side, hop, k, kind)
+        for side, place, sign in ((RIGHT, 8 - hop, -1), (LEFT, hop, 1)):
+            copies.arrive(side, tail_kind, hop - 1)
+            if hop < 3 or side == RIGHT:
+                target = tails.at[place + sign]
+                copies.send((side, tail_kind, hop), tails.at[place], target, target, peers[side])
+    copies.arrive(RIGHT, tail_kind, 3)
+    total = tails[0]
+    for place in range(1, RING):
+        total = total + tails[place]
+    tail_sums[me.tp] = total
+    for way, peer, quarter in (
+        (OVER_X, me.x_peer, me.x_quarter),
+        (OVER_CORE, me.core_peer, me.core_quarter),
+        (OVER_FAR, me.far_peer, me.far_quarter),
+    ):
+        copies.send(
+            (way, tail_kind), tail_sums.at[me.tp], tail_sums.at[me.tp], tail_sums.at[quarter], peer
+        )
+    ready(0)
+    for kind in range(kinds + 1):
+        for side in (RIGHT, LEFT):
+            take_in(side, 3, 0, kind)
+    for kind in range(kinds):
+        sum_in[kind] = held_in[0, kind].astype(jnp.float32)
+    sum_out[...] = held_out[0].astype(jnp.float32)
+    for way in (OVER_X, OVER_CORE, OVER_FAR):
+        copies.arrive(way, tail_kind)
+    sum_tail[...] = tail_sums[...]
+    copies.finish()
+
+
+def collect_weights(grad_in, grad_out, tail, collective_id):
+    kinds, ring, depth, width = grad_in.shape
+    rows, columns = grad_out.shape[0], grad_out.shape[1] // ring
+    f32 = jnp.float32
+    return pl.pallas_call(
+        collect_kernel,
+        out_shape=(
+            jax.ShapeDtypeStruct((kinds, depth, width), f32),
+            jax.ShapeDtypeStruct((rows, columns), f32),
+            jax.ShapeDtypeStruct((4,) + tail.shape, f32),
+        ),
+        in_specs=[IN_PLACE, IN_PLACE, IN_VMEM],
+        out_specs=(IN_VMEM,) * 3,
+        scratch_shapes=[
+            pltpu.VMEM((RING, kinds, depth, width), grad_in.dtype),
+            pltpu.VMEM((RING, rows, columns), grad_out.dtype),
+            pltpu.VMEM((2, 4, kinds, depth, width), grad_in.dtype),
+            pltpu.VMEM((2, 4, rows, columns), grad_out.dtype),
+            pltpu.VMEM((RING,) + tail.shape, f32),
+            pltpu.VMEM((4,) + tail.shape, f32),
+        ]
+        + semaphores(96),
+        compiler_params=remote_params(collective_id),
+        name="collect_weights",
+    )(grad_in, grad_out, tail)
+
+
+def greet_along_z(me):
+    barrier = pltpu.get_barrier_semaphore()
+    pl.semaphore_signal(barrier, inc=1, device_id=me.y_peer, device_id_type=MESH_ID)
+
+    @pl.when(me.z > 0)
+    def _():
+        peer = (me.ep - 2, me.tp)
+        pl.semaphore_signal(barrier, inc=1, device_id=peer, device_id_type=MESH_ID)
+
+    @pl.when(me.z < 3)
+    def _():
+        peer = (me.ep + 2, me.tp)
+        pl.semaphore_signal(barrier, inc=1, device_id=peer, device_id_type=MESH_ID)
+
+    pl.semaphore_wait(barrier, 1 + (me.z + 2) // 3 + (5 - me.z) // 3)
+
+
+def share_kernel(own, out, send_sems, recv_sems):
+    me = Peers()
+    kinds, tokens, _ = own.shape
+    pieces = 2
+    size = tokens // pieces
+    parts = [(kind, pl.ds(piece * size, size)) for kind in range(kinds) for piece in range(pieces)]
+    count = len(parts)
+    greet_along_z(me)
+
+    def copy(index, source, target, peer):
+        return Copies(send_sems, recv_sems).describe(source, target, peer, index)
+
+    def upward(index, kind, rows):
+        return copy(index, own.at[kind, rows], out.at[kind, 0, rows], (me.ep + 2, me.tp))
+
+    def sideways(index, kind, rows):
+        return copy(count + index, own.at[kind, rows], out.at[kind, 1, rows], me.y_peer)
+
+    def onward(index, kind, rows):
+        return copy(count + index, out.at[kind, 0, rows], out.at[kind, 1, rows], me.y_peer)
+
+    @pl.when(me.z < 3)
+    def _():
+        for index, (kind, rows) in enumerate(parts):
+            upward(index, kind, rows).start()
+
+    @pl.when(me.y == 0)
+    def _():
+        for index, (kind, rows) in enumerate(parts):
+            sideways(index, kind, rows).start()
+
+    out[:, 2] = own[...]
+
+    @pl.when(me.z == 0)
+    def _():
+        out[:, 0] = jnp.zeros_like(own)
+
+    @pl.when((me.z == 0) & (me.y == 0))
+    def _():
+        out[:, 1] = jnp.zeros_like(own)
+
+    @pl.when(me.z > 0)
+    def _():
+        for index, (kind, rows) in enumerate(parts):
+            upward(index, kind, rows).wait_recv()
+
+            @pl.when(me.y == 1)
+            def _():
+                onward(index, kind, rows).start()
+
+    @pl.when(me.y == 1)
+    def _():
+        for index, (kind, rows) in enumerate(parts):
+            sideways(index, kind, rows).wait_recv()
+
+    @pl.when((me.y == 0) & (me.z > 0))
+    def _():
+        for index, (kind, rows) in enumerate(parts):
+            onward(index, kind, rows).wait_recv()
+
+    @pl.when(me.z < 3)
+    def _():
+        for index, (kind, rows) in enumerate(parts):
+            upward(index, kind, rows).wait_send()
+
+    @pl.when((me.y == 0) | (me.z > 0))
+    def _():
+        for index, (kind, rows) in enumerate(parts):
+            sideways(index, kind, rows).wait_send()
+
+
+def share_keys(own, collective_id):
+    kinds, tokens, width = own.shape
+    return pl.pallas_call(
+        share_kernel,
+        out_shape=jax.ShapeDtypeStruct((kinds, 3, tokens, width), own.dtype),
+        in_specs=[IN_VMEM],
+        out_specs=IN_VMEM,
+        scratch_shapes=semaphores(8),
+        compiler_params=remote_params(collective_id),
+        name="share_keys",
+    )(own)
+
+
+def return_kernel(grads, cosine, sine, out, total, from_y, from_z, send_sems, recv_sems):
+    me = Peers()
+    kinds, _, tokens, _ = grads.shape
+    pieces = 2
+    size = tokens // pieces
+    parts = [(kind, pl.ds(piece * size, size)) for kind in range(kinds) for piece in range(pieces)]
+    count = len(parts)
+    greet_along_z(me)
+
+    def copy(index, source, target, peer):
+        return Copies(send_sems, recv_sems).describe(source, target, peer, index)
+
+    def sideways(index, kind, rows):
+        return copy(index, grads.at[kind, 1, rows], from_y.at[kind, rows], me.y_peer)
+
+    def downward(index, kind, rows, source):
+        return copy(count + index, source.at[kind, rows], from_z.at[kind, rows], (me.ep - 2, me.tp))
+
+    for index, (kind, rows) in enumerate(parts):
+        sideways(index, kind, rows).start()
+
+    @pl.when((me.z > 0) & (me.y == 0))
+    def _():
+        for index, (kind, rows) in enumerate(parts):
+            downward(index, kind, rows, grads.at[:, 0]).start()
+
+    for index, (kind, rows) in enumerate(parts):
+        sideways(index, kind, rows).wait_recv()
+        here = grads[kind, 2, rows, :].astype(jnp.float32)
+
+        @pl.when(me.y == 0)
+        def _():
+            total[kind, rows, :] = here + from_y[kind, rows, :].astype(jnp.float32)
+
+        @pl.when(me.y == 1)
+        def _():
+            total[kind, rows, :] = here
+            two_back = grads[kind, 0, rows, :].astype(jnp.float32)
+            summed = two_back + from_y[kind, rows, :].astype(jnp.float32)
+            from_y[kind, rows, :] = summed.astype(from_y.dtype)
+
+        @pl.when((me.z > 0) & (me.y == 1))
+        def _():
+            downward(index, kind, rows, from_y).start()
+
+    @pl.when(me.z < 3)
+    def _():
+        for index, (kind, rows) in enumerate(parts):
+            downward(index, kind, rows, from_y).wait_recv()
+            total[kind, rows, :] += from_z[kind, rows, :].astype(jnp.float32)
+
+    for start in range(0, total.shape[2], HD):
+        head = slice(start, start + HD)
+        out[0, :, head] = turned(total[0, :, head], cosine[...], -sine[...]).astype(out.dtype)
+    out[1] = total[1].astype(out.dtype)
+    for index, (kind, rows) in enumerate(parts):
+        sideways(index, kind, rows).wait_send()
+
+    @pl.when(me.z > 0)
+    def _():
+        for index, (kind, rows) in enumerate(parts):
+            downward(index, kind, rows, from_y).wait_send()
+
+
+def return_keys(grads, cosine, sine, collective_id):
+    kinds, _, tokens, width = grads.shape
+    return pl.pallas_call(
+        return_kernel,
+        out_shape=jax.ShapeDtypeStruct((kinds, tokens, width), grads.dtype),
+        in_specs=[IN_VMEM] * 3,
+        out_specs=IN_VMEM,
+        scratch_shapes=[
+            pltpu.VMEM((kinds, tokens, width), jnp.float32),
+            pltpu.VMEM((kinds, tokens, width), grads.dtype),
+            pltpu.VMEM((kinds, tokens, width), grads.dtype),
+        ]
+        + semaphores(8),
+        compiler_params=remote_params(collective_id),
+        name="return_keys",
+    )(grads, cosine, sine)
+
+
+def reduce_kernel(flip, left, right, out, core_out, core_in, x_out, x_in, send_sems, recv_sems):
+    me = Peers()
+    copies = Copies(send_sems, recv_sems)
+    terms = left.shape[0]
+    count = out.shape[0]
+    f32 = jnp.float32
+    greet([me.x_peer, me.core_peer])
+
+    def quarter(index):
+        rows = pl.ds(pl.multiple_of(index * count, count), count)
+        total = None
+        for term in range(terms):
+            one = product(left[term, rows, :], right[term], NT if flip else NN)
+            total = one if total is None else total + one
+        return total
+
+    for slot, index in ((1, me.far_quarter), (0, me.core_quarter)):
+        core_out[slot] = quarter(index).astype(core_out.dtype)
+        target = core_in.at[slot]
+        copies.send((OVER_CORE, slot), core_out.at[slot], target, target, me.core_peer)
+    mine = quarter(me.x_quarter)
+    copies.arrive(OVER_CORE, 1)
+    x_out[...] = (mine + core_in[1].astype(f32)).astype(x_out.dtype)
+    copies.send((OVER_X,), x_out, x_in, x_in, me.x_peer)
+    mine = quarter(me.quarter)
+    copies.arrive(OVER_CORE, 0)
+    out[...] = mine + core_in[0].astype(f32)
+    copies.arrive(OVER_X)
+    out[...] += x_in[...].astype(f32)
+    copies.finish()
+
+
+def product_to_owner(left, right, flip, collective_id):
+    tokens = left.shape[1]
+    width = right.shape[1] if flip else right.shape[2]
+    count = tokens // 4
+    bf16 = jnp.bfloat16
+    return pl.pallas_call(
+        functools.partial(reduce_kernel, flip),
+        out_shape=jax.ShapeDtypeStruct((count, width), jnp.float32),
+        in_specs=[IN_VMEM] * 2,
+        out_specs=IN_VMEM,
+        scratch_shapes=[
+            pltpu.VMEM((2, count, width), bf16),
+            pltpu.VMEM((2, count, width), bf16),
+            pltpu.VMEM((count, width), bf16),
+            pltpu.VMEM((count, width), bf16),
+        ]
+        + semaphores(3),
+        compiler_params=remote_params(collective_id),
+        name="product_to_owner",
+    )(left, right)
+
+
+def tensor_kernel(rows, out, send_sems, recv_sems):
+    me = Peers()
+    copies = Copies(send_sems, recv_sems)
+    greet([me.x_peer, me.core_peer])
+    mine = out.at[me.quarter]
+    copies.send((OVER_X,), rows, mine, out.at[me.x_quarter], me.x_peer)
+    copies.send((OVER_CORE, 0), rows, mine, out.at[me.core_quarter], me.core_peer)
+    copies.local((LOCAL,), rows, mine)
+    copies.arrive(OVER_X)
+    beside = out.at[me.x_quarter]
+    copies.send((OVER_CORE, 1), beside, beside, out.at[me.far_quarter], me.core_peer)
+    copies.finish()
+
+
+def tensor_gather(rows, collective_id):
+    return pl.pallas_call(
+        tensor_kernel,
+        out_shape=jax.ShapeDtypeStruct((4,) + rows.shape, rows.dtype),
+        in_specs=[IN_PLACE],
+        out_specs=IN_PLACE,
+        scratch_shapes=semaphores(4),
+        compiler_params=remote_params(collective_id),
+        name="tensor_gather",
+    )(rows)
+
+
+def own_rows(block, tp_index, count):
+    return lax.dynamic_slice_in_dim(block, tp_index * count, count, 0)
+
+
+def after(value, earlier):
+    return lax.optimization_barrier((value, earlier))[0]
+
+
+def per_device_dense(
+    layer_input,
+    attention_gain,
+    attention_in,
+    attention_bias,
+    attention_out,
+    feedforward_gain,
+    shared_in,
+    shared_down,
+    shared_gate,
+    router,
+    expert_in,
+    expert_down,
+    routes,
+    document_lengths,
+    cotangent,
+):
+    bf16 = jnp.bfloat16
+    f32 = jnp.float32
+    both = (EP, TP)
+    tok_count, model_width = layer_input.shape
+    expert_count = router.shape[1]
+    top_count = routes.shape[1]
+    ep_size = lax.axis_size(EP)
+    tp_size = lax.axis_size(TP)
+    ep_index = lax.axis_index(EP)
+    tp_index = lax.axis_index(TP)
+    own_count = tok_count // tp_size
+    all_count = tok_count * ep_size
+    capacity = tp_size * (
+        (5 * tok_count * top_count + 4 * expert_count * tp_size - 1) // (4 * expert_count * tp_size)
+    )
+    reach_back = min((WINDOW + tok_count - 2) // tok_count, ep_size - 1)
+    local_experts = expert_in.shape[0]
+    in_blocks, out_full = spread_weights(attention_in, attention_out, 0)
+    in_full = in_blocks.reshape(3, model_width, -1)
+    all_cotangent = lax.all_gather(
+        after(own_rows(cotangent, tp_index, own_count), in_blocks), both, axis=0, tiled=True
+    )
+    shard_width = shared_in.shape[1]
+    slice_hidden = shared_in.shape[2] // ep_size
+    shared_shards = jnp.concatenate([jnp.swapaxes(shared_in, 1, 2), shared_down[None]])
+    shared_shards = jnp.swapaxes(
+        shared_shards.reshape(3, ep_size, slice_hidden, shard_width), 0, 1
+    )
+    shared_slices = lax.all_to_all(
+        after(shared_shards, in_blocks), EP, split_axis=0, concat_axis=0, tiled=True
+    )
+    shared_slices = jnp.transpose(shared_slices, (1, 2, 0, 3)).reshape(
+        3, slice_hidden, model_width
+    )
+    expert_both = jnp.swapaxes(expert_in, 1, 2).reshape(local_experts, model_width, -1)
+
+    positions = ep_index * tok_count + jnp.arange(tok_count, dtype=jnp.int32)
+    key_count = (reach_back + 1) * tok_count
+    key_positions = (ep_index - reach_back) * tok_count + jnp.arange(key_count, dtype=jnp.int32)
+    query_doc, rope_pos, valid_mask = doc_table(document_lengths, positions)
+    query_doc = query_doc[:, None]
+    key_doc = doc_table(document_lengths, key_positions)[0][None, :]
+    valid_rows = valid_mask.astype(f32)[:, None]
+    cosine, sine = (part[:, 0] for part in rope_angles(rope_pos, HD))
+    cosine = jnp.concatenate([cosine, cosine], axis=1)
+    sine = jnp.concatenate([-sine, sine], axis=1)
+    normed_attention, queries, own_kv = project(
+        layer_input, attention_gain, in_full, attention_bias, cosine, sine
+    )
+    keys_values = share_keys(own_kv, 1)
+    heads_low, log_totals = attend(queries, keys_values, query_doc, key_doc, valid_rows)
+    attention_sum = product_to_owner(heads_low[None], out_full[None], False, 2)
+    input_rows = own_rows(layer_input, tp_index, own_count).astype(f32)
+    residual = input_rows + attention_sum
+    inverse_two, normed_two = rms_parts(residual)
+    normed_ffn = normed_two * feedforward_gain
+    normed_low = normed_ffn.astype(bf16)
+    shared_scale = jax.nn.sigmoid(jnp.dot(normed_ffn, shared_gate, precision=HIGHEST))
+    router_probs = jax.nn.softmax(jnp.dot(normed_ffn, router, precision=HIGHEST), axis=-1)
+    routes_own = own_rows(routes, tp_index, own_count)
+    expert_ids = jnp.arange(expert_count, dtype=jnp.int32)
+    picked = jnp.any(routes_own[:, :, None] == expert_ids[None, None, :], axis=1)
+    chosen = jnp.where(picked, router_probs, 0.0)
+    chosen_total = jnp.sum(chosen, axis=1, keepdims=True)
+    gates = chosen / chosen_total
+    scale_count = -(-(expert_count + 1 + top_count) // 8) * 8
+    scale_rows = jnp.zeros((scale_count, own_count), f32)
+    scale_rows = scale_rows.at[:expert_count].set(gates.T).at[expert_count].set(shared_scale)
+    scale_rows = scale_rows.at[expert_count + 1 : expert_count + 1 + top_count].set(
+        routes_own.T.astype(f32)
+    )
+    all_rows, all_scales = gather_rows(normed_low, scale_rows, 3)
+    all_rows = all_rows.reshape(ep_size, tok_count, model_width)
+    all_cotangent = all_cotangent.reshape(ep_size, tok_count, model_width)
+    all_scales = jnp.swapaxes(all_scales, 1, 2).reshape(ep_size, scale_count, tok_count)
+    my_gates = lax.dynamic_slice_in_dim(all_scales, ep_index * local_experts, local_experts, 1)
+    my_ids = ep_index * local_experts + jnp.arange(local_experts, dtype=jnp.int32)
+    all_routes = all_scales[:, expert_count + 1 : expert_count + 1 + top_count].astype(jnp.int32)
+    taken = jnp.any(all_routes[:, None] == my_ids[None, :, None, None], axis=2)
+    earlier_mask = jnp.tril(jnp.ones((tok_count, tok_count), bf16), -1)
+    rank = product(
+        taken.astype(bf16).reshape(-1, tok_count), earlier_mask, NT
+    ).astype(jnp.int32).reshape(taken.shape)
+    rank = jnp.where(taken & (rank < capacity), rank, NO_SLOT)
+    (
+        ffn_part,
+        back_part,
+        slot_rows,
+        slot_cotangent,
+        grad_pre,
+        gated,
+        grad_shared_pre,
+        scaled_hidden,
+        token_grad,
+        scale_grad,
+    ) = feed(
+        rank,
+        my_gates,
+        all_scales[:, expert_count][:, :, None],
+        all_rows,
+        all_cotangent,
+        expert_both,
+        expert_down,
+        shared_slices,
+        capacity,
+    )
+    ffn_sum = lax.psum_scatter(
+        ffn_part.reshape(all_count, model_width), both, scatter_dimension=0, tiled=True
+    )
+    layer_output = lax.all_gather(
+        (residual + ffn_sum.astype(f32)).astype(bf16), TP, axis=0, tiled=True
+    )
+    scalar_part = jnp.zeros((ep_size, scale_count, tok_count), f32)
+    scalar_part = lax.dynamic_update_slice(
+        scalar_part, token_grad, (0, ep_index * local_experts, 0)
+    )
+    scalar_part = scalar_part.at[:, expert_count].set(scale_grad[:, :, 0])
+    scalar_part = jnp.swapaxes(
+        scalar_part.reshape(ep_size, scale_count, tp_size, own_count), 1, 2
+    )
+    back_sum, scalar_sum = scatter_rows(
+        back_part.reshape(ep_size, tp_size, own_count, model_width), scalar_part, 4
+    )
+    scalar_sum = scalar_sum.T
+    slot_rows = slot_rows.reshape(local_experts, -1, model_width)
+    slot_cotangent = slot_cotangent.reshape(slot_rows.shape)
+    grad_pre = grad_pre.reshape(2, local_experts, slot_rows.shape[1], -1)
+    gated = gated.reshape(local_experts, slot_rows.shape[1], -1)
+    grad_expert_down = jnp.einsum(
+        "erf,erd->efd", gated, slot_cotangent, preferred_element_type=f32
+    )
+    grad_expert_in = jnp.einsum(
+        "erd,serf->esdf", slot_rows, grad_pre, preferred_element_type=f32
+    )
+    flat_rows = all_rows.reshape(all_count, model_width)
+    flat_cotangent = all_cotangent.reshape(all_count, model_width)
+    shared_grads = [
+        product(flat_rows, grad_shared_pre[0].reshape(all_count, -1), TN),
+        product(flat_rows, grad_shared_pre[1].reshape(all_count, -1), TN),
+        product(flat_cotangent, scaled_hidden.reshape(all_count, -1), TN),
+    ]
+    shared_grads = jnp.stack([grad.astype(bf16) for grad in shared_grads])
+    shared_grads = jnp.transpose(
+        shared_grads.reshape(3, ep_size, shard_width, slice_hidden), (1, 0, 3, 2)
+    )
+    shared_grads = lax.all_to_all(shared_grads, EP, split_axis=0, concat_axis=0, tiled=True)
+    shared_grads = (
+        jnp.swapaxes(shared_grads, 0, 1).reshape(3, -1, shard_width).astype(f32)
+    )
+    grad_shared_in = jnp.swapaxes(shared_grads[:2], 1, 2)
+    grad_shared_down = shared_grads[2]
+
+    grad_gates = scalar_sum[:, :expert_count]
+    grad_probs = jnp.where(
+        picked,
+        (grad_gates - jnp.sum(grad_gates * gates, axis=1, keepdims=True)) / chosen_total,
+        0.0,
+    )
+    grad_logits = router_probs * (
+        grad_probs - jnp.sum(grad_probs * router_probs, axis=1, keepdims=True)
+    )
+    grad_router = jnp.einsum("td,te->de", normed_ffn, grad_logits, precision=HIGHEST)
+    grad_scale_pre = scalar_sum[:, expert_count] * shared_scale * (1.0 - shared_scale)
+    grad_shared_gate = jnp.dot(grad_scale_pre, normed_ffn, precision=HIGHEST)
+    grad_normed = (
+        back_sum
+        + jnp.einsum("te,de->td", grad_logits, router, precision=HIGHEST)
+        + grad_scale_pre[:, None] * shared_gate[None, :]
+    )
+    grad_mid_norm, grad_feedforward_gain = norm_back(
+        grad_normed, feedforward_gain, inverse_two, normed_two
+    )
+    small = jnp.concatenate([grad_feedforward_gain[None], grad_shared_gate[None], grad_router.T])
+    small = lax.psum(small, both)
+    grad_residual = own_rows(cotangent, tp_index, own_count).astype(f32) + grad_mid_norm
+    grad_attention = tensor_gather(grad_residual.astype(bf16), 5).reshape(tok_count, model_width)
+    grad_attention_out = product(heads_low, grad_attention, TN)
+    grad_heads = (product(grad_attention, out_full, NT) * valid_rows).astype(bf16)
+    grad_queries, grad_kv = attend_back(
+        queries, keys_values, query_doc, key_doc, log_totals, grad_heads, cosine, sine
+    )
+    grad_own_kv = return_keys(grad_kv, cosine, sine, 6)
+    grad_raw = jnp.concatenate([grad_queries[None], grad_own_kv])
+    grad_attention_bias = jnp.sum(grad_raw.astype(f32), axis=1)
+    grad_normed_attention = product_to_owner(grad_raw, in_full, True, 7)
+    inverse_one, normed_one = rms_parts(input_rows)
+    grad_in_norm, grad_attention_gain = norm_back(
+        grad_normed_attention, attention_gain, inverse_one, normed_one
+    )
+    grad_input = tensor_gather((grad_residual + grad_in_norm).astype(bf16), 8)
+    grad_attention_in = jnp.einsum(
+        "td,ste->sde", normed_attention, grad_raw, preferred_element_type=f32
+    )
+    columns = grad_attention_bias.shape[1]
+    tail = jnp.concatenate(
+        [
+            grad_attention_bias,
+            grad_attention_gain.reshape(-1, columns),
+            jnp.zeros((8 - 3 - model_width // columns, columns), f32),
+        ]
+    )
+    grad_attention_in, grad_attention_out, tails = collect_weights(
+        grad_attention_in.astype(bf16).reshape(in_blocks.shape),
+        grad_attention_out.astype(bf16),
+        tail,
+        9,
+    )
+    grad_attention_bias = lax.dynamic_index_in_dim(tails, tp_index, 0, keepdims=False)[:3]
+    grad_attention_gain = jnp.sum(tails[:, 3:], axis=0)[: model_width // columns].reshape(-1)
+    return (
+        layer_output,
+        grad_input.reshape(tok_count, model_width),
+        grad_attention_gain,
+        grad_attention_in,
+        grad_attention_bias,
+        grad_attention_out,
+        small[0],
+        grad_shared_in,
+        grad_shared_down,
+        small[1],
+        small[2:].T,
+        grad_expert_in,
+        grad_expert_down,
+    )
+
+
+def per_device(*arguments):
+    small_slice = lax.axis_size(EP) == RING and lax.axis_size(TP) == 4
+    return (per_device_dense if small_slice else per_device_sparse)(*arguments)
+
+
+def per_device_sparse(
     layer_input,
     attention_gain,
     attention_in,
@@ -98,8 +1486,8 @@
     model_width = layer_input.shape[1]
     expert_count = router.shape[1]
     top_count = routes.shape[1]
-    ep_size = lax.axis_size("ep")
-    tp_size = lax.axis_size("tp")
+    ep_size = lax.axis_size(EP)
+    tp_size = lax.axis_size(TP)
     capacity = tp_size * (
         (5 * tok_count * top_count + 4 * expert_count * tp_size - 1) // (4 * expert_count * tp_size)
     )
@@ -108,12 +1496,12 @@
     local_heads = attention_in.shape[2] // head_dim
     score_scale = 1.0 / math.sqrt(head_dim)
     in_full, out_full, shared_in_full, shared_down_full = (
-        lax.all_gather(attention_in, "ep", axis=1, tiled=True),
-        lax.all_gather(attention_out, "ep", axis=1, tiled=True),
-        lax.all_gather(shared_in, "ep", axis=1, tiled=True),
-        lax.all_gather(shared_down, "ep", axis=1, tiled=True),
-    )
-    ep_index = lax.axis_index("ep")
+        lax.all_gather(attention_in, EP, axis=1, tiled=True),
+        lax.all_gather(attention_out, EP, axis=1, tiled=True),
+        lax.all_gather(shared_in, EP, axis=1, tiled=True),
+        lax.all_gather(shared_down, EP, axis=1, tiled=True),
+    )
+    ep_index = lax.axis_index(EP)
     positions = ep_index * tok_count + jnp.arange(tok_count, dtype=jnp.int32)
     key_count = (reach_back + 1) * tok_count
     key_positions = (ep_index - reach_back) * tok_count + jnp.arange(key_count, dtype=jnp.int32)
@@ -140,7 +1528,7 @@
     key_value = jnp.stack([keys_own, values_own])
     earlier = []
     for hop_count in range(reach_back, 0, -1):
-        earlier.append(shifted(key_value, "ep", hop_count))
+        earlier.append(shifted(key_value, EP, hop_count))
     all_kv = jnp.concatenate(earlier + [key_value], axis=1)
     all_keys = all_kv[0]
     all_values = all_kv[1]
@@ -188,13 +1576,13 @@
     send_rows = padded_rows[slot_token].reshape(expert_count, capacity, model_width)
 
     def expert_trip(outgoing, work):
-        row_block = lax.all_to_all(outgoing, "ep", split_axis=0, concat_axis=1, tiled=True)
+        row_block = lax.all_to_all(outgoing, EP, split_axis=0, concat_axis=1, tiled=True)
         partial_rows, extras = work(row_block)
-        share_rows = lax.psum_scatter(partial_rows, "tp", scatter_dimension=1, tiled=True).astype(
+        share_rows = lax.psum_scatter(partial_rows, TP, scatter_dimension=1, tiled=True).astype(
             bf16
         )
-        whole_rows = lax.all_gather(share_rows, "tp", axis=1, tiled=True)
-        return (lax.all_to_all(whole_rows, "ep", split_axis=1, concat_axis=0, tiled=True), extras)
+        whole_rows = lax.all_gather(share_rows, TP, axis=1, tiled=True)
+        return (lax.all_to_all(whole_rows, EP, split_axis=1, concat_axis=0, tiled=True), extras)
 
     def expert_forward(row_block):
         pre_acts = jnp.einsum("erd,esdf->serf", row_block, expert_in, preferred_element_type=f32)
@@ -313,7 +1701,7 @@
     for hop_count in range(1, reach_back + 1):
         segment_start = (reach_back - hop_count) * tok_count
         segment = grad_kv[:, segment_start : segment_start + tok_count]
-        own_part = own_part + shifted(segment, "ep", -hop_count)
+        own_part = own_part + shifted(segment, EP, -hop_count)
     grad_raw = (
         jnp.stack(
             [
@@ -338,16 +1726,16 @@
     grad_input = (grad_residual + grad_in_norm).astype(bf16)
     grad_attention_in, grad_attention_out, grad_shared_in, grad_shared_down = (
         lax.psum_scatter(
-            grad_attention_in.astype(jnp.bfloat16), "ep", scatter_dimension=1, tiled=True
+            grad_attention_in.astype(jnp.bfloat16), EP, scatter_dimension=1, tiled=True
         ).astype(jnp.float32),
         lax.psum_scatter(
-            grad_attention_out.astype(jnp.bfloat16), "ep", scatter_dimension=1, tiled=True
+            grad_attention_out.astype(jnp.bfloat16), EP, scatter_dimension=1, tiled=True
         ).astype(jnp.float32),
         lax.psum_scatter(
-            grad_shared_in.astype(jnp.bfloat16), "ep", scatter_dimension=1, tiled=True
+            grad_shared_in.astype(jnp.bfloat16), EP, scatter_dimension=1, tiled=True
         ).astype(jnp.float32),
         lax.psum_scatter(
-            grad_shared_down.astype(jnp.bfloat16), "ep", scatter_dimension=1, tiled=True
+            grad_shared_down.astype(jnp.bfloat16), EP, scatter_dimension=1, tiled=True
         ).astype(jnp.float32),
     )
     (
@@ -357,11 +1745,11 @@
         grad_shared_gate,
         grad_router,
     ) = (
-        lax.psum(grad_attention_gain.astype(jnp.bfloat16), "ep").astype(jnp.float32),
-        lax.psum(grad_attention_bias.astype(jnp.bfloat16), "ep").astype(jnp.float32),
-        lax.psum(grad_feedforward_gain.astype(jnp.bfloat16), "ep").astype(jnp.float32),
-        lax.psum(grad_shared_gate.astype(jnp.bfloat16), "ep").astype(jnp.float32),
-        lax.psum(grad_router.astype(jnp.bfloat16), "ep").astype(jnp.float32),
+        lax.psum(grad_attention_gain.astype(jnp.bfloat16), EP).astype(jnp.float32),
+        lax.psum(grad_attention_bias.astype(jnp.bfloat16), EP).astype(jnp.float32),
+        lax.psum(grad_feedforward_gain.astype(jnp.bfloat16), EP).astype(jnp.float32),
+        lax.psum(grad_shared_gate.astype(jnp.bfloat16), EP).astype(jnp.float32),
+        lax.psum(grad_router.astype(jnp.bfloat16), EP).astype(jnp.float32),
     )
     return (
         layer_output,
@@ -385,36 +1773,36 @@
         per_device,
         mesh=mesh,
         in_specs=(
-            P("ep", None),
+            P(EP, None),
             P(),
-            P(None, "ep", "tp"),
-            P(None, "tp"),
-            P("tp", "ep"),
+            P(None, EP, TP),
+            P(None, TP),
+            P(TP, EP),
             P(),
-            P(None, "ep", "tp"),
-            P("tp", "ep"),
+            P(None, EP, TP),
+            P(TP, EP),
             P(),
             P(),
-            P("ep", None, None, "tp"),
-            P("ep", "tp", None),
-            P("ep", None),
+            P(EP, None, None, TP),
+            P(EP, TP, None),
+            P(EP, None),
             P(),
-            P("ep", None),
+            P(EP, None),
         ),
         out_specs=(
-            P("ep", None),
-            P("ep", None),
+            P(EP, None),
+            P(EP, None),
             P(),
-            P(None, "ep", "tp"),
-            P(None, "tp"),
-            P("tp", "ep"),
+            P(None, EP, TP),
+            P(None, TP),
+            P(TP, EP),
             P(),
-            P(None, "ep", "tp"),
-            P("tp", "ep"),
+            P(None, EP, TP),
+            P(TP, EP),
             P(),
             P(),
-            P("ep", None, None, "tp"),
-            P("ep", "tp", None),
+            P(EP, None, None, TP),
+            P(EP, TP, None),
         ),
         check_vma=False,
     )

time: 2730 us -> 1000 us (0.37)
  waiting for transfers between devices: 1960 us -> 4.86 us
  Pallas kernels: 0 us -> 798 us
  local copies, waits for them, and re-layouts: 313 us -> 73.4 us
  matrix products: 226 us -> 58.8 us
  other arithmetic: 131 us -> 22.5 us
  blocking collectives: 37.4 us -> 0 us
    pallas_call x0 -> x14, Pallas kernels: none -> 798 us  [the longest x1 148 us: scatter_rows(): pl.pallas_call(scatter_kernel, out_shape=(jax.ShapeDtypeStruct((count, wi...]
    all_gather x6 -> x2, waiting for transfers between devices: 617 us -> 0.02 us  [the longest x1 0.02 us: per_device_dense(): lax.all_gather((residual + ffn_sum.astype(f32)).astype(bf16), TP, axis=0,...]
    all_to_all x4 -> x2, waiting for transfers between devices: 479 us -> 0.01 us  [the longest x1 0.01 us: per_device_dense(): lax.all_to_all(after(shared_shards, in_blocks), EP, split_axis=0, concat_...]
    reduce_scatter x6 -> x1, waiting for transfers between devices: 422 us -> 0.02 us  [per_device_dense(): lax.psum_scatter(ffn_part.reshape(all_count, model_width), both, scatter_...]
    psum x4 -> x1, waiting for transfers between devices: 312 us -> 4.74 us  [per_device_dense(): small = lax.psum(small, both)]
    dot_general x29 -> x14, matrix products: 226 us -> 58.8 us  [the longest x6 21.3 us: product(): lax.dot_general(left, right, dims, preferred_element_type=jnp.float32)]
    ppermute x4 -> x0, waiting for transfers between devices: 132 us -> none  [shifted(): lax.ppermute(value, axis, [(source, source + steps) for source in range(l...]
    gather x10 -> x0, local copies, waits for them, and re-layouts: 118 us -> none  [the longest x1 22 us: per_device(): padded_rows[slot_token].reshape(expert_count, capacity, model_width)]
  transfers between devices with their start and end apart: 24 -> 6, of which waited for: 19 -> 1; matrix products, arithmetic and copies ran while one was open for 20% -> 13% of each run, Pallas kernels for 0% -> 62%
where the time goes in v1:
time: 1000 us; the launch traced here: 989 us
  Pallas kernels  798 us (80%)
  local copies, waits for them, and re-layouts  73.4 us (7%)
  matrix products  58.8 us (6%)
  other arithmetic  22.5 us (2%)
  starting transfers between devices  16.4 us (2%)
  between operations  15.4 us (2%)
    pallas_call x1, Pallas kernels, scatter_rows(): pl.pallas_call(scatter_kernel, out_shape=(jax.ShapeDtypeStruct((count, wi...  148 us
    pallas_call x1, Pallas kernels, gather_rows(): pl.pallas_call(gather_kernel, out_shape=(jax.ShapeDtypeStruct((RING, 4) +...  105 us
    pallas_call x1, Pallas kernels, collect_weights(): pl.pallas_call(collect_kernel, out_shape=(jax.ShapeDtypeStruct((kinds, de...  104 us
    pallas_call x1, Pallas kernels, feed(): pl.pallas_call(feed_kernel, grid=(blocks,), in_specs=[row_spec, pl.BlockS...  98.7 us
    pallas_call x1, Pallas kernels, spread_weights(): pl.pallas_call(spread_kernel, out_shape=(jax.ShapeDtypeStruct((kinds, RIN...  84.3 us
    pallas_call x1, Pallas kernels, share_keys(): pl.pallas_call(share_kernel, out_shape=jax.ShapeDtypeStruct((kinds, 3, to...  77.2 us
    pallas_call x2, Pallas kernels, tensor_gather(): pl.pallas_call(tensor_kernel, out_shape=jax.ShapeDtypeStruct((4,) + rows....  52 us
    pallas_call x2, Pallas kernels, product_to_owner(): pl.pallas_call(functools.partial(reduce_kernel, flip), out_shape=jax.Shap...  52 us
  transfers between devices with their start and end apart: 6, of which 1 were waited for; matrix products, arithmetic and copies ran while one was open for 13% of the time, Pallas kernels for 62%

profile of v1, /device:TPU:0, one launch (start us, length us, event | category | flops | bytes accessed | tf_op | source)
XLA Modules:
  0.0 988.9 jit_solution(1337053818955603767)
XLA Ops:
  9.4 84.3 %spread_weights.1 = (bf16[3,8,256,512]{3,2,1,0:T(8,128)(2,1)}, bf16[512,2048]{1,0:T(8,128)(2,1)S(1)}) custom-call(bf16[3,256,512]{2,1,0:T(8,128)(2,1)S(1)} %copy-done.18, bf16[512,256]{1,0:T(8,128)(2,1)S(1)} %copy-done.20), custom_call_target="tpu_custom_call" | custom-call | tf_op jit(solution)/shard_map/spread_weights/pallas_call | solution.py:815
  95.0 1.9 constant_dynamic-slice_fusion
  99.0 1.5 copy.119
  100.4 4.8 all-to-all-start
  109.4 2.8 copy-done.3
  112.1 5.1 project.1
  118.6 77.2 %share_keys.1.keys.values = bf16[2,3,512,512]{3,2,1,0:T(8,128)(2,1)S(1)} custom-call(bf16[2,512,512]{2,1,0:T(8,128)(2,1)S(1)} %get-tuple-element.91.own), custom_call_target="tpu_custom_call" | custom-call | tf_op jit(solution)/shard_map/share_keys/pallas_call | solution.py:1037
  195.8 9.9 %attend.1 = (bf16[512,512]{1,0:T(8,128)(2,1)S(1)}, f32[4,512,1]{2,1,0:T(8,128)S(1)}) custom-call(bf16[512,512]{1,0:T(8,128)(2,1)S(1)} %get-tuple-element.90.queries, bf16[2,3,512,512]{3,2,1,0:T(8,128)(2,1)S(1)} %share_keys.1.keys.values, bf16[2,3,512,512]{3,2,1,0:T(8,128)(2,1)S(1)} %share_keys.1.keys.values, s32[512,1]{1,0:T(8,128)S(1)} %fusion.37.query_doc, ...), custom_call_target="tpu_custom_call" | custom-call | tf_op jit(solution)/shard_map/attend/pallas_call | solution.py:333
  206.7 28.4 %product_to_owner.2 = f32[128,2048]{1,0:T(8,128)S(1)} custom-call(bf16[1,512,512]{2,1,0:T(8,128)(2,1)S(1)} %bitcast.150, bf16[1,512,2048]{2,1,0:T(8,128)(2,1)S(1)} %bitcast.144), custom_call_target="tpu_custom_call" | custom-call | tf_op jit(solution)/shard_map/product_to_owner/pallas_call | solution.py:1167
  240.7 104.8 %gather_rows.1 = (bf16[8,4,128,2048]{3,2,1,0:T(8,128)(2,1)}, f32[8,4,24,128]{3,2,1,0:T(8,128)S(1)}) custom-call(bf16[128,2048]{1,0:T(8,128)(2,1)S(1)} %fusion.22.rows, f32[24,128]{1,0:T(8,128)S(1)} %scatter.16.scales), custom_call_target="tpu_custom_call" | custom-call | tf_op jit(solution)/shard_map/gather_rows/pallas_call | solution.py:582
  347.7 2.0 copy.115
  349.7 2.0 and_select_fusion
  354.0 1.9 broadcast_in_dim_squeeze.4.scale_column
  355.9 8.5 copy.123.expert_in
  364.4 1.5 constant_dynamic-slice_fusion.1.gate_row
  365.9 3.2 copy.142
  369.1 98.7 %feed.1 = (bf16[8,512,2048]{2,1,0:T(8,128)(2,1)}, bf16[8,512,2048]{2,1,0:T(8,128)(2,1)}, bf16[2,8,160,2048]{3,2,1,0:T(8,128)(2,1)}, bf16[2,8,160,2048]{3,2,1,0:T...) custom-call(s32[8,2,512]{2,1,0:T(2,128)} %copy.121.rank_row, ...), custom_call_target="tpu_custom_call" | custom-call | tf_op jit(solution)/shard_map/feed/pallas_call | solution.py:185
  470.7 147.6 %scatter_rows.1 = (f32[128,2048]{1,0:T(8,128)S(1)}, f32[24,128]{1,0:T(8,128)S(1)}) custom-call(bf16[8,4,128,2048]{3,2,1,0:T(8,128)(2,1)} %bitcast.166, f32[8,4,24,128]{3,2,1,0:T(8,128)S(1)} %bitcast_bitcast_fusion.scalars), custom_call_target="tpu_custom_call" | custom-call | tf_op jit(solution)/shard_map/scatter_rows/pallas_call | solution.py:744
  618.5 1.9 multiply_reduce_fusion
  622.9 26.9 %tensor_gather.2 = bf16[4,128,2048]{2,1,0:T(8,128)(2,1)S(1)} custom-call(bf16[128,2048]{1,0:T(8,128)(2,1)S(1)} %fusion.52.rows), custom_call_target="tpu_custom_call" | custom-call | tf_op jit(solution)/shard_map/tensor_gather/pallas_call | solution.py:1199
  652.0 13.1 %attend_back.1 = (bf16[512,512]{1,0:T(8,128)(2,1)S(1)}, bf16[2,3,512,512]{3,2,1,0:T(8,128)(2,1)}) custom-call(bf16[512,512]{1,0:T(8,128)(2,1)S(1)} %copy-done.13, bf16[2,3,512,512]{3,2,1,0:T(8,128)(2,1)} %copy-done.2, bf16[2,3,512,512]{3,2,1,0:T(8,128)(2,1)} %copy-done.2, s32[512,1]{1,0:T(8,128)S(1)} %fusion.37.query_doc, s32[1,1536]{1,0:T(1,128)S(1)} %copy-done.24, ...), custom_call_target="tpu_custom_call" | custom-call | tf_op jit(solution)/shard_map/attend_back/pallas_call | solution.py:375
  665.0 1.9 copy-done.5
  667.0 48.4 %return_keys.1 = bf16[2,512,512]{2,1,0:T(8,128)(2,1)S(1)} custom-call(bf16[2,3,512,512]{3,2,1,0:T(8,128)(2,1)S(1)} %copy-done.5, f32[512,128]{1,0:T(8,128)S(1)} %get-tuple-element.190.cosine, f32[512,128]{1,0:T(8,128)S(1)} %get-tuple-element.191.sine), custom_call_target="tpu_custom_call" | custom-call | tf_op jit(solution)/shard_map/return_keys/pallas_call | solution.py:1114
  715.6 23.6 %product_to_owner.3 = f32[128,2048]{1,0:T(8,128)S(1)} custom-call(bf16[3,512,512]{2,1,0:T(8,128)(2,1)S(1)} %pad_maximum_fusion.left, bf16[3,2048,512]{2,1,0:T(8,128)(2,1)} %bitcast.141), custom_call_target="tpu_custom_call" | custom-call | tf_op jit(solution)/shard_map/product_to_owner/pallas_call | solution.py:1167
  739.2 5.4 convert_bitcast_fusion
  744.6 9.0 copy.127
  753.6 1.9 fusion.16
  755.6 9.7 convolution_convert_fusion.1
  765.6 1.7 fusion.53
  767.3 1.6 slice-done.3
  769.0 3.2 convolution_convert_fusion.2
  773.7 3.2 convolution_convert_fusion.3
  777.3 1.6 maximum_bitcast_fusion.1
  778.8 11.3 %all-to-all-start.1 = ((bf16[8,3,176,256]{3,2,1,0:T(8,128)(2,1)}), bf16[8,3,176,256]{3,2,1,0:T(8,128)(2,1)}, u32[]{:S(2)}, u32[]{:S(2)}) async-start(bf16[8,3,176,256]{3,2,1,0:T(8,128)(2,1)} %maximum_bitcast_fusion.1), calls=%async_computation.2 | async-start | bytes 4325376 | tf_op jit(solution)/shard_map/all_to_all | solution.py:1380
  790.7 2.1 fusion.20
  794.3 3.6 convolution_convert_fusion.grad_out
  798.1 11.2 %fusion.56 = f32[2,352,2048]{2,1,0:T(8,128)} fusion(bf16[2,1280,352]{2,1,0:T(8,128)(2,1)} %bitcast.169, bf16[2,1280,2048]{2,1,0:T(8,128)(2,1)} %bitcast.167), kind=kOutput, calls=%fused_computation.127 | convolution fusion | flops 3690987520 | bytes 18055168 | tf_op jit(solution)/shard_map/erf,erd->efd/dot_general | solution.py:1363
  809.4 104.4 %collect_weights.1 = (f32[3,256,512]{2,1,0:T(8,128)S(1)}, f32[512,256]{1,0:T(8,128)S(1)}, f32[4,8,512]{2,1,0:T(8,128)S(1)}) custom-call(bf16[3,8,256,512]{3,2,1,0:T(8,128)(2,1)} %bitcast.157, bf16[512,2048]{1,0:T(8,128)(2,1)S(1)} %copy-done.11, f32[8,512]{1,0:T(8,128)S(1)} %maximum_maximum_fusion.tail), custom_call_target="tpu_custom_call" | custom-call | tf_op jit(solution)/shard_map/collect_weights/pallas_call | solution.py:924
  915.0 3.0 fusion.15
  919.2 14.1 %convolution_bitcast_fusion = f32[2,2,2048,352]{2,3,1,0:T(8,128)} fusion(bf16[2,1280,2048,1]{2,1,3,0:T(8,128)(2,1)} %bitcast.192, bf16[2,2,1280,352]{3,2,1,0:T(8,128)(2,1)} %bitcast.193), kind=kOutput, calls=%fused_computation.1 | convolution fusion | flops 7381975040 | bytes 25624576 | tf_op jit(solution)/shard_map/erd,serf->esdf/dot_general | solution.py:1366
  933.3 4.7 all-reduce.3.cloned.1.call-done
  938.1 1.5 fusion.54
  939.6 1.6 slice_bitcast_fusion
  941.2 2.1 convert_bitcast_fusion.1
  943.3 1.8 slice.148
  946.2 3.5 copy.134
  949.8 25.1 %tensor_gather.3 = bf16[4,128,2048]{2,1,0:T(8,128)(2,1)S(1)} custom-call(bf16[128,2048]{1,0:T(8,128)(2,1)S(1)} %get-tuple-element.180.rows), custom_call_target="tpu_custom_call" | custom-call | tf_op jit(solution)/shard_map/tensor_gather/pallas_call | solution.py:1199
  974.9 3.2 copy.161
  (254 shorter events, 41.0 us)
Async XLA Ops:
  7.2 229.4 %copy-start = (f32[2048,16]{0,1:T(8,128)S(1)}, f32[2048,16]{0,1:T(8,128)}, u32[]{:S(2)}) copy-start(f32[2048,16]{0,1:T(8,128)} %param.32) | copy-start | bytes 393220
  7.2 361.9 %all-gather.3.cloned.1.call-start = ((), (), s32[]{:S(2)}) async-start(), calls=%async_computation.3 | async-start | bytes 17301504 | tf_op jit(solution)/shard_map/all_gather | solution.py:1254
  9.4 87.6 %copy-start.37 = (bf16[2,256,1408]{2,1,0:T(8,128)(2,1)S(1)}, bf16[2,256,1408]{2,1,0:T(8,128)(2,1)}, u32[]{:S(2)}) copy-start(bf16[2,256,1408]{2,1,0:T(8,128)(2,1)} %param.29) | copy-start | bytes 4325380
  100.4 4.9 copy-start.76
  100.4 265.4 %all-to-all-start = ((bf16[8,3,176,256]{3,2,1,0:T(8,128)(2,1)}), bf16[8,3,176,256]{3,2,1,0:T(8,128)(2,1)}, u32[]{:S(2)}, u32[]{:S(2)}) async-start(bf16[8,3,176,256]{3,2,1,0:T(8,128)(2,1)} %copy.119), calls=%async_computation | async-start | bytes 4325376 | tf_op jit(solution)/shard_map/all_to_all | solution.py:1263
  105.3 809.6 %reduce-scatter.2.cloned.1.call-start = ((), (), s32[]{:S(2)}) async-start(), calls=%async_computation.4 | async-start | bytes 17301504 | tf_op jit(solution)/shard_map/reduce_scatter | solution.py:1341
  108.6 87.2 %copy-start.23 = (s32[1,1536]{1,0:T(1,128)}, s32[1,1536]{1,0:T(1,128)S(1)}, u32[]{:S(2)}) copy-start(s32[1,1536]{1,0:T(1,128)S(1)} %compare_select_fusion.key_doc) | copy-start | bytes 18436
  118.6 77.2 %copy-start.12 = (bf16[512,512]{1,0:T(8,128)(2,1)}, bf16[512,512]{1,0:T(8,128)(2,1)S(1)}, u32[]{:S(2)}) copy-start(bf16[512,512]{1,0:T(8,128)(2,1)S(1)} %get-tuple-element.90.queries) | copy-start | bytes 1572868
  195.7 10.0 %copy-start.2 = (bf16[2,3,512,512]{3,2,1,0:T(8,128)(2,1)}, bf16[2,3,512,512]{3,2,1,0:T(8,128)(2,1)S(1)}, u32[]{:S(2)}) copy-start(bf16[2,3,512,512]{3,2,1,0:T(8,128)(2,1)S(1)} %share_keys.1.keys.values) | copy-start | bytes 9437188
  195.8 10.9 %copy-start.7 = (bf16[512,2048]{1,0:T(8,128)(2,1)S(1)}, bf16[512,2048]{1,0:T(8,128)(2,1)}, u32[]{:S(2)}) copy-start(bf16[512,2048]{1,0:T(8,128)(2,1)} %copy-done.6) | copy-start | bytes 6291460
  206.7 29.9 %copy-start.19 = (bf16[512,512]{1,0:T(8,128)(2,1)}, bf16[512,512]{1,0:T(8,128)(2,1)S(1)}, u32[]{:S(2)}) copy-start(bf16[512,512]{1,0:T(8,128)(2,1)S(1)} %get-tuple-element.92) | copy-start | bytes 1572868
  236.6 108.8 %copy-start.45 = (f32[128]{0:T(128)}, f32[128]{0:T(128)S(1)}, u32[]{:S(2)}) copy-start(f32[128]{0:T(128)S(1)} %add_rsqrt_fusion.1) | copy-start | bytes 1540
  237.7 108.6 %copy-start.51 = (f32[128]{0:T(128)}, f32[128]{0:T(128)S(1)}, u32[]{:S(2)}) copy-start(f32[128]{0:T(128)S(1)} %get-tuple-element.187) | copy-start | bytes 1540
  237.7 108.6 %copy-start.55 = (f32[128]{0:T(128)}, f32[128]{0:T(128)S(1)}, u32[]{:S(2)}) copy-start(f32[128]{0:T(128)S(1)} %fusion.42) | copy-start | bytes 1540
  237.8 108.6 %copy-start.58 = (f32[128]{0:T(128)}, f32[128]{0:T(128)S(1)}, u32[]{:S(2)}) copy-start(f32[128]{0:T(128)S(1)} %fusion.43) | copy-start | bytes 1540
  238.8 107.6 %copy-start.69 = (f32[128]{0:T(128)}, f32[128]{0:T(128)S(1)}, u32[]{:S(2)}) copy-start(f32[128]{0:T(128)S(1)} %fusion.10) | copy-start | bytes 1540
  470.6 147.7 %copy-start.43 = (f32[128,16]{0,1:T(8,128)S(1)}, f32[128,16]{0,1:T(8,128)}, u32[]{:S(2)}) copy-start(f32[128,16]{0,1:T(8,128)} %copy-done.42) | copy-start | bytes 24580
  470.6 147.7 %copy-start.52 = (f32[128]{0:T(128)S(1)}, f32[128]{0:T(128)}, u32[]{:S(2)}) copy-start(f32[128]{0:T(128)} %copy-done.51) | copy-start | bytes 1540
  470.6 147.7 %copy-start.56 = (f32[128]{0:T(128)S(1)}, f32[128]{0:T(128)}, u32[]{:S(2)}) copy-start(f32[128]{0:T(128)} %copy-done.55) | copy-start | bytes 1540
  470.6 147.7 %copy-start.59 = (f32[128]{0:T(128)S(1)}, f32[128]{0:T(128)}, u32[]{:S(2)}) copy-start(f32[128]{0:T(128)} %copy-done.58) | copy-start | bytes 1540
  470.6 147.8 %copy-start.70 = (f32[128]{0:T(128)S(1)}, f32[128]{0:T(128)}, u32[]{:S(2)}) copy-start(f32[128]{0:T(128)} %copy-done.69) | copy-start | bytes 1540
  470.6 147.8 %copy-start.29 = (f32[128,2048]{1,0:T(8,128)S(1)}, f32[128,2048]{1,0:T(8,128)}, u32[]{:S(2)}) copy-start(f32[128,2048]{1,0:T(8,128)} %copy-done.28) | copy-start | bytes 3145732
  470.6 147.8 %copy-start.40 = (f32[2048]{0:T(1024)S(1)}, f32[2048]{0:T(1024)}, u32[]{:S(2)}) copy-start(f32[2048]{0:T(1024)} %param.28) | copy-start | bytes 24580
  470.7 147.8 %copy-start.46 = (f32[128]{0:T(128)S(1)}, f32[128]{0:T(128)}, u32[]{:S(2)}) copy-start(f32[128]{0:T(128)} %copy-done.45) | copy-start | bytes 1540
  470.7 147.8 %copy-start.49 = (f32[2048]{0:T(1024)S(1)}, f32[2048]{0:T(1024)}, u32[]{:S(2)}) copy-start(f32[2048]{0:T(1024)} %param.31) | copy-start | bytes 24580
  618.4 4.4 copy-start.61
  618.4 4.4 copy-start.63
  620.5 29.3 %copy-start.71 = (f32[128]{0:T(128)}, f32[128]{0:T(128)S(1)}, u32[]{:S(2)}) copy-start(f32[128]{0:T(128)S(1)} %broadcast_multiply_fusion.1) | copy-start | bytes 1540
  622.8 27.0 %copy-start.8 = (bf16[512,2048]{1,0:T(8,128)(2,1)S(1)}, bf16[512,2048]{1,0:T(8,128)(2,1)}, u32[]{:S(2)}) copy-start(bf16[512,2048]{1,0:T(8,128)(2,1)} %copy-done.6) | copy-start | bytes 6291460
  715.5 23.6 %copy-start.27 = (bf16[512,2048]{1,0:T(8,128)(2,1)S(1)}, bf16[512,2048]{1,0:T(8,128)(2,1)}, u32[]{:S(2)}) copy-start(bf16[512,2048]{1,0:T(8,128)(2,1)} %copy-done.26) | copy-start | bytes 6291460
  744.6 9.0 copy-start.22
  744.6 9.0 copy-start.65
  755.6 10.1 %copy-start.34 = (bf16[2,8,512,176]{3,2,1,0:T(8,128)(2,1)S(1)}, bf16[2,8,512,176]{3,2,1,0:T(8,128)(2,1)}, u32[]{:S(2)}) copy-start(bf16[2,8,512,176]{3,2,1,0:T(8,128)(2,1)} %get-tuple-element.111) | copy-start | bytes 8650756
  755.6 11.8 %slice-start = ((s8[16777216]{0:T(1024)(128)(4,1)}), s8[4194304]{0:T(1024)(128)(4,1)S(1)}, s32[]{:S(2)}) async-start(s8[16777216]{0:T(1024)(128)(4,1)} %bitcast.161), calls=%async_computation.7 | async-start | bytes 8388608
  755.6 11.8 %slice-start.1 = ((s8[16777216]{0:T(1024)(128)(4,1)}), s8[4194304]{0:T(1024)(128)(4,1)S(1)}, s32[]{:S(2)}) async-start(s8[16777216]{0:T(1024)(128)(4,1)} %bitcast.161), calls=%async_computation.8 | async-start | bytes 8388608
  755.6 11.8 %slice-start.2 = ((s8[16777216]{0:T(1024)(128)(4,1)}), s8[4194304]{0:T(1024)(128)(4,1)S(1)}, s32[]{:S(2)}) async-start(s8[16777216]{0:T(1024)(128)(4,1)} %bitcast.161), calls=%async_computation.9 | async-start | bytes 8388608
  778.8 11.8 %copy-start.41 = (f32[2048]{0:T(1024)S(1)}, f32[2048]{0:T(1024)}, u32[]{:S(2)}) copy-start(f32[2048]{0:T(1024)} %param.28) | copy-start | bytes 24580
  778.8 11.8 %copy-start.47 = (f32[128]{0:T(128)S(1)}, f32[128]{0:T(128)}, u32[]{:S(2)}) copy-start(f32[128]{0:T(128)} %copy-done.45) | copy-start | bytes 1540
  778.8 11.8 %copy-start.68 = (f32[128]{0:T(128)S(1)}, f32[128]{0:T(128)}, u32[]{:S(2)}) copy-start(f32[128]{0:T(128)} %copy-done.67) | copy-start | bytes 1540
  778.8 162.4 %all-to-all-start.1 = ((bf16[8,3,176,256]{3,2,1,0:T(8,128)(2,1)}), bf16[8,3,176,256]{3,2,1,0:T(8,128)(2,1)}, u32[]{:S(2)}, u32[]{:S(2)}) async-start(bf16[8,3,176,256]{3,2,1,0:T(8,128)(2,1)} %maximum_bitcast_fusion.1), calls=%async_computation.2 | async-start | bytes 4325376 | tf_op jit(solution)/shard_map/all_to_all | solution.py:1380
  790.2 147.9 %all-reduce.3.cloned.1.call-start = ((), (), s32[]{:S(2)}) async-start(), calls=%async_computation.6 | async-start | bytes 393216 | tf_op jit(solution)/shard_map/psum | solution.py:1408
  798.0 176.9 %all-gather.5.cloned.1.call-start = ((), (), s32[]{:S(2)}) async-start(), calls=%async_computation.5 | async-start | bytes 2621440 | tf_op jit(solution)/shard_map/all_gather | solution.py:1344
  798.0 11.2 %copy-start.74 = (f32[8]{0:T(128)S(1)}, f32[8]{0:T(128)}, u32[]{:S(2)}) copy-start(f32[8]{0:T(128)} %pad.17.clone) | copy-start | bytes 100
  798.0 11.3 %copy-start.11 = (bf16[512,2048]{1,0:T(8,128)(2,1)S(1)}, bf16[512,2048]{1,0:T(8,128)(2,1)}, u32[]{:S(2)}) copy-start(bf16[512,2048]{1,0:T(8,128)(2,1)} %convolution_convert_fusion.grad_out) | copy-start | bytes 6291460
  809.3 105.6 %copy-start.73 = (f32[128]{0:T(128)S(1)}, f32[128]{0:T(128)}, u32[]{:S(2)}) copy-start(f32[128]{0:T(128)} %get-tuple-element.170) | copy-start | bytes 1540
  809.3 105.6 %copy-start.31 = (f32[128,2048]{1,0:T(8,128)S(1)}, f32[128,2048]{1,0:T(8,128)}, u32[]{:S(2)}) copy-start(f32[128,2048]{1,0:T(8,128)} %copy-done.28) | copy-start | bytes 3145732
  809.3 105.6 %copy-start.66 = (f32[128]{0:T(128)S(1)}, f32[128]{0:T(128)}, u32[]{:S(2)}) copy-start(f32[128]{0:T(128)} %add_rsqrt_fusion) | copy-start | bytes 1540
  809.4 105.6 %copy-start.72 = (f32[128]{0:T(128)S(1)}, f32[128]{0:T(128)}, u32[]{:S(2)}) copy-start(f32[128]{0:T(128)} %copy-done.71) | copy-start | bytes 1540
  (39 other events, 91.4 us)
Sparse Core Ops, SparseCore 0:
  97.1 170.4 all-gather.2
  468.0 247.7 reduce-scatter.1
  798.1 139.9 all-reduce.2
  940.1 32.9 all-gather.4

commit v2 on v1

--- a/solution.py
+++ b/solution.py
@@ -86,147 +86,6 @@
 
 def product(left, right, dims=NN):
     return lax.dot_general(left, right, dims, preferred_element_type=jnp.float32)
-
-
-def feed_kernel(
-    rank_row, rank_column, gate_row, scale_column, rows, cotangent,
-    expert_in, expert_down, shared,
-    out_part, back_part, slot_rows, slot_cotangent, grad_pre, gated,
-    grad_shared_pre, scaled, token_grad, scale_grad, out_terms, back_terms,
-):
-    bf16, f32 = jnp.bfloat16, jnp.float32
-    experts, _, slots, _ = slot_rows.shape
-    tokens = rows.shape[1]
-    hidden_count = gated.shape[3]
-    all_slots = experts * slots
-    token_rows, token_cotangent = rows[0], cotangent[0]
-    shared_count = scaled.shape[2]
-
-    @pl.when(pl.program_id(0) == 0)
-    def _():
-        out_terms[all_slots:, :] = shared[2]
-        back_terms[all_slots : all_slots + shared_count, :] = shared[0]
-        back_terms[all_slots + shared_count :, :] = shared[1]
-
-    silu, slope = silu_parts(product(token_rows, shared[0], NT))
-    up = product(token_rows, shared[1], NT)
-    hidden = (silu * up).astype(bf16).astype(f32)
-    scale = scale_column[0]
-    scaled_hidden = (scale * hidden).astype(bf16)
-    scaled[0] = scaled_hidden
-    back = product(token_cotangent, shared[2], NT)
-    scale_grad[0] = jnp.sum(hidden * back, axis=1, keepdims=True)
-    back = scale * back
-    gate_grad = (back * up * slope).astype(bf16)
-    up_grad = (back * silu).astype(bf16)
-    grad_shared_pre[0, 0] = gate_grad
-    grad_shared_pre[1, 0] = up_grad
-    order = lax.broadcasted_iota(jnp.int32, (all_slots, tokens), 0)
-    spread_order = lax.broadcasted_iota(jnp.int32, (tokens, all_slots), 1)
-    hits, spread = None, None
-    for expert in range(experts):
-        row_hits = order == rank_row[0, expert : expert + 1, :] + expert * slots
-        column_hits = spread_order == rank_column[0, :, expert : expert + 1] + expert * slots
-        hits = row_hits if hits is None else hits | row_hits
-        spread = column_hits if spread is None else spread | column_hits
-    place = hits.astype(bf16)
-    taken = product(place, token_rows).astype(bf16)
-    taken_cotangent = product(place, token_cotangent).astype(bf16)
-    for expert in range(experts):
-        mine = slice(expert * slots, (expert + 1) * slots)
-        slot_rows[expert, 0] = taken[mine]
-        slot_cotangent[expert, 0] = taken_cotangent[mine]
-        gate = jnp.sum(
-            jnp.where(hits[mine], gate_row[0, expert : expert + 1, :], 0.0), axis=1, keepdims=True
-        )
-        pre = product(taken[mine], expert_in[expert])
-        silu, slope = silu_parts(pre[:, :hidden_count])
-        up = pre[:, hidden_count:]
-        hidden = (silu * up).astype(bf16).astype(f32)
-        gated_hidden = (gate * hidden).astype(bf16)
-        gated[expert, 0] = gated_hidden
-        back = product(taken_cotangent[mine], expert_down[expert], NT)
-        slot_grad = jnp.sum(hidden * back, axis=1, keepdims=True)
-        token_grad[0, expert : expert + 1, :] = jnp.sum(
-            jnp.where(hits[mine], slot_grad, 0.0), axis=0, keepdims=True
-        )
-        back = gate * back
-        gate_grad_e = (back * up * slope).astype(bf16)
-        up_grad_e = (back * silu).astype(bf16)
-        grad_pre[0, expert, 0] = gate_grad_e
-        grad_pre[1, expert, 0] = up_grad_e
-        out_terms[mine, :] = product(gated_hidden, expert_down[expert]).astype(bf16)
-        both_grads = jnp.concatenate([gate_grad_e, up_grad_e], axis=1)
-        back_terms[mine, :] = product(both_grads, expert_in[expert], NT).astype(bf16)
-    spread = spread.astype(bf16)
-    out_part[0] = product(
-        jnp.concatenate([spread, scaled_hidden], axis=1), out_terms[...]
-    ).astype(bf16)
-    back_part[0] = product(
-        jnp.concatenate([spread, gate_grad, up_grad], axis=1), back_terms[...]
-    ).astype(bf16)
-
-
-def feed(rank, gates, scale, rows, cotangent, expert_in, expert_down, shared, capacity):
-    bf16, f32 = jnp.bfloat16, jnp.float32
-    blocks, experts, tokens = rank.shape
-    width = rows.shape[2]
-    hidden = expert_in.shape[2] // 2
-    slice_hidden = shared.shape[1]
-    once = pl.Buffered(1)
-
-    def whole(array):
-        return pl.BlockSpec(array.shape, lambda b: (0,) * array.ndim, pipeline_mode=once)
-
-    row_spec = pl.BlockSpec((1, experts, tokens), lambda b: (b, 0, 0))
-    token_spec = pl.BlockSpec((1, tokens, width), lambda b: (b, 0, 0))
-    slot_spec = pl.BlockSpec((experts, 1, capacity, width), lambda b: (0, b, 0, 0))
-    shape = jax.ShapeDtypeStruct
-    return pl.pallas_call(
-        feed_kernel,
-        grid=(blocks,),
-        in_specs=[
-            row_spec,
-            pl.BlockSpec((1, tokens, experts), lambda b: (b, 0, 0)),
-            row_spec,
-            pl.BlockSpec((1, tokens, 1), lambda b: (b, 0, 0)),
-            token_spec,
-            token_spec,
-            whole(expert_in),
-            whole(expert_down),
-            whole(shared),
-        ],
-        out_specs=(
-            token_spec,
-            token_spec,
-            slot_spec,
-            slot_spec,
-            pl.BlockSpec((2, experts, 1, capacity, hidden), lambda b: (0, 0, b, 0, 0)),
-            pl.BlockSpec((experts, 1, capacity, hidden), lambda b: (0, b, 0, 0)),
-            pl.BlockSpec((2, 1, tokens, slice_hidden), lambda b: (0, b, 0, 0)),
-            pl.BlockSpec((1, tokens, slice_hidden), lambda b: (b, 0, 0)),
-            row_spec,
-            pl.BlockSpec((1, tokens, 1), lambda b: (b, 0, 0)),
-        ),
-        out_shape=(
-            shape((blocks, tokens, width), bf16),
-            shape((blocks, tokens, width), bf16),
-            shape((experts, blocks, capacity, width), bf16),
-            shape((experts, blocks, capacity, width), bf16),
-            shape((2, experts, blocks, capacity, hidden), bf16),
-            shape((experts, blocks, capacity, hidden), bf16),
-            shape((2, blocks, tokens, slice_hidden), bf16),
-            shape((blocks, tokens, slice_hidden), bf16),
-            shape((blocks, experts, tokens), f32),
-            shape((blocks, tokens, 1), f32),
-        ),
-        scratch_shapes=[
-            pltpu.VMEM((experts * capacity + slice_hidden, width), bf16),
-            pltpu.VMEM((experts * capacity + 2 * slice_hidden, width), bf16),
-        ],
-        compiler_params=pltpu.CompilerParams(vmem_limit_bytes=60 * 2**20),
-        name="feed",
-    )(rank, jnp.swapaxes(rank, 1, 2), gates, scale, rows, cotangent, expert_in, expert_down, shared)
 
 
 def turned(values, cosine, sine):
@@ -486,111 +345,399 @@
 IN_VMEM = pl.BlockSpec(memory_space=pltpu.VMEM)
 
 
-def gather_kernel(rows, scales, out, out_scales, send_sems, recv_sems):
+class LateCopies(Copies):
+    def send(self, key, source, target, landing, peer):
+        index = self.count
+        self.count += 1
+        self.describe(source(), target(), peer, index).start()
+        self.sent.append(lambda: self.describe(source(), target(), peer, index).wait_send())
+        self.landing[key] = lambda: self.describe(landing(), landing(), peer, index).wait_recv()
+
+    def local(self, key, source, target):
+        index = self.count
+        self.count += 1
+
+        def copy():
+            return pltpu.make_async_copy(source(), target(), self.send_sems.at[index])
+
+        copy().start()
+        self.landing[key] = lambda: copy().wait()
+
+    def finish(self):
+        for wait in list(self.landing.values()) + self.sent:
+            wait()
+
+
+def feed_block(
+    block, rank_row, rank_column, gate_rows, scale, token_rows, token_cotangent,
+    expert_in, expert_down, shared, staged, between, out_terms, back_terms, scale_grad, token_grad,
+):
+    (
+        out_part, back_part, slot_rows, slot_cotangent, grad_pre, gated, grad_shared_pre, scaled,
+    ) = staged
+    bf16, f32 = jnp.bfloat16, jnp.float32
+    experts, slots, _ = slot_rows.shape
+    tokens = token_rows.shape[0]
+    hidden_count = gated.shape[2]
+    padded = expert_in.shape[2] // 2
+    all_slots = experts * slots
+    silu, slope = silu_parts(product(token_rows, shared[0], NT))
+    up = product(token_rows, shared[1], NT)
+    hidden = (silu * up).astype(bf16).astype(f32)
+    scaled_hidden = (scale * hidden).astype(bf16)
+    back = product(token_cotangent, shared[2], NT)
+    scale_grad[block] = jnp.sum(hidden * back, axis=1, keepdims=True)
+    back = scale * back
+    gate_grad = (back * up * slope).astype(bf16)
+    up_grad = (back * silu).astype(bf16)
+    between()
+    scaled[...] = scaled_hidden
+    grad_shared_pre[0] = gate_grad
+    grad_shared_pre[1] = up_grad
+    order = lax.broadcasted_iota(jnp.int32, (all_slots, tokens), 0)
+    spread_order = lax.broadcasted_iota(jnp.int32, (tokens, all_slots), 1)
+    hits, spread = None, None
+    for expert in range(experts):
+        row_hits = order == rank_row[expert : expert + 1, :] + expert * slots
+        column_hits = spread_order == rank_column[:, expert : expert + 1] + expert * slots
+        hits = row_hits if hits is None else hits | row_hits
+        spread = column_hits if spread is None else spread | column_hits
+    place = hits.astype(bf16)
+    taken = product(place, token_rows).astype(bf16)
+    taken_cotangent = product(place, token_cotangent).astype(bf16)
+    for ref, values in ((slot_rows, taken), (slot_cotangent, taken_cotangent)):
+        for expert in range(experts):
+            ref[expert] = values[expert * slots : (expert + 1) * slots]
+    for expert in range(experts):
+        mine = slice(expert * slots, (expert + 1) * slots)
+        gate = jnp.sum(
+            jnp.where(hits[mine], gate_rows[expert : expert + 1], 0.0), axis=1, keepdims=True
+        )
+        pre = product(taken[mine], expert_in[expert])
+        silu, slope = silu_parts(pre[:, :hidden_count])
+        up = pre[:, padded : padded + hidden_count]
+        hidden = (silu * up).astype(bf16).astype(f32)
+        gated_hidden = (gate * hidden).astype(bf16)
+        gated[expert] = gated_hidden
+        back = product(taken_cotangent[mine], expert_down[expert], NT)
+        slot_grad = jnp.sum(hidden * back, axis=1, keepdims=True)
+        token_grad[block, expert : expert + 1, :] = jnp.sum(
+            jnp.where(hits[mine], slot_grad, 0.0), axis=0, keepdims=True
+        )
+        back = gate * back
+        gate_grad_e = (back * up * slope).astype(bf16)
+        up_grad_e = (back * silu).astype(bf16)
+        grad_pre[0, expert] = gate_grad_e
+        grad_pre[1, expert] = up_grad_e
+        out_terms[mine, :] = product(gated_hidden, expert_down[expert]).astype(bf16)
+        gap = jnp.zeros((slots, padded - hidden_count), bf16)
+        both_grads = jnp.concatenate([gate_grad_e, gap, up_grad_e, gap], axis=1)
+        back_terms[mine, :] = product(both_grads, expert_in[expert], NT).astype(bf16)
+    spread = spread.astype(bf16)
+    out_part[...] = product(
+        jnp.concatenate([spread, scaled_hidden], axis=1), out_terms[...]
+    ).astype(bf16)
+    back_part[...] = product(
+        jnp.concatenate([spread, gate_grad, up_grad], axis=1), back_terms[...]
+    ).astype(bf16)
+
+
+def gather_feed_kernel(
+    rows, cotangent, scales, rank_row, rank_column, expert_in, expert_down, shared,
+    all_rows, all_cotangent, all_scales,
+    out_part, back_part, slot_rows, slot_cotangent, grad_pre, gated, grad_shared_pre, scaled,
+    token_grad, scale_grad,
+    expert_both, out_terms, back_terms, held_rows, held_cotangent,
+    stage_out, stage_back, stage_rows, stage_cotangent, stage_pre, stage_gated, stage_shared,
+    stage_scaled,
+    load_sems, store_sems, send_sems, recv_sems,
+):
     me = Peers()
-    copies = Copies(send_sems, recv_sems)
+    copies = LateCopies(send_sems, recv_sems)
     count = rows.shape[0]
     half, part = count // 2, count // 4
     q, qx, qc, qd = me.quarter, me.x_quarter, me.core_quarter, me.far_quarter
-    here = me.block(0)
+    blocks = {step: me.block(step) for step in range(-4, 5)}
     low, high, whole = pl.ds(0, half), pl.ds(half, half), pl.ds(0, count)
     own, other, scale = range(3)
+    full = (all_rows, all_cotangent)
     sides = ((RIGHT, me.right, -1, 0), (LEFT, me.left, 1, 1))
     greet([me.right, me.left, me.x_peer, me.core_peer, me.far_peer])
 
-    def cells(step, quarter, which):
-        return out.at[me.block(step), quarter, which]
-
-    def push(key, step, quarter, which, peer, landing_step, landing_quarter, source=None):
-        cell = cells(step, quarter, which)
-        copies.send(
-            key,
-            cell if source is None else source,
-            cell,
-            cells(landing_step, landing_quarter, which),
-            peer,
-        )
-
-    push((OVER_X, other, 0), 0, q, low, me.x_peer, 0, qx, rows.at[low])
-    push((RIGHT, own, 1), 0, q, whole, me.right, -1, q, rows)
-    push((LEFT, own, 1), 0, q, whole, me.left, 1, q, rows)
-    push((OVER_X, own, 0), 0, q, high, me.x_peer, 0, qx, rows.at[high])
-    push((OVER_CORE, own, 0), 0, q, whole, me.core_peer, 0, qc, rows)
-    copies.local((LOCAL, own), rows, out.at[here, q])
+    def push(key, kind, step, quarter, which, peer, landing_step, landing_quarter, source=None):
+        def cell():
+            return full[kind].at[blocks[step], quarter, which]
+
+        def landing():
+            return full[kind].at[blocks[landing_step], landing_quarter, which]
+
+        copies.send((kind,) + key, source or cell, cell, landing, peer)
+
+    push((OVER_X, other, 0), 0, 0, q, low, me.x_peer, 0, qx, lambda: rows.at[low])
+    for side, peer, sign, keep in sides:
+        push((side, own, 1), 1, 0, q, whole, peer, sign, q, lambda: cotangent.at[q])
+        push((side, other, 1), 1, 0, qx, low, peer, sign, qx, lambda: cotangent.at[qx, low])
+    push((OVER_X, own, 0), 0, 0, q, high, me.x_peer, 0, qx, lambda: rows.at[high])
+    push((OVER_CORE, own, 0), 0, 0, q, whole, me.core_peer, 0, qc, lambda: rows)
+    for side, peer, sign, keep in sides:
+        push((side, own, 1), 0, 0, q, whole, peer, sign, q, lambda: rows)
+    copies.local((LOCAL, 0), lambda: rows, lambda: all_rows.at[blocks[0], q])
+    copies.local((LOCAL, 1), lambda: cotangent, lambda: all_cotangent.at[blocks[0]])
+
+    def scales_of(quarter):
+        return lambda: all_scales.at[blocks[0], quarter]
+
     for way, peer, quarter in (
         (OVER_X, me.x_peer, qx),
         (OVER_CORE, me.core_peer, qc),
         (OVER_FAR, me.far_peer, qd),
     ):
-        copies.send(
-            (way, scale, 0), scales, out_scales.at[here, q], out_scales.at[here, quarter], peer
-        )
-    copies.local((LOCAL, scale), scales, out_scales.at[here, q])
-    copies.arrive(OVER_X, other, 0)
+        copies.send((way, scale, 0), lambda: scales, scales_of(q), scales_of(quarter), peer)
+    copies.local((LOCAL, scale), lambda: scales, scales_of(q))
+    experts, _, width, hidden_count = expert_in.shape
+    padded = expert_both.shape[2] // 2
+    all_slots = experts * slot_rows.shape[2]
+    shared_count = shared.shape[1]
+    gap = jnp.zeros((width, padded - hidden_count), expert_in.dtype)
+    for expert in range(experts):
+        for index in range(2):
+            start = index * padded
+            expert_both[expert, :, start : start + hidden_count] = expert_in[expert, index]
+            expert_both[expert, :, start + hidden_count : start + padded] = gap
+    out_terms[all_slots:, :] = shared[2]
+    back_terms[all_slots : all_slots + shared_count, :] = shared[0]
+    back_terms[all_slots + shared_count :, :] = shared[1]
+    copies.arrive(0, OVER_X, other, 0)
     for side, peer, sign, keep in sides:
-        push((side, other, 1), 0, qx, low, peer, sign, qx)
+        push((side, other, 1), 0, 0, qx, low, peer, sign, qx)
     for way in (OVER_X, OVER_CORE, OVER_FAR):
         copies.arrive(way, scale, 0)
     copies.arrive(LOCAL, scale)
 
     def push_scales(step, side, peer, sign):
-        blocks = out_scales.at[me.block(step)]
+        def cell():
+            return all_scales.at[blocks[step]]
+
         copies.send(
-            (side, scale, abs(step) + 1), blocks, blocks, out_scales.at[me.block(step + sign)], peer
+            (side, scale, abs(step) + 1), cell, cell, lambda: all_scales.at[blocks[step + sign]], peer
         )
 
     for side, peer, sign, keep in sides:
         push_scales(0, side, peer, sign)
-    copies.arrive(OVER_X, own, 0)
-    push((OVER_CORE, other, 0), 0, qx, whole, me.core_peer, 0, qd)
-    waiting = []
-    for hop in (1, 2, 3):
+    copies.arrive(0, OVER_X, own, 0)
+    push((OVER_CORE, other, 0), 0, 0, qx, whole, me.core_peer, 0, qd)
+
+    def hop_in(kind, hop):
         for side, peer, sign, keep in sides:
             step = sign * hop
-            copies.arrive(side, own, hop)
-            which = whole if hop < 3 else pl.ds(keep * half, half)
-            push((side, own, hop + 1), step, q, which, peer, step + sign, q)
-            push((OVER_X, own, step), step, q, high, me.x_peer, step, qx)
-            push((OVER_CORE, own, step), step, q, whole, me.core_peer, step, qc)
+            if hop < 4:
+                copies.arrive(kind, side, own, hop)
+                which = whole if hop < 3 else pl.ds(keep * half, half)
+                push((side, own, hop + 1), kind, step, q, which, peer, step + sign, q)
+                push((OVER_X, own, step), kind, step, q, high, me.x_peer, step, qx)
+                push((OVER_CORE, own, step), kind, step, q, whole, me.core_peer, step, qc)
+                copies.arrive(kind, side, other, hop)
+                which = low if hop < 3 else pl.ds(keep * part, part)
+                push((side, other, hop + 1), kind, step, qx, which, peer, step + sign, qx)
+                push((OVER_CORE, other, step), kind, step, qx, low, me.core_peer, step, qd)
+        if hop == 4:
+            copies.arrive(kind, LEFT, own, 4)
+            push((OVER_X, own, 4), kind, 4, q, high, me.x_peer, 4, qx)
+            copies.arrive(kind, RIGHT, own, 4)
+            push((OVER_CORE, own, 4), kind, 4, q, whole, me.core_peer, 4, qc)
+            copies.arrive(kind, LEFT, other, 4)
+            copies.arrive(kind, RIGHT, other, 4)
+            push((OVER_CORE, other, 4), kind, 4, qx, low, me.core_peer, 4, qd)
+
+    def over_x(kind, steps):
+        for step in steps:
+            copies.arrive(kind, OVER_X, own, step)
+            push((OVER_CORE, scale, step), kind, step, qx, high, me.core_peer, step, qd)
+
+    def scales_in(hop):
         for side, peer, sign, keep in sides:
-            step = sign * hop
-            copies.arrive(side, other, hop)
-            which = low if hop < 3 else pl.ds(keep * part, part)
-            push((side, other, hop + 1), step, qx, which, peer, step + sign, qx)
-            push((OVER_CORE, other, step), step, qx, low, me.core_peer, step, qd)
-            copies.arrive(side, scale, hop)
-            if hop < 3 or side == RIGHT:
-                push_scales(step, side, peer, sign)
-        for step in waiting:
-            copies.arrive(OVER_X, own, step)
-            push((OVER_CORE, scale, step), step, qx, high, me.core_peer, step, qd)
-        waiting = [-hop, hop]
-    copies.arrive(LEFT, own, 4)
-    push((OVER_X, own, 4), 4, q, high, me.x_peer, 4, qx)
-    copies.arrive(RIGHT, own, 4)
-    push((OVER_CORE, own, 4), 4, q, whole, me.core_peer, 4, qc)
-    copies.arrive(LEFT, other, 4)
-    copies.arrive(RIGHT, other, 4)
-    push((OVER_CORE, other, 4), 4, qx, low, me.core_peer, 4, qd)
-    for step in waiting + [4]:
-        copies.arrive(OVER_X, own, step)
-        push((OVER_CORE, scale, step), step, qx, high, me.core_peer, step, qd)
+            if hop < 4 or side == RIGHT:
+                copies.arrive(side, scale, hop)
+                if hop < 3 or (hop == 3 and side == RIGHT):
+                    push_scales(sign * hop, side, peer, sign)
+
+    def load(slot, step):
+        pairs = ((all_rows, held_rows), (all_cotangent, held_cotangent))
+        return [
+            pltpu.make_async_copy(source.at[blocks[step]], held.at[slot], load_sems.at[slot, kind])
+            for kind, (source, held) in enumerate(pairs)
+        ]
+
+    def complete(steps, slots):
+        for step in steps:
+            for kind in range(2):
+                if step != 0:
+                    for piece in (own, other, scale):
+                        copies.arrive(kind, OVER_CORE, piece, step)
+        moves = [load(slot, step) for slot, step in zip(slots, steps)]
+        for move in moves[0] + moves[-1] if len(moves) > 1 else moves[0]:
+            move.start()
+        for move in moves[0]:
+            move.wait()
+
+    staged = (
+        stage_out, stage_back, stage_rows, stage_cotangent, stage_pre, stage_gated, stage_shared,
+        stage_scaled,
+    )
+
+    def stores(block):
+        targets = (
+            out_part.at[block], back_part.at[block], slot_rows.at[:, block],
+            slot_cotangent.at[:, block], grad_pre.at[:, :, block], gated.at[:, block],
+            grad_shared_pre.at[:, block], scaled.at[block],
+        )
+        return [
+            pltpu.make_async_copy(stage, target, store_sems.at[index])
+            for index, (stage, target) in enumerate(zip(staged, targets))
+        ]
+
+    first_expert = me.ep * experts
+
+    copies.arrive(LOCAL, 0)
+    copies.arrive(LOCAL, 1)
+    for piece in (own, other):
+        copies.arrive(0, OVER_CORE, piece, 0)
+    complete((0,), (0,))
+
+    def turn(index, carry):
+        far = (index + 1) // 2
+        step = far * (1 - 2 * (index % 2)) + (index // 7) * 8
+        block = ring_member((me.place + step + RING) % RING)
+        slot = index % 2
+
+        def between():
+            for hop in (1, 2, 3, 4):
+
+                @pl.when(index == max(0, 2 * hop - 3))
+                def _():
+                    hop_in(1, hop)
+
+            @pl.when(index > 0)
+            def _():
+                for move in stores(0):
+                    move.wait()
+
+        rows_here = held_rows[slot].reshape(4 * count, width)
+        cotangent_here = held_cotangent[slot].reshape(4 * count, width)
+        quarters = [all_scales[block, quarter] for quarter in range(4)]
+        columns = jnp.concatenate([jnp.swapaxes(values, 0, 1) for values in quarters], axis=0)
+        scale_at = me_scale_row(all_scales, experts)
+        gate_rows = [
+            jnp.concatenate(
+                [all_scales[block, quarter, pl.ds(first_expert + e, 1), :] for quarter in range(4)],
+                axis=1,
+            )
+            for e in range(experts)
+        ]
+        feed_block(
+            block,
+            rank_row[block],
+            rank_column[block],
+            jnp.concatenate(gate_rows, axis=0),
+            columns[:, scale_at : scale_at + 1],
+            rows_here,
+            cotangent_here,
+            expert_both,
+            expert_down,
+            shared,
+            staged,
+            between,
+            out_terms,
+            back_terms,
+            scale_grad,
+            token_grad,
+        )
+        for move in stores(block):
+            move.start()
+
+        for hop in (1, 2, 3, 4):
+
+            @pl.when(index == max(0, 2 * hop - 3))
+            def _():
+                scales_in(hop)
+                hop_in(0, hop)
+                if hop > 1:
+                    for move in load(0, hop - 1):
+                        move.wait()
+
+            @pl.when(index == 2 * hop - 2)
+            def _():
+                steps = (-hop, hop) if hop < 4 else (4,)
+                over_x(1, steps)
+                over_x(0, steps)
+                complete(steps, (1, 0))
+
+        return carry
+
+    lax.fori_loop(0, RING, turn, 0)
+    for move in stores(0):
+        move.wait()
     copies.finish()
 
 
-def gather_rows(rows, scales, collective_id):
+def me_scale_row(all_scales, experts):
+    return RING * experts
+
+
+def gather_feed(
+    rows, cotangent, scales, rank, expert_in, expert_down, shared, capacity, collective_id
+):
+    bf16, f32 = jnp.bfloat16, jnp.float32
+    blocks, experts, tokens = rank.shape
+    count, width = rows.shape
+    hidden = expert_in.shape[3]
+    padded = -(-hidden // 128) * 128
+    slice_hidden = shared.shape[1]
+    shape = jax.ShapeDtypeStruct
+    stages = (
+        (tokens, width),
+        (tokens, width),
+        (experts, capacity, width),
+        (experts, capacity, width),
+        (2, experts, capacity, hidden),
+        (experts, capacity, hidden),
+        (2, tokens, slice_hidden),
+        (tokens, slice_hidden),
+    )
     return pl.pallas_call(
-        gather_kernel,
+        gather_feed_kernel,
         out_shape=(
-            jax.ShapeDtypeStruct((RING, 4) + rows.shape, rows.dtype),
-            jax.ShapeDtypeStruct((RING, 4) + scales.shape, scales.dtype),
+            shape((RING, 4, count, width), bf16),
+            shape((RING, 4, count, width), bf16),
+            shape((RING, 4) + scales.shape, f32),
+            shape((blocks, tokens, width), bf16),
+            shape((blocks, tokens, width), bf16),
+            shape((experts, blocks, capacity, width), bf16),
+            shape((experts, blocks, capacity, width), bf16),
+            shape((2, experts, blocks, capacity, hidden), bf16),
+            shape((experts, blocks, capacity, hidden), bf16),
+            shape((2, blocks, tokens, slice_hidden), bf16),
+            shape((blocks, tokens, slice_hidden), bf16),
+            shape((blocks, experts, tokens), f32),
+            shape((blocks, tokens, 1), f32),
         ),
-        in_specs=[IN_PLACE] * 2,
-        out_specs=(IN_PLACE,) * 2,
-        scratch_shapes=semaphores(80),
-        compiler_params=remote_params(collective_id),
-        name="gather_rows",
-    )(rows, scales)
+        in_specs=[IN_VMEM] * 8,
+        out_specs=(IN_PLACE,) * 2 + (IN_VMEM,) + (IN_PLACE,) * 8 + (IN_VMEM,) * 2,
+        scratch_shapes=[
+            pltpu.VMEM((experts, width, 2 * padded), bf16),
+            pltpu.VMEM((experts * capacity + slice_hidden, width), bf16),
+            pltpu.VMEM((experts * capacity + 2 * slice_hidden, width), bf16),
+            pltpu.VMEM((2, 4, count, width), bf16),
+            pltpu.VMEM((2, 4, count, width), bf16),
+        ]
+        + [pltpu.VMEM(stage, bf16) for stage in stages]
+        + [pltpu.SemaphoreType.DMA((2, 2)), pltpu.SemaphoreType.DMA((len(stages),))]
+        + semaphores(160),
+        compiler_params=remote_params(collective_id, 62),
+        name="gather_feed",
+    )(
+        rows, cotangent, scales, rank, jnp.swapaxes(rank, 1, 2), expert_in, expert_down, shared,
+    )
 
 
 def add_into(total, term, rows, tile=32):
@@ -767,7 +914,9 @@
     )(part, scalars)
 
 
-def spread_kernel(shard_in, shard_out, full_in, full_out, send_sems, recv_sems):
+def spread_kernel(
+    shard_in, shard_out, routes, full_in, full_out, full_routes, send_sems, recv_sems
+):
     me = Peers()
     copies = Copies(send_sems, recv_sems)
     kinds, depth, _ = shard_in.shape
@@ -779,10 +928,14 @@
         block = me.block(step)
         if kind < kinds:
             return full_in.at[kind, block, pl.ds(part * (depth // parts), depth // parts)]
+        if kind > kinds:
+            return full_routes.at[block]
         across = pl.ds(pl.multiple_of(block * columns, columns), columns)
         return full_out.at[pl.ds(part * (rows // parts), rows // parts), across]
 
     def pass_on(side, peer, sign, kind, hop, source=None):
+        if kind > kinds and hop == 3 and side == LEFT:
+            return
         parts = 2 if hop == 3 else 1
         part = side if hop == 3 else 0
         step = sign * hop
@@ -795,9 +948,9 @@
             peer,
         )
 
-    order = tuple(range(kinds - 1, -1, -1)) + (kinds,)
+    order = (kinds + 1,) + tuple(range(kinds - 1, -1, -1)) + (kinds,)
     for kind in order:
-        source = shard_in.at[kind] if kind < kinds else shard_out
+        source = shard_in.at[kind] if kind < kinds else shard_out if kind == kinds else routes
         for side, peer, sign in sides:
             pass_on(side, peer, sign, kind, 0, source)
         copies.local((LOCAL, kind), source, cell(kind, 0, 0, 1))
@@ -809,7 +962,7 @@
     copies.finish()
 
 
-def spread_weights(shard_in, shard_out, collective_id):
+def spread_weights(shard_in, shard_out, routes, collective_id):
     kinds, depth, width = shard_in.shape
     rows, columns = shard_out.shape
     return pl.pallas_call(
@@ -817,13 +970,14 @@
         out_shape=(
             jax.ShapeDtypeStruct((kinds, RING, depth, width), shard_in.dtype),
             jax.ShapeDtypeStruct((rows, RING * columns), shard_out.dtype),
+            jax.ShapeDtypeStruct((RING,) + routes.shape, routes.dtype),
         ),
-        in_specs=[IN_PLACE] * 2,
-        out_specs=(IN_PLACE,) * 2,
-        scratch_shapes=semaphores(9 * (kinds + 1)),
+        in_specs=[IN_VMEM] * 3,
+        out_specs=(IN_PLACE,) * 2 + (IN_VMEM,),
+        scratch_shapes=semaphores(9 * (kinds + 2)),
         compiler_params=remote_params(collective_id),
         name="spread_weights",
-    )(shard_in, shard_out)
+    )(shard_in, shard_out, routes)
 
 
 def collect_kernel(
@@ -1199,7 +1353,7 @@
     return pl.pallas_call(
         tensor_kernel,
         out_shape=jax.ShapeDtypeStruct((4,) + rows.shape, rows.dtype),
-        in_specs=[IN_PLACE],
+        in_specs=[IN_VMEM],
         out_specs=IN_PLACE,
         scratch_shapes=semaphores(4),
         compiler_params=remote_params(collective_id),
@@ -1249,11 +1403,11 @@
     )
     reach_back = min((WINDOW + tok_count - 2) // tok_count, ep_size - 1)
     local_experts = expert_in.shape[0]
-    in_blocks, out_full = spread_weights(attention_in, attention_out, 0)
+    route_rows = jnp.concatenate(
+        [routes.T, jnp.zeros((-top_count % 8, tok_count), routes.dtype)]
+    )
+    in_blocks, out_full, all_routes = spread_weights(attention_in, attention_out, route_rows, 0)
     in_full = in_blocks.reshape(3, model_width, -1)
-    all_cotangent = lax.all_gather(
-        after(own_rows(cotangent, tp_index, own_count), in_blocks), both, axis=0, tiled=True
-    )
     shard_width = shared_in.shape[1]
     slice_hidden = shared_in.shape[2] // ep_size
     shared_shards = jnp.concatenate([jnp.swapaxes(shared_in, 1, 2), shared_down[None]])
@@ -1266,7 +1420,13 @@
     shared_slices = jnp.transpose(shared_slices, (1, 2, 0, 3)).reshape(
         3, slice_hidden, model_width
     )
-    expert_both = jnp.swapaxes(expert_in, 1, 2).reshape(local_experts, model_width, -1)
+    my_ids = ep_index * local_experts + jnp.arange(local_experts, dtype=jnp.int32)
+    taken = jnp.any(all_routes[:, None, :top_count] == my_ids[None, :, None, None], axis=2)
+    earlier_mask = jnp.tril(jnp.ones((tok_count, tok_count), bf16), -1)
+    rank = product(
+        taken.astype(bf16).reshape(-1, tok_count), earlier_mask, NT
+    ).astype(jnp.int32).reshape(taken.shape)
+    rank = jnp.where(taken & (rank < capacity), rank, NO_SLOT)
 
     positions = ep_index * tok_count + jnp.arange(tok_count, dtype=jnp.int32)
     key_count = (reach_back + 1) * tok_count
@@ -1297,26 +1457,13 @@
     chosen = jnp.where(picked, router_probs, 0.0)
     chosen_total = jnp.sum(chosen, axis=1, keepdims=True)
     gates = chosen / chosen_total
-    scale_count = -(-(expert_count + 1 + top_count) // 8) * 8
-    scale_rows = jnp.zeros((scale_count, own_count), f32)
-    scale_rows = scale_rows.at[:expert_count].set(gates.T).at[expert_count].set(shared_scale)
-    scale_rows = scale_rows.at[expert_count + 1 : expert_count + 1 + top_count].set(
-        routes_own.T.astype(f32)
-    )
-    all_rows, all_scales = gather_rows(normed_low, scale_rows, 3)
-    all_rows = all_rows.reshape(ep_size, tok_count, model_width)
-    all_cotangent = all_cotangent.reshape(ep_size, tok_count, model_width)
-    all_scales = jnp.swapaxes(all_scales, 1, 2).reshape(ep_size, scale_count, tok_count)
-    my_gates = lax.dynamic_slice_in_dim(all_scales, ep_index * local_experts, local_experts, 1)
-    my_ids = ep_index * local_experts + jnp.arange(local_experts, dtype=jnp.int32)
-    all_routes = all_scales[:, expert_count + 1 : expert_count + 1 + top_count].astype(jnp.int32)
-    taken = jnp.any(all_routes[:, None] == my_ids[None, :, None, None], axis=2)
-    earlier_mask = jnp.tril(jnp.ones((tok_count, tok_count), bf16), -1)
-    rank = product(
-        taken.astype(bf16).reshape(-1, tok_count), earlier_mask, NT
-    ).astype(jnp.int32).reshape(taken.shape)
-    rank = jnp.where(taken & (rank < capacity), rank, NO_SLOT)
+    scale_count = -(-(expert_count + 1) // 8) * 8
+    spare = jnp.zeros((scale_count - expert_count - 1, own_count), f32)
+    scale_rows = jnp.concatenate([gates.T, shared_scale[None], spare])
     (
+        all_rows,
+        all_cotangent,
+        all_scales,
         ffn_part,
         back_part,
         slot_rows,
@@ -1327,16 +1474,16 @@
         scaled_hidden,
         token_grad,
         scale_grad,
-    ) = feed(
+    ) = gather_feed(
+        normed_low,
+        cotangent.reshape(tp_size, own_count, model_width),
+        scale_rows,
         rank,
-        my_gates,
-        all_scales[:, expert_count][:, :, None],
-        all_rows,
-        all_cotangent,
-        expert_both,
+        expert_in,
         expert_down,
         shared_slices,
         capacity,
+        3,
     )
     ffn_sum = lax.psum_scatter(
         ffn_part.reshape(all_count, model_width), both, scatter_dimension=0, tiled=True
@@ -1344,11 +1491,13 @@
     layer_output = lax.all_gather(
         (residual + ffn_sum.astype(f32)).astype(bf16), TP, axis=0, tiled=True
     )
-    scalar_part = jnp.zeros((ep_size, scale_count, tok_count), f32)
+    spare = jnp.zeros((ep_size, scale_count - expert_count - 1, tok_count), f32)
+    scalar_part = jnp.concatenate(
+        [jnp.zeros((ep_size, expert_count, tok_count), f32), scale_grad[:, None, :, 0], spare], axis=1
+    )
     scalar_part = lax.dynamic_update_slice(
         scalar_part, token_grad, (0, ep_index * local_experts, 0)
     )
-    scalar_part = scalar_part.at[:, expert_count].set(scale_grad[:, :, 0])
     scalar_part = jnp.swapaxes(
         scalar_part.reshape(ep_size, scale_count, tp_size, own_count), 1, 2
     )

time: 1000 us -> 951 us (0.951)
  Pallas kernels: 798 us -> 747 us
    pallas_call x1, Pallas kernels: 77.2 us -> 43.1 us  [share_keys(): pl.pallas_call(share_kernel, out_shape=jax.ShapeDtypeStruct((kinds, 3, to...]
    pallas_call x2, Pallas kernels: 52 us -> 40.7 us  [product_to_owner(): pl.pallas_call(functools.partial(reduce_kernel, flip), out_shape=jax.Shap...]
    unnamed x173 -> x148, local copies, waits for them, and re-layouts: 29.9 us -> 40.3 us
    pallas_call x2 -> x1, Pallas kernels: 203 us -> 200 us  [gather_feed(): pl.pallas_call(gather_feed_kernel, out_shape=(shape((RING, 4, count, widt...]
  transfers between devices with their start and end apart: 6 -> 5, of which waited for: 1 -> 1; matrix products, arithmetic and copies ran while one was open for 13% -> 14% of each run, Pallas kernels for 62% -> 49%
where the time goes in v2:
time: 951 us; the launch traced here: 945 us
  Pallas kernels  747 us (79%)
  local copies, waits for them, and re-layouts  69.8 us (7%)
  matrix products  67.8 us (7%)
  other arithmetic  24.4 us (3%)
  starting transfers between devices  18.9 us (2%)
  between operations  15.1 us (2%)
    pallas_call x1, Pallas kernels, gather_feed(): pl.pallas_call(gather_feed_kernel, out_shape=(shape((RING, 4, count, widt...  200 us
    pallas_call x1, Pallas kernels, scatter_rows(): pl.pallas_call(scatter_kernel, out_shape=(jax.ShapeDtypeStruct((count, wi...  141 us
    pallas_call x1, Pallas kernels, collect_weights(): pl.pallas_call(collect_kernel, out_shape=(jax.ShapeDtypeStruct((kinds, de...  107 us
    pallas_call x1, Pallas kernels, spread_weights(): pl.pallas_call(spread_kernel, out_shape=(jax.ShapeDtypeStruct((kinds, RIN...  85.9 us
    pallas_call x2, Pallas kernels, tensor_gather(): pl.pallas_call(tensor_kernel, out_shape=jax.ShapeDtypeStruct((4,) + rows....  52.7 us
    pallas_call x1, Pallas kernels, return_keys(): pl.pallas_call(return_kernel, out_shape=jax.ShapeDtypeStruct((kinds, toke...  49.1 us
    pallas_call x1, Pallas kernels, share_keys(): pl.pallas_call(share_kernel, out_shape=jax.ShapeDtypeStruct((kinds, 3, to...  43.1 us
    pallas_call x2, Pallas kernels, product_to_owner(): pl.pallas_call(functools.partial(reduce_kernel, flip), out_shape=jax.Shap...  40.7 us
  transfers between devices with their start and end apart: 5, of which 1 were waited for; matrix products, arithmetic and copies ran while one was open for 14% of the time, Pallas kernels for 49%

profile of v2, /device:TPU:0, one launch (start us, length us, event | category | flops | bytes accessed | tf_op | source)
XLA Modules:
  0.0 944.8 jit_solution(10607902302333091171)
XLA Ops:
  7.2 1.8 copy.86
  10.2 85.9 %spread_weights.1 = (bf16[3,8,256,512]{3,2,1,0:T(8,128)(2,1)}, bf16[512,2048]{1,0:T(8,128)(2,1)S(1)}, s32[8,8,512]{2,1,0:T(8,128)S(1)}) custom-call(bf16[3,256,512]{2,1,0:T(8,128)(2,1)S(1)} %copy-done.20, bf16[512,256]{1,0:T(8,128)(2,1)S(1)} %copy-done.24, s32[8,512]{1,0:T(8,128)S(1)} %concatenate.36.routes), custom_call_target="tpu_custom_call" | custom-call | tf_op jit(solution)/shard_map/spread_weights/pallas_call | solution.py:968
  97.4 1.5 copy.87
  98.9 4.9 all-to-all-start
  107.0 1.4 copy.84
  108.4 2.8 copy-done.4
  111.2 5.1 project.1
  117.6 43.1 %share_keys.1.keys.values = bf16[2,3,512,512]{3,2,1,0:T(8,128)(2,1)S(1)} custom-call(bf16[2,512,512]{2,1,0:T(8,128)(2,1)S(1)} %get-tuple-element.43.own), custom_call_target="tpu_custom_call" | custom-call | tf_op jit(solution)/shard_map/share_keys/pallas_call | solution.py:1191
  160.7 1.7 copy-done.2
  163.6 2.0 copy.83
  165.6 3.4 and_select_fusion
  169.0 2.8 copy.89.rank_row
  171.8 8.4 copy.90.expert_in
  182.1 1.9 copy-done.3
  184.0 9.9 %attend.1 = (bf16[512,512]{1,0:T(8,128)(2,1)S(1)}, f32[4,512,1]{2,1,0:T(8,128)S(1)}) custom-call(bf16[512,512]{1,0:T(8,128)(2,1)S(1)} %get-tuple-element.42.queries, bf16[2,3,512,512]{3,2,1,0:T(8,128)(2,1)S(1)} %copy-done.3, bf16[2,3,512,512]{3,2,1,0:T(8,128)(2,1)S(1)} %copy-done.3, s32[512,1]{1,0:T(8,128)S(1)} %fusion.37.query_doc, ...), custom_call_target="tpu_custom_call" | custom-call | tf_op jit(solution)/shard_map/attend/pallas_call | solution.py:192
  195.7 17.1 %product_to_owner.2 = f32[128,2048]{1,0:T(8,128)S(1)} custom-call(bf16[1,512,512]{2,1,0:T(8,128)(2,1)S(1)} %bitcast.140, bf16[1,512,2048]{2,1,0:T(8,128)(2,1)S(1)} %bitcast.134), custom_call_target="tpu_custom_call" | custom-call | tf_op jit(solution)/shard_map/product_to_owner/pallas_call | solution.py:1321
  213.8 1.5 multiply_reduce_fusion.2
  219.2 3.2 copy.108
  222.5 200.1 %gather_feed.1 = (bf16[8,4,128,2048]{3,2,1,0:T(8,128)(2,1)}, bf16[8,4,128,2048]{3,2,1,0:T(8,128)(2,1)}, f32[8,4,24,128]{3,2,1,0:T(8,128)}, bf16[8,512,2048]{2,1,...) custom-call(bf16[128,2048]{1,0:T(8,128)(2,1)} %fusion.22.rows, ...), custom_call_target="tpu_custom_call" | custom-call | tf_op jit(solution)/shard_map/gather_feed/pallas_call | solution.py:707
  425.3 140.7 %scatter_rows.1 = (f32[128,2048]{1,0:T(8,128)S(1)}, f32[24,128]{1,0:T(8,128)S(1)}) custom-call(bf16[8,4,128,2048]{3,2,1,0:T(8,128)(2,1)} %bitcast.150, f32[8,4,24,128]{3,2,1,0:T(8,128)S(1)} %bitcast_bitcast_fusion.scalars), custom_call_target="tpu_custom_call" | custom-call | tf_op jit(solution)/shard_map/scatter_rows/pallas_call | solution.py:891
  566.1 1.9 multiply_reduce_fusion
  570.5 27.4 %tensor_gather.2 = bf16[4,128,2048]{2,1,0:T(8,128)(2,1)S(1)} custom-call(bf16[128,2048]{1,0:T(8,128)(2,1)S(1)} %fusion.52.rows), custom_call_target="tpu_custom_call" | custom-call | tf_op jit(solution)/shard_map/tensor_gather/pallas_call | solution.py:1353
  600.0 13.0 %attend_back.1 = (bf16[512,512]{1,0:T(8,128)(2,1)S(1)}, bf16[2,3,512,512]{3,2,1,0:T(8,128)(2,1)}) custom-call(bf16[512,512]{1,0:T(8,128)(2,1)S(1)} %copy-done.17, bf16[2,3,512,512]{3,2,1,0:T(8,128)(2,1)} %copy-done.2, bf16[2,3,512,512]{3,2,1,0:T(8,128)(2,1)} %copy-done.2, s32[512,1]{1,0:T(8,128)S(1)} %fusion.37.query_doc, s32[1,1536]{1,0:T(1,128)S(1)} %copy-done.28, ...), custom_call_target="tpu_custom_call" | custom-call | tf_op jit(solution)/shard_map/attend_back/pallas_call | solution.py:234
  613.0 1.9 copy-done.9
  614.9 49.1 %return_keys.1 = bf16[2,512,512]{2,1,0:T(8,128)(2,1)S(1)} custom-call(bf16[2,3,512,512]{3,2,1,0:T(8,128)(2,1)S(1)} %copy-done.9, f32[512,128]{1,0:T(8,128)S(1)} %get-tuple-element.127.cosine, f32[512,128]{1,0:T(8,128)S(1)} %get-tuple-element.128.sine), custom_call_target="tpu_custom_call" | custom-call | tf_op jit(solution)/shard_map/return_keys/pallas_call | solution.py:1268
  664.2 23.7 %product_to_owner.3 = f32[128,2048]{1,0:T(8,128)S(1)} custom-call(bf16[3,512,512]{2,1,0:T(8,128)(2,1)S(1)} %pad_maximum_fusion.left, bf16[3,2048,512]{2,1,0:T(8,128)(2,1)} %bitcast.131), custom_call_target="tpu_custom_call" | custom-call | tf_op jit(solution)/shard_map/product_to_owner/pallas_call | solution.py:1321
  687.9 5.6 convert_bitcast_fusion
  693.4 8.7 copy.94
  702.1 1.9 fusion.16
  704.0 9.7 %convolution_convert_fusion.1 = bf16[2048,176]{0,1:T(8,128)(2,1)S(1)} fusion(bf16[4096,2048]{1,0:T(8,128)(2,1)} %bitcast.179, bf16[4096,176]{1,0:T(8,128)(2,1)} %bitcast.182), kind=kOutput, calls=%fused_computation.6 | convolution fusion | flops 2953150464 | bytes 18939904 | tf_op jit(solution)/shard_map/dot_general | solution.py:88
  714.5 7.6 convolution_convert_fusion.2
  722.4 7.6 convolution_convert_fusion.3
  730.3 1.6 maximum_bitcast_fusion.1
  731.8 13.7 %all-to-all-start.1 = ((bf16[8,3,176,256]{3,2,1,0:T(8,128)(2,1)}), bf16[8,3,176,256]{3,2,1,0:T(8,128)(2,1)}, u32[]{:S(2)}, u32[]{:S(2)}) async-start(bf16[8,3,176,256]{3,2,1,0:T(8,128)(2,1)} %maximum_bitcast_fusion.1), calls=%async_computation.2 | async-start | bytes 4325376 | tf_op jit(solution)/shard_map/all_to_all | solution.py:1529
  745.9 2.1 fusion.20
  749.6 3.6 convolution_convert_fusion.grad_out
  753.5 11.2 %fusion.56 = f32[2,352,2048]{2,1,0:T(8,128)} fusion(bf16[2,1280,352]{2,1,0:T(8,128)(2,1)} %bitcast.153, bf16[2,1280,2048]{2,1,0:T(8,128)(2,1)} %bitcast.151), kind=kOutput, calls=%fused_computation.123 | convolution fusion | flops 3690987520 | bytes 18055168 | tf_op jit(solution)/shard_map/erf,erd->efd/dot_general | solution.py:1512
  764.8 106.7 %collect_weights.1 = (f32[3,256,512]{2,1,0:T(8,128)S(1)}, f32[512,256]{1,0:T(8,128)S(1)}, f32[4,8,512]{2,1,0:T(8,128)S(1)}) custom-call(bf16[3,8,256,512]{3,2,1,0:T(8,128)(2,1)} %bitcast.147, bf16[512,2048]{1,0:T(8,128)(2,1)S(1)} %copy-done.15, f32[8,512]{1,0:T(8,128)S(1)} %maximum_maximum_fusion.1.tail), custom_call_target="tpu_custom_call" | custom-call | tf_op jit(solution)/shard_map/collect_weights/pallas_call | solution.py:1078
  872.4 3.3 fusion.15
  877.0 14.1 %convolution_bitcast_fusion = f32[2,2,2048,352]{2,3,1,0:T(8,128)} fusion(bf16[2,1280,2048,1]{2,1,3,0:T(8,128)(2,1)} %bitcast.180, bf16[2,2,1280,352]{3,2,1,0:T(8,128)(2,1)} %bitcast.181), kind=kOutput, calls=%fused_computation.1 | convolution fusion | flops 7381975040 | bytes 25624576 | tf_op jit(solution)/shard_map/erd,serf->esdf/dot_general | solution.py:1515
  891.1 1.8 all-reduce.3.cloned.1.call-done
  892.9 1.5 fusion.54
  894.4 1.6 slice_bitcast_fusion
  896.0 2.1 convert_bitcast_fusion.1
  898.1 1.8 slice.74
  901.1 3.5 copy.101
  904.6 25.3 %tensor_gather.3 = bf16[4,128,2048]{2,1,0:T(8,128)(2,1)S(1)} custom-call(bf16[128,2048]{1,0:T(8,128)(2,1)S(1)} %get-tuple-element.117.rows), custom_call_target="tpu_custom_call" | custom-call | tf_op jit(solution)/shard_map/tensor_gather/pallas_call | solution.py:1353
  931.2 3.3 copy.123
  (220 shorter events, 35.5 us)
Async XLA Ops:
  7.2 208.2 %copy-start = (f32[2048,16]{0,1:T(8,128)S(1)}, f32[2048,16]{0,1:T(8,128)}, u32[]{:S(2)}) copy-start(f32[2048,16]{0,1:T(8,128)} %param.24) | copy-start | bytes 393220
  98.9 5.0 copy-start.67
  98.9 120.4 %all-to-all-start = ((bf16[8,3,176,256]{3,2,1,0:T(8,128)(2,1)}), bf16[8,3,176,256]{3,2,1,0:T(8,128)(2,1)}, u32[]{:S(2)}, u32[]{:S(2)}) async-start(bf16[8,3,176,256]{3,2,1,0:T(8,128)(2,1)} %copy.87), calls=%async_computation | async-start | bytes 4325376 | tf_op jit(solution)/shard_map/all_to_all | solution.py:1417
  103.8 4.6 copy-start.7
  103.8 4.6 copy-start.25
  103.8 4.6 copy-start.29
  103.8 768.6 %reduce-scatter.2.cloned.1.call-start = ((), (), s32[]{:S(2)}) async-start(), calls=%async_computation.3 | async-start | bytes 17301504 | tf_op jit(solution)/shard_map/reduce_scatter | solution.py:1488
  108.4 2.8 copy-start.4
  117.6 64.5 %copy-start.16 = (bf16[512,512]{1,0:T(8,128)(2,1)}, bf16[512,512]{1,0:T(8,128)(2,1)S(1)}, u32[]{:S(2)}) copy-start(bf16[512,512]{1,0:T(8,128)(2,1)S(1)} %get-tuple-element.42.queries) | copy-start | bytes 1572868
  181.1 12.8 %copy-start.27 = (s32[1,1536]{1,0:T(1,128)}, s32[1,1536]{1,0:T(1,128)S(1)}, u32[]{:S(2)}) copy-start(s32[1,1536]{1,0:T(1,128)S(1)} %compare_select_fusion.key_doc) | copy-start | bytes 18436
  184.0 11.7 %copy-start.11 = (bf16[512,2048]{1,0:T(8,128)(2,1)S(1)}, bf16[512,2048]{1,0:T(8,128)(2,1)}, u32[]{:S(2)}) copy-start(bf16[512,2048]{1,0:T(8,128)(2,1)} %copy-done.10) | copy-start | bytes 6291460
  213.7 2.8 copy-start.45
  215.3 2.9 copy-start.32
  215.4 352.7 %copy-start.43 = (f32[128]{0:T(128)}, f32[128]{0:T(128)S(1)}, u32[]{:S(2)}) copy-start(f32[128]{0:T(128)S(1)} %add_rsqrt_fusion.1) | copy-start | bytes 1540
  216.4 349.7 %copy-start.41 = (f32[128,16]{0,1:T(8,128)}, f32[128,16]{0,1:T(8,128)S(1)}, u32[]{:S(2)}) copy-start(f32[128,16]{0,1:T(8,128)S(1)} %get-tuple-element.125) | copy-start | bytes 24580
  216.4 349.7 %copy-start.47 = (f32[128]{0:T(128)}, f32[128]{0:T(128)S(1)}, u32[]{:S(2)}) copy-start(f32[128]{0:T(128)S(1)} %get-tuple-element.124) | copy-start | bytes 1540
  216.5 349.7 %copy-start.50 = (f32[128]{0:T(128)}, f32[128]{0:T(128)S(1)}, u32[]{:S(2)}) copy-start(f32[128]{0:T(128)S(1)} %fusion.42) | copy-start | bytes 1540
  216.5 349.6 %copy-start.52 = (f32[128]{0:T(128)}, f32[128]{0:T(128)S(1)}, u32[]{:S(2)}) copy-start(f32[128]{0:T(128)S(1)} %fusion.43) | copy-start | bytes 1540
  422.7 2.6 copy-start.49
  425.3 140.8 %copy-start.33 = (f32[128,2048]{1,0:T(8,128)S(1)}, f32[128,2048]{1,0:T(8,128)}, u32[]{:S(2)}) copy-start(f32[128,2048]{1,0:T(8,128)} %copy-done.32) | copy-start | bytes 3145732
  566.0 4.4 copy-start.55
  566.1 4.4 copy-start.57
  566.1 4.4 copy-start.61
  568.1 29.7 %copy-start.63 = (f32[128]{0:T(128)}, f32[128]{0:T(128)S(1)}, u32[]{:S(2)}) copy-start(f32[128]{0:T(128)S(1)} %broadcast_multiply_fusion.1) | copy-start | bytes 1540
  570.5 27.4 %copy-start.12 = (bf16[512,2048]{1,0:T(8,128)(2,1)S(1)}, bf16[512,2048]{1,0:T(8,128)(2,1)}, u32[]{:S(2)}) copy-start(bf16[512,2048]{1,0:T(8,128)(2,1)} %copy-done.10) | copy-start | bytes 6291460
  664.2 23.7 %copy-start.31 = (bf16[512,2048]{1,0:T(8,128)(2,1)S(1)}, bf16[512,2048]{1,0:T(8,128)(2,1)}, u32[]{:S(2)}) copy-start(bf16[512,2048]{1,0:T(8,128)(2,1)} %copy-done.30) | copy-start | bytes 6291460
  693.4 8.7 copy-start.26
  693.4 8.7 copy-start.59
  704.0 10.0 %copy-start.36 = (bf16[2,8,512,176]{3,2,1,0:T(8,128)(2,1)S(1)}, bf16[2,8,512,176]{3,2,1,0:T(8,128)(2,1)}, u32[]{:S(2)}) copy-start(bf16[2,8,512,176]{3,2,1,0:T(8,128)(2,1)} %get-tuple-element.62) | copy-start | bytes 8650756
  731.8 14.1 %copy-start.40 = (f32[2048]{0:T(1024)S(1)}, f32[2048]{0:T(1024)}, u32[]{:S(2)}) copy-start(f32[2048]{0:T(1024)} %param.20) | copy-start | bytes 24580
  731.8 14.1 %copy-start.44 = (f32[128]{0:T(128)S(1)}, f32[128]{0:T(128)}, u32[]{:S(2)}) copy-start(f32[128]{0:T(128)} %copy-done.43) | copy-start | bytes 1540
  731.8 14.1 %copy-start.62 = (f32[128]{0:T(128)S(1)}, f32[128]{0:T(128)}, u32[]{:S(2)}) copy-start(f32[128]{0:T(128)} %copy-done.61) | copy-start | bytes 1540
  731.8 164.2 %all-to-all-start.1 = ((bf16[8,3,176,256]{3,2,1,0:T(8,128)(2,1)}), bf16[8,3,176,256]{3,2,1,0:T(8,128)(2,1)}, u32[]{:S(2)}, u32[]{:S(2)}) async-start(bf16[8,3,176,256]{3,2,1,0:T(8,128)(2,1)} %maximum_bitcast_fusion.1), calls=%async_computation.2 | async-start | bytes 4325376 | tf_op jit(solution)/shard_map/all_to_all | solution.py:1529
  745.5 2.5 copy-start.42
  745.5 2.5 copy-start.48
  745.6 2.5 copy-start.51
  745.6 2.5 copy-start.53
  745.6 3.3 copy-start.46
  745.6 147.3 %all-reduce.3.cloned.1.call-start = ((), (), s32[]{:S(2)}) async-start(), calls=%async_computation.5 | async-start | bytes 393216 | tf_op jit(solution)/shard_map/psum | solution.py:1557
  745.9 3.7 copy-start.14
  753.3 177.9 %all-gather.2.cloned.1.call-start = ((), (), s32[]{:S(2)}) async-start(), calls=%async_computation.4 | async-start | bytes 2621440 | tf_op jit(solution)/shard_map/all_gather | solution.py:1491
  753.5 11.2 %copy-start.66 = (f32[8]{0:T(128)S(1)}, f32[8]{0:T(128)}, u32[]{:S(2)}) copy-start(f32[8]{0:T(128)} %pad.9.clone) | copy-start | bytes 100
  753.5 11.3 %copy-start.15 = (bf16[512,2048]{1,0:T(8,128)(2,1)S(1)}, bf16[512,2048]{1,0:T(8,128)(2,1)}, u32[]{:S(2)}) copy-start(bf16[512,2048]{1,0:T(8,128)(2,1)} %convolution_convert_fusion.grad_out) | copy-start | bytes 6291460
  764.8 107.5 %copy-start.65 = (f32[128]{0:T(128)S(1)}, f32[128]{0:T(128)}, u32[]{:S(2)}) copy-start(f32[128]{0:T(128)} %get-tuple-element.109) | copy-start | bytes 1540
  764.8 107.6 %copy-start.60 = (f32[128]{0:T(128)S(1)}, f32[128]{0:T(128)}, u32[]{:S(2)}) copy-start(f32[128]{0:T(128)} %add_rsqrt_fusion) | copy-start | bytes 1540
  764.8 107.6 %copy-start.64 = (f32[128]{0:T(128)S(1)}, f32[128]{0:T(128)}, u32[]{:S(2)}) copy-start(f32[128]{0:T(128)} %copy-done.63) | copy-start | bytes 1540
  931.2 3.3 copy-start.6
  934.5 3.5 copy-start.1
  (25 other events, 39.3 us)
Sparse Core Ops, SparseCore 0:
  422.8 247.5 reduce-scatter.1
  753.4 139.4 all-reduce.2
  895.0 33.1 all-gather.1

commit v3 on v2

--- a/solution.py
+++ b/solution.py
@@ -247,7 +247,7 @@
 
 RING = 8
 NO_SLOT = 1 << 20
-RIGHT, LEFT, OVER_X, OVER_CORE, OVER_FAR, OVER_Y, OVER_Z, LOCAL = range(8)
+RIGHT, LEFT, OVER_X, OVER_CORE, OVER_FAR, LOCAL, SCALARS = range(7)
 MESH_ID = pl.DeviceIdType.MESH
 
 
@@ -379,7 +379,6 @@
     experts, slots, _ = slot_rows.shape
     tokens = token_rows.shape[0]
     hidden_count = gated.shape[2]
-    padded = expert_in.shape[2] // 2
     all_slots = experts * slots
     silu, slope = silu_parts(product(token_rows, shared[0], NT))
     up = product(token_rows, shared[1], NT)
@@ -413,9 +412,9 @@
         gate = jnp.sum(
             jnp.where(hits[mine], gate_rows[expert : expert + 1], 0.0), axis=1, keepdims=True
         )
-        pre = product(taken[mine], expert_in[expert])
+        pre = product(taken[mine], expert_in[expert], NT)
         silu, slope = silu_parts(pre[:, :hidden_count])
-        up = pre[:, padded : padded + hidden_count]
+        up = pre[:, hidden_count:]
         hidden = (silu * up).astype(bf16).astype(f32)
         gated_hidden = (gate * hidden).astype(bf16)
         gated[expert] = gated_hidden
@@ -430,9 +429,8 @@
         grad_pre[0, expert] = gate_grad_e
         grad_pre[1, expert] = up_grad_e
         out_terms[mine, :] = product(gated_hidden, expert_down[expert]).astype(bf16)
-        gap = jnp.zeros((slots, padded - hidden_count), bf16)
-        both_grads = jnp.concatenate([gate_grad_e, gap, up_grad_e, gap], axis=1)
-        back_terms[mine, :] = product(both_grads, expert_in[expert], NT).astype(bf16)
+        both_grads = jnp.concatenate([gate_grad_e, up_grad_e], axis=1)
+        back_terms[mine, :] = product(both_grads, expert_in[expert]).astype(bf16)
     spread = spread.astype(bf16)
     out_part[...] = product(
         jnp.concatenate([spread, scaled_hidden], axis=1), out_terms[...]
@@ -447,7 +445,7 @@
     all_rows, all_cotangent, all_scales,
     out_part, back_part, slot_rows, slot_cotangent, grad_pre, gated, grad_shared_pre, scaled,
     token_grad, scale_grad,
-    expert_both, out_terms, back_terms, held_rows, held_cotangent,
+    out_terms, back_terms, held_rows, held_cotangent,
     stage_out, stage_back, stage_rows, stage_cotangent, stage_pre, stage_gated, stage_shared,
     stage_scaled,
     load_sems, store_sems, send_sems, recv_sems,
@@ -494,16 +492,9 @@
     ):
         copies.send((way, scale, 0), lambda: scales, scales_of(q), scales_of(quarter), peer)
     copies.local((LOCAL, scale), lambda: scales, scales_of(q))
-    experts, _, width, hidden_count = expert_in.shape
-    padded = expert_both.shape[2] // 2
+    experts, _, width = expert_in.shape
     all_slots = experts * slot_rows.shape[2]
     shared_count = shared.shape[1]
-    gap = jnp.zeros((width, padded - hidden_count), expert_in.dtype)
-    for expert in range(experts):
-        for index in range(2):
-            start = index * padded
-            expert_both[expert, :, start : start + hidden_count] = expert_in[expert, index]
-            expert_both[expert, :, start + hidden_count : start + padded] = gap
     out_terms[all_slots:, :] = shared[2]
     back_terms[all_slots : all_slots + shared_count, :] = shared[0]
     back_terms[all_slots + shared_count :, :] = shared[1]
@@ -642,7 +633,7 @@
             columns[:, scale_at : scale_at + 1],
             rows_here,
             cotangent_here,
-            expert_both,
+            expert_in,
             expert_down,
             shared,
             staged,
@@ -690,8 +681,7 @@
     bf16, f32 = jnp.bfloat16, jnp.float32
     blocks, experts, tokens = rank.shape
     count, width = rows.shape
-    hidden = expert_in.shape[3]
-    padded = -(-hidden // 128) * 128
+    hidden = expert_in.shape[1] // 2
     slice_hidden = shared.shape[1]
     shape = jax.ShapeDtypeStruct
     stages = (
@@ -724,7 +714,6 @@
         in_specs=[IN_VMEM] * 8,
         out_specs=(IN_PLACE,) * 2 + (IN_VMEM,) + (IN_PLACE,) * 8 + (IN_VMEM,) * 2,
         scratch_shapes=[
-            pltpu.VMEM((experts, width, 2 * padded), bf16),
             pltpu.VMEM((experts * capacity + slice_hidden, width), bf16),
             pltpu.VMEM((experts * capacity + 2 * slice_hidden, width), bf16),
             pltpu.VMEM((2, 4, count, width), bf16),
@@ -752,166 +741,348 @@
     lax.fori_loop(0, rows // tile, step, 0)
 
 
+class WeightGrads:
+    def __init__(self, jobs, left, right, sums, low, sems, out_sems):
+        self.jobs, self.left, self.right = jobs, left, right
+        self.sums, self.low, self.sems, self.out_sems = sums, low, sems, out_sems
+        self.next = 0
+        self.stores = {}
+        self.fetch(0, 0, 0).start()
+
+    def fetch(self, job, index, slot):
+        left, right, _ = self.jobs[job]
+        chunk, rows, columns, _ = self.size(job)
+        here = pl.ds(pl.multiple_of(index * chunk, chunk), chunk)
+        return Pair(
+            pltpu.make_async_copy(
+                left.at[here], self.left[rows].at[slot, pl.ds(0, chunk)], self.sems.at[slot, 0]
+            ),
+            pltpu.make_async_copy(
+                right.at[here], self.right.at[slot, pl.ds(0, chunk)], self.sems.at[slot, 1]
+            ),
+        )
+
+    def size(self, job):
+        left, right, _ = self.jobs[job]
+        depth, rows = left.shape
+        chunk = min(self.right.shape[1], depth)
+        while depth % (2 * chunk):
+            chunk -= 128
+        return chunk, rows, right.shape[1], depth // chunk
+
+    def run(self, count=1):
+        for job in range(self.next, min(self.next + count, len(self.jobs))):
+            self.one(job)
+
+    def one(self, job):
+        self.next = job + 1
+        chunk, rows, _, steps = self.size(job)
+        which = job % 2
+        if which in self.stores:
+            self.stores.pop(which).wait()
+        total = self.sums.at[which, pl.ds(0, rows)]
+
+        def step(index, carry):
+            slot = index % 2
+
+            @pl.when(index + 1 < steps)
+            def _():
+                self.fetch(job, index + 1, 1 - slot).start()
+
+            if job + 1 < len(self.jobs):
+
+                @pl.when(index + 1 == steps)
+                def _():
+                    self.fetch(job + 1, 0, 0).start()
+
+            self.fetch(job, index, slot).wait()
+            term = product(
+                self.left[rows][slot, pl.ds(0, chunk)], self.right[slot, pl.ds(0, chunk)], TN
+            )
+
+            @pl.when(index == 0)
+            def _():
+                total[...] = term
+
+            @pl.when(index > 0)
+            def _():
+                total[...] += term
+
+            return carry
+
+        lax.fori_loop(0, steps, step, 0)
+        out = self.jobs[job][2]
+        source = total
+        if out.dtype != total.dtype:
+            source = self.low.at[which, pl.ds(0, rows)]
+            source[...] = total[...].astype(out.dtype)
+        self.stores[which] = pltpu.make_async_copy(source, out, self.out_sems.at[which])
+        self.stores[which].start()
+
+    def finish(self):
+        self.run(len(self.jobs))
+        for store in self.stores.values():
+            store.wait()
+
+
+class Pair:
+    def __init__(self, *moves):
+        self.moves = moves
+
+    def start(self):
+        for move in self.moves:
+            move.start()
+
+    def wait(self):
+        for move in self.moves:
+            move.wait()
+
+
 def scatter_kernel(
-    part, scalars, out, out_scalars,
+    back_part, ffn_part, scalars, slot_rows, slot_cotangent, grad_pre, gated,
+    all_rows, all_cotangent, grad_shared_pre, scaled,
+    back_sum, ffn_sum, out_scalars, grad_expert_in, grad_expert_down, grad_shared,
     held, core_in, x_in, ring_q, ring_x, last_in,
     s_held, s_core, s_x, s_ring,
-    send_sems, recv_sems,
+    job_left, job_short, job_right, job_sums, job_low, job_sems, job_out_sems,
+    free, send_sems, recv_sems,
 ):
     me = Peers()
     copies = Copies(send_sems, recv_sems)
-    count = part.shape[2]
+    parts, outs = (back_part, ffn_part), (back_sum, ffn_sum)
+    count = back_part.shape[2]
     half, piece = count // 2, count // 4
     q, qx, qc, qd = me.quarter, me.x_quarter, me.core_quarter, me.far_quarter
-    own, other, scale, last = range(4)
+    own, other, last = range(3)
     peers = {RIGHT: me.right, LEFT: me.left}
     greet([me.right, me.left, me.x_peer, me.core_peer])
     order = (4, 3, 5, 2, 6, 1, 7, 0)
-    for k in order:
-        for slot, mine, theirs in ((0, q, qc), (1, qx, qd)):
-            copies.local((LOCAL, k, slot), part.at[me.block(k), mine], held.at[k, slot])
-            target = core_in.at[k, slot]
-            copies.send(
-                (OVER_CORE, k, slot), part.at[me.block(k), theirs], target, target, me.core_peer
-            )
+
+    def load(kind):
+        for k in order:
+            for slot, mine in ((0, q), (1, qx)):
+                copies.local(
+                    (kind, LOCAL, k, slot), parts[kind].at[me.block(k), mine], held.at[kind, k, slot]
+                )
+
+    def swap_cores(kind):
+        for k in order:
+            for slot, theirs in ((0, qc), (1, qd)):
+                target = core_in.at[k, slot]
+                copies.send(
+                    (kind, OVER_CORE, k, slot),
+                    parts[kind].at[me.block(k), theirs],
+                    target,
+                    target,
+                    me.core_peer,
+                )
+
+    swap_cores(0)
+    load(0)
     for k in range(RING):
         for slot, mine, theirs in ((0, q, qc), (1, qx, qd)):
-            copies.local((LOCAL, scale, k, slot), scalars.at[me.block(k), mine], s_held.at[slot, k])
+            copies.local((SCALARS, LOCAL, k, slot), scalars.at[me.block(k), mine], s_held.at[slot, k])
             target = s_core.at[slot, k]
             copies.send(
-                (OVER_CORE, scale, k, slot),
+                (SCALARS, OVER_CORE, k, slot),
                 scalars.at[me.block(k), theirs],
                 target,
                 target,
                 me.core_peer,
             )
 
-    def prepare(k):
-        for slot in (1, 0):
-            copies.arrive(LOCAL, k, slot)
-            copies.arrive(OVER_CORE, k, slot)
-            add_into(held.at[k, slot], core_in.at[k, slot], count)
-            if slot == 1:
-                source = held.at[k, 1, pl.ds(half, half)]
-                copies.send((OVER_X, k), source, x_in.at[k], x_in.at[k], me.x_peer)
-
-    def over_x(k):
-        copies.arrive(OVER_X, k)
-        add_into(held.at[k, 0, pl.ds(half, half)], x_in.at[k], half)
-
-    def pass_on(side, hop, k):
+    def prepare(kind, *blocks):
+        for k in blocks:
+            for slot in (1, 0):
+                copies.arrive(kind, LOCAL, k, slot)
+                copies.arrive(kind, OVER_CORE, k, slot)
+                add_into(held.at[kind, k, slot], core_in.at[k, slot], count)
+                if slot == 1:
+                    source = held.at[kind, k, 1, pl.ds(half, half)]
+                    target = x_in.at[kind, k]
+                    copies.send((kind, OVER_X, k), source, target, target, me.x_peer)
+
+    def over_x(kind, *blocks):
+        for k in blocks:
+            copies.arrive(kind, OVER_X, k)
+            add_into(held.at[kind, k, 0, pl.ds(half, half)], x_in.at[kind, k], half)
+
+    def pass_on(kind, side, hop, k):
         if hop == 0:
             rows_q, rows_x = pl.ds(side * half, half), pl.ds(side * piece, piece)
         else:
             rows_q, rows_x = pl.ds(0, count), pl.ds(0, half)
-        for kind, landing, rows in ((own, ring_q, rows_q), (other, ring_x, rows_x)):
-            target = landing.at[side, hop, rows]
-            copies.send((side, kind, hop), held.at[k, kind].at[rows], target, target, peers[side])
-
-    def take_in(side, hop, k):
+        for which, landing, rows in ((own, ring_q, rows_q), (other, ring_x, rows_x)):
+            target = landing.at[kind, side, hop, rows]
+            source = held.at[kind, k, which, rows]
+            copies.send((kind, side, which, hop), source, target, target, peers[side])
+
+    def take_in(kind, side, hop, k):
         if hop == 0:
             span_q, span_x, at_q, at_x = half, piece, side * half, side * piece
         else:
             span_q, span_x, at_q, at_x = count, half, 0, 0
-        for kind, landing, span, at in ((own, ring_q, span_q, at_q), (other, ring_x, span_x, at_x)):
-            copies.arrive(side, kind, hop)
+        for which, landing, span, at in (
+            (own, ring_q, span_q, at_q),
+            (other, ring_x, span_x, at_x),
+        ):
+            copies.arrive(kind, side, which, hop)
             rows = pl.ds(at, span)
-            add_into(held.at[k, kind, rows], landing.at[side, hop, rows], span)
+            add_into(held.at[kind, k, which, rows], landing.at[kind, side, hop, rows], span)
+
+    def hop_on(kind, hop):
+        right_block, left_block = 4 - hop, 4 + hop
+        if hop == 0:
+            pass_on(kind, RIGHT, 0, 4)
+            pass_on(kind, LEFT, 0, 4)
+            return
+        take_in(kind, RIGHT, hop - 1, right_block)
+        pass_on(kind, RIGHT, hop, right_block)
+        take_in(kind, LEFT, hop - 1, left_block)
+        pass_on(kind, LEFT, hop, left_block)
 
     def pass_scalars(side, hop, k):
         target = s_ring.at[side, hop]
-        copies.send((side, scale, hop), s_held.at[0, k], target, target, peers[side])
+        copies.send((SCALARS, side, hop), s_held.at[0, k], target, target, peers[side])
 
     def take_scalars(side, hop, k):
-        copies.arrive(side, scale, hop)
+        copies.arrive(SCALARS, side, hop)
         s_held[0, k] += s_ring[side, hop]
 
-    prepare(4)
-    prepare(3)
-    prepare(5)
-    over_x(4)
-    pass_on(RIGHT, 0, 4)
-    pass_on(LEFT, 0, 4)
-    prepare(2)
-    prepare(6)
+    def home(kind):
+        take_in(kind, RIGHT, 3, 0)
+        take_in(kind, LEFT, 3, 0)
+        source, target = held.at[kind, 0, 1, pl.ds(0, half)], last_in.at[kind]
+        copies.send((kind, OVER_X, last, last), source, target, target, me.x_peer)
+
+    def home_out(kind):
+        out = outs[kind]
+        out[pl.ds(half, half), :] = held[kind, 0, 0, pl.ds(half, half), :].astype(out.dtype)
+        copies.arrive(kind, OVER_X, last, last)
+        out[pl.ds(0, half), :] = (
+            held[kind, 0, 0, pl.ds(0, half), :].astype(jnp.float32)
+            + last_in[kind].astype(jnp.float32)
+        ).astype(out.dtype)
+
+    experts = slot_rows.shape[0]
+    jobs = []
+    for expert in range(experts):
+        for index in range(2):
+            jobs.append(
+                (grad_pre.at[index, expert], slot_rows.at[expert], grad_expert_in.at[expert, index])
+            )
+        jobs.append((gated.at[expert], slot_cotangent.at[expert], grad_expert_down.at[expert]))
+    for index in range(2):
+        jobs.append((grad_shared_pre.at[index], all_rows, grad_shared.at[index]))
+    jobs.append((scaled, all_cotangent, grad_shared.at[2]))
+    prepare(0, 4, 3, 5)
+    over_x(0, 4)
+    hop_on(0, 0)
+    prepare(0, 2, 6)
     for k in range(RING):
         for slot in (0, 1):
-            copies.arrive(LOCAL, scale, k, slot)
-            copies.arrive(OVER_CORE, scale, k, slot)
+            copies.arrive(SCALARS, LOCAL, k, slot)
+            copies.arrive(SCALARS, OVER_CORE, k, slot)
     s_held[...] += s_core[...]
-    copies.send((OVER_X, scale, scale), s_held.at[1], s_x, s_x, me.x_peer)
-    over_x(3)
-    over_x(5)
-    for hop, right_block, left_block, later in ((1, 3, 5, (1, 7)), (2, 2, 6, (0,)), (3, 1, 7, ())):
-        take_in(RIGHT, hop - 1, right_block)
-        pass_on(RIGHT, hop, right_block)
-        take_in(LEFT, hop - 1, left_block)
-        pass_on(LEFT, hop, left_block)
-        if hop == 1:
-            copies.arrive(OVER_X, scale, scale)
-            s_held[0] += s_x[...]
-            pass_scalars(RIGHT, 0, 4)
-        else:
-            take_scalars(RIGHT, hop - 2, right_block + 1)
-            if hop == 3:
-                take_scalars(LEFT, hop - 2, left_block - 1)
-            pass_scalars(RIGHT, hop - 1, right_block + 1)
-            pass_scalars(LEFT, hop - 1, left_block - 1)
-        for k in later:
-            prepare(k)
-        if hop == 1:
-            over_x(2)
-            over_x(6)
-        elif hop == 2:
-            over_x(1)
-            over_x(7)
-    over_x(0)
-    take_in(RIGHT, 3, 0)
+    copies.send((SCALARS, OVER_X), s_held.at[1], s_x, s_x, me.x_peer)
+    over_x(0, 3, 5)
+    hop_on(0, 1)
+    copies.arrive(SCALARS, OVER_X)
+    s_held[0] += s_x[...]
+    pass_scalars(RIGHT, 0, 4)
+    prepare(0, 1, 7, 0)
+    pl.semaphore_signal(free, inc=1, device_id=me.core_peer, device_id_type=MESH_ID)
+    load(1)
+    lefts = {job_left.shape[2]: job_left, job_short.shape[2]: job_short}
+    grads = WeightGrads(jobs, lefts, job_right, job_sums, job_low, job_sems, job_out_sems)
+    over_x(0, 2, 6)
+    hop_on(0, 2)
+    take_scalars(RIGHT, 0, 3)
+    pass_scalars(RIGHT, 1, 3)
+    pass_scalars(LEFT, 1, 5)
+    pl.semaphore_wait(free, 1)
+    swap_cores(1)
+    over_x(0, 1, 7)
+    grads.run(1)
+    prepare(1, 4, 3, 5)
+    hop_on(0, 3)
+    take_scalars(RIGHT, 1, 2)
+    take_scalars(LEFT, 1, 6)
+    pass_scalars(RIGHT, 2, 2)
+    pass_scalars(LEFT, 2, 6)
+    over_x(0, 0)
+    over_x(1, 4)
+    hop_on(1, 0)
+    prepare(1, 2, 6)
+    over_x(1, 3, 5)
+    grads.run(2)
+    home(0)
     for side, k in ((RIGHT, 1), (LEFT, 7)):
         take_scalars(side, 2, k)
         pass_scalars(side, 3, k)
-    take_in(LEFT, 3, 0)
-    copies.send((OVER_X, last, last), held.at[0, 1, pl.ds(0, half)], last_in, last_in, me.x_peer)
+    hop_on(1, 1)
+    home_out(0)
+    prepare(1, 1, 7, 0)
+    over_x(1, 2, 6)
+    grads.run(2)
+    hop_on(1, 2)
+    over_x(1, 1, 7, 0)
+    grads.run(2)
+    hop_on(1, 3)
     take_scalars(RIGHT, 3, 0)
     take_scalars(LEFT, 3, 0)
     out_scalars[...] = s_held[0, 0]
-    out[pl.ds(half, half), :] = held[0, 0, pl.ds(half, half), :].astype(out.dtype)
-    copies.arrive(OVER_X, last, last)
-    out[pl.ds(0, half), :] = (
-        held[0, 0, pl.ds(0, half), :].astype(jnp.float32) + last_in[...].astype(jnp.float32)
-    ).astype(out.dtype)
+    grads.finish()
+    home(1)
+    home_out(1)
     copies.finish()
 
 
-def scatter_rows(part, scalars, collective_id):
-    ring, quarters, count, width = part.shape
+def scatter_rows(back_part, ffn_part, scalars, fed, collective_id):
+    slot_rows, slot_cotangent, grad_pre, gated, all_rows, all_cotangent, grad_shared_pre, scaled = fed
+    _, _, count, width = back_part.shape
     half = count // 2
-    dtype = part.dtype
+    dtype, f32 = back_part.dtype, jnp.float32
     s_shape = scalars.shape[2:]
+    experts, hidden = gated.shape[0], gated.shape[2]
+    shared_hidden = scaled.shape[1]
+    shape = jax.ShapeDtypeStruct
     return pl.pallas_call(
         scatter_kernel,
         out_shape=(
-            jax.ShapeDtypeStruct((count, width), jnp.float32),
-            jax.ShapeDtypeStruct(s_shape, jnp.float32),
+            shape((count, width), f32),
+            shape((count, width), f32),
+            shape(s_shape, f32),
+            shape((experts, 2, hidden, width), f32),
+            shape((experts, hidden, width), f32),
+            shape((3, shared_hidden, width), dtype),
         ),
-        in_specs=[IN_PLACE] * 2,
-        out_specs=(IN_VMEM,) * 2,
+        in_specs=[IN_PLACE] * 11,
+        out_specs=(IN_VMEM,) * 3 + (IN_PLACE,) * 3,
         scratch_shapes=[
+            pltpu.VMEM((2, RING, 2, count, width), dtype),
             pltpu.VMEM((RING, 2, count, width), dtype),
-            pltpu.VMEM((RING, 2, count, width), dtype),
-            pltpu.VMEM((RING, half, width), dtype),
-            pltpu.VMEM((2, 4, count, width), dtype),
-            pltpu.VMEM((2, 4, half, width), dtype),
-            pltpu.VMEM((half, width), dtype),
-            pltpu.VMEM((2, RING) + s_shape, jnp.float32),
-            pltpu.VMEM((2, RING) + s_shape, jnp.float32),
-            pltpu.VMEM((RING,) + s_shape, jnp.float32),
-            pltpu.VMEM((2, 4) + s_shape, jnp.float32),
+            pltpu.VMEM((2, RING, half, width), dtype),
+            pltpu.VMEM((2, 2, 4, count, width), dtype),
+            pltpu.VMEM((2, 2, 4, half, width), dtype),
+            pltpu.VMEM((2, half, width), dtype),
+            pltpu.VMEM((2, RING) + s_shape, f32),
+            pltpu.VMEM((2, RING) + s_shape, f32),
+            pltpu.VMEM((RING,) + s_shape, f32),
+            pltpu.VMEM((2, 4) + s_shape, f32),
+            pltpu.VMEM((2, 640, hidden), dtype),
+            pltpu.VMEM((2, 640, shared_hidden), dtype),
+            pltpu.VMEM((2, 640, width), dtype),
+            pltpu.VMEM((2, hidden, width), f32),
+            pltpu.VMEM((2, shared_hidden, width), dtype),
+            pltpu.SemaphoreType.DMA((2, 2)),
+            pltpu.SemaphoreType.DMA((2,)),
+            pltpu.SemaphoreType.REGULAR,
         ]
-        + semaphores(112),
-        compiler_params=remote_params(collective_id),
+        + semaphores(168),
+        compiler_params=remote_params(collective_id, 62),
         name="scatter_rows",
-    )(part, scalars)
+    )(back_part, ffn_part, scalars, *fed)
 
 
 def spread_kernel(
@@ -980,19 +1151,22 @@
     )(shard_in, shard_out, routes)
 
 
-def collect_kernel(
-    grad_in, grad_out, tail, sum_in, sum_out, sum_tail,
+def finish_kernel(
+    normed, grad_raw, heads, grad_attention, weights, gain, rows, grad_residual, tail,
+    sum_in, sum_out, sum_tail, grad_input,
     held_in, held_out, ring_in, ring_out, tails, tail_sums,
+    core_out, core_in, x_out, x_in, grad_rows, mine,
     send_sems, recv_sems,
 ):
     me = Peers()
     copies = Copies(send_sems, recv_sems)
-    kinds, _, depth, width = grad_in.shape
-    rows, columns = sum_out.shape
+    bf16, f32 = jnp.bfloat16, jnp.float32
+    kinds = grad_raw.shape[0]
+    depth, width = sum_in.shape[1], sum_in.shape[2]
+    out_rows, columns = sum_out.shape
+    count = rows.shape[0]
     peers = {RIGHT: me.right, LEFT: me.left}
-    tail_kind = kinds + 1
     greet([me.right, me.left, me.x_peer, me.core_peer, me.far_peer])
-    order = (4, 3, 5, 2, 6, 1, 7, 0)
 
     def held(kind, k):
         return held_in.at[k, kind] if kind < kinds else held_out.at[k]
@@ -1001,7 +1175,7 @@
         return ring_in.at[side, hop, kind] if kind < kinds else ring_out.at[side, hop]
 
     def span(kind, side, hop):
-        whole = depth if kind < kinds else rows
+        whole = depth if kind < kinds else out_rows
         return (side * (whole // 2), whole // 2) if hop == 0 else (0, whole)
 
     def pass_on(side, hop, k, kind):
@@ -1015,87 +1189,158 @@
         at = pl.ds(start, size)
         add_into(held(kind, k).at[at], ring(kind, side, hop).at[at], size)
 
-    tails[0] = tail[...]
+    def work_out(*blocks):
+        for k in blocks:
+            block = me.block(k)
+            features = normed[:, pl.ds(pl.multiple_of(block * depth, depth), depth)]
+            for kind in range(kinds):
+                held_in[k, kind] = product(features, grad_raw[kind], TN).astype(bf16)
+            across = grad_attention[:, pl.ds(pl.multiple_of(block * columns, columns), columns)]
+            held_out[k] = product(heads[...], across, TN).astype(bf16)
+
+    def hop_on(hop):
+        if hop == 0:
+            for kind in range(kinds + 1):
+                for side in (RIGHT, LEFT):
+                    pass_on(side, 0, 4, kind)
+            return
+        for kind in range(kinds + 1):
+            for side, k in ((RIGHT, 4 - hop), (LEFT, 4 + hop)):
+                take_in(side, hop - 1, k, kind)
+                pass_on(side, hop, k, kind)
+
+    def quarter(index):
+        here = pl.ds(pl.multiple_of(index * count, count), count)
+        total = None
+        for kind in range(kinds):
+            term = product(grad_raw[kind, here, :], weights[kind], NT)
+            total = term if total is None else total + term
+        return total
+
+    work_out(4)
+    hop_on(0)
+    for slot, index in ((1, me.far_quarter), (0, me.core_quarter)):
+        core_out[slot] = quarter(index).astype(bf16)
+        target = core_in.at[slot]
+        copies.send((SCALARS, OVER_CORE, slot), core_out.at[slot], target, target, me.core_peer)
+    mine[...] = quarter(me.x_quarter)
+    copies.arrive(SCALARS, OVER_CORE, 1)
+    x_out[...] = (mine[...] + core_in[1].astype(f32)).astype(bf16)
+    copies.send((SCALARS, OVER_X), x_out, x_in, x_in, me.x_peer)
+    work_out(3, 5)
+    hop_on(1)
+    mine[...] = quarter(me.quarter)
+    copies.arrive(SCALARS, OVER_CORE, 0)
+    work_out(2, 6)
+    copies.arrive(SCALARS, OVER_X)
+    total = mine[...] + core_in[0].astype(f32) + x_in[...].astype(f32)
+    inverse, scaled_rows = rms_parts(rows[...].astype(f32))
+    scaled = total * gain[...]
+    slope = inverse * (
+        scaled - scaled_rows * jnp.mean(scaled * scaled_rows, axis=-1, keepdims=True)
+    )
+    grad_rows[...] = (grad_residual[...] + slope).astype(bf16)
+    here = grad_input.at[me.quarter]
+    copies.send((SCALARS, RIGHT, OVER_X), grad_rows, here, grad_input.at[me.x_quarter], me.x_peer)
+    copies.send(
+        (SCALARS, RIGHT, OVER_CORE), grad_rows, here, grad_input.at[me.core_quarter], me.core_peer
+    )
+    copies.local((LOCAL,), grad_rows, here)
+    gain_grad = jnp.sum(total * scaled_rows, axis=0, keepdims=True)
+    tails[0, 0:kinds, :] = tail[...]
+    for index in range(gain_grad.shape[1] // width):
+        part = slice(index * width, (index + 1) * width)
+        tails[0, kinds + index : kinds + index + 1, :] = gain_grad[:, part]
+    tail_kind = kinds + 1
+
+    def pass_tail(side, hop, place):
+        sign = -1 if side == RIGHT else 1
+        target = tails.at[(place + sign) % RING]
+        copies.send((side, tail_kind, hop), tails.at[place], target, target, peers[side])
+
+    pass_tail(RIGHT, 0, 0)
+    pass_tail(LEFT, 0, 0)
+    hop_on(2)
+    work_out(1, 7)
+    copies.arrive(SCALARS, RIGHT, OVER_X)
+    beside = grad_input.at[me.x_quarter]
+    copies.send(
+        (SCALARS, LEFT, OVER_CORE), beside, beside, grad_input.at[me.far_quarter], me.core_peer
+    )
     for side, place in ((RIGHT, 7), (LEFT, 1)):
-        copies.send((side, tail_kind, 0), tail, tails.at[place], tails.at[place], peers[side])
-    for k in order:
-        block = me.block(k)
-        for kind in range(kinds):
-            copies.local((LOCAL, kind, k), grad_in.at[kind, block], held(kind, k))
-        across = pl.ds(pl.multiple_of(block * columns, columns), columns)
-        copies.local((LOCAL, kinds, k), grad_out.at[:, across], held(kinds, k))
-
-    def ready(*blocks):
-        for k in blocks:
-            for kind in range(kinds + 1):
-                copies.arrive(LOCAL, kind, k)
-
-    ready(4)
+        copies.arrive(side, tail_kind, 0)
+        pass_tail(side, 1, place)
+    hop_on(3)
+    for side, place in ((RIGHT, 6), (LEFT, 2)):
+        copies.arrive(side, tail_kind, 1)
+        pass_tail(side, 2, place)
+    work_out(0)
+    copies.arrive(RIGHT, tail_kind, 2)
+    pass_tail(RIGHT, 3, 5)
+    copies.arrive(LEFT, tail_kind, 2)
     for kind in range(kinds + 1):
         for side in (RIGHT, LEFT):
-            pass_on(side, 0, 4, kind)
-    for hop, right_block, left_block in ((1, 3, 5), (2, 2, 6), (3, 1, 7)):
-        ready(right_block, left_block)
-        for kind in range(kinds + 1):
-            for side, k in ((RIGHT, right_block), (LEFT, left_block)):
-                take_in(side, hop - 1, k, kind)
-                pass_on(side, hop, k, kind)
-        for side, place, sign in ((RIGHT, 8 - hop, -1), (LEFT, hop, 1)):
-            copies.arrive(side, tail_kind, hop - 1)
-            if hop < 3 or side == RIGHT:
-                target = tails.at[place + sign]
-                copies.send((side, tail_kind, hop), tails.at[place], target, target, peers[side])
+            take_in(side, 3, 0, kind)
+        if kind < kinds:
+            sum_in[kind] = held_in[0, kind].astype(f32)
+    sum_out[...] = held_out[0].astype(f32)
     copies.arrive(RIGHT, tail_kind, 3)
     total = tails[0]
     for place in range(1, RING):
         total = total + tails[place]
     tail_sums[me.tp] = total
-    for way, peer, quarter in (
+    for way, peer, index in (
         (OVER_X, me.x_peer, me.x_quarter),
         (OVER_CORE, me.core_peer, me.core_quarter),
         (OVER_FAR, me.far_peer, me.far_quarter),
     ):
         copies.send(
-            (way, tail_kind), tail_sums.at[me.tp], tail_sums.at[me.tp], tail_sums.at[quarter], peer
+            (way, tail_kind), tail_sums.at[me.tp], tail_sums.at[me.tp], tail_sums.at[index], peer
         )
-    ready(0)
-    for kind in range(kinds + 1):
-        for side in (RIGHT, LEFT):
-            take_in(side, 3, 0, kind)
-    for kind in range(kinds):
-        sum_in[kind] = held_in[0, kind].astype(jnp.float32)
-    sum_out[...] = held_out[0].astype(jnp.float32)
     for way in (OVER_X, OVER_CORE, OVER_FAR):
         copies.arrive(way, tail_kind)
     sum_tail[...] = tail_sums[...]
     copies.finish()
 
 
-def collect_weights(grad_in, grad_out, tail, collective_id):
-    kinds, ring, depth, width = grad_in.shape
-    rows, columns = grad_out.shape[0], grad_out.shape[1] // ring
-    f32 = jnp.float32
+def finish(
+    normed, grad_raw, heads, grad_attention, weights, gain, rows, grad_residual, bias, collective_id
+):
+    tokens, width = normed.shape
+    kinds, _, columns = grad_raw.shape
+    count = rows.shape[0]
+    depth = width // RING
+    bf16, f32 = jnp.bfloat16, jnp.float32
+    shape = jax.ShapeDtypeStruct
+    tail_shape = (-(-(kinds + width // columns) // 8) * 8, columns)
     return pl.pallas_call(
-        collect_kernel,
+        finish_kernel,
         out_shape=(
-            jax.ShapeDtypeStruct((kinds, depth, width), f32),
-            jax.ShapeDtypeStruct((rows, columns), f32),
-            jax.ShapeDtypeStruct((4,) + tail.shape, f32),
+            shape((kinds, depth, columns), f32),
+            shape((columns, depth), f32),
+            shape((4,) + tail_shape, f32),
+            shape((4, count, width), bf16),
         ),
-        in_specs=[IN_PLACE, IN_PLACE, IN_VMEM],
-        out_specs=(IN_VMEM,) * 3,
+        in_specs=[IN_VMEM] * 9,
+        out_specs=(IN_VMEM,) * 3 + (IN_PLACE,),
         scratch_shapes=[
-            pltpu.VMEM((RING, kinds, depth, width), grad_in.dtype),
-            pltpu.VMEM((RING, rows, columns), grad_out.dtype),
-            pltpu.VMEM((2, 4, kinds, depth, width), grad_in.dtype),
-            pltpu.VMEM((2, 4, rows, columns), grad_out.dtype),
-            pltpu.VMEM((RING,) + tail.shape, f32),
-            pltpu.VMEM((4,) + tail.shape, f32),
+            pltpu.VMEM((RING, kinds, depth, columns), bf16),
+            pltpu.VMEM((RING, columns, depth), bf16),
+            pltpu.VMEM((2, 4, kinds, depth, columns), bf16),
+            pltpu.VMEM((2, 4, columns, depth), bf16),
+            pltpu.VMEM((RING,) + tail_shape, f32),
+            pltpu.VMEM((4,) + tail_shape, f32),
+            pltpu.VMEM((2, count, width), bf16),
+            pltpu.VMEM((2, count, width), bf16),
+            pltpu.VMEM((count, width), bf16),
+            pltpu.VMEM((count, width), bf16),
+            pltpu.VMEM((count, width), bf16),
+            pltpu.VMEM((count, width), f32),
         ]
-        + semaphores(96),
-        compiler_params=remote_params(collective_id),
-        name="collect_weights",
-    )(grad_in, grad_out, tail)
+        + semaphores(56),
+        compiler_params=remote_params(collective_id, 60),
+        name="finish",
+    )(normed, grad_raw, heads, grad_attention, weights, gain[None], rows, grad_residual, bias)
 
 
 def greet_along_z(me):
@@ -1479,18 +1724,12 @@
         cotangent.reshape(tp_size, own_count, model_width),
         scale_rows,
         rank,
-        expert_in,
+        jnp.swapaxes(expert_in, 2, 3).reshape(local_experts, -1, model_width),
         expert_down,
         shared_slices,
         capacity,
         3,
     )
-    ffn_sum = lax.psum_scatter(
-        ffn_part.reshape(all_count, model_width), both, scatter_dimension=0, tiled=True
-    )
-    layer_output = lax.all_gather(
-        (residual + ffn_sum.astype(f32)).astype(bf16), TP, axis=0, tiled=True
-    )
     spare = jnp.zeros((ep_size, scale_count - expert_count - 1, tok_count), f32)
     scalar_part = jnp.concatenate(
         [jnp.zeros((ep_size, expert_count, tok_count), f32), scale_grad[:, None, :, 0], spare], axis=1
@@ -1501,30 +1740,26 @@
     scalar_part = jnp.swapaxes(
         scalar_part.reshape(ep_size, scale_count, tp_size, own_count), 1, 2
     )
-    back_sum, scalar_sum = scatter_rows(
-        back_part.reshape(ep_size, tp_size, own_count, model_width), scalar_part, 4
+    part_shape = (ep_size, tp_size, own_count, model_width)
+    slot_count = ep_size * capacity
+    fed = (
+        slot_rows.reshape(local_experts, slot_count, model_width),
+        slot_cotangent.reshape(local_experts, slot_count, model_width),
+        grad_pre.reshape(2, local_experts, slot_count, -1),
+        gated.reshape(local_experts, slot_count, -1),
+        all_rows.reshape(all_count, model_width),
+        all_cotangent.reshape(all_count, model_width),
+        grad_shared_pre.reshape(2, all_count, slice_hidden),
+        scaled_hidden.reshape(all_count, slice_hidden),
+    )
+    back_sum, ffn_sum, scalar_sum, grad_expert_in, grad_expert_down, shared_grads = scatter_rows(
+        back_part.reshape(part_shape), ffn_part.reshape(part_shape), scalar_part, fed, 4
     )
     scalar_sum = scalar_sum.T
-    slot_rows = slot_rows.reshape(local_experts, -1, model_width)
-    slot_cotangent = slot_cotangent.reshape(slot_rows.shape)
-    grad_pre = grad_pre.reshape(2, local_experts, slot_rows.shape[1], -1)
-    gated = gated.reshape(local_experts, slot_rows.shape[1], -1)
-    grad_expert_down = jnp.einsum(
-        "erf,erd->efd", gated, slot_cotangent, preferred_element_type=f32
-    )
-    grad_expert_in = jnp.einsum(
-        "erd,serf->esdf", slot_rows, grad_pre, preferred_element_type=f32
-    )
-    flat_rows = all_rows.reshape(all_count, model_width)
-    flat_cotangent = all_cotangent.reshape(all_count, model_width)
-    shared_grads = [
-        product(flat_rows, grad_shared_pre[0].reshape(all_count, -1), TN),
-        product(flat_rows, grad_shared_pre[1].reshape(all_count, -1), TN),
-        product(flat_cotangent, scaled_hidden.reshape(all_count, -1), TN),
-    ]
-    shared_grads = jnp.stack([grad.astype(bf16) for grad in shared_grads])
+    grad_expert_in = jnp.swapaxes(grad_expert_in, 2, 3)
+    layer_output = lax.all_gather((residual + ffn_sum).astype(bf16), TP, axis=0, tiled=True)
     shared_grads = jnp.transpose(
-        shared_grads.reshape(3, ep_size, shard_width, slice_hidden), (1, 0, 3, 2)
+        shared_grads.reshape(3, slice_hidden, ep_size, shard_width), (2, 0, 1, 3)
     )
     shared_grads = lax.all_to_all(shared_grads, EP, split_axis=0, concat_axis=0, tiled=True)
     shared_grads = (
@@ -1557,7 +1792,6 @@
     small = lax.psum(small, both)
     grad_residual = own_rows(cotangent, tp_index, own_count).astype(f32) + grad_mid_norm
     grad_attention = tensor_gather(grad_residual.astype(bf16), 5).reshape(tok_count, model_width)
-    grad_attention_out = product(heads_low, grad_attention, TN)
     grad_heads = (product(grad_attention, out_full, NT) * valid_rows).astype(bf16)
     grad_queries, grad_kv = attend_back(
         queries, keys_values, query_doc, key_doc, log_totals, grad_heads, cosine, sine
@@ -1565,31 +1799,20 @@
     grad_own_kv = return_keys(grad_kv, cosine, sine, 6)
     grad_raw = jnp.concatenate([grad_queries[None], grad_own_kv])
     grad_attention_bias = jnp.sum(grad_raw.astype(f32), axis=1)
-    grad_normed_attention = product_to_owner(grad_raw, in_full, True, 7)
-    inverse_one, normed_one = rms_parts(input_rows)
-    grad_in_norm, grad_attention_gain = norm_back(
-        grad_normed_attention, attention_gain, inverse_one, normed_one
-    )
-    grad_input = tensor_gather((grad_residual + grad_in_norm).astype(bf16), 8)
-    grad_attention_in = jnp.einsum(
-        "td,ste->sde", normed_attention, grad_raw, preferred_element_type=f32
-    )
-    columns = grad_attention_bias.shape[1]
-    tail = jnp.concatenate(
-        [
-            grad_attention_bias,
-            grad_attention_gain.reshape(-1, columns),
-            jnp.zeros((8 - 3 - model_width // columns, columns), f32),
-        ]
-    )
-    grad_attention_in, grad_attention_out, tails = collect_weights(
-        grad_attention_in.astype(bf16).reshape(in_blocks.shape),
-        grad_attention_out.astype(bf16),
-        tail,
-        9,
+    grad_attention_in, grad_attention_out, tails, grad_input = finish(
+        normed_attention,
+        grad_raw,
+        heads_low,
+        grad_attention,
+        in_full,
+        attention_gain,
+        own_rows(layer_input, tp_index, own_count),
+        grad_residual,
+        grad_attention_bias,
+        7,
     )
     grad_attention_bias = lax.dynamic_index_in_dim(tails, tp_index, 0, keepdims=False)[:3]
-    grad_attention_gain = jnp.sum(tails[:, 3:], axis=0)[: model_width // columns].reshape(-1)
+    grad_attention_gain = jnp.sum(tails[:, 3:], axis=0)[: model_width // tails.shape[2]].reshape(-1)
     return (
         layer_output,
         grad_input.reshape(tok_count, model_width),

time: 951 us -> 808 us (0.85)
  Pallas kernels: 747 us -> 680 us
  matrix products: 67.8 us -> 10.5 us
  starting transfers between devices: 18.9 us -> 9.34 us
    pallas_call x2 -> x1, Pallas kernels: 52.7 us -> 20.3 us  [tensor_gather(): pl.pallas_call(tensor_kernel, out_shape=jax.ShapeDtypeStruct((4,) + rows....]
    dot_general x3 -> x0, matrix products: 30.9 us -> none  [the longest x1 14.1 us: per_device_dense(): jnp.einsum('erd,serf->esdf', slot_rows, grad_pre, preferred_element_type=...]
    dot_general x6 -> x2, matrix products: 30.1 us -> 4 us  [product(): lax.dot_general(left, right, dims, preferred_element_type=jnp.float32)]
    pallas_call x2 -> x1, Pallas kernels: 40.7 us -> 17.1 us  [product_to_owner(): pl.pallas_call(functools.partial(reduce_kernel, flip), out_shape=jax.Shap...]
    pallas_call x1, Pallas kernels: 49.1 us -> 30.1 us  [return_keys(): pl.pallas_call(return_kernel, out_shape=jax.ShapeDtypeStruct((kinds, toke...]
    pallas_call x2, Pallas kernels: 247 us -> 257 us  [the longest x1 153 us: scatter_rows(): pl.pallas_call(scatter_kernel, out_shape=(shape((count, width), f32), sha...]
    unnamed x148 -> x96, local copies, waits for them, and re-layouts: 40.3 us -> 38.2 us
  transfers between devices with their start and end apart: 5 -> 4, of which waited for: 1 -> 0; matrix products, arithmetic and copies ran while one was open for 14% -> 5% of each run, Pallas kernels for 49% -> 30%
where the time goes in v3:
time: 808 us; the launch traced here: 801 us
  Pallas kernels  680 us (84%)
  local copies, waits for them, and re-layouts  60.6 us (8%)
  other arithmetic  24.7 us (3%)
  between operations  16.4 us (2%)
  matrix products  10.5 us (1%)
  starting transfers between devices  9.34 us (1%)
    pallas_call x1, Pallas kernels, gather_feed(): pl.pallas_call(gather_feed_kernel, out_shape=(shape((RING, 4, count, widt...  199 us
    pallas_call x1, Pallas kernels, scatter_rows(): pl.pallas_call(scatter_kernel, out_shape=(shape((count, width), f32), sha...  153 us
    pallas_call x1, Pallas kernels, finish(): pl.pallas_call(finish_kernel, out_shape=(shape((kinds, depth, columns), f...  104 us
    pallas_call x1, Pallas kernels, spread_weights(): pl.pallas_call(spread_kernel, out_shape=(jax.ShapeDtypeStruct((kinds, RIN...  85.9 us
    pallas_call x1, Pallas kernels, share_keys(): pl.pallas_call(share_kernel, out_shape=jax.ShapeDtypeStruct((kinds, 3, to...  41.9 us
    unnamed x96, local copies, waits for them, and re-layouts  38.2 us
    pallas_call x1, Pallas kernels, return_keys(): pl.pallas_call(return_kernel, out_shape=jax.ShapeDtypeStruct((kinds, toke...  30.1 us
    pallas_call x1, Pallas kernels, tensor_gather(): pl.pallas_call(tensor_kernel, out_shape=jax.ShapeDtypeStruct((4,) + rows....  20.3 us
  transfers between devices with their start and end apart: 4, of which 0 were waited for; matrix products, arithmetic and copies ran while one was open for 5% of the time, Pallas kernels for 30%

profile of v3, /device:TPU:0, one launch (start us, length us, event | category | flops | bytes accessed | tf_op | source)
XLA Modules:
  0.0 801.1 jit_solution(634767106482155430)
XLA Ops:
  8.1 1.8 copy.67
  11.0 85.9 %spread_weights.1 = (bf16[3,8,256,512]{3,2,1,0:T(8,128)(2,1)}, bf16[512,2048]{1,0:T(8,128)(2,1)S(1)}, s32[8,8,512]{2,1,0:T(8,128)S(1)}) custom-call(bf16[3,256,512]{2,1,0:T(8,128)(2,1)S(1)} %copy-done.16, bf16[512,256]{1,0:T(8,128)(2,1)S(1)} %copy-done.17, s32[8,512]{1,0:T(8,128)S(1)} %concatenate.32.routes), custom_call_target="tpu_custom_call" | custom-call | tf_op jit(solution)/shard_map/spread_weights/pallas_call | solution.py:1139
  96.9 1.3 copy-done.9
  98.2 1.5 copy.68
  99.7 4.9 all-to-all-start
  107.0 1.0 fusion.27
  109.0 1.4 copy.65
  110.4 2.8 copy-done.4
  113.2 5.1 project.1
  118.3 1.3 copy-done.11
  119.7 41.9 %share_keys.1.keys.values = bf16[2,3,512,512]{3,2,1,0:T(8,128)(2,1)S(1)} custom-call(bf16[2,512,512]{2,1,0:T(8,128)(2,1)S(1)} %get-tuple-element.48.own), custom_call_target="tpu_custom_call" | custom-call | tf_op jit(solution)/shard_map/share_keys/pallas_call | solution.py:1436
  161.6 1.7 copy-done.2
  163.8 2.0 copy.64
  165.8 2.1 and_select_fusion
  167.9 1.3 copy.70.rank_row
  171.8 1.9 copy-done.3
  173.7 9.9 %attend.1 = (bf16[512,512]{1,0:T(8,128)(2,1)S(1)}, f32[4,512,1]{2,1,0:T(8,128)S(1)}) custom-call(bf16[512,512]{1,0:T(8,128)(2,1)S(1)} %get-tuple-element.47.queries, bf16[2,3,512,512]{3,2,1,0:T(8,128)(2,1)S(1)} %copy-done.3, bf16[2,3,512,512]{3,2,1,0:T(8,128)(2,1)S(1)} %copy-done.3, s32[512,1]{1,0:T(8,128)S(1)} %fusion.25.query_doc, ...), custom_call_target="tpu_custom_call" | custom-call | tf_op jit(solution)/shard_map/attend/pallas_call | solution.py:192
  184.6 17.1 %product_to_owner.1 = f32[128,2048]{1,0:T(8,128)S(1)} custom-call(bf16[1,512,512]{2,1,0:T(8,128)(2,1)S(1)} %bitcast.104, bf16[1,512,2048]{2,1,0:T(8,128)(2,1)S(1)} %bitcast.105), custom_call_target="tpu_custom_call" | custom-call | tf_op jit(solution)/shard_map/product_to_owner/pallas_call | solution.py:1566
  202.4 2.0 multiply_reduce_fusion.2
  204.5 1.0 fusion.42
  205.6 1.0 fusion.5
  208.2 3.2 copy.78
  211.5 199.2 %gather_feed.1 = (bf16[8,4,128,2048]{3,2,1,0:T(8,128)(2,1)}, bf16[8,4,128,2048]{3,2,1,0:T(8,128)(2,1)}, f32[8,4,24,128]{3,2,1,0:T(8,128)}, bf16[8,512,2048]{2,1,...) custom-call(bf16[128,2048]{1,0:T(8,128)(2,1)} %fusion.10.rows, ...), custom_call_target="tpu_custom_call" | custom-call | tf_op jit(solution)/shard_map/gather_feed/pallas_call | solution.py:697
  410.7 2.2 reduce
  413.9 153.0 %scatter_rows.1 = (f32[128,2048]{1,0:T(8,128)}, f32[128,2048]{1,0:T(8,128)}, f32[24,128]{1,0:T(8,128)}, f32[2,2,352,2048]{3,2,1,0:T(8,128)}, f32[2,352,2048]{2,1,0:T(8,128)}, /*index=5*/bf16[3,176,2048]{2,1,0:T(8,128)(2,1)}) custom-call(bf16[8,4,128,2048]{3,2,1,0:T(8,128)(2,1)} %bitcast.114, bf16[8,4,128,2048]{3,2,1,0:T(8,128)(2,1)} %bitcast.113, ...), custom_call_target="tpu_custom_call" | custom-call | tf_op jit(solution)/shard_map/scatter_rows/pallas_call | solution.py:1050
  569.8 1.4 fusion.7
  571.3 2.3 multiply_reduce_fusion
  574.4 3.1 copy.83
  577.4 4.4 all-to-all-start.1
  581.9 3.3 fusion.40
  585.8 20.3 %tensor_gather.1 = bf16[4,128,2048]{2,1,0:T(8,128)(2,1)S(1)} custom-call(bf16[128,2048]{1,0:T(8,128)(2,1)S(1)} %get-tuple-element.120.rows), custom_call_target="tpu_custom_call" | custom-call | tf_op jit(solution)/shard_map/tensor_gather/pallas_call | solution.py:1598
  606.1 3.7 fusion.1.grad_heads
  609.9 13.1 %attend_back.1 = (bf16[512,512]{1,0:T(8,128)(2,1)S(1)}, bf16[2,3,512,512]{3,2,1,0:T(8,128)(2,1)}) custom-call(bf16[512,512]{1,0:T(8,128)(2,1)S(1)} %copy-done.13, bf16[2,3,512,512]{3,2,1,0:T(8,128)(2,1)} %copy-done.2, bf16[2,3,512,512]{3,2,1,0:T(8,128)(2,1)} %copy-done.2, s32[512,1]{1,0:T(8,128)S(1)} %fusion.25.query_doc, ...), custom_call_target="tpu_custom_call" | custom-call | tf_op jit(solution)/shard_map/attend_back/pallas_call | solution.py:234
  622.9 1.9 copy-done.7
  624.8 30.1 %return_keys.1 = bf16[2,512,512]{2,1,0:T(8,128)(2,1)S(1)} custom-call(bf16[2,3,512,512]{3,2,1,0:T(8,128)(2,1)S(1)} %copy-done.7, f32[512,128]{1,0:T(8,128)S(1)} %get-tuple-element.134.cosine, f32[512,128]{1,0:T(8,128)S(1)} %get-tuple-element.135.sine), custom_call_target="tpu_custom_call" | custom-call | tf_op jit(solution)/shard_map/return_keys/pallas_call | solution.py:1513
  655.8 1.3 pad_maximum_fusion.grad_raw
  657.1 104.0 %finish.1 = (f32[3,256,512]{2,1,0:T(8,128)}, f32[512,256]{1,0:T(8,128)}, f32[4,8,512]{2,1,0:T(8,128)}, bf16[4,128,2048]{2,1,0:T(8,128)(2,1)}) custom-call(bf16[512,2048]{1,0:T(8,128)(2,1)} %copy-done.11, bf16[3,512,512]{2,1,0:T(8,128)(2,1)} %pad_maximum_fusion.grad_raw, bf16[512,512]{1,0:T(8,128)(2,1)} %copy-done.8, bf16[512,2048]{1,0:T(8,128)(2,1)} %bitcast.103, ...), custom_call_target="tpu_custom_call" | custom-call | tf_op jit(solution)/shard_map/finish/pallas_call | solution.py:1316
  762.6 1.3 dynamic-slice_bitcast_fusion
  763.9 1.5 fusion.41
  765.4 1.6 slice_bitcast_fusion
  767.0 2.1 convert_bitcast_fusion
  769.3 1.2 slice.67
  770.5 2.2 copy.75
  772.8 3.3 copy.92
  776.1 1.3 copy.93
  778.2 1.1 copy.94
  780.2 10.8 %copy.96 = f32[2,2,2048,352]{2,3,1,0:T(8,128)} copy(f32[2,2,2048,352]{2,3,1,0:T(8,128)} %bitcast.115) | data formatting | bytes 23068672
  790.9 2.5 copy.97
  (145 shorter events, 20.5 us)
Async XLA Ops:
  8.0 196.4 %copy-start = (f32[2048,16]{0,1:T(8,128)S(1)}, f32[2048,16]{0,1:T(8,128)}, u32[]{:S(2)}) copy-start(f32[2048,16]{0,1:T(8,128)} %param.24) | copy-start | bytes 393220
  8.0 1.8 copy-start.35
  8.0 1.8 copy-start.26
  9.8 1.1 copy-start.16
  9.9 1.2 copy-start.17
  96.9 1.3 copy-start.9
  99.7 5.0 copy-start.40
  99.7 108.5 %all-to-all-start = ((bf16[8,3,176,256]{3,2,1,0:T(8,128)(2,1)}), bf16[8,3,176,256]{3,2,1,0:T(8,128)(2,1)}, u32[]{:S(2)}, u32[]{:S(2)}) async-start(bf16[8,3,176,256]{3,2,1,0:T(8,128)(2,1)} %copy.68), calls=%async_computation | async-start | bytes 4325376 | tf_op jit(solution)/shard_map/all_to_all | solution.py:1662
  104.6 5.8 copy-start.6
  104.6 5.8 copy-start.18
  104.6 5.8 copy-start.19
  104.6 659.3 %all-reduce.3.cloned.1.call-start = ((), (), s32[]{:S(2)}) async-start(), calls=%async_computation.3 | async-start | bytes 393216 | tf_op jit(solution)/shard_map/psum | solution.py:1792
  104.9 2.1 copy-start.37
  106.2 12.2 %copy-start.33 = (s32[512]{0:T(512)}, s32[512]{0:T(512)S(1)}, u32[]{:S(2)}) copy-start(s32[512]{0:T(512)S(1)} %convert_reduce_fusion.2) | copy-start | bytes 6148
  110.4 2.8 copy-start.4
  118.3 1.3 copy-start.11
  119.6 52.2 %copy-start.12 = (bf16[512,512]{1,0:T(8,128)(2,1)}, bf16[512,512]{1,0:T(8,128)(2,1)S(1)}, u32[]{:S(2)}) copy-start(bf16[512,512]{1,0:T(8,128)(2,1)S(1)} %get-tuple-element.47.queries) | copy-start | bytes 1572868
  119.6 43.6 %copy-start.34 = (s32[512]{0:T(512)S(1)}, s32[512]{0:T(512)}, u32[]{:S(2)}) copy-start(s32[512]{0:T(512)} %copy-done.33) | copy-start | bytes 6148
  119.6 43.7 %copy-start.30 = (pred[8,2,512]{2,1,0:T(4,128)(4,1)S(1)}, pred[8,2,512]{2,1,0:T(4,128)(4,1)}, u32[]{:S(2)}) copy-start(pred[8,2,512]{2,1,0:T(4,128)(4,1)} %copy.63) | copy-start | bytes 24580
  119.6 43.8 %copy-start.38 = (s32[512]{0:T(512)S(1)}, s32[512]{0:T(512)}, u32[]{:S(2)}) copy-start(s32[512]{0:T(512)} %iota_add_fusion.2) | copy-start | bytes 6148
  161.6 1.7 copy-start.2
  167.9 3.2 copy-start.22
  171.8 1.9 copy-start.3
  173.7 10.9 %copy-start.10 = (bf16[512,2048]{1,0:T(8,128)(2,1)S(1)}, bf16[512,2048]{1,0:T(8,128)(2,1)}, u32[]{:S(2)}) copy-start(bf16[512,2048]{1,0:T(8,128)(2,1)} %copy-done.9) | copy-start | bytes 6291460
  183.6 1.0 copy-start.14
  184.6 19.8 %copy-start.8 = (bf16[512,512]{1,0:T(8,128)(2,1)}, bf16[512,512]{1,0:T(8,128)(2,1)S(1)}, u32[]{:S(2)}) copy-start(bf16[512,512]{1,0:T(8,128)(2,1)S(1)} %get-tuple-element.49.heads) | copy-start | bytes 1572868
  201.7 2.7 copy-start.28
  202.4 3.2 copy-start.31
  202.4 4.2 copy-start.36
  204.4 2.9 copy-start.20
  410.7 2.3 copy-start.39
  410.7 2.4 copy-start.32
  413.9 154.5 %copy-start.21 = (f32[128,2048]{1,0:T(8,128)S(1)}, f32[128,2048]{1,0:T(8,128)}, u32[]{:S(2)}) copy-start(f32[128,2048]{1,0:T(8,128)} %copy-done.20) | copy-start | bytes 3145732
  566.9 4.4 copy-start.25
  566.9 4.4 copy-start.29
  577.4 189.6 %all-to-all-start.1 = ((bf16[8,3,176,256]{3,2,1,0:T(8,128)(2,1)}), bf16[8,3,176,256]{3,2,1,0:T(8,128)(2,1)}, u32[]{:S(2)}, u32[]{:S(2)}) async-start(bf16[8,3,176,256]{3,2,1,0:T(8,128)(2,1)} %bitcast.119), calls=%async_computation.1 | async-start | bytes 4325376 | tf_op jit(solution)/shard_map/all_to_all | solution.py:1764
  581.8 185.2 %all-gather.2.cloned.1.call-start = ((), (), s32[]{:S(2)}) async-start(), calls=%async_computation.2 | async-start | bytes 2621440 | tf_op jit(solution)/shard_map/all_gather | solution.py:1760
  606.1 3.7 copy-start.5
  606.1 3.7 copy-start.13
  606.1 3.7 copy-start.15
  622.9 1.9 copy-start.7
  772.8 3.3 copy-start.23
  776.1 2.2 copy-start.24
  776.1 3.3 copy-start.27
  778.2 12.7 %slice-start = ((s8[5767168]{0:T(1024)(128)(4,1)}), s8[4194304]{0:T(1024)(128)(4,1)S(1)}, s32[]{:S(2)}) async-start(s8[5767168]{0:T(1024)(128)(4,1)} %bitcast.121), calls=%async_computation.4 | async-start | bytes 8388608
  780.2 10.8 %slice-start.1 = ((s8[5767168]{0:T(1024)(128)(4,1)}), s8[1572864]{0:T(1024)(128)(4,1)S(1)}, s32[]{:S(2)}) async-start(s8[5767168]{0:T(1024)(128)(4,1)} %bitcast.121), calls=%async_computation.5 | async-start | bytes 3145728
  790.9 2.5 copy-start.1
Sparse Core Ops, SparseCore 0:
  574.5 143.0 all-reduce.2
Sparse Core Ops, SparseCore 1:
  585.2 27.3 all-gather.1

commit v4 on v3

--- a/solution.py
+++ b/solution.py
@@ -92,64 +92,6 @@
     half = values.shape[1] // 2
     swapped = jnp.concatenate([values[:, half:], values[:, :half]], axis=1)
     return values * cosine + swapped * sine
-
-
-def project_kernel(rows, gain, weights, bias, cosine, sine, normed, queries, keys_values):
-    bf16, f32 = jnp.bfloat16, jnp.float32
-
-    @pl.when(pl.program_id(0) == 0)
-    def _():
-        _, scaled = rms_parts(rows[...].astype(f32))
-        normed[...] = (scaled * gain[...]).astype(bf16)
-
-    columns = queries.shape[1]
-    for kind in range(3):
-        raw = product(normed[...], weights[kind]) + bias[kind : kind + 1, :]
-        for start in range(0, columns, HD):
-            head = slice(start, start + HD)
-            part = raw[:, head]
-            if kind < 2:
-                part = turned(part, cosine[...], sine[...])
-            if kind == 0:
-                queries[:, head] = part.astype(bf16)
-            else:
-                keys_values[kind - 1, :, head] = part.astype(bf16)
-
-
-def project(rows, gain, weights, bias, cosine, sine):
-    tokens, width = rows.shape
-    columns = weights.shape[2]
-    step = min(2 * HD, columns)
-    shape = jax.ShapeDtypeStruct
-    bf16 = jnp.bfloat16
-
-    def whole(*dims):
-        return pl.BlockSpec(dims, lambda h: (0,) * len(dims))
-
-    return pl.pallas_call(
-        project_kernel,
-        grid=(columns // step,),
-        in_specs=[
-            whole(tokens, width),
-            whole(1, width),
-            pl.BlockSpec((3, width, step), lambda h: (0, 0, h)),
-            pl.BlockSpec((3, step), lambda h: (0, h)),
-            whole(tokens, HD),
-            whole(tokens, HD),
-        ],
-        out_specs=(
-            whole(tokens, width),
-            pl.BlockSpec((tokens, step), lambda h: (0, h)),
-            pl.BlockSpec((2, tokens, step), lambda h: (0, 0, h)),
-        ),
-        out_shape=(
-            shape((tokens, width), bf16),
-            shape((tokens, columns), bf16),
-            shape((2, tokens, columns), bf16),
-        ),
-        compiler_params=pltpu.CompilerParams(vmem_limit_bytes=40 * 2**20),
-        name="project",
-    )(rows, gain[None], weights, bias, cosine, sine)
 
 
 def masked_scores(queries, keys, query_doc, key_doc):
@@ -812,10 +754,8 @@
 
         lax.fori_loop(0, steps, step, 0)
         out = self.jobs[job][2]
-        source = total
-        if out.dtype != total.dtype:
-            source = self.low.at[which, pl.ds(0, rows)]
-            source[...] = total[...].astype(out.dtype)
+        source = self.low.at[which, pl.ds(0, rows)]
+        source[...] = total[...].astype(out.dtype)
         self.stores[which] = pltpu.make_async_copy(source, out, self.out_sems.at[which])
         self.stores[which].start()
 
@@ -1053,8 +993,8 @@
             shape((count, width), f32),
             shape((count, width), f32),
             shape(s_shape, f32),
-            shape((experts, 2, hidden, width), f32),
-            shape((experts, hidden, width), f32),
+            shape((experts, 2, hidden, width), dtype),
+            shape((experts, hidden, width), dtype),
             shape((3, shared_hidden, width), dtype),
         ),
         in_specs=[IN_PLACE] * 11,
@@ -1074,7 +1014,7 @@
             pltpu.VMEM((2, 640, shared_hidden), dtype),
             pltpu.VMEM((2, 640, width), dtype),
             pltpu.VMEM((2, hidden, width), f32),
-            pltpu.VMEM((2, shared_hidden, width), dtype),
+            pltpu.VMEM((2, hidden, width), dtype),
             pltpu.SemaphoreType.DMA((2, 2)),
             pltpu.SemaphoreType.DMA((2,)),
             pltpu.SemaphoreType.REGULAR,
@@ -1085,15 +1025,19 @@
     )(back_part, ffn_part, scalars, *fed)
 
 
-def spread_kernel(
-    shard_in, shard_out, routes, full_in, full_out, full_routes, send_sems, recv_sems
+def open_kernel(
+    shard_in, shard_out, routes, rows, gain, bias, cosine, sine,
+    full_in, full_out, full_routes, normed, queries, keys_values,
+    sums, share_send, share_recv, send_sems, recv_sems,
 ):
     me = Peers()
     copies = Copies(send_sems, recv_sems)
-    kinds, depth, _ = shard_in.shape
-    rows, columns = shard_out.shape
+    bf16, f32 = jnp.bfloat16, jnp.float32
+    kinds, depth, width = shard_in.shape
+    out_rows, columns = shard_out.shape
+    tokens = rows.shape[0]
     sides = ((RIGHT, me.right, -1), (LEFT, me.left, 1))
-    greet([me.right, me.left])
+    greet_along_z(me)
 
     def cell(kind, step, part, parts):
         block = me.block(step)
@@ -1102,7 +1046,7 @@
         if kind > kinds:
             return full_routes.at[block]
         across = pl.ds(pl.multiple_of(block * columns, columns), columns)
-        return full_out.at[pl.ds(part * (rows // parts), rows // parts), across]
+        return full_out.at[pl.ds(part * (out_rows // parts), out_rows // parts), across]
 
     def pass_on(side, peer, sign, kind, hop, source=None):
         if kind > kinds and hop == 3 and side == LEFT:
@@ -1119,36 +1063,152 @@
             peer,
         )
 
-    order = (kinds + 1,) + tuple(range(kinds - 1, -1, -1)) + (kinds,)
-    for kind in order:
-        source = shard_in.at[kind] if kind < kinds else shard_out if kind == kinds else routes
-        for side, peer, sign in sides:
-            pass_on(side, peer, sign, kind, 0, source)
-        copies.local((LOCAL, kind), source, cell(kind, 0, 0, 1))
-    for hop in (1, 2, 3):
+    def hop_on(hop, order):
         for kind in order:
+            source = None
+            if hop == 0:
+                source = shard_in.at[kind] if kind < kinds else shard_out if kind == kinds else routes
+                cell(kind, 0, 0, 1)[...] = source[...]
             for side, peer, sign in sides:
-                copies.arrive(side, kind, hop)
-                pass_on(side, peer, sign, kind, hop)
+                if hop > 0:
+                    copies.arrive(side, kind, hop)
+                pass_on(side, peer, sign, kind, hop, source)
+
+    def multiply(kind, step):
+        block = me.block(step)
+        features = normed[:, pl.ds(pl.multiple_of(block * depth, depth), depth)]
+        term = product(features, full_in[kind, block])
+        if step == 0:
+            sums[kind] = term + bias[kind : kind + 1, :]
+        else:
+            sums[kind] += term
+
+    def go_round(order):
+        taken = [kind for kind in order if kind < kinds]
+        for hop in (1, 2, 3):
+            hop_on(hop, order)
+            for kind in taken:
+                for step in (-hop, hop):
+                    multiply(kind, step)
+        for kind in order:
+            for side, _, _ in sides:
+                if kind <= kinds or side == RIGHT:
+                    copies.arrive(side, kind, 4)
+        for kind in taken:
+            multiply(kind, 4)
+
+    def heads_of(kind, turn):
+        for start in range(0, width, HD):
+            head = slice(start, start + HD)
+            part = sums[kind, :, head]
+            if turn:
+                part = turned(part, cosine[...], sine[...])
+            yield head, part.astype(bf16)
+
+    first, second = (kinds + 1,) + tuple(range(kinds - 1, 0, -1)), (0, kinds)
+    hop_on(0, first)
+    _, scaled = rms_parts(rows[...].astype(f32))
+    normed[...] = (scaled * gain[...]).astype(bf16)
+    for kind in range(kinds):
+        if kind:
+            multiply(kind, 0)
+    go_round(first)
+    for index in range(2):
+        for head, part in heads_of(index + 1, index == 0):
+            keys_values[index, 2, :, head] = part
+    pieces = 2
+    size = tokens // pieces
+    parts = [(kind, pl.ds(piece * size, size)) for kind in range(2) for piece in range(pieces)]
+    count = len(parts)
+    share = Copies(share_send, share_recv)
+
+    def upward(index, kind, at):
+        target = keys_values.at[kind, 0, at]
+        return share.describe(keys_values.at[kind, 2, at], target, (me.ep + 2, me.tp), index)
+
+    def sideways(index, kind, at):
+        target = keys_values.at[kind, 1, at]
+        return share.describe(keys_values.at[kind, 2, at], target, me.y_peer, count + index)
+
+    def onward(index, kind, at):
+        target = keys_values.at[kind, 1, at]
+        return share.describe(keys_values.at[kind, 0, at], target, me.y_peer, count + index)
+
+    def each(copy, action):
+        for index, (kind, at) in enumerate(parts):
+            action(copy(index, kind, at))
+
+    @pl.when(me.z < 3)
+    def _():
+        each(upward, lambda copy: copy.start())
+
+    @pl.when(me.y == 0)
+    def _():
+        each(sideways, lambda copy: copy.start())
+
+    hop_on(0, second)
+    multiply(0, 0)
+
+    @pl.when(me.z == 0)
+    def _():
+        keys_values[:, 0] = jnp.zeros((2, tokens, width), bf16)
+
+    @pl.when((me.z == 0) & (me.y == 0))
+    def _():
+        keys_values[:, 1] = jnp.zeros((2, tokens, width), bf16)
+
+    @pl.when(me.z > 0)
+    def _():
+        for index, (kind, at) in enumerate(parts):
+            upward(index, kind, at).wait_recv()
+
+            @pl.when(me.y == 1)
+            def _():
+                onward(index, kind, at).start()
+
+    go_round(second)
+    for head, part in heads_of(0, True):
+        queries[:, head] = part
+
+    @pl.when((me.y == 1) | (me.z > 0))
+    def _():
+        each(sideways, lambda copy: copy.wait_recv())
+
+    @pl.when(me.z < 3)
+    def _():
+        each(upward, lambda copy: copy.wait_send())
+
+    @pl.when((me.y == 0) | (me.z > 0))
+    def _():
+        each(sideways, lambda copy: copy.wait_send())
+
     copies.finish()
 
 
-def spread_weights(shard_in, shard_out, routes, collective_id):
+def open_attention(shard_in, shard_out, routes, rows, gain, bias, cosine, sine, collective_id):
     kinds, depth, width = shard_in.shape
-    rows, columns = shard_out.shape
+    out_rows, columns = shard_out.shape
+    tokens, features = rows.shape
+    bf16 = jnp.bfloat16
+    shape = jax.ShapeDtypeStruct
     return pl.pallas_call(
-        spread_kernel,
+        open_kernel,
         out_shape=(
-            jax.ShapeDtypeStruct((kinds, RING, depth, width), shard_in.dtype),
-            jax.ShapeDtypeStruct((rows, RING * columns), shard_out.dtype),
-            jax.ShapeDtypeStruct((RING,) + routes.shape, routes.dtype),
+            shape((kinds, RING, depth, width), bf16),
+            shape((out_rows, RING * columns), bf16),
+            shape((RING,) + routes.shape, routes.dtype),
+            shape((tokens, features), bf16),
+            shape((tokens, width), bf16),
+            shape((2, 3, tokens, width), bf16),
         ),
-        in_specs=[IN_VMEM] * 3,
-        out_specs=(IN_PLACE,) * 2 + (IN_VMEM,),
-        scratch_shapes=semaphores(9 * (kinds + 2)),
+        in_specs=[IN_VMEM] * 8,
+        out_specs=(IN_VMEM,) * 6,
+        scratch_shapes=[pltpu.VMEM((kinds, tokens, width), jnp.float32)]
+        + semaphores(8)
+        + semaphores(8 * (kinds + 2)),
         compiler_params=remote_params(collective_id),
-        name="spread_weights",
-    )(shard_in, shard_out, routes)
+        name="open_attention",
+    )(shard_in, shard_out, routes, rows, gain[None], bias, cosine, sine)
 
 
 def finish_kernel(
@@ -1360,90 +1420,6 @@
     pl.semaphore_wait(barrier, 1 + (me.z + 2) // 3 + (5 - me.z) // 3)
 
 
-def share_kernel(own, out, send_sems, recv_sems):
-    me = Peers()
-    kinds, tokens, _ = own.shape
-    pieces = 2
-    size = tokens // pieces
-    parts = [(kind, pl.ds(piece * size, size)) for kind in range(kinds) for piece in range(pieces)]
-    count = len(parts)
-    greet_along_z(me)
-
-    def copy(index, source, target, peer):
-        return Copies(send_sems, recv_sems).describe(source, target, peer, index)
-
-    def upward(index, kind, rows):
-        return copy(index, own.at[kind, rows], out.at[kind, 0, rows], (me.ep + 2, me.tp))
-
-    def sideways(index, kind, rows):
-        return copy(count + index, own.at[kind, rows], out.at[kind, 1, rows], me.y_peer)
-
-    def onward(index, kind, rows):
-        return copy(count + index, out.at[kind, 0, rows], out.at[kind, 1, rows], me.y_peer)
-
-    @pl.when(me.z < 3)
-    def _():
-        for index, (kind, rows) in enumerate(parts):
-            upward(index, kind, rows).start()
-
-    @pl.when(me.y == 0)
-    def _():
-        for index, (kind, rows) in enumerate(parts):
-            sideways(index, kind, rows).start()
-
-    out[:, 2] = own[...]
-
-    @pl.when(me.z == 0)
-    def _():
-        out[:, 0] = jnp.zeros_like(own)
-
-    @pl.when((me.z == 0) & (me.y == 0))
-    def _():
-        out[:, 1] = jnp.zeros_like(own)
-
-    @pl.when(me.z > 0)
-    def _():
-        for index, (kind, rows) in enumerate(parts):
-            upward(index, kind, rows).wait_recv()
-
-            @pl.when(me.y == 1)
-            def _():
-                onward(index, kind, rows).start()
-
-    @pl.when(me.y == 1)
-    def _():
-        for index, (kind, rows) in enumerate(parts):
-            sideways(index, kind, rows).wait_recv()
-
-    @pl.when((me.y == 0) & (me.z > 0))
-    def _():
-        for index, (kind, rows) in enumerate(parts):
-            onward(index, kind, rows).wait_recv()
-
-    @pl.when(me.z < 3)
-    def _():
-        for index, (kind, rows) in enumerate(parts):
-            upward(index, kind, rows).wait_send()
-
-    @pl.when((me.y == 0) | (me.z > 0))
-    def _():
-        for index, (kind, rows) in enumerate(parts):
-            sideways(index, kind, rows).wait_send()
-
-
-def share_keys(own, collective_id):
-    kinds, tokens, width = own.shape
-    return pl.pallas_call(
-        share_kernel,
-        out_shape=jax.ShapeDtypeStruct((kinds, 3, tokens, width), own.dtype),
-        in_specs=[IN_VMEM],
-        out_specs=IN_VMEM,
-        scratch_shapes=semaphores(8),
-        compiler_params=remote_params(collective_id),
-        name="share_keys",
-    )(own)
-
-
 def return_kernel(grads, cosine, sine, out, total, from_y, from_z, send_sems, recv_sems):
     me = Peers()
     kinds, _, tokens, _ = grads.shape
@@ -1651,28 +1627,6 @@
     route_rows = jnp.concatenate(
         [routes.T, jnp.zeros((-top_count % 8, tok_count), routes.dtype)]
     )
-    in_blocks, out_full, all_routes = spread_weights(attention_in, attention_out, route_rows, 0)
-    in_full = in_blocks.reshape(3, model_width, -1)
-    shard_width = shared_in.shape[1]
-    slice_hidden = shared_in.shape[2] // ep_size
-    shared_shards = jnp.concatenate([jnp.swapaxes(shared_in, 1, 2), shared_down[None]])
-    shared_shards = jnp.swapaxes(
-        shared_shards.reshape(3, ep_size, slice_hidden, shard_width), 0, 1
-    )
-    shared_slices = lax.all_to_all(
-        after(shared_shards, in_blocks), EP, split_axis=0, concat_axis=0, tiled=True
-    )
-    shared_slices = jnp.transpose(shared_slices, (1, 2, 0, 3)).reshape(
-        3, slice_hidden, model_width
-    )
-    my_ids = ep_index * local_experts + jnp.arange(local_experts, dtype=jnp.int32)
-    taken = jnp.any(all_routes[:, None, :top_count] == my_ids[None, :, None, None], axis=2)
-    earlier_mask = jnp.tril(jnp.ones((tok_count, tok_count), bf16), -1)
-    rank = product(
-        taken.astype(bf16).reshape(-1, tok_count), earlier_mask, NT
-    ).astype(jnp.int32).reshape(taken.shape)
-    rank = jnp.where(taken & (rank < capacity), rank, NO_SLOT)
-
     positions = ep_index * tok_count + jnp.arange(tok_count, dtype=jnp.int32)
     key_count = (reach_back + 1) * tok_count
     key_positions = (ep_index - reach_back) * tok_count + jnp.arange(key_count, dtype=jnp.int32)
@@ -1683,10 +1637,37 @@
     cosine, sine = (part[:, 0] for part in rope_angles(rope_pos, HD))
     cosine = jnp.concatenate([cosine, cosine], axis=1)
     sine = jnp.concatenate([-sine, sine], axis=1)
-    normed_attention, queries, own_kv = project(
-        layer_input, attention_gain, in_full, attention_bias, cosine, sine
-    )
-    keys_values = share_keys(own_kv, 1)
+    in_blocks, out_full, all_routes, normed_attention, queries, keys_values = open_attention(
+        attention_in,
+        attention_out,
+        route_rows,
+        layer_input,
+        attention_gain,
+        attention_bias,
+        cosine,
+        sine,
+        0,
+    )
+    in_full = in_blocks.reshape(3, model_width, -1)
+    shard_width = shared_in.shape[1]
+    slice_hidden = shared_in.shape[2] // ep_size
+    shared_shards = jnp.concatenate([jnp.swapaxes(shared_in, 1, 2), shared_down[None]])
+    shared_shards = jnp.swapaxes(
+        shared_shards.reshape(3, ep_size, slice_hidden, shard_width), 0, 1
+    )
+    shared_slices = lax.all_to_all(
+        after(shared_shards, queries), EP, split_axis=0, concat_axis=0, tiled=True
+    )
+    shared_slices = jnp.transpose(shared_slices, (1, 2, 0, 3)).reshape(
+        3, slice_hidden, model_width
+    )
+    my_ids = ep_index * local_experts + jnp.arange(local_experts, dtype=jnp.int32)
+    taken = jnp.any(all_routes[:, None, :top_count] == my_ids[None, :, None, None], axis=2)
+    earlier_mask = jnp.tril(jnp.ones((tok_count, tok_count), bf16), -1)
+    rank = product(
+        taken.astype(bf16).reshape(-1, tok_count), earlier_mask, NT
+    ).astype(jnp.int32).reshape(taken.shape)
+    rank = jnp.where(taken & (rank < capacity), rank, NO_SLOT)
     heads_low, log_totals = attend(queries, keys_values, query_doc, key_doc, valid_rows)
     attention_sum = product_to_owner(heads_low[None], out_full[None], False, 2)
     input_rows = own_rows(layer_input, tp_index, own_count).astype(f32)
@@ -1756,7 +1737,8 @@
         back_part.reshape(part_shape), ffn_part.reshape(part_shape), scalar_part, fed, 4
     )
     scalar_sum = scalar_sum.T
-    grad_expert_in = jnp.swapaxes(grad_expert_in, 2, 3)
+    grad_expert_in = jnp.swapaxes(grad_expert_in, 2, 3).astype(f32)
+    grad_expert_down = grad_expert_down.astype(f32)
     layer_output = lax.all_gather((residual + ffn_sum).astype(bf16), TP, axis=0, tiled=True)
     shared_grads = jnp.transpose(
         shared_grads.reshape(3, slice_hidden, ep_size, shard_width), (2, 0, 1, 3)

time: 808 us -> 767 us (0.949)
  Pallas kernels: 680 us -> 644 us
  local copies, waits for them, and re-layouts: 60.6 us -> 40.7 us
  other arithmetic: 24.7 us -> 39.2 us
    pallas_call x1, Pallas kernels: 199 us -> 179 us  [gather_feed(): pl.pallas_call(gather_feed_kernel, out_shape=(shape((RING, 4, count, widt...]
    unnamed x96 -> x60, local copies, waits for them, and re-layouts: 38.2 us -> 18.3 us
    pallas_call x3 -> x1, Pallas kernels: 133 us -> 116 us  [open_attention(): pl.pallas_call(open_kernel, out_shape=(shape((kinds, RING, depth, width),...]
    convert_element_type x0 -> x2, other arithmetic: none -> 12 us  [the longest x1 8.67 us: per_device_dense(): grad_expert_in = jnp.swapaxes(grad_expert_in, 2, 3).astype(f32)]
  transfers between devices with their start and end apart: 4 -> 4, of which waited for: 0 -> 1; matrix products, arithmetic and copies ran while one was open for 5% -> 6% of each run, Pallas kernels for 30% -> 26%
where the time goes in v4:
time: 767 us; the launch traced here: 760 us
  Pallas kernels  644 us (84%)
  local copies, waits for them, and re-layouts  40.7 us (5%)
  other arithmetic  39.2 us (5%)
  between operations  16.3 us (2%)
  matrix products  10.5 us (1%)
  starting transfers between devices  9.71 us (1%)
    pallas_call x1, Pallas kernels, gather_feed(): pl.pallas_call(gather_feed_kernel, out_shape=(shape((RING, 4, count, widt...  179 us
    pallas_call x1, Pallas kernels, scatter_rows(): pl.pallas_call(scatter_kernel, out_shape=(shape((count, width), f32), sha...  154 us
    pallas_call x1, Pallas kernels, open_attention(): pl.pallas_call(open_kernel, out_shape=(shape((kinds, RING, depth, width),...  116 us
    pallas_call x1, Pallas kernels, finish(): pl.pallas_call(finish_kernel, out_shape=(shape((kinds, depth, columns), f...  105 us
    pallas_call x1, Pallas kernels, return_keys(): pl.pallas_call(return_kernel, out_shape=jax.ShapeDtypeStruct((kinds, toke...  29.7 us
    pallas_call x1, Pallas kernels, tensor_gather(): pl.pallas_call(tensor_kernel, out_shape=jax.ShapeDtypeStruct((4,) + rows....  20.3 us
    unnamed x60, local copies, waits for them, and re-layouts  18.3 us
    pallas_call x1, Pallas kernels, product_to_owner(): pl.pallas_call(functools.partial(reduce_kernel, flip), out_shape=jax.Shap...  17.1 us
  transfers between devices with their start and end apart: 4, of which 1 were waited for; matrix products, arithmetic and copies ran while one was open for 6% of the time, Pallas kernels for 26%

profile of v4, /device:TPU:0, one launch (start us, length us, event | category | flops | bytes accessed | tf_op | source)
XLA Modules:
  0.0 760.4 jit_solution(11684755622570518653)
XLA Ops:
  8.0 0.9 reduce-window.4
  11.8 1.7 copy.67
  13.5 1.0 fusion.27
  14.5 1.4 maximum_bitcast_fusion
  16.1 116.4 %open_attention.1 = (bf16[3,8,256,512]{3,2,1,0:T(8,128)(2,1)}, bf16[512,2048]{1,0:T(8,128)(2,1)S(1)}, s32[8,8,512]{2,1,0:T(8,128)S(1)}, bf16[512,2048]{1,0:T(8,1...) custom-call(bf16[3,256,512]{2,1,0:T(8,128)(2,1)S(1)} %copy-done.11, ...), custom_call_target="tpu_custom_call" | custom-call | tf_op jit(solution)/shard_map/open_attention/pallas_call | solution.py:1194
  132.5 1.3 copy-done.5
  133.8 1.5 copy.68
  135.3 4.7 all-to-all-start
  140.8 0.8 copy.65
  142.1 2.0 copy.64
  144.1 3.3 and_select_fusion
  147.4 2.8 copy.70.rank_row
  151.3 1.9 copy-done.1
  153.2 9.9 %attend.1 = (bf16[512,512]{1,0:T(8,128)(2,1)S(1)}, f32[4,512,1]{2,1,0:T(8,128)S(1)}) custom-call(bf16[512,512]{1,0:T(8,128)(2,1)S(1)} %get-tuple-element.46.queries, bf16[2,3,512,512]{3,2,1,0:T(8,128)(2,1)S(1)} %copy-done.1, bf16[2,3,512,512]{3,2,1,0:T(8,128)(2,1)S(1)} %copy-done.1, s32[512,1]{1,0:T(8,128)S(1)} %fusion.25.query_doc, ...), custom_call_target="tpu_custom_call" | custom-call | tf_op jit(solution)/shard_map/attend/pallas_call | solution.py:134
  163.2 1.0 copy-done.9
  164.1 17.1 %product_to_owner.1 = f32[128,2048]{1,0:T(8,128)S(1)} custom-call(bf16[1,512,512]{2,1,0:T(8,128)(2,1)S(1)} %bitcast.103, bf16[1,512,2048]{2,1,0:T(8,128)(2,1)S(1)} %bitcast.104), custom_call_target="tpu_custom_call" | custom-call | tf_op jit(solution)/shard_map/product_to_owner/pallas_call | solution.py:1542
  181.9 2.0 multiply_reduce_fusion.2
  184.0 1.0 fusion.42
  185.1 1.0 fusion.5
  186.8 0.9 fusion.10.rows
  188.0 3.2 copy.78
  191.2 178.9 %gather_feed.1 = (bf16[8,4,128,2048]{3,2,1,0:T(8,128)(2,1)}, bf16[8,4,128,2048]{3,2,1,0:T(8,128)(2,1)}, f32[8,4,24,128]{3,2,1,0:T(8,128)}, bf16[8,512,2048]{2,1,...) custom-call(bf16[128,2048]{1,0:T(8,128)(2,1)} %fusion.10.rows, ...), custom_call_target="tpu_custom_call" | custom-call | tf_op jit(solution)/shard_map/gather_feed/pallas_call | solution.py:639
  370.2 2.2 reduce
  373.3 153.8 %scatter_rows.1 = (f32[128,2048]{1,0:T(8,128)}, f32[128,2048]{1,0:T(8,128)}, f32[24,128]{1,0:T(8,128)}, bf16[2,2,352,2048]{3,2,1,0:T(8,128)(2,1)}, bf16[2,352,20...) custom-call(bf16[8,4,128,2048]{3,2,1,0:T(8,128)(2,1)} %bitcast.113, bf16[8,4,128,2048]{3,2,1,0:T(8,128)(2,1)} %bitcast.112, ...), custom_call_target="tpu_custom_call" | custom-call | tf_op jit(solution)/shard_map/scatter_rows/pallas_call | solution.py:990
  530.1 1.4 fusion.7
  531.5 2.3 multiply_reduce_fusion
  534.6 3.1 copy.83
  537.7 4.4 all-to-all-start.1
  542.1 3.3 fusion.40
  546.1 20.3 %tensor_gather.1 = bf16[4,128,2048]{2,1,0:T(8,128)(2,1)S(1)} custom-call(bf16[128,2048]{1,0:T(8,128)(2,1)S(1)} %get-tuple-element.120.rows), custom_call_target="tpu_custom_call" | custom-call | tf_op jit(solution)/shard_map/tensor_gather/pallas_call | solution.py:1574
  566.4 3.7 fusion.1.grad_heads
  570.1 13.0 %attend_back.1 = (bf16[512,512]{1,0:T(8,128)(2,1)S(1)}, bf16[2,3,512,512]{3,2,1,0:T(8,128)(2,1)}) custom-call(bf16[512,512]{1,0:T(8,128)(2,1)S(1)} %copy-done.8, bf16[2,3,512,512]{3,2,1,0:T(8,128)(2,1)} %get-tuple-element.47.keys.values, bf16[2,3,512,512]{3,2,1,0:T(8,128)(2,1)} %get-tuple-element.47.keys.values, s32[512,1]{1,0:T(8,128)S(1)} %fusion.25.query_doc, ...), custom_call_target="tpu_custom_call" | custom-call | tf_op jit(solution)/shard_map/attend_back/pallas_call | solution.py:176
  583.2 1.9 copy-done.3
  585.1 29.7 %return_keys.1 = bf16[2,512,512]{2,1,0:T(8,128)(2,1)S(1)} custom-call(bf16[2,3,512,512]{3,2,1,0:T(8,128)(2,1)S(1)} %copy-done.3, f32[512,128]{1,0:T(8,128)S(1)} %get-tuple-element.134.cosine, f32[512,128]{1,0:T(8,128)S(1)} %get-tuple-element.135.sine), custom_call_target="tpu_custom_call" | custom-call | tf_op jit(solution)/shard_map/return_keys/pallas_call | solution.py:1489
  615.6 1.3 pad_maximum_fusion.grad_raw
  616.9 104.5 %finish.1 = (f32[3,256,512]{2,1,0:T(8,128)}, f32[512,256]{1,0:T(8,128)}, f32[4,8,512]{2,1,0:T(8,128)}, bf16[4,128,2048]{2,1,0:T(8,128)(2,1)}) custom-call(bf16[512,2048]{1,0:T(8,128)(2,1)} %get-tuple-element.65.normed, bf16[3,512,512]{2,1,0:T(8,128)(2,1)} %pad_maximum_fusion.grad_raw, bf16[512,512]{1,0:T(8,128)(2,1)} %copy-done.4, ...), custom_call_target="tpu_custom_call" | custom-call | tf_op jit(solution)/shard_map/finish/pallas_call | solution.py:1376
  721.4 0.9 slice_reduce_fusion
  722.9 3.3 convert_element_type.84
  726.2 1.3 dynamic-slice_bitcast_fusion
  727.5 8.7 %convert_bitcast_fusion = f32[2,2,2048,352]{2,3,1,0:T(8,128)} fusion(bf16[2,2,352,2048]{3,2,1,0:T(8,128)(2,1)} %get-tuple-element.77), kind=kLoop, calls=%fused_computation | loop fusion | flops 2883584 | bytes 17301504 | tf_op jit(solution)/shard_map/convert_element_type | solution.py:1740
  736.2 1.5 fusion.41
  737.7 1.6 slice_bitcast_fusion
  739.3 2.1 convert_bitcast_fusion.1
  741.6 1.2 slice.67
  742.8 2.2 copy.75
  745.0 3.3 copy.90
  748.3 1.3 copy.91
  750.5 1.1 copy.92
  (108 shorter events, 15.9 us)
Async XLA Ops:
  8.0 175.9 %copy-start = (f32[2048,16]{0,1:T(8,128)S(1)}, f32[2048,16]{0,1:T(8,128)}, u32[]{:S(2)}) copy-start(f32[2048,16]{0,1:T(8,128)} %param.24) | copy-start | bytes 393220
  14.5 1.6 copy-start.11
  14.5 1.6 copy-start.12
  14.5 1.6 copy-start.13
  14.5 1.6 copy-start.14
  132.5 1.3 copy-start.5
  133.8 17.5 %copy-start.7 = (bf16[512,512]{1,0:T(8,128)(2,1)}, bf16[512,512]{1,0:T(8,128)(2,1)S(1)}, u32[]{:S(2)}) copy-start(bf16[512,512]{1,0:T(8,128)(2,1)S(1)} %get-tuple-element.46.queries) | copy-start | bytes 1572868
  135.3 52.6 %all-to-all-start = ((bf16[8,3,176,256]{3,2,1,0:T(8,128)(2,1)}), bf16[8,3,176,256]{3,2,1,0:T(8,128)(2,1)}, u32[]{:S(2)}, u32[]{:S(2)}) async-start(bf16[8,3,176,256]{3,2,1,0:T(8,128)(2,1)} %copy.68), calls=%async_computation | async-start | bytes 4325376 | tf_op jit(solution)/shard_map/all_to_all | solution.py:1658
  140.1 596.1 %all-reduce.3.cloned.1.call-start = ((), (), s32[]{:S(2)}) async-start(), calls=%async_computation.3 | async-start | bytes 393216 | tf_op jit(solution)/shard_map/psum | solution.py:1774
  151.3 1.9 copy-start.1
  153.2 10.9 %copy-start.6 = (bf16[512,2048]{1,0:T(8,128)(2,1)S(1)}, bf16[512,2048]{1,0:T(8,128)(2,1)}, u32[]{:S(2)}) copy-start(bf16[512,2048]{1,0:T(8,128)(2,1)} %copy-done.5) | copy-start | bytes 6291460
  163.2 1.0 copy-start.9
  164.1 19.8 %copy-start.4 = (bf16[512,512]{1,0:T(8,128)(2,1)}, bf16[512,512]{1,0:T(8,128)(2,1)S(1)}, u32[]{:S(2)}) copy-start(bf16[512,512]{1,0:T(8,128)(2,1)S(1)} %get-tuple-element.48.heads) | copy-start | bytes 1572868
  181.2 2.7 copy-start.22
  181.9 3.2 copy-start.24
  183.9 2.9 copy-start.15
  370.2 2.3 copy-start.25
  373.3 155.3 %copy-start.16 = (f32[128,2048]{1,0:T(8,128)S(1)}, f32[128,2048]{1,0:T(8,128)}, u32[]{:S(2)}) copy-start(f32[128,2048]{1,0:T(8,128)} %copy-done.15) | copy-start | bytes 3145732
  527.1 4.4 copy-start.20
  527.1 4.4 copy-start.23
  537.7 201.6 %all-to-all-start.1 = ((bf16[8,3,176,256]{3,2,1,0:T(8,128)(2,1)}), bf16[8,3,176,256]{3,2,1,0:T(8,128)(2,1)}, u32[]{:S(2)}, u32[]{:S(2)}) async-start(bf16[8,3,176,256]{3,2,1,0:T(8,128)(2,1)} %bitcast.117), calls=%async_computation.1 | async-start | bytes 4325376 | tf_op jit(solution)/shard_map/all_to_all | solution.py:1746
  542.1 197.2 %all-gather.2.cloned.1.call-start = ((), (), s32[]{:S(2)}) async-start(), calls=%async_computation.2 | async-start | bytes 2621440 | tf_op jit(solution)/shard_map/all_gather | solution.py:1742
  566.4 3.7 copy-start.2
  566.4 3.7 copy-start.8
  566.4 3.7 copy-start.10
  583.2 1.9 copy-start.3
  616.9 106.0 %copy-start.17 = (bf16[2,352,2048]{2,1,0:T(8,128)(2,1)S(1)}, bf16[2,352,2048]{2,1,0:T(8,128)(2,1)}, u32[]{:S(2)}) copy-start(bf16[2,352,2048]{2,1,0:T(8,128)(2,1)} %get-tuple-element.78) | copy-start | bytes 8650756
  745.0 3.3 copy-start.18
  748.3 2.2 copy-start.19
  750.5 1.4 copy-start.21
Sparse Core Ops, SparseCore 0:
  534.8 143.3 all-reduce.2
Sparse Core Ops, SparseCore 1:
  545.5 26.7 all-gather.1

commit v5 on v4

--- a/solution.py
+++ b/solution.py
@@ -145,48 +145,6 @@
     )(queries, keys_values, keys_values, query_doc, key_doc, valid)
 
 
-def attend_back_kernel(
-    queries, keys, values, query_doc, key_doc, log_totals, grad_heads, cosine, sine,
-    grad_queries, grad_keys_values,
-):
-    bf16 = jnp.bfloat16
-    scale = 1.0 / math.sqrt(HD)
-    blocks, tokens = keys.shape[1], keys.shape[2]
-    keys, values = (ref[0].reshape(blocks * tokens, HD) for ref in (keys, values))
-    scores = masked_scores(queries[...], keys, query_doc[...], key_doc[...])
-    probs = jnp.exp(scores - log_totals[0])
-    grads = grad_heads[...]
-    slopes = product(grads, values, NT)
-    slopes = probs * (slopes - jnp.sum(probs * slopes, axis=1, keepdims=True))
-    grad_scores = slopes.astype(bf16)
-    turned_back = turned(product(grad_scores, keys) * scale, cosine[...], -sine[...])
-    grad_queries[...] = turned_back.astype(bf16)
-    grad_keys = product(grad_scores, queries[...], TN) * scale
-    grad_keys_values[0] = grad_keys.astype(bf16).reshape(blocks, tokens, HD)
-    grad_values = product(probs.astype(bf16), grads, TN)
-    grad_keys_values[1] = grad_values.astype(bf16).reshape(blocks, tokens, HD)
-
-
-def attend_back(queries, keys_values, query_doc, key_doc, log_totals, grad_heads, cosine, sine):
-    tokens, columns = queries.shape
-    blocks = keys_values.shape[1]
-    head, keys, values, column, row, logs = attention_specs(tokens, blocks)
-    angle = pl.BlockSpec((tokens, HD), lambda h: (0, 0))
-    shape = jax.ShapeDtypeStruct
-    return pl.pallas_call(
-        attend_back_kernel,
-        grid=(columns // HD,),
-        in_specs=[head, keys, values, column, row, logs, head, angle, angle],
-        out_specs=(head, pl.BlockSpec((2, blocks, tokens, HD), lambda h: (0, 0, 0, h))),
-        out_shape=(
-            shape((tokens, columns), jnp.bfloat16),
-            shape(keys_values.shape, jnp.bfloat16),
-        ),
-        compiler_params=pltpu.CompilerParams(vmem_limit_bytes=48 * 2**20),
-        name="attend_back",
-    )(queries, keys_values, keys_values, query_doc, key_doc, log_totals, grad_heads, cosine, sine)
-
-
 RING = 8
 NO_SLOT = 1 << 20
 RIGHT, LEFT, OVER_X, OVER_CORE, OVER_FAR, LOCAL, SCALARS = range(7)
@@ -311,8 +269,8 @@
 
 
 def feed_block(
-    block, rank_row, rank_column, gate_rows, scale, token_rows, token_cotangent,
-    expert_in, expert_down, shared, staged, between, out_terms, back_terms, scale_grad, token_grad,
+    rank_row, rank_column, gate_rows, scale, token_rows, token_cotangent,
+    expert_in, expert_down, shared, staged, between, out_terms, back_terms, scalar_out,
 ):
     (
         out_part, back_part, slot_rows, slot_cotangent, grad_pre, gated, grad_shared_pre, scaled,
@@ -327,7 +285,7 @@
     hidden = (silu * up).astype(bf16).astype(f32)
     scaled_hidden = (scale * hidden).astype(bf16)
     back = product(token_cotangent, shared[2], NT)
-    scale_grad[block] = jnp.sum(hidden * back, axis=1, keepdims=True)
+    scalar_out(None, jnp.sum(jnp.swapaxes(hidden * back, 0, 1), axis=0, keepdims=True))
     back = scale * back
     gate_grad = (back * up * slope).astype(bf16)
     up_grad = (back * silu).astype(bf16)
@@ -362,8 +320,8 @@
         gated[expert] = gated_hidden
         back = product(taken_cotangent[mine], expert_down[expert], NT)
         slot_grad = jnp.sum(hidden * back, axis=1, keepdims=True)
-        token_grad[block, expert : expert + 1, :] = jnp.sum(
-            jnp.where(hits[mine], slot_grad, 0.0), axis=0, keepdims=True
+        scalar_out(
+            expert, jnp.sum(jnp.where(hits[mine], slot_grad, 0.0), axis=0, keepdims=True)
         )
         back = gate * back
         gate_grad_e = (back * up * slope).astype(bf16)
@@ -383,11 +341,11 @@
 
 
 def gather_feed_kernel(
-    rows, cotangent, scales, rank_row, rank_column, expert_in, expert_down, shared,
+    rows, cotangent, scales, routes, expert_in, expert_down, shared_blocks,
     all_rows, all_cotangent, all_scales,
     out_part, back_part, slot_rows, slot_cotangent, grad_pre, gated, grad_shared_pre, scaled,
-    token_grad, scale_grad,
-    out_terms, back_terms, held_rows, held_cotangent,
+    scalars,
+    rank_row, rank_column, shared, out_terms, back_terms, held_rows, held_cotangent,
     stage_out, stage_back, stage_rows, stage_cotangent, stage_pre, stage_gated, stage_shared,
     stage_scaled,
     load_sems, store_sems, send_sems, recv_sems,
@@ -436,10 +394,31 @@
     copies.local((LOCAL, scale), lambda: scales, scales_of(q))
     experts, _, width = expert_in.shape
     all_slots = experts * slot_rows.shape[2]
-    shared_count = shared.shape[1]
+    shared_count, across = shared.shape[1], shared_blocks.shape[3]
+    for block in range(RING):
+        shared[:, :, block * across : (block + 1) * across] = shared_blocks[block]
     out_terms[all_slots:, :] = shared[2]
     back_terms[all_slots : all_slots + shared_count, :] = shared[0]
     back_terms[all_slots + shared_count :, :] = shared[1]
+    first_expert, scale_at = me.ep * experts, me_scale_row(experts)
+    tokens = routes.shape[2]
+    taken = []
+    for block in range(RING):
+        for expert in range(experts):
+            chosen = routes[block] == first_expert + expert
+            taken.append(jnp.max(chosen.astype(jnp.float32), axis=0, keepdims=True))
+    taken = jnp.concatenate(taken, axis=0)
+    down = lax.broadcasted_iota(jnp.int32, (tokens, tokens), 0)
+    right = lax.broadcasted_iota(jnp.int32, (tokens, tokens), 1)
+    rank = product(taken.astype(jnp.bfloat16), (right < down).astype(jnp.bfloat16), NT)
+    kept = (taken > 0.0) & (rank < slot_rows.shape[2])
+    rank = jnp.where(kept, rank, float(NO_SLOT))
+    column = product((right == down).astype(jnp.bfloat16), rank.astype(jnp.bfloat16), NT)
+    for block in range(RING):
+        mine = slice(block * experts, (block + 1) * experts)
+        rank_row[block] = rank[mine].astype(jnp.int32)
+        rank_column[block] = column[:, mine].astype(jnp.int32)
+    scalars[...] = jnp.zeros_like(scalars)
     copies.arrive(0, OVER_X, other, 0)
     for side, peer, sign, keep in sides:
         push((side, other, 1), 0, 0, qx, low, peer, sign, qx)
@@ -529,7 +508,6 @@
             for index, (stage, target) in enumerate(zip(staged, targets))
         ]
 
-    first_expert = me.ep * experts
 
     copies.arrive(LOCAL, 0)
     copies.arrive(LOCAL, 1)
@@ -555,11 +533,16 @@
                 for move in stores(0):
                     move.wait()
 
+        def scalar_out(expert, values):
+            row = scale_at if expert is None else first_expert + expert
+            for quarter in range(4):
+                part = values[:, quarter * count : (quarter + 1) * count]
+                scalars[block, quarter, pl.ds(row, 1), :] = part
+
         rows_here = held_rows[slot].reshape(4 * count, width)
         cotangent_here = held_cotangent[slot].reshape(4 * count, width)
         quarters = [all_scales[block, quarter] for quarter in range(4)]
         columns = jnp.concatenate([jnp.swapaxes(values, 0, 1) for values in quarters], axis=0)
-        scale_at = me_scale_row(all_scales, experts)
         gate_rows = [
             jnp.concatenate(
                 [all_scales[block, quarter, pl.ds(first_expert + e, 1), :] for quarter in range(4)],
@@ -568,7 +551,6 @@
             for e in range(experts)
         ]
         feed_block(
-            block,
             rank_row[block],
             rank_column[block],
             jnp.concatenate(gate_rows, axis=0),
@@ -582,8 +564,7 @@
             between,
             out_terms,
             back_terms,
-            scale_grad,
-            token_grad,
+            scalar_out,
         )
         for move in stores(block):
             move.start()
@@ -613,18 +594,19 @@
     copies.finish()
 
 
-def me_scale_row(all_scales, experts):
+def me_scale_row(experts):
     return RING * experts
 
 
 def gather_feed(
-    rows, cotangent, scales, rank, expert_in, expert_down, shared, capacity, collective_id
+    rows, cotangent, scales, routes, expert_in, expert_down, shared, capacity, collective_id
 ):
     bf16, f32 = jnp.bfloat16, jnp.float32
-    blocks, experts, tokens = rank.shape
+    blocks, _, tokens = routes.shape
+    experts = expert_in.shape[0]
     count, width = rows.shape
     hidden = expert_in.shape[1] // 2
-    slice_hidden = shared.shape[1]
+    slice_hidden = shared.shape[2]
     shape = jax.ShapeDtypeStruct
     stages = (
         (tokens, width),
@@ -650,12 +632,14 @@
             shape((experts, blocks, capacity, hidden), bf16),
             shape((2, blocks, tokens, slice_hidden), bf16),
             shape((blocks, tokens, slice_hidden), bf16),
-            shape((blocks, experts, tokens), f32),
-            shape((blocks, tokens, 1), f32),
+            shape((RING, 4) + scales.shape, f32),
         ),
-        in_specs=[IN_VMEM] * 8,
-        out_specs=(IN_PLACE,) * 2 + (IN_VMEM,) + (IN_PLACE,) * 8 + (IN_VMEM,) * 2,
+        in_specs=[IN_VMEM] * 7,
+        out_specs=(IN_PLACE,) * 2 + (IN_VMEM,) + (IN_PLACE,) * 8 + (IN_VMEM,),
         scratch_shapes=[
+            pltpu.VMEM((blocks, experts, tokens), jnp.int32),
+            pltpu.VMEM((blocks, tokens, experts), jnp.int32),
+            pltpu.VMEM((3, slice_hidden, width), bf16),
             pltpu.VMEM((experts * capacity + slice_hidden, width), bf16),
             pltpu.VMEM((experts * capacity + 2 * slice_hidden, width), bf16),
             pltpu.VMEM((2, 4, count, width), bf16),
@@ -666,9 +650,7 @@
         + semaphores(160),
         compiler_params=remote_params(collective_id, 62),
         name="gather_feed",
-    )(
-        rows, cotangent, scales, rank, jnp.swapaxes(rank, 1, 2), expert_in, expert_down, shared,
-    )
+    )(rows, cotangent, scales, routes, expert_in, expert_down, shared)
 
 
 def add_into(total, term, rows, tile=32):
@@ -756,7 +738,17 @@
         out = self.jobs[job][2]
         source = self.low.at[which, pl.ds(0, rows)]
         source[...] = total[...].astype(out.dtype)
-        self.stores[which] = pltpu.make_async_copy(source, out, self.out_sems.at[which])
+        if out.ndim == source.ndim:
+            moves = [pltpu.make_async_copy(source, out, self.out_sems.at[which, 0])]
+        else:
+            across = out.shape[2]
+            moves = [
+                pltpu.make_async_copy(
+                    source.at[:, pl.ds(place * across, across)], out.at[place], self.out_sems.at[which, place]
+                )
+                for place in range(out.shape[0])
+            ]
+        self.stores[which] = Pair(*moves)
         self.stores[which].start()
 
     def finish(self):
@@ -913,8 +905,8 @@
             )
         jobs.append((gated.at[expert], slot_cotangent.at[expert], grad_expert_down.at[expert]))
     for index in range(2):
-        jobs.append((grad_shared_pre.at[index], all_rows, grad_shared.at[index]))
-    jobs.append((scaled, all_cotangent, grad_shared.at[2]))
+        jobs.append((grad_shared_pre.at[index], all_rows, grad_shared.at[:, index]))
+    jobs.append((scaled, all_cotangent, grad_shared.at[:, 2]))
     prepare(0, 4, 3, 5)
     over_x(0, 4)
     hop_on(0, 0)
@@ -995,7 +987,7 @@
             shape(s_shape, f32),
             shape((experts, 2, hidden, width), dtype),
             shape((experts, hidden, width), dtype),
-            shape((3, shared_hidden, width), dtype),
+            shape((RING, 3, shared_hidden, width // RING), dtype),
         ),
         in_specs=[IN_PLACE] * 11,
         out_specs=(IN_VMEM,) * 3 + (IN_PLACE,) * 3,
@@ -1016,7 +1008,7 @@
             pltpu.VMEM((2, hidden, width), f32),
             pltpu.VMEM((2, hidden, width), dtype),
             pltpu.SemaphoreType.DMA((2, 2)),
-            pltpu.SemaphoreType.DMA((2,)),
+            pltpu.SemaphoreType.DMA((2, RING)),
             pltpu.SemaphoreType.REGULAR,
         ]
         + semaphores(168),
@@ -1403,9 +1395,10 @@
     )(normed, grad_raw, heads, grad_attention, weights, gain[None], rows, grad_residual, bias)
 
 
-def greet_along_z(me):
+def greet_along_z(me, others=()):
     barrier = pltpu.get_barrier_semaphore()
-    pl.semaphore_signal(barrier, inc=1, device_id=me.y_peer, device_id_type=MESH_ID)
+    for peer in (me.y_peer,) + others:
+        pl.semaphore_signal(barrier, inc=1, device_id=peer, device_id_type=MESH_ID)
 
     @pl.when(me.z > 0)
     def _():
@@ -1417,89 +1410,174 @@
         peer = (me.ep + 2, me.tp)
         pl.semaphore_signal(barrier, inc=1, device_id=peer, device_id_type=MESH_ID)
 
-    pl.semaphore_wait(barrier, 1 + (me.z + 2) // 3 + (5 - me.z) // 3)
-
-
-def return_kernel(grads, cosine, sine, out, total, from_y, from_z, send_sems, recv_sems):
+    pl.semaphore_wait(barrier, 1 + len(others) + (me.z + 2) // 3 + (5 - me.z) // 3)
+
+
+def back_kernel(
+    rows, weights, valid, queries, keys_values, query_doc, key_doc, log_totals, cosine, sine,
+    grad_attention, grad_raw,
+    grad_heads, grads, total, from_y, from_z,
+    y_send, y_recv, z_send, z_recv, send_sems, recv_sems,
+):
     me = Peers()
-    kinds, _, tokens, _ = grads.shape
-    pieces = 2
-    size = tokens // pieces
-    parts = [(kind, pl.ds(piece * size, size)) for kind in range(kinds) for piece in range(pieces)]
-    count = len(parts)
-    greet_along_z(me)
-
-    def copy(index, source, target, peer):
-        return Copies(send_sems, recv_sems).describe(source, target, peer, index)
-
-    def sideways(index, kind, rows):
-        return copy(index, grads.at[kind, 1, rows], from_y.at[kind, rows], me.y_peer)
-
-    def downward(index, kind, rows, source):
-        return copy(count + index, source.at[kind, rows], from_z.at[kind, rows], (me.ep - 2, me.tp))
-
-    for index, (kind, rows) in enumerate(parts):
-        sideways(index, kind, rows).start()
-
-    @pl.when((me.z > 0) & (me.y == 0))
-    def _():
-        for index, (kind, rows) in enumerate(parts):
-            downward(index, kind, rows, grads.at[:, 0]).start()
-
-    for index, (kind, rows) in enumerate(parts):
-        sideways(index, kind, rows).wait_recv()
-        here = grads[kind, 2, rows, :].astype(jnp.float32)
-
-        @pl.when(me.y == 0)
+    copies = Copies(send_sems, recv_sems)
+    bf16, f32 = jnp.bfloat16, jnp.float32
+    count = rows.shape[0]
+    tokens, width = queries.shape
+    blocks = keys_values.shape[1]
+    head_count = width // HD
+    greet_along_z(me, (me.x_peer, me.core_peer))
+
+    mine = grad_attention.at[me.quarter]
+    copies.send((OVER_X,), rows, mine, grad_attention.at[me.x_quarter], me.x_peer)
+    copies.send((OVER_CORE, 0), rows, mine, grad_attention.at[me.core_quarter], me.core_peer)
+    mine[...] = rows[...]
+
+    def heads_of(quarter):
+        at = pl.ds(pl.multiple_of(quarter * count, count), count)
+        part = product(grad_attention[quarter], weights[...], NT) * valid[at, :]
+        grad_heads[at, :] = part.astype(bf16)
+
+    heads_of(me.quarter)
+    copies.arrive(OVER_CORE, 0)
+    heads_of(me.core_quarter)
+    copies.arrive(OVER_X)
+    beside = grad_attention.at[me.x_quarter]
+    copies.send((OVER_CORE, 1), beside, beside, grad_attention.at[me.far_quarter], me.core_peer)
+    heads_of(me.x_quarter)
+    copies.arrive(OVER_CORE, 1)
+    heads_of(me.far_quarter)
+
+    across = Copies(y_send, y_recv)
+    along = Copies(z_send, z_recv)
+
+    def columns(head):
+        return pl.ds(pl.multiple_of(head * HD, HD), HD)
+
+    def sideways(head, kind):
+        at = columns(head)
+        source, target = grads.at[kind, 1, :, at], from_y.at[kind, :, at]
+        return across.describe(source, target, me.y_peer, 2 * head + kind)
+
+    def downward(head, kind, source):
+        at = columns(head)
+        return along.describe(
+            source.at[kind, :, at], from_z.at[kind, :, at], (me.ep - 2, me.tp), 2 * head + kind
+        )
+
+    scale = 1.0 / math.sqrt(HD)
+
+    def one_head(head, carry):
+        at = columns(head)
+        keys = keys_values[0, :, :, at].reshape(blocks * tokens, HD)
+        values = keys_values[1, :, :, at].reshape(blocks * tokens, HD)
+        query = queries[:, at]
+        out_grads = grad_heads[:, at]
+        scores = masked_scores(query, keys, query_doc[...], key_doc[...])
+        probs = jnp.exp(scores - log_totals[head])
+        slopes = product(out_grads, values, NT)
+        slopes = probs * (slopes - jnp.sum(probs * slopes, axis=1, keepdims=True))
+        grad_scores = slopes.astype(bf16)
+        grad_keys = product(grad_scores, query, TN) * scale
+        grads[0, :, :, at] = grad_keys.astype(bf16).reshape(blocks, tokens, HD)
+        grad_values = product(probs.astype(bf16), out_grads, TN)
+        grads[1, :, :, at] = grad_values.astype(bf16).reshape(blocks, tokens, HD)
+        for kind in range(2):
+            sideways(head, kind).start()
+
+        @pl.when((me.z > 0) & (me.y == 0))
         def _():
-            total[kind, rows, :] = here + from_y[kind, rows, :].astype(jnp.float32)
-
-        @pl.when(me.y == 1)
+            for kind in range(2):
+                downward(head, kind, grads.at[:, 0]).start()
+
+        turned_back = turned(product(grad_scores, keys) * scale, cosine[...], -sine[...])
+        grad_raw[0, :, at] = turned_back.astype(bf16)
+        return carry
+
+    lax.fori_loop(0, head_count, one_head, 0)
+
+    def from_beside(head, carry):
+        at = columns(head)
+        for kind in range(2):
+            sideways(head, kind).wait_recv()
+            here = grads[kind, 2, :, at].astype(f32)
+
+            @pl.when(me.y == 0)
+            def _():
+                total[kind, :, at] = here + from_y[kind, :, at].astype(f32)
+
+            @pl.when(me.y == 1)
+            def _():
+                total[kind, :, at] = here
+                two_back = grads[kind, 0, :, at].astype(f32)
+                summed = two_back + from_y[kind, :, at].astype(f32)
+                from_y[kind, :, at] = summed.astype(bf16)
+
+            @pl.when((me.z > 0) & (me.y == 1))
+            def _():
+                downward(head, kind, from_y).start()
+
+        return carry
+
+    lax.fori_loop(0, head_count, from_beside, 0)
+
+    def from_above(head, carry):
+        at = columns(head)
+
+        @pl.when(me.z < 3)
         def _():
-            total[kind, rows, :] = here
-            two_back = grads[kind, 0, rows, :].astype(jnp.float32)
-            summed = two_back + from_y[kind, rows, :].astype(jnp.float32)
-            from_y[kind, rows, :] = summed.astype(from_y.dtype)
-
-        @pl.when((me.z > 0) & (me.y == 1))
+            for kind in range(2):
+                downward(head, kind, from_y).wait_recv()
+                total[kind, :, at] += from_z[kind, :, at].astype(f32)
+
+        grad_raw[1, :, at] = turned(total[0, :, at], cosine[...], -sine[...]).astype(bf16)
+        grad_raw[2, :, at] = total[1, :, at].astype(bf16)
+        return carry
+
+    lax.fori_loop(0, head_count, from_above, 0)
+
+    def sent(head, carry):
+        for kind in range(2):
+            sideways(head, kind).wait_send()
+
+        @pl.when(me.z > 0)
         def _():
-            downward(index, kind, rows, from_y).start()
-
-    @pl.when(me.z < 3)
-    def _():
-        for index, (kind, rows) in enumerate(parts):
-            downward(index, kind, rows, from_y).wait_recv()
-            total[kind, rows, :] += from_z[kind, rows, :].astype(jnp.float32)
-
-    for start in range(0, total.shape[2], HD):
-        head = slice(start, start + HD)
-        out[0, :, head] = turned(total[0, :, head], cosine[...], -sine[...]).astype(out.dtype)
-    out[1] = total[1].astype(out.dtype)
-    for index, (kind, rows) in enumerate(parts):
-        sideways(index, kind, rows).wait_send()
-
-    @pl.when(me.z > 0)
-    def _():
-        for index, (kind, rows) in enumerate(parts):
-            downward(index, kind, rows, from_y).wait_send()
-
-
-def return_keys(grads, cosine, sine, collective_id):
-    kinds, _, tokens, width = grads.shape
+            for kind in range(2):
+                downward(head, kind, from_y).wait_send()
+
+        return carry
+
+    lax.fori_loop(0, head_count, sent, 0)
+    copies.finish()
+
+
+def back_attention(
+    rows, weights, valid, queries, keys_values, query_doc, key_doc, log_totals, cosine, sine,
+    collective_id,
+):
+    count, features = rows.shape
+    tokens, width = queries.shape
+    bf16, f32 = jnp.bfloat16, jnp.float32
+    shape = jax.ShapeDtypeStruct
+    pieces = 2 * (width // HD)
     return pl.pallas_call(
-        return_kernel,
-        out_shape=jax.ShapeDtypeStruct((kinds, tokens, width), grads.dtype),
-        in_specs=[IN_VMEM] * 3,
-        out_specs=IN_VMEM,
+        back_kernel,
+        out_shape=(shape((4, count, features), bf16), shape((3, tokens, width), bf16)),
+        in_specs=[IN_VMEM] * 10,
+        out_specs=(IN_VMEM,) * 2,
         scratch_shapes=[
-            pltpu.VMEM((kinds, tokens, width), jnp.float32),
-            pltpu.VMEM((kinds, tokens, width), grads.dtype),
-            pltpu.VMEM((kinds, tokens, width), grads.dtype),
+            pltpu.VMEM((tokens, width), bf16),
+            pltpu.VMEM(keys_values.shape, bf16),
+            pltpu.VMEM((2, tokens, width), f32),
+            pltpu.VMEM((2, tokens, width), bf16),
+            pltpu.VMEM((2, tokens, width), bf16),
         ]
-        + semaphores(8),
-        compiler_params=remote_params(collective_id),
-        name="return_keys",
-    )(grads, cosine, sine)
+        + semaphores(pieces)
+        + semaphores(pieces)
+        + semaphores(3),
+        compiler_params=remote_params(collective_id, 60),
+        name="back_attention",
+    )(rows, weights, valid, queries, keys_values, query_doc, key_doc, log_totals, cosine, sine)
 
 
 def reduce_kernel(flip, left, right, out, core_out, core_in, x_out, x_in, send_sems, recv_sems):
@@ -1554,32 +1632,6 @@
         compiler_params=remote_params(collective_id),
         name="product_to_owner",
     )(left, right)
-
-
-def tensor_kernel(rows, out, send_sems, recv_sems):
-    me = Peers()
-    copies = Copies(send_sems, recv_sems)
-    greet([me.x_peer, me.core_peer])
-    mine = out.at[me.quarter]
-    copies.send((OVER_X,), rows, mine, out.at[me.x_quarter], me.x_peer)
-    copies.send((OVER_CORE, 0), rows, mine, out.at[me.core_quarter], me.core_peer)
-    copies.local((LOCAL,), rows, mine)
-    copies.arrive(OVER_X)
-    beside = out.at[me.x_quarter]
-    copies.send((OVER_CORE, 1), beside, beside, out.at[me.far_quarter], me.core_peer)
-    copies.finish()
-
-
-def tensor_gather(rows, collective_id):
-    return pl.pallas_call(
-        tensor_kernel,
-        out_shape=jax.ShapeDtypeStruct((4,) + rows.shape, rows.dtype),
-        in_specs=[IN_VMEM],
-        out_specs=IN_PLACE,
-        scratch_shapes=semaphores(4),
-        compiler_params=remote_params(collective_id),
-        name="tensor_gather",
-    )(rows)
 
 
 def own_rows(block, tp_index, count):
@@ -1625,7 +1677,7 @@
     reach_back = min((WINDOW + tok_count - 2) // tok_count, ep_size - 1)
     local_experts = expert_in.shape[0]
     route_rows = jnp.concatenate(
-        [routes.T, jnp.zeros((-top_count % 8, tok_count), routes.dtype)]
+        [routes.T, jnp.full((-top_count % 8, tok_count), -1, routes.dtype)]
     )
     positions = ep_index * tok_count + jnp.arange(tok_count, dtype=jnp.int32)
     key_count = (reach_back + 1) * tok_count
@@ -1658,16 +1710,6 @@
     shared_slices = lax.all_to_all(
         after(shared_shards, queries), EP, split_axis=0, concat_axis=0, tiled=True
     )
-    shared_slices = jnp.transpose(shared_slices, (1, 2, 0, 3)).reshape(
-        3, slice_hidden, model_width
-    )
-    my_ids = ep_index * local_experts + jnp.arange(local_experts, dtype=jnp.int32)
-    taken = jnp.any(all_routes[:, None, :top_count] == my_ids[None, :, None, None], axis=2)
-    earlier_mask = jnp.tril(jnp.ones((tok_count, tok_count), bf16), -1)
-    rank = product(
-        taken.astype(bf16).reshape(-1, tok_count), earlier_mask, NT
-    ).astype(jnp.int32).reshape(taken.shape)
-    rank = jnp.where(taken & (rank < capacity), rank, NO_SLOT)
     heads_low, log_totals = attend(queries, keys_values, query_doc, key_doc, valid_rows)
     attention_sum = product_to_owner(heads_low[None], out_full[None], False, 2)
     input_rows = own_rows(layer_input, tp_index, own_count).astype(f32)
@@ -1698,28 +1740,17 @@
         gated,
         grad_shared_pre,
         scaled_hidden,
-        token_grad,
-        scale_grad,
+        scalar_part,
     ) = gather_feed(
         normed_low,
         cotangent.reshape(tp_size, own_count, model_width),
         scale_rows,
-        rank,
+        all_routes,
         jnp.swapaxes(expert_in, 2, 3).reshape(local_experts, -1, model_width),
         expert_down,
         shared_slices,
         capacity,
         3,
-    )
-    spare = jnp.zeros((ep_size, scale_count - expert_count - 1, tok_count), f32)
-    scalar_part = jnp.concatenate(
-        [jnp.zeros((ep_size, expert_count, tok_count), f32), scale_grad[:, None, :, 0], spare], axis=1
-    )
-    scalar_part = lax.dynamic_update_slice(
-        scalar_part, token_grad, (0, ep_index * local_experts, 0)
-    )
-    scalar_part = jnp.swapaxes(
-        scalar_part.reshape(ep_size, scale_count, tp_size, own_count), 1, 2
     )
     part_shape = (ep_size, tp_size, own_count, model_width)
     slot_count = ep_size * capacity
@@ -1740,9 +1771,6 @@
     grad_expert_in = jnp.swapaxes(grad_expert_in, 2, 3).astype(f32)
     grad_expert_down = grad_expert_down.astype(f32)
     layer_output = lax.all_gather((residual + ffn_sum).astype(bf16), TP, axis=0, tiled=True)
-    shared_grads = jnp.transpose(
-        shared_grads.reshape(3, slice_hidden, ep_size, shard_width), (2, 0, 1, 3)
-    )
     shared_grads = lax.all_to_all(shared_grads, EP, split_axis=0, concat_axis=0, tiled=True)
     shared_grads = (
         jnp.swapaxes(shared_grads, 0, 1).reshape(3, -1, shard_width).astype(f32)
@@ -1773,13 +1801,20 @@
     small = jnp.concatenate([grad_feedforward_gain[None], grad_shared_gate[None], grad_router.T])
     small = lax.psum(small, both)
     grad_residual = own_rows(cotangent, tp_index, own_count).astype(f32) + grad_mid_norm
-    grad_attention = tensor_gather(grad_residual.astype(bf16), 5).reshape(tok_count, model_width)
-    grad_heads = (product(grad_attention, out_full, NT) * valid_rows).astype(bf16)
-    grad_queries, grad_kv = attend_back(
-        queries, keys_values, query_doc, key_doc, log_totals, grad_heads, cosine, sine
-    )
-    grad_own_kv = return_keys(grad_kv, cosine, sine, 6)
-    grad_raw = jnp.concatenate([grad_queries[None], grad_own_kv])
+    grad_attention, grad_raw = back_attention(
+        grad_residual.astype(bf16),
+        out_full,
+        valid_rows,
+        queries,
+        keys_values,
+        query_doc,
+        key_doc,
+        log_totals,
+        cosine,
+        sine,
+        5,
+    )
+    grad_attention = grad_attention.reshape(tok_count, model_width)
     grad_attention_bias = jnp.sum(grad_raw.astype(f32), axis=1)
     grad_attention_in, grad_attention_out, tails, grad_input = finish(
         normed_attention,

time: 767 us -> 750 us (0.978)
  local copies, waits for them, and re-layouts: 40.7 us -> 24.1 us
  waiting for transfers between devices: 0.25 us -> 10.9 us
    all_to_all x1, waiting for transfers between devices: 0.21 us -> 10.8 us  [per_device_dense(): lax.all_to_all(after(shared_shards, queries), EP, split_axis=0, concat_ax...]
    reshape x5 -> x0, local copies, waits for them, and re-layouts: 8.37 us -> none  [the longest x1 3.24 us: per_device_dense(): jnp.transpose(shared_slices, (1, 2, 0, 3))]
    pallas_call x3 -> x1, Pallas kernels: 63.1 us -> 68.6 us  [back_attention(): pl.pallas_call(back_kernel, out_shape=(shape((4, count, features), bf16),...]
    unnamed x60 -> x66, local copies, waits for them, and re-layouts: 18.3 us -> 17.2 us
  transfers between devices with their start and end apart: 4 -> 4, of which waited for: 1 -> 1; matrix products, arithmetic and copies ran while one was open for 6% -> 4% of each run, Pallas kernels for 26% -> 27%
where the time goes in v5:
time: 750 us; the launch traced here: 744 us
  Pallas kernels  644 us (86%)
  other arithmetic  32.9 us (4%)
  local copies, waits for them, and re-layouts  24.1 us (3%)
  between operations  16.2 us (2%)
  waiting for transfers between devices  10.9 us (1%)
  starting transfers between devices  9.55 us (1%)
    pallas_call x1, Pallas kernels, gather_feed(): pl.pallas_call(gather_feed_kernel, out_shape=(shape((RING, 4, count, widt...  177 us
    pallas_call x1, Pallas kernels, scatter_rows(): pl.pallas_call(scatter_kernel, out_shape=(shape((count, width), f32), sha...  152 us
    pallas_call x1, Pallas kernels, open_attention(): pl.pallas_call(open_kernel, out_shape=(shape((kinds, RING, depth, width),...  117 us
    pallas_call x1, Pallas kernels, finish(): pl.pallas_call(finish_kernel, out_shape=(shape((kinds, depth, columns), f...  103 us
    pallas_call x1, Pallas kernels, back_attention(): pl.pallas_call(back_kernel, out_shape=(shape((4, count, features), bf16),...  68.6 us
    unnamed x66, local copies, waits for them, and re-layouts  17.2 us
    pallas_call x1, Pallas kernels, product_to_owner(): pl.pallas_call(functools.partial(reduce_kernel, flip), out_shape=jax.Shap...  17.1 us
  transfers between devices with their start and end apart: 4, of which 1 were waited for; matrix products, arithmetic and copies ran while one was open for 4% of the time, Pallas kernels for 27%

profile of v5, /device:TPU:0, one launch (start us, length us, event | category | flops | bytes accessed | tf_op | source)
XLA Modules:
  0.0 743.6 jit_solution(1041984019655713876)
XLA Ops:
  8.1 0.9 reduce-window.4
  9.5 0.7 bitcast_subtract_fusion
  10.2 0.7 pad_add_fusion
  11.1 1.7 copy.36
  12.8 1.0 fusion.21
  13.9 1.5 maximum_bitcast_fusion
  15.6 116.5 %open_attention.1 = (bf16[3,8,256,512]{3,2,1,0:T(8,128)(2,1)}, bf16[512,2048]{1,0:T(8,128)(2,1)S(1)}, s32[8,8,512]{2,1,0:T(8,128)S(1)}, bf16[512,2048]{1,0:T(8,1...) custom-call(bf16[3,256,512]{2,1,0:T(8,128)(2,1)S(1)} %copy-done.11, ...), custom_call_target="tpu_custom_call" | custom-call | tf_op jit(solution)/shard_map/open_attention/pallas_call | solution.py:1186
  132.2 1.3 copy-done.2
  134.1 5.1 all-to-all-start
  139.6 0.7 fusion.20.valid
  140.4 2.0 copy-done.1
  142.4 9.9 %attend.1 = (bf16[512,512]{1,0:T(8,128)(2,1)S(1)}, f32[4,512,1]{2,1,0:T(8,128)S(1)}) custom-call(bf16[512,512]{1,0:T(8,128)(2,1)S(1)} %get-tuple-element.45.queries, bf16[2,3,512,512]{3,2,1,0:T(8,128)(2,1)S(1)} %copy-done.1, bf16[2,3,512,512]{3,2,1,0:T(8,128)(2,1)S(1)} %copy-done.1, s32[512,1]{1,0:T(8,128)S(1)} %fusion.19.query_doc, ...), custom_call_target="tpu_custom_call" | custom-call | tf_op jit(solution)/shard_map/attend/pallas_call | solution.py:134
  152.3 1.0 copy-done.10
  153.3 17.1 %product_to_owner.1 = f32[128,2048]{1,0:T(8,128)S(1)} custom-call(bf16[1,512,512]{2,1,0:T(8,128)(2,1)S(1)} %bitcast.80, bf16[1,512,2048]{2,1,0:T(8,128)(2,1)S(1)} %bitcast.79), custom_call_target="tpu_custom_call" | custom-call | tf_op jit(solution)/shard_map/product_to_owner/pallas_call | solution.py:1620
  170.4 2.0 multiply_reduce_fusion.2
  172.4 1.0 fusion.34
  173.6 1.0 fusion.4
  174.6 0.7 maximum_maximum_fusion.scales
  175.3 1.0 fusion.8.rows
  176.2 10.8 %all-to-all-done.shared_blocks = bf16[8,3,176,256]{3,2,1,0:T(8,128)(2,1)} async-done(((bf16[8,3,176,256]{3,2,1,0:T(8,128)(2,1)}), bf16[8,3,176,256]{3,2,1,0:T(8,128)(2,1)}, u32[]{:S(2)}, u32[]{:S(2)}) %all-to-all-start) | async-done | bytes 2162720 | tf_op jit(solution)/shard_map/all_to_all | solution.py:1710
  187.1 177.3 %gather_feed.1 = (bf16[8,4,128,2048]{3,2,1,0:T(8,128)(2,1)}, bf16[8,4,128,2048]{3,2,1,0:T(8,128)(2,1)}, f32[8,4,24,128]{3,2,1,0:T(8,128)}, bf16[8,512,2048]{2,1,...) custom-call(bf16[128,2048]{1,0:T(8,128)(2,1)} %fusion.8.rows, ...), custom_call_target="tpu_custom_call" | custom-call | tf_op jit(solution)/shard_map/gather_feed/pallas_call | solution.py:621
  364.4 152.4 %scatter_rows.1 = (f32[128,2048]{1,0:T(8,128)}, f32[128,2048]{1,0:T(8,128)}, f32[24,128]{1,0:T(8,128)}, bf16[2,2,352,2048]{3,2,1,0:T(8,128)(2,1)}, bf16[2,352,20...) custom-call(bf16[8,4,128,2048]{3,2,1,0:T(8,128)(2,1)} %bitcast.86, bf16[8,4,128,2048]{3,2,1,0:T(8,128)(2,1)} %bitcast.85, ...), custom_call_target="tpu_custom_call" | custom-call | tf_op jit(solution)/shard_map/scatter_rows/pallas_call | solution.py:982
  516.8 0.8 fusion.28
  517.6 0.7 multiply_reduce_fusion.4
  518.3 0.7 multiply_reduce_fusion.3
  519.1 0.7 fusion.6
  519.8 1.4 fusion.5
  521.3 1.4 multiply_reduce_fusion
  522.7 4.4 all-to-all-start.1
  527.1 0.7 pad_maximum_fusion.2
  527.9 3.1 fusion.32
  531.0 68.6 %back_attention.1 = (bf16[4,128,2048]{2,1,0:T(8,128)(2,1)}, bf16[3,512,512]{2,1,0:T(8,128)(2,1)}) custom-call(bf16[128,2048]{1,0:T(8,128)(2,1)} %get-tuple-element.105.rows, bf16[512,2048]{1,0:T(8,128)(2,1)} %copy-done.2, f32[512,1]{1,0:T(8,128)} %copy-done.7, bf16[512,512]{1,0:T(8,128)(2,1)} %copy-done.9, ...), custom_call_target="tpu_custom_call" | custom-call | tf_op jit(solution)/shard_map/back_attention/pallas_call | solution.py:1563
  599.6 2.2 convert_reduce_fusion.tail
  601.8 102.5 %finish.1 = (f32[3,256,512]{2,1,0:T(8,128)}, f32[512,256]{1,0:T(8,128)}, f32[4,8,512]{2,1,0:T(8,128)}, bf16[4,128,2048]{2,1,0:T(8,128)(2,1)}) custom-call(bf16[512,2048]{1,0:T(8,128)(2,1)} %get-tuple-element.63.normed, bf16[3,512,512]{2,1,0:T(8,128)(2,1)} %get-tuple-element.67.grad_raw, bf16[512,512]{1,0:T(8,128)(2,1)} %copy-done.8, ...), custom_call_target="tpu_custom_call" | custom-call | tf_op jit(solution)/shard_map/finish/pallas_call | solution.py:1368
  704.4 0.9 slice_reduce_fusion
  705.9 3.3 convert_element_type.71
  709.2 1.3 dynamic-slice_bitcast_fusion
  710.5 8.7 %convert_bitcast_fusion = f32[2,2,2048,352]{2,3,1,0:T(8,128)} fusion(bf16[2,2,352,2048]{3,2,1,0:T(8,128)(2,1)} %get-tuple-element.75), kind=kLoop, calls=%fused_computation | loop fusion | flops 2883584 | bytes 17301504 | tf_op jit(solution)/shard_map/convert_element_type | solution.py:1771
  719.2 1.5 fusion.33
  720.7 1.6 slice_bitcast_fusion
  722.3 2.1 convert_bitcast_fusion.1
  724.4 1.2 slice.63
  726.1 2.2 copy.39
  728.3 3.3 copy.48
  731.6 1.3 copy.49
  732.9 0.8 copy-done.21
  733.8 1.1 copy.50
  735.2 0.8 copy.51
  (87 shorter events, 3.7 us)
Async XLA Ops:
  8.0 164.4 %copy-start = (f32[2048,16]{0,1:T(8,128)S(1)}, f32[2048,16]{0,1:T(8,128)}, u32[]{:S(2)}) copy-start(f32[2048,16]{0,1:T(8,128)} %param.24) | copy-start | bytes 393220
  8.0 4.8 copy-start.28
  8.0 5.8 copy-start.23
  13.8 1.8 copy-start.11
  13.9 1.8 copy-start.12
  13.9 1.8 copy-start.15
  13.9 1.8 copy-start.16
  15.6 118.6 %copy-start.4 = (f32[512,128]{1,0:T(8,128)}, f32[512,128]{1,0:T(8,128)S(1)}, u32[]{:S(2)}) copy-start(f32[512,128]{1,0:T(8,128)S(1)} %get-tuple-element.119.cosine) | copy-start | bytes 786436
  15.6 118.5 %copy-start.5 = (f32[512,128]{1,0:T(8,128)}, f32[512,128]{1,0:T(8,128)S(1)}, u32[]{:S(2)}) copy-start(f32[512,128]{1,0:T(8,128)S(1)} %get-tuple-element.120.sine) | copy-start | bytes 786436
  132.2 1.3 copy-start.2
  133.5 0.7 copy-start.13
  134.1 6.2 copy-start.9
  134.1 52.9 %all-to-all-start = ((bf16[8,3,176,256]{3,2,1,0:T(8,128)(2,1)}), bf16[8,3,176,256]{3,2,1,0:T(8,128)(2,1)}, u32[]{:S(2)}, u32[]{:S(2)}) async-start(bf16[8,3,176,256]{3,2,1,0:T(8,128)(2,1)} %maximum_bitcast_fusion), calls=%async_computation | async-start | bytes 4325376 | tf_op jit(solution)/shard_map/all_to_all | solution.py:1710
  140.3 12.0 %copy-start.7 = (f32[512,1]{1,0:T(8,128)}, f32[512,1]{1,0:T(8,128)S(1)}, u32[]{:S(2)}) copy-start(f32[512,1]{1,0:T(8,128)S(1)} %fusion.20.valid) | copy-start | bytes 6148
  140.3 12.0 %copy-start.14 = (s32[1,1536]{1,0:T(1,128)}, s32[1,1536]{1,0:T(1,128)S(1)}, u32[]{:S(2)}) copy-start(s32[1,1536]{1,0:T(1,128)S(1)} %compare_select_fusion.key_doc) | copy-start | bytes 18436
  140.4 12.0 %copy-start.6 = (s32[512,1]{1,0:T(8,128)}, s32[512,1]{1,0:T(8,128)S(1)}, u32[]{:S(2)}) copy-start(s32[512,1]{1,0:T(8,128)S(1)} %fusion.19.query_doc) | copy-start | bytes 6148
  140.4 2.0 copy-start.1
  142.4 10.9 %copy-start.3 = (bf16[512,2048]{1,0:T(8,128)(2,1)S(1)}, bf16[512,2048]{1,0:T(8,128)(2,1)}, u32[]{:S(2)}) copy-start(bf16[512,2048]{1,0:T(8,128)(2,1)} %copy-done.2) | copy-start | bytes 6291460
  152.3 1.0 copy-start.10
  153.3 19.1 %copy-start.8 = (bf16[512,512]{1,0:T(8,128)(2,1)}, bf16[512,512]{1,0:T(8,128)(2,1)S(1)}, u32[]{:S(2)}) copy-start(bf16[512,512]{1,0:T(8,128)(2,1)S(1)} %get-tuple-element.47.heads) | copy-start | bytes 1572868
  170.4 2.0 copy-start.25
  170.4 3.1 copy-start.27
  172.4 2.9 copy-start.17
  364.4 154.7 %copy-start.18 = (f32[128,2048]{1,0:T(8,128)S(1)}, f32[128,2048]{1,0:T(8,128)}, u32[]{:S(2)}) copy-start(f32[128,2048]{1,0:T(8,128)} %copy-done.17) | copy-start | bytes 3145732
  516.8 4.4 copy-start.22
  516.8 4.4 copy-start.26
  522.7 199.6 %all-to-all-start.1 = ((bf16[8,3,176,256]{3,2,1,0:T(8,128)(2,1)}), bf16[8,3,176,256]{3,2,1,0:T(8,128)(2,1)}, u32[]{:S(2)}, u32[]{:S(2)}) async-start(bf16[8,3,176,256]{3,2,1,0:T(8,128)(2,1)} %get-tuple-element.74), calls=%async_computation.1 | async-start | bytes 4325376 | tf_op jit(solution)/shard_map/all_to_all | solution.py:1774
  527.1 192.1 %all-reduce.3.cloned.1.call-start = ((), (), s32[]{:S(2)}) async-start(), calls=%async_computation.3 | async-start | bytes 393216 | tf_op jit(solution)/shard_map/psum | solution.py:1802
  527.9 194.4 %all-gather.2.cloned.1.call-start = ((), (), s32[]{:S(2)}) async-start(), calls=%async_computation.2 | async-start | bytes 2621440 | tf_op jit(solution)/shard_map/all_gather | solution.py:1773
  601.8 104.0 %copy-start.19 = (bf16[2,352,2048]{2,1,0:T(8,128)(2,1)S(1)}, bf16[2,352,2048]{2,1,0:T(8,128)(2,1)}, u32[]{:S(2)}) copy-start(bf16[2,352,2048]{2,1,0:T(8,128)(2,1)} %get-tuple-element.76) | copy-start | bytes 8650756
  728.3 3.3 copy-start.20
  731.6 2.2 copy-start.21
  733.8 1.4 copy-start.24
Sparse Core Ops, SparseCore 0:
  533.5 143.7 all-reduce.2
Sparse Core Ops, SparseCore 1:
  531.1 30.5 all-gather.1

commit v6 on v5

--- a/solution.py
+++ b/solution.py
@@ -354,9 +354,12 @@
     copies = LateCopies(send_sems, recv_sems)
     count = rows.shape[0]
     half, part = count // 2, count // 4
+    first_rows = (half, half - count // 8)
     q, qx, qc, qd = me.quarter, me.x_quarter, me.core_quarter, me.far_quarter
     blocks = {step: me.block(step) for step in range(-4, 5)}
-    low, high, whole = pl.ds(0, half), pl.ds(half, half), pl.ds(0, count)
+    low = [pl.ds(0, rows_low) for rows_low in first_rows]
+    high = [pl.ds(rows_low, count - rows_low) for rows_low in first_rows]
+    whole = pl.ds(0, count)
     own, other, scale = range(3)
     full = (all_rows, all_cotangent)
     sides = ((RIGHT, me.right, -1, 0), (LEFT, me.left, 1, 1))
@@ -371,11 +374,11 @@
 
         copies.send((kind,) + key, source or cell, cell, landing, peer)
 
-    push((OVER_X, other, 0), 0, 0, q, low, me.x_peer, 0, qx, lambda: rows.at[low])
+    push((OVER_X, other, 0), 0, 0, q, low[0], me.x_peer, 0, qx, lambda: rows.at[low[0]])
     for side, peer, sign, keep in sides:
         push((side, own, 1), 1, 0, q, whole, peer, sign, q, lambda: cotangent.at[q])
-        push((side, other, 1), 1, 0, qx, low, peer, sign, qx, lambda: cotangent.at[qx, low])
-    push((OVER_X, own, 0), 0, 0, q, high, me.x_peer, 0, qx, lambda: rows.at[high])
+        push((side, other, 1), 1, 0, qx, low[1], peer, sign, qx, lambda: cotangent.at[qx, low[1]])
+    push((OVER_X, own, 0), 0, 0, q, high[0], me.x_peer, 0, qx, lambda: rows.at[high[0]])
     push((OVER_CORE, own, 0), 0, 0, q, whole, me.core_peer, 0, qc, lambda: rows)
     for side, peer, sign, keep in sides:
         push((side, own, 1), 0, 0, q, whole, peer, sign, q, lambda: rows)
@@ -421,7 +424,7 @@
     scalars[...] = jnp.zeros_like(scalars)
     copies.arrive(0, OVER_X, other, 0)
     for side, peer, sign, keep in sides:
-        push((side, other, 1), 0, 0, qx, low, peer, sign, qx)
+        push((side, other, 1), 0, 0, qx, low[0], peer, sign, qx)
     for way in (OVER_X, OVER_CORE, OVER_FAR):
         copies.arrive(way, scale, 0)
     copies.arrive(LOCAL, scale)
@@ -446,25 +449,26 @@
                 copies.arrive(kind, side, own, hop)
                 which = whole if hop < 3 else pl.ds(keep * half, half)
                 push((side, own, hop + 1), kind, step, q, which, peer, step + sign, q)
-                push((OVER_X, own, step), kind, step, q, high, me.x_peer, step, qx)
+                push((OVER_X, own, step), kind, step, q, high[kind], me.x_peer, step, qx)
                 push((OVER_CORE, own, step), kind, step, q, whole, me.core_peer, step, qc)
                 copies.arrive(kind, side, other, hop)
-                which = low if hop < 3 else pl.ds(keep * part, part)
+                last = pl.ds(part, first_rows[kind] - part) if keep else pl.ds(0, part)
+                which = low[kind] if hop < 3 else last
                 push((side, other, hop + 1), kind, step, qx, which, peer, step + sign, qx)
-                push((OVER_CORE, other, step), kind, step, qx, low, me.core_peer, step, qd)
+                push((OVER_CORE, other, step), kind, step, qx, low[kind], me.core_peer, step, qd)
         if hop == 4:
             copies.arrive(kind, LEFT, own, 4)
-            push((OVER_X, own, 4), kind, 4, q, high, me.x_peer, 4, qx)
             copies.arrive(kind, RIGHT, own, 4)
+            push((OVER_X, own, 4), kind, 4, q, high[kind], me.x_peer, 4, qx)
             push((OVER_CORE, own, 4), kind, 4, q, whole, me.core_peer, 4, qc)
             copies.arrive(kind, LEFT, other, 4)
             copies.arrive(kind, RIGHT, other, 4)
-            push((OVER_CORE, other, 4), kind, 4, qx, low, me.core_peer, 4, qd)
+            push((OVER_CORE, other, 4), kind, 4, qx, low[kind], me.core_peer, 4, qd)
 
     def over_x(kind, steps):
         for step in steps:
             copies.arrive(kind, OVER_X, own, step)
-            push((OVER_CORE, scale, step), kind, step, qx, high, me.core_peer, step, qd)
+            push((OVER_CORE, scale, step), kind, step, qx, high[kind], me.core_peer, step, qd)
 
     def scales_in(hop):
         for side, peer, sign, keep in sides:
@@ -1018,8 +1022,8 @@
 
 
 def open_kernel(
-    shard_in, shard_out, routes, rows, gain, bias, cosine, sine,
-    full_in, full_out, full_routes, normed, queries, keys_values,
+    shard_in, shard_out, routes, rows, gain, bias, cosine, sine, shared_in, shared_down,
+    full_in, full_out, full_routes, normed, queries, keys_values, shared_shards,
     sums, share_send, share_recv, send_sems, recv_sems,
 ):
     me = Peers()
@@ -1104,6 +1108,11 @@
     for kind in range(kinds):
         if kind:
             multiply(kind, 0)
+    places, _, slice_hidden, across = shared_shards.shape
+    for index in range(2):
+        turned_shard = jnp.swapaxes(shared_in[index].astype(f32), 0, 1).astype(bf16)
+        shared_shards[:, index] = turned_shard.reshape(places, slice_hidden, across)
+    shared_shards[:, 2] = shared_down[...].reshape(places, slice_hidden, across)
     go_round(first)
     for index in range(2):
         for head, part in heads_of(index + 1, index == 0):
@@ -1177,7 +1186,9 @@
     copies.finish()
 
 
-def open_attention(shard_in, shard_out, routes, rows, gain, bias, cosine, sine, collective_id):
+def open_attention(
+    shard_in, shard_out, routes, rows, gain, bias, cosine, sine, shared_in, shared_down, collective_id
+):
     kinds, depth, width = shard_in.shape
     out_rows, columns = shard_out.shape
     tokens, features = rows.shape
@@ -1192,15 +1203,16 @@
             shape((tokens, features), bf16),
             shape((tokens, width), bf16),
             shape((2, 3, tokens, width), bf16),
+            shape((RING, 3, shared_in.shape[2] // RING, shared_in.shape[1]), bf16),
         ),
-        in_specs=[IN_VMEM] * 8,
-        out_specs=(IN_VMEM,) * 6,
+        in_specs=[IN_VMEM] * 10,
+        out_specs=(IN_VMEM,) * 7,
         scratch_shapes=[pltpu.VMEM((kinds, tokens, width), jnp.float32)]
         + semaphores(8)
         + semaphores(8 * (kinds + 2)),
         compiler_params=remote_params(collective_id),
         name="open_attention",
-    )(shard_in, shard_out, routes, rows, gain[None], bias, cosine, sine)
+    )(shard_in, shard_out, routes, rows, gain[None], bias, cosine, sine, shared_in, shared_down)
 
 
 def finish_kernel(
@@ -1638,10 +1650,6 @@
     return lax.dynamic_slice_in_dim(block, tp_index * count, count, 0)
 
 
-def after(value, earlier):
-    return lax.optimization_barrier((value, earlier))[0]
-
-
 def per_device_dense(
     layer_input,
     attention_gain,
@@ -1689,7 +1697,15 @@
     cosine, sine = (part[:, 0] for part in rope_angles(rope_pos, HD))
     cosine = jnp.concatenate([cosine, cosine], axis=1)
     sine = jnp.concatenate([-sine, sine], axis=1)
-    in_blocks, out_full, all_routes, normed_attention, queries, keys_values = open_attention(
+    (
+        in_blocks,
+        out_full,
+        all_routes,
+        normed_attention,
+        queries,
+        keys_values,
+        shared_shards,
+    ) = open_attention(
         attention_in,
         attention_out,
         route_rows,
@@ -1698,18 +1714,14 @@
         attention_bias,
         cosine,
         sine,
+        shared_in,
+        shared_down,
         0,
     )
     in_full = in_blocks.reshape(3, model_width, -1)
     shard_width = shared_in.shape[1]
     slice_hidden = shared_in.shape[2] // ep_size
-    shared_shards = jnp.concatenate([jnp.swapaxes(shared_in, 1, 2), shared_down[None]])
-    shared_shards = jnp.swapaxes(
-        shared_shards.reshape(3, ep_size, slice_hidden, shard_width), 0, 1
-    )
-    shared_slices = lax.all_to_all(
-        after(shared_shards, queries), EP, split_axis=0, concat_axis=0, tiled=True
-    )
+    shared_slices = lax.all_to_all(shared_shards, EP, split_axis=0, concat_axis=0, tiled=True)
     heads_low, log_totals = attend(queries, keys_values, query_doc, key_doc, valid_rows)
     attention_sum = product_to_owner(heads_low[None], out_full[None], False, 2)
     input_rows = own_rows(layer_input, tp_index, own_count).astype(f32)

time: 750 us -> 749 us (level)
    unnamed x66 -> x61, local copies, waits for them, and re-layouts: 17.2 us -> 18 us
where the time goes in v6:
time: 749 us; the launch traced here: 742 us
  Pallas kernels  642 us (86%)
  other arithmetic  31.5 us (4%)
  local copies, waits for them, and re-layouts  26.3 us (4%)
  between operations  16.1 us (2%)
  waiting for transfers between devices  10.2 us (1%)
  starting transfers between devices  9.54 us (1%)
    pallas_call x1, Pallas kernels, gather_feed(): pl.pallas_call(gather_feed_kernel, out_shape=(shape((RING, 4, count, widt...  173 us
    pallas_call x1, Pallas kernels, scatter_rows(): pl.pallas_call(scatter_kernel, out_shape=(shape((count, width), f32), sha...  152 us
    pallas_call x1, Pallas kernels, open_attention(): pl.pallas_call(open_kernel, out_shape=(shape((kinds, RING, depth, width),...  118 us
    pallas_call x1, Pallas kernels, finish(): pl.pallas_call(finish_kernel, out_shape=(shape((kinds, depth, columns), f...  103 us
    pallas_call x1, Pallas kernels, back_attention(): pl.pallas_call(back_kernel, out_shape=(shape((4, count, features), bf16),...  69.1 us
    unnamed x61, local copies, waits for them, and re-layouts  18 us
    pallas_call x1, Pallas kernels, product_to_owner(): pl.pallas_call(functools.partial(reduce_kernel, flip), out_shape=jax.Shap...  17.1 us
  transfers between devices with their start and end apart: 4, of which 1 were waited for; matrix products, arithmetic and copies ran while one was open for 4% of the time, Pallas kernels for 27%

profile of v6, /device:TPU:0, one launch (start us, length us, event | category | flops | bytes accessed | tf_op | source)
XLA Modules:
  0.0 742.1 jit_solution(13114675309705164458)
XLA Ops:
  8.0 0.9 reduce-window.4
  10.3 0.7 pad_add_fusion
  11.2 0.7 concatenate.18.routes
  11.9 1.0 fusion.21
  13.1 1.3 copy-done.11
  14.4 1.1 copy-done.12
  15.5 0.9 copy-done.13
  17.2 0.7 copy-done.17
  17.9 117.7 %open_attention.1 = (bf16[3,8,256,512]{3,2,1,0:T(8,128)(2,1)}, bf16[512,2048]{1,0:T(8,128)(2,1)}, s32[8,8,512]{2,1,0:T(8,128)S(1)}, bf16[512,2048]{1,0:T(8,128)(...) custom-call(bf16[3,256,512]{2,1,0:T(8,128)(2,1)S(1)} %copy-done.11, ...), custom_call_target="tpu_custom_call" | custom-call | tf_op jit(solution)/shard_map/open_attention/pallas_call | solution.py:1197
  135.6 5.1 all-to-all-start
  141.9 2.0 copy-done.1
  143.8 9.9 %attend.1 = (bf16[512,512]{1,0:T(8,128)(2,1)S(1)}, f32[4,512,1]{2,1,0:T(8,128)S(1)}) custom-call(bf16[512,512]{1,0:T(8,128)(2,1)S(1)} %get-tuple-element.45.queries, bf16[2,3,512,512]{3,2,1,0:T(8,128)(2,1)S(1)} %copy-done.1, bf16[2,3,512,512]{3,2,1,0:T(8,128)(2,1)S(1)} %copy-done.1, s32[512,1]{1,0:T(8,128)S(1)} %fusion.19.query_doc, ...), custom_call_target="tpu_custom_call" | custom-call | tf_op jit(solution)/shard_map/attend/pallas_call | solution.py:134
  153.8 1.0 copy-done.10
  154.8 17.1 %product_to_owner.1 = f32[128,2048]{1,0:T(8,128)S(1)} custom-call(bf16[1,512,512]{2,1,0:T(8,128)(2,1)S(1)} %bitcast.74, bf16[1,512,2048]{2,1,0:T(8,128)(2,1)S(1)} %bitcast.73), custom_call_target="tpu_custom_call" | custom-call | tf_op jit(solution)/shard_map/product_to_owner/pallas_call | solution.py:1632
  172.6 2.0 multiply_reduce_fusion.2
  174.6 1.0 fusion.34
  175.7 1.0 fusion.4
  176.7 0.7 maximum_maximum_fusion.scales
  177.4 1.0 fusion.8.rows
  178.3 10.2 %all-to-all-done.shared_blocks = bf16[8,3,176,256]{3,2,1,0:T(8,128)(2,1)} async-done(((bf16[8,3,176,256]{3,2,1,0:T(8,128)(2,1)}), bf16[8,3,176,256]{3,2,1,0:T(8,128)(2,1)}, u32[]{:S(2)}, u32[]{:S(2)}) %all-to-all-start) | async-done | bytes 2162720 | tf_op jit(solution)/shard_map/all_to_all | solution.py:1724
  188.5 173.4 %gather_feed.1 = (bf16[8,4,128,2048]{3,2,1,0:T(8,128)(2,1)}, bf16[8,4,128,2048]{3,2,1,0:T(8,128)(2,1)}, f32[8,4,24,128]{3,2,1,0:T(8,128)}, bf16[8,512,2048]{2,1,...) custom-call(bf16[128,2048]{1,0:T(8,128)(2,1)} %fusion.8.rows, ...), custom_call_target="tpu_custom_call" | custom-call | tf_op jit(solution)/shard_map/gather_feed/pallas_call | solution.py:625
  361.9 152.2 %scatter_rows.1 = (f32[128,2048]{1,0:T(8,128)}, f32[128,2048]{1,0:T(8,128)}, f32[24,128]{1,0:T(8,128)}, bf16[2,2,352,2048]{3,2,1,0:T(8,128)(2,1)}, bf16[2,352,20...) custom-call(bf16[8,4,128,2048]{3,2,1,0:T(8,128)(2,1)} %bitcast.80, bf16[8,4,128,2048]{3,2,1,0:T(8,128)(2,1)} %bitcast.79, ...), custom_call_target="tpu_custom_call" | custom-call | tf_op jit(solution)/shard_map/scatter_rows/pallas_call | solution.py:986
  514.1 0.8 fusion.28
  514.9 0.7 multiply_reduce_fusion.4
  515.6 0.7 multiply_reduce_fusion.3
  516.3 0.7 fusion.6
  517.1 1.4 fusion.5
  518.5 2.1 multiply_reduce_fusion
  520.6 4.4 all-to-all-start.1
  525.0 0.7 pad_maximum_fusion.2
  525.8 3.1 fusion.32
  528.9 69.1 %back_attention.1 = (bf16[4,128,2048]{2,1,0:T(8,128)(2,1)}, bf16[3,512,512]{2,1,0:T(8,128)(2,1)}) custom-call(bf16[128,2048]{1,0:T(8,128)(2,1)} %get-tuple-element.105.rows, bf16[512,2048]{1,0:T(8,128)(2,1)} %get-tuple-element.48.weights, f32[512,1]{1,0:T(8,128)} %copy-done.6, bf16[512,512]{1,0:T(8,128)(2,1)} %copy-done.8, ...), custom_call_target="tpu_custom_call" | custom-call | tf_op jit(solution)/shard_map/back_attention/pallas_call | solution.py:1575
  598.1 2.2 convert_reduce_fusion.tail
  600.3 102.8 %finish.1 = (f32[3,256,512]{2,1,0:T(8,128)}, f32[512,256]{1,0:T(8,128)}, f32[4,8,512]{2,1,0:T(8,128)}, bf16[4,128,2048]{2,1,0:T(8,128)(2,1)}) custom-call(bf16[512,2048]{1,0:T(8,128)(2,1)} %get-tuple-element.63.normed, bf16[3,512,512]{2,1,0:T(8,128)(2,1)} %get-tuple-element.67.grad_raw, bf16[512,512]{1,0:T(8,128)(2,1)} %copy-done.7, ...), custom_call_target="tpu_custom_call" | custom-call | tf_op jit(solution)/shard_map/finish/pallas_call | solution.py:1380
  703.1 0.9 slice_reduce_fusion
  704.6 3.3 convert_element_type.71
  707.9 1.3 dynamic-slice_bitcast_fusion
  709.2 8.7 %convert_bitcast_fusion = f32[2,2,2048,352]{2,3,1,0:T(8,128)} fusion(bf16[2,2,352,2048]{3,2,1,0:T(8,128)(2,1)} %get-tuple-element.75), kind=kLoop, calls=%fused_computation | loop fusion | flops 2883584 | bytes 17301504 | tf_op jit(solution)/shard_map/convert_element_type | solution.py:1783
  717.9 1.5 fusion.33
  719.4 1.6 slice_bitcast_fusion
  721.0 2.1 convert_bitcast_fusion.1
  723.1 1.2 slice.63
  724.8 2.2 copy.35
  727.0 3.3 copy.42
  730.3 1.3 copy.43
  731.6 0.8 copy-done.22
  732.5 1.1 copy.44
  733.6 0.8 copy.45
  (81 shorter events, 5.4 us)
Async XLA Ops:
  8.0 166.5 %copy-start = (f32[2048,16]{0,1:T(8,128)S(1)}, f32[2048,16]{0,1:T(8,128)}, u32[]{:S(2)}) copy-start(f32[2048,16]{0,1:T(8,128)} %param.24) | copy-start | bytes 393220
  8.0 5.1 copy-start.9
  13.1 122.5 %copy-start.3 = (f32[512,128]{1,0:T(8,128)}, f32[512,128]{1,0:T(8,128)S(1)}, u32[]{:S(2)}) copy-start(f32[512,128]{1,0:T(8,128)S(1)} %get-tuple-element.119.cosine) | copy-start | bytes 786436
  13.1 122.5 %copy-start.4 = (f32[512,128]{1,0:T(8,128)}, f32[512,128]{1,0:T(8,128)S(1)}, u32[]{:S(2)}) copy-start(f32[512,128]{1,0:T(8,128)S(1)} %get-tuple-element.120.sine) | copy-start | bytes 786436
  13.1 1.3 copy-start.11
  14.4 1.1 copy-start.12
  15.5 0.9 copy-start.13
  16.5 0.7 copy-start.16
  17.2 0.7 copy-start.17
  135.6 6.3 copy-start.14
  135.6 18.2 %copy-start.8 = (bf16[512,512]{1,0:T(8,128)(2,1)}, bf16[512,512]{1,0:T(8,128)(2,1)S(1)}, u32[]{:S(2)}) copy-start(bf16[512,512]{1,0:T(8,128)(2,1)S(1)} %get-tuple-element.45.queries) | copy-start | bytes 1572868
  135.6 52.9 %all-to-all-start = ((bf16[8,3,176,256]{3,2,1,0:T(8,128)(2,1)}), bf16[8,3,176,256]{3,2,1,0:T(8,128)(2,1)}, u32[]{:S(2)}, u32[]{:S(2)}) async-start(bf16[8,3,176,256]{3,2,1,0:T(8,128)(2,1)} %get-tuple-element.50), calls=%async_computation | async-start | bytes 4325376 | tf_op jit(solution)/shard_map/all_to_all | solution.py:1724
  141.7 12.0 %copy-start.6 = (f32[512,1]{1,0:T(8,128)}, f32[512,1]{1,0:T(8,128)S(1)}, u32[]{:S(2)}) copy-start(f32[512,1]{1,0:T(8,128)S(1)} %fusion.20.valid) | copy-start | bytes 6148
  141.8 12.0 %copy-start.15 = (s32[1,1536]{1,0:T(1,128)}, s32[1,1536]{1,0:T(1,128)S(1)}, u32[]{:S(2)}) copy-start(s32[1,1536]{1,0:T(1,128)S(1)} %compare_select_fusion.key_doc) | copy-start | bytes 18436
  141.8 12.0 %copy-start.5 = (s32[512,1]{1,0:T(8,128)}, s32[512,1]{1,0:T(8,128)S(1)}, u32[]{:S(2)}) copy-start(s32[512,1]{1,0:T(8,128)S(1)} %fusion.19.query_doc) | copy-start | bytes 6148
  141.8 2.0 copy-start.1
  143.8 10.9 %copy-start.2 = (bf16[512,2048]{1,0:T(8,128)(2,1)S(1)}, bf16[512,2048]{1,0:T(8,128)(2,1)}, u32[]{:S(2)}) copy-start(bf16[512,2048]{1,0:T(8,128)(2,1)} %get-tuple-element.48.weights) | copy-start | bytes 6291460
  153.8 1.0 copy-start.10
  154.8 19.8 %copy-start.7 = (bf16[512,512]{1,0:T(8,128)(2,1)}, bf16[512,512]{1,0:T(8,128)(2,1)S(1)}, u32[]{:S(2)}) copy-start(bf16[512,512]{1,0:T(8,128)(2,1)S(1)} %get-tuple-element.47.heads) | copy-start | bytes 1572868
  154.8 19.8 %copy-start.25 = (f32[2048]{0:T(1024)S(1)}, f32[2048]{0:T(1024)}, u32[]{:S(2)}) copy-start(f32[2048]{0:T(1024)} %param.20) | copy-start | bytes 24580
  171.9 3.8 copy-start.26
  174.5 2.9 copy-start.18
  361.9 154.4 %copy-start.19 = (f32[128,2048]{1,0:T(8,128)S(1)}, f32[128,2048]{1,0:T(8,128)}, u32[]{:S(2)}) copy-start(f32[128,2048]{1,0:T(8,128)} %copy-done.18) | copy-start | bytes 3145732
  514.1 4.4 copy-start.23
  520.6 200.4 %all-to-all-start.1 = ((bf16[8,3,176,256]{3,2,1,0:T(8,128)(2,1)}), bf16[8,3,176,256]{3,2,1,0:T(8,128)(2,1)}, u32[]{:S(2)}, u32[]{:S(2)}) async-start(bf16[8,3,176,256]{3,2,1,0:T(8,128)(2,1)} %get-tuple-element.74), calls=%async_computation.1 | async-start | bytes 4325376 | tf_op jit(solution)/shard_map/all_to_all | solution.py:1786
  525.0 192.9 %all-reduce.3.cloned.1.call-start = ((), (), s32[]{:S(2)}) async-start(), calls=%async_computation.3 | async-start | bytes 393216 | tf_op jit(solution)/shard_map/psum | solution.py:1814
  525.8 195.2 %all-gather.2.cloned.1.call-start = ((), (), s32[]{:S(2)}) async-start(), calls=%async_computation.2 | async-start | bytes 2621440 | tf_op jit(solution)/shard_map/all_gather | solution.py:1785
  600.3 104.3 %copy-start.20 = (bf16[2,352,2048]{2,1,0:T(8,128)(2,1)S(1)}, bf16[2,352,2048]{2,1,0:T(8,128)(2,1)}, u32[]{:S(2)}) copy-start(bf16[2,352,2048]{2,1,0:T(8,128)(2,1)} %get-tuple-element.76) | copy-start | bytes 8650756
  727.0 3.3 copy-start.21
  730.3 2.2 copy-start.22
  730.3 3.3 copy-start.24
Sparse Core Ops, SparseCore 0:
  531.4 144.4 all-reduce.2
Sparse Core Ops, SparseCore 1:
  529.0 31.4 all-gather.1

commit v7 on v6

--- a/solution.py
+++ b/solution.py
@@ -777,7 +777,7 @@
 def scatter_kernel(
     back_part, ffn_part, scalars, slot_rows, slot_cotangent, grad_pre, gated,
     all_rows, all_cotangent, grad_shared_pre, scaled,
-    back_sum, ffn_sum, out_scalars, grad_expert_in, grad_expert_down, grad_shared,
+    back_sum, ffn_sum, out_scalars, grad_experts, grad_shared,
     held, core_in, x_in, ring_q, ring_x, last_in,
     s_held, s_core, s_x, s_ring,
     job_left, job_short, job_right, job_sums, job_low, job_sems, job_out_sems,
@@ -905,9 +905,9 @@
     for expert in range(experts):
         for index in range(2):
             jobs.append(
-                (grad_pre.at[index, expert], slot_rows.at[expert], grad_expert_in.at[expert, index])
+                (grad_pre.at[index, expert], slot_rows.at[expert], grad_experts.at[expert, index])
             )
-        jobs.append((gated.at[expert], slot_cotangent.at[expert], grad_expert_down.at[expert]))
+        jobs.append((gated.at[expert], slot_cotangent.at[expert], grad_experts.at[expert, 2]))
     for index in range(2):
         jobs.append((grad_shared_pre.at[index], all_rows, grad_shared.at[:, index]))
     jobs.append((scaled, all_cotangent, grad_shared.at[:, 2]))
@@ -989,12 +989,11 @@
             shape((count, width), f32),
             shape((count, width), f32),
             shape(s_shape, f32),
-            shape((experts, 2, hidden, width), dtype),
-            shape((experts, hidden, width), dtype),
+            shape((experts, 3, hidden, width), dtype),
             shape((RING, 3, shared_hidden, width // RING), dtype),
         ),
         in_specs=[IN_PLACE] * 11,
-        out_specs=(IN_VMEM,) * 3 + (IN_PLACE,) * 3,
+        out_specs=(IN_VMEM,) * 3 + (IN_PLACE,) * 2,
         scratch_shapes=[
             pltpu.VMEM((2, RING, 2, count, width), dtype),
             pltpu.VMEM((RING, 2, count, width), dtype),
@@ -1405,6 +1404,60 @@
         compiler_params=remote_params(collective_id, 60),
         name="finish",
     )(normed, grad_raw, heads, grad_attention, weights, gain[None], rows, grad_residual, bias)
+
+
+def widen_kernel(
+    experts, shared, rows, expert_in, expert_down, shared_in, shared_down, rows_out
+):
+    f32 = jnp.float32
+    expert_in[...] = experts[:, :2].astype(f32)
+    expert_down[...] = experts[:, 2].astype(f32)
+    rows_out[...] = rows[0]
+
+    @pl.when(pl.program_id(0) == 0)
+    def _():
+        places, _, hidden, across = shared.shape
+        for index in range(2):
+            slices = shared[:, index].astype(f32).reshape(places * hidden, across)
+            shared_in[index] = jnp.swapaxes(slices, 0, 1)
+        shared_down[...] = shared[:, 2].astype(f32).reshape(places * hidden, across)
+
+
+def widen(experts, shared, rows):
+    count, _, hidden, width = experts.shape
+    places, _, slice_hidden, across = shared.shape
+    quarters, own, _ = rows.shape
+    parts = places // count
+    columns = width // parts
+    step = quarters * own // places
+    f32 = jnp.float32
+    shape = jax.ShapeDtypeStruct
+    shared_hidden = places * slice_hidden
+    return pl.pallas_call(
+        widen_kernel,
+        grid=(places,),
+        in_specs=[
+            pl.BlockSpec((1, 3, hidden, columns), lambda i: (i // parts, 0, 0, i % parts)),
+            pl.BlockSpec(shared.shape, lambda i: (0, 0, 0, 0)),
+            pl.BlockSpec((1, step, width), lambda i: (i * step // own, i % (own // step), 0)),
+        ],
+        out_specs=(
+            pl.BlockSpec((1, 2, hidden, columns), lambda i: (i // parts, 0, 0, i % parts)),
+            pl.BlockSpec((1, hidden, columns), lambda i: (i // parts, 0, i % parts)),
+            pl.BlockSpec((2, across, shared_hidden), lambda i: (0, 0, 0)),
+            pl.BlockSpec((shared_hidden, across), lambda i: (0, 0)),
+            pl.BlockSpec((step, width), lambda i: (i, 0)),
+        ),
+        out_shape=(
+            shape((count, 2, hidden, width), f32),
+            shape((count, hidden, width), f32),
+            shape((2, across, shared_hidden), f32),
+            shape((shared_hidden, across), f32),
+            shape((quarters * own, width), rows.dtype),
+        ),
+        compiler_params=pltpu.CompilerParams(vmem_limit_bytes=60 * 2**20),
+        name="widen",
+    )(experts, shared, rows)
 
 
 def greet_along_z(me, others=()):
@@ -1776,20 +1829,12 @@
         grad_shared_pre.reshape(2, all_count, slice_hidden),
         scaled_hidden.reshape(all_count, slice_hidden),
     )
-    back_sum, ffn_sum, scalar_sum, grad_expert_in, grad_expert_down, shared_grads = scatter_rows(
+    back_sum, ffn_sum, scalar_sum, grad_experts, shared_grads = scatter_rows(
         back_part.reshape(part_shape), ffn_part.reshape(part_shape), scalar_part, fed, 4
     )
     scalar_sum = scalar_sum.T
-    grad_expert_in = jnp.swapaxes(grad_expert_in, 2, 3).astype(f32)
-    grad_expert_down = grad_expert_down.astype(f32)
     layer_output = lax.all_gather((residual + ffn_sum).astype(bf16), TP, axis=0, tiled=True)
     shared_grads = lax.all_to_all(shared_grads, EP, split_axis=0, concat_axis=0, tiled=True)
-    shared_grads = (
-        jnp.swapaxes(shared_grads, 0, 1).reshape(3, -1, shard_width).astype(f32)
-    )
-    grad_shared_in = jnp.swapaxes(shared_grads[:2], 1, 2)
-    grad_shared_down = shared_grads[2]
-
     grad_gates = scalar_sum[:, :expert_count]
     grad_probs = jnp.where(
         picked,
@@ -1842,9 +1887,12 @@
     )
     grad_attention_bias = lax.dynamic_index_in_dim(tails, tp_index, 0, keepdims=False)[:3]
     grad_attention_gain = jnp.sum(tails[:, 3:], axis=0)[: model_width // tails.shape[2]].reshape(-1)
+    grad_expert_in, grad_expert_down, grad_shared_in, grad_shared_down, grad_input = widen(
+        grad_experts, shared_grads, grad_input
+    )
     return (
         layer_output,
-        grad_input.reshape(tok_count, model_width),
+        grad_input,
         grad_attention_gain,
         grad_attention_in,
         grad_attention_bias,
@@ -1854,7 +1902,7 @@
         grad_shared_down,
         small[1],
         small[2:].T,
-        grad_expert_in,
+        jnp.swapaxes(grad_expert_in, 2, 3),
         grad_expert_down,
     )
 

time: 749 us -> 740 us (0.988)
  Pallas kernels: 642 us -> 656 us
  other arithmetic: 31.5 us -> 17.5 us
  local copies, waits for them, and re-layouts: 26.3 us -> 17.5 us
    pallas_call x0 -> x1, Pallas kernels: none -> 14.3 us  [widen(): pl.pallas_call(widen_kernel, grid=(places,), in_specs=[pl.BlockSpec((1, 3...]
    convert_element_type x3 -> x0, other arithmetic: 14.1 us -> none  [the longest x1 8.67 us: per_device_dense(): grad_expert_in = jnp.swapaxes(grad_expert_in, 2, 3).astype(f32)]
    unnamed x61 -> x59, local copies, waits for them, and re-layouts: 18 us -> 10.9 us
  transfers between devices with their start and end apart: 4 -> 4, of which waited for: 1 -> 1; matrix products, arithmetic and copies ran while one was open for 4% -> 3% of each run, Pallas kernels for 27% -> 27%
where the time goes in v7:
time: 740 us; the launch traced here: 733 us
  Pallas kernels  656 us (89%)
  local copies, waits for them, and re-layouts  17.5 us (2%)
  other arithmetic  17.5 us (2%)
  between operations  16.2 us (2%)
  waiting for transfers between devices  10.2 us (1%)
  starting transfers between devices  9.56 us (1%)
    pallas_call x1, Pallas kernels, gather_feed(): pl.pallas_call(gather_feed_kernel, out_shape=(shape((RING, 4, count, widt...  173 us
    pallas_call x1, Pallas kernels, scatter_rows(): pl.pallas_call(scatter_kernel, out_shape=(shape((count, width), f32), sha...  153 us
    pallas_call x1, Pallas kernels, open_attention(): pl.pallas_call(open_kernel, out_shape=(shape((kinds, RING, depth, width),...  118 us
    pallas_call x1, Pallas kernels, finish(): pl.pallas_call(finish_kernel, out_shape=(shape((kinds, depth, columns), f...  103 us
    pallas_call x1, Pallas kernels, back_attention(): pl.pallas_call(back_kernel, out_shape=(shape((4, count, features), bf16),...  68.3 us
    pallas_call x1, Pallas kernels, product_to_owner(): pl.pallas_call(functools.partial(reduce_kernel, flip), out_shape=jax.Shap...  17.1 us
  transfers between devices with their start and end apart: 4, of which 1 were waited for; matrix products, arithmetic and copies ran while one was open for 3% of the time, Pallas kernels for 27%

profile of v7, /device:TPU:0, one launch (start us, length us, event | category | flops | bytes accessed | tf_op | source)
XLA Modules:
  0.0 732.9 jit_solution(11187397519950827168)
XLA Ops:
  8.1 0.9 reduce-window.4
  9.0 0.6 slice.34
  9.6 0.7 bitcast_subtract_fusion
  10.3 0.8 pad_add_fusion
  11.3 0.7 concatenate.18.routes
  12.0 1.0 fusion.21
  13.2 1.3 copy-done.11
  14.5 0.9 copy-done.13
  15.5 117.8 %open_attention.1 = (bf16[3,8,256,512]{3,2,1,0:T(8,128)(2,1)}, bf16[512,2048]{1,0:T(8,128)(2,1)}, s32[8,8,512]{2,1,0:T(8,128)S(1)}, bf16[512,2048]{1,0:T(8,128)(...) custom-call(bf16[3,256,512]{2,1,0:T(8,128)(2,1)S(1)} %copy-done.11, ...), custom_call_target="tpu_custom_call" | custom-call | tf_op jit(solution)/shard_map/open_attention/pallas_call | solution.py:1196
  133.3 0.6 copy-done.14
  133.9 5.1 all-to-all-start
  139.3 0.7 fusion.20.valid
  140.2 2.0 copy-done.1
  142.1 9.9 %attend.1 = (bf16[512,512]{1,0:T(8,128)(2,1)S(1)}, f32[4,512,1]{2,1,0:T(8,128)S(1)}) custom-call(bf16[512,512]{1,0:T(8,128)(2,1)S(1)} %get-tuple-element.49.queries, bf16[2,3,512,512]{3,2,1,0:T(8,128)(2,1)S(1)} %copy-done.1, bf16[2,3,512,512]{3,2,1,0:T(8,128)(2,1)S(1)} %copy-done.1, s32[512,1]{1,0:T(8,128)S(1)} %fusion.19.query_doc, ...), custom_call_target="tpu_custom_call" | custom-call | tf_op jit(solution)/shard_map/attend/pallas_call | solution.py:134
  152.1 1.0 copy-done.10
  153.1 17.1 %product_to_owner.1 = f32[128,2048]{1,0:T(8,128)S(1)} custom-call(bf16[1,512,512]{2,1,0:T(8,128)(2,1)S(1)} %bitcast.66, bf16[1,512,2048]{2,1,0:T(8,128)(2,1)S(1)} %bitcast.65), custom_call_target="tpu_custom_call" | custom-call | tf_op jit(solution)/shard_map/product_to_owner/pallas_call | solution.py:1685
  170.2 0.7 constant_dynamic-slice_fusion
  170.8 2.0 multiply_reduce_fusion.2
  172.9 1.0 fusion.34
  174.0 1.0 fusion.4
  175.0 0.7 maximum_maximum_fusion.scales
  175.7 1.0 fusion.8.rows
  176.6 10.2 %all-to-all-done.shared_blocks = bf16[8,3,176,256]{3,2,1,0:T(8,128)(2,1)} async-done(((bf16[8,3,176,256]{3,2,1,0:T(8,128)(2,1)}), bf16[8,3,176,256]{3,2,1,0:T(8,128)(2,1)}, u32[]{:S(2)}, u32[]{:S(2)}) %all-to-all-start) | async-done | bytes 2162720 | tf_op jit(solution)/shard_map/all_to_all | solution.py:1777
  186.8 173.3 %gather_feed.1 = (bf16[8,4,128,2048]{3,2,1,0:T(8,128)(2,1)}, bf16[8,4,128,2048]{3,2,1,0:T(8,128)(2,1)}, f32[8,4,24,128]{3,2,1,0:T(8,128)}, bf16[8,512,2048]{2,1,...) custom-call(bf16[128,2048]{1,0:T(8,128)(2,1)} %fusion.8.rows, ...), custom_call_target="tpu_custom_call" | custom-call | tf_op jit(solution)/shard_map/gather_feed/pallas_call | solution.py:625
  360.1 153.2 %scatter_rows.1 = (f32[128,2048]{1,0:T(8,128)}, f32[128,2048]{1,0:T(8,128)}, f32[24,128]{1,0:T(8,128)}, bf16[2,3,352,2048]{3,2,1,0:T(8,128)(2,1)}, bf16[8,3,176,256]{3,2,1,0:T(8,128)(2,1)}) custom-call(bf16[8,4,128,2048]{3,2,1,0:T(8,128)(2,1)} %bitcast.72, bf16[8,4,128,2048]{3,2,1,0:T(8,128)(2,1)} %bitcast.71, f32[8,4,24,128]{3,2,1,0:T(8,128)} %get-tuple-element.57.scalars, ...), custom_call_target="tpu_custom_call" | custom-call | tf_op jit(solution)/shard_map/scatter_rows/pallas_call | solution.py:986
  513.4 0.8 fusion.28
  514.1 0.7 multiply_reduce_fusion.4
  514.9 0.7 multiply_reduce_fusion.3
  515.6 0.7 fusion.6
  516.3 1.4 fusion.5
  517.8 1.4 multiply_reduce_fusion
  519.2 4.4 all-to-all-start.1
  523.7 0.7 pad_maximum_fusion.2
  524.5 3.1 fusion.32
  527.6 68.3 %back_attention.1 = (bf16[4,128,2048]{2,1,0:T(8,128)(2,1)}, bf16[3,512,512]{2,1,0:T(8,128)(2,1)}) custom-call(bf16[128,2048]{1,0:T(8,128)(2,1)} %get-tuple-element.87.rows, bf16[512,2048]{1,0:T(8,128)(2,1)} %get-tuple-element.52.weights, f32[512,1]{1,0:T(8,128)} %copy-done.6, bf16[512,512]{1,0:T(8,128)(2,1)} %copy-done.8, ...), custom_call_target="tpu_custom_call" | custom-call | tf_op jit(solution)/shard_map/back_attention/pallas_call | solution.py:1628
  595.9 2.2 convert_reduce_fusion.tail
  598.1 102.6 %finish.1 = (f32[3,256,512]{2,1,0:T(8,128)}, f32[512,256]{1,0:T(8,128)}, f32[4,8,512]{2,1,0:T(8,128)}, bf16[4,128,2048]{2,1,0:T(8,128)(2,1)}) custom-call(bf16[512,2048]{1,0:T(8,128)(2,1)} %get-tuple-element.69.normed, bf16[3,512,512]{2,1,0:T(8,128)(2,1)} %get-tuple-element.73.grad_raw, bf16[512,512]{1,0:T(8,128)(2,1)} %copy-done.7, ...), custom_call_target="tpu_custom_call" | custom-call | tf_op jit(solution)/shard_map/finish/pallas_call | solution.py:1379
  700.7 0.9 slice_reduce_fusion
  701.6 0.6 copy.32
  702.2 1.3 dynamic-slice_bitcast_fusion
  703.5 1.5 fusion.33
  705.0 1.6 slice_bitcast_fusion
  706.6 14.3 %widen.1 = (f32[2,2,352,2048]{3,2,1,0:T(8,128)}, f32[2,352,2048]{2,1,0:T(8,128)}, f32[2,256,1408]{2,1,0:T(8,128)}, f32[1408,256]{1,0:T(8,128)}, bf16[512,2048]{1,0:T(8,128)(2,1)}) custom-call(bf16[2,3,352,2048]{3,2,1,0:T(8,128)(2,1)} %get-tuple-element.67.experts, bf16[8,3,176,256]{3,2,1,0:T(8,128)(2,1)} %all-to-all-done.1.shared, ...), custom_call_target="tpu_custom_call" | custom-call | tf_op jit(solution)/shard_map/widen/pallas_call | solution.py:1436
  720.9 1.3 copy.37
  722.2 0.8 copy-done.21
  723.1 1.1 copy.38
  724.2 0.3 copy-done.23
  724.5 0.8 copy.39
  (74 shorter events, 1.1 us)
Async XLA Ops:
  8.0 164.8 %copy-start = (f32[2048,16]{0,1:T(8,128)S(1)}, f32[2048,16]{0,1:T(8,128)}, u32[]{:S(2)}) copy-start(f32[2048,16]{0,1:T(8,128)} %param.24) | copy-start | bytes 393220
  8.0 5.2 copy-start.9
  8.0 5.2 copy-start.17
  8.0 5.2 copy-start.16
  10.3 3.0 copy-start.12
  13.2 120.1 %copy-start.3 = (f32[512,128]{1,0:T(8,128)}, f32[512,128]{1,0:T(8,128)S(1)}, u32[]{:S(2)}) copy-start(f32[512,128]{1,0:T(8,128)S(1)} %get-tuple-element.101.cosine) | copy-start | bytes 786436
  13.2 120.1 %copy-start.4 = (f32[512,128]{1,0:T(8,128)}, f32[512,128]{1,0:T(8,128)S(1)}, u32[]{:S(2)}) copy-start(f32[512,128]{1,0:T(8,128)S(1)} %get-tuple-element.102.sine) | copy-start | bytes 786436
  13.2 1.3 copy-start.11
  14.5 0.9 copy-start.13
  133.2 0.7 copy-start.14
  133.3 6.9 copy-start.8
  133.9 52.9 %all-to-all-start = ((bf16[8,3,176,256]{3,2,1,0:T(8,128)(2,1)}), bf16[8,3,176,256]{3,2,1,0:T(8,128)(2,1)}, u32[]{:S(2)}, u32[]{:S(2)}) async-start(bf16[8,3,176,256]{3,2,1,0:T(8,128)(2,1)} %get-tuple-element.54), calls=%async_computation | async-start | bytes 4325376 | tf_op jit(solution)/shard_map/all_to_all | solution.py:1777
  140.0 12.0 %copy-start.6 = (f32[512,1]{1,0:T(8,128)}, f32[512,1]{1,0:T(8,128)S(1)}, u32[]{:S(2)}) copy-start(f32[512,1]{1,0:T(8,128)S(1)} %fusion.20.valid) | copy-start | bytes 6148
  140.1 12.0 %copy-start.15 = (s32[1,1536]{1,0:T(1,128)}, s32[1,1536]{1,0:T(1,128)S(1)}, u32[]{:S(2)}) copy-start(s32[1,1536]{1,0:T(1,128)S(1)} %compare_select_fusion.key_doc) | copy-start | bytes 18436
  140.1 12.0 %copy-start.5 = (s32[512,1]{1,0:T(8,128)}, s32[512,1]{1,0:T(8,128)S(1)}, u32[]{:S(2)}) copy-start(s32[512,1]{1,0:T(8,128)S(1)} %fusion.19.query_doc) | copy-start | bytes 6148
  140.1 2.0 copy-start.1
  142.1 10.9 %copy-start.2 = (bf16[512,2048]{1,0:T(8,128)(2,1)S(1)}, bf16[512,2048]{1,0:T(8,128)(2,1)}, u32[]{:S(2)}) copy-start(bf16[512,2048]{1,0:T(8,128)(2,1)} %get-tuple-element.52.weights) | copy-start | bytes 6291460
  152.1 1.0 copy-start.10
  153.1 19.8 %copy-start.7 = (bf16[512,512]{1,0:T(8,128)(2,1)}, bf16[512,512]{1,0:T(8,128)(2,1)S(1)}, u32[]{:S(2)}) copy-start(bf16[512,512]{1,0:T(8,128)(2,1)S(1)} %get-tuple-element.51.heads) | copy-start | bytes 1572868
  170.1 2.7 copy-start.24
  170.8 3.1 copy-start.26
  172.8 2.9 copy-start.18
  360.1 155.5 %copy-start.19 = (f32[128,2048]{1,0:T(8,128)S(1)}, f32[128,2048]{1,0:T(8,128)}, u32[]{:S(2)}) copy-start(f32[128,2048]{1,0:T(8,128)} %copy-done.18) | copy-start | bytes 3145732
  513.4 4.4 copy-start.22
  513.4 4.4 copy-start.25
  519.2 187.4 %all-to-all-start.1 = ((bf16[8,3,176,256]{3,2,1,0:T(8,128)(2,1)}), bf16[8,3,176,256]{3,2,1,0:T(8,128)(2,1)}, u32[]{:S(2)}, u32[]{:S(2)}) async-start(bf16[8,3,176,256]{3,2,1,0:T(8,128)(2,1)} %get-tuple-element.68), calls=%async_computation.1 | async-start | bytes 4325376 | tf_op jit(solution)/shard_map/all_to_all | solution.py:1837
  523.6 179.9 %all-reduce.3.cloned.1.call-start = ((), (), s32[]{:S(2)}) async-start(), calls=%async_computation.3 | async-start | bytes 393216 | tf_op jit(solution)/shard_map/psum | solution.py:1859
  524.4 182.2 %all-gather.2.cloned.1.call-start = ((), (), s32[]{:S(2)}) async-start(), calls=%async_computation.2 | async-start | bytes 2621440 | tf_op jit(solution)/shard_map/all_gather | solution.py:1836
  706.6 14.3 %copy-start.20 = (bf16[512,2048]{1,0:T(8,128)(2,1)S(1)}, bf16[512,2048]{1,0:T(8,128)(2,1)}, u32[]{:S(2)}) copy-start(bf16[512,2048]{1,0:T(8,128)(2,1)} %all-gather.2.cloned.1.call-done) | copy-start | bytes 6291460
  720.9 2.2 copy-start.21
  723.1 1.4 copy-start.23
Sparse Core Ops, SparseCore 0:
  530.0 143.4 all-reduce.2
Sparse Core Ops, SparseCore 1:
  527.7 30.5 all-gather.1

commit v8 on v7

--- a/solution.py
+++ b/solution.py
@@ -1124,7 +1124,8 @@
 
     def upward(index, kind, at):
         target = keys_values.at[kind, 0, at]
-        return share.describe(keys_values.at[kind, 2, at], target, (me.ep + 2, me.tp), index)
+        peer = ((me.ep + 2) % RING, me.tp)
+        return share.describe(keys_values.at[kind, 2, at], target, peer, index)
 
     def sideways(index, kind, at):
         target = keys_values.at[kind, 1, at]
@@ -1526,9 +1527,8 @@
 
     def downward(head, kind, source):
         at = columns(head)
-        return along.describe(
-            source.at[kind, :, at], from_z.at[kind, :, at], (me.ep - 2, me.tp), 2 * head + kind
-        )
+        peer = ((me.ep + RING - 2) % RING, me.tp)
+        return along.describe(source.at[kind, :, at], from_z.at[kind, :, at], peer, 2 * head + kind)
 
     scale = 1.0 / math.sqrt(HD)
 

time: 740 us -> 740 us (level)
  no operation moved by 1% of the time
where the time goes in v8:
time: 740 us; the launch traced here: 733 us
  Pallas kernels  656 us (89%)
  local copies, waits for them, and re-layouts  17.5 us (2%)
  other arithmetic  17.5 us (2%)
  between operations  16.2 us (2%)
  waiting for transfers between devices  10.2 us (1%)
  starting transfers between devices  9.56 us (1%)
    pallas_call x1, Pallas kernels, gather_feed(): pl.pallas_call(gather_feed_kernel, out_shape=(shape((RING, 4, count, widt...  173 us
    pallas_call x1, Pallas kernels, scatter_rows(): pl.pallas_call(scatter_kernel, out_shape=(shape((count, width), f32), sha...  153 us
    pallas_call x1, Pallas kernels, open_attention(): pl.pallas_call(open_kernel, out_shape=(shape((kinds, RING, depth, width),...  118 us
    pallas_call x1, Pallas kernels, finish(): pl.pallas_call(finish_kernel, out_shape=(shape((kinds, depth, columns), f...  103 us
    pallas_call x1, Pallas kernels, back_attention(): pl.pallas_call(back_kernel, out_shape=(shape((4, count, features), bf16),...  68.3 us
    pallas_call x1, Pallas kernels, product_to_owner(): pl.pallas_call(functools.partial(reduce_kernel, flip), out_shape=jax.Shap...  17.1 us
  transfers between devices with their start and end apart: 4, of which 1 were waited for; matrix products, arithmetic and copies ran while one was open for 3% of the time, Pallas kernels for 27%

profile of v8, /device:TPU:0, one launch (start us, length us, event | category | flops | bytes accessed | tf_op | source)
XLA Modules:
  0.0 733.0 jit_solution(13632188380765985450)
XLA Ops:
  8.1 0.9 reduce-window.4
  9.0 0.6 slice.34
  9.6 0.7 bitcast_subtract_fusion
  10.3 0.8 pad_add_fusion
  11.3 0.7 concatenate.18.routes
  12.0 1.0 fusion.21
  13.2 1.3 copy-done.11
  14.5 0.9 copy-done.13
  15.5 117.8 %open_attention.1 = (bf16[3,8,256,512]{3,2,1,0:T(8,128)(2,1)}, bf16[512,2048]{1,0:T(8,128)(2,1)}, s32[8,8,512]{2,1,0:T(8,128)S(1)}, bf16[512,2048]{1,0:T(8,128)(...) custom-call(bf16[3,256,512]{2,1,0:T(8,128)(2,1)S(1)} %copy-done.11, ...), custom_call_target="tpu_custom_call" | custom-call | tf_op jit(solution)/shard_map/open_attention/pallas_call | solution.py:1197
  133.3 0.6 copy-done.14
  133.9 5.1 all-to-all-start
  139.3 0.7 fusion.20.valid
  140.2 2.0 copy-done.1
  142.1 9.9 %attend.1 = (bf16[512,512]{1,0:T(8,128)(2,1)S(1)}, f32[4,512,1]{2,1,0:T(8,128)S(1)}) custom-call(bf16[512,512]{1,0:T(8,128)(2,1)S(1)} %get-tuple-element.49.queries, bf16[2,3,512,512]{3,2,1,0:T(8,128)(2,1)S(1)} %copy-done.1, bf16[2,3,512,512]{3,2,1,0:T(8,128)(2,1)S(1)} %copy-done.1, s32[512,1]{1,0:T(8,128)S(1)} %fusion.19.query_doc, ...), custom_call_target="tpu_custom_call" | custom-call | tf_op jit(solution)/shard_map/attend/pallas_call | solution.py:134
  152.1 1.0 copy-done.10
  153.1 17.1 %product_to_owner.1 = f32[128,2048]{1,0:T(8,128)S(1)} custom-call(bf16[1,512,512]{2,1,0:T(8,128)(2,1)S(1)} %bitcast.66, bf16[1,512,2048]{2,1,0:T(8,128)(2,1)S(1)} %bitcast.65), custom_call_target="tpu_custom_call" | custom-call | tf_op jit(solution)/shard_map/product_to_owner/pallas_call | solution.py:1685
  170.2 0.7 constant_dynamic-slice_fusion
  170.8 2.0 multiply_reduce_fusion.2
  172.9 1.0 fusion.34
  174.0 1.0 fusion.4
  175.0 0.7 maximum_maximum_fusion.scales
  175.7 1.0 fusion.8.rows
  176.6 10.2 %all-to-all-done.shared_blocks = bf16[8,3,176,256]{3,2,1,0:T(8,128)(2,1)} async-done(((bf16[8,3,176,256]{3,2,1,0:T(8,128)(2,1)}), bf16[8,3,176,256]{3,2,1,0:T(8,128)(2,1)}, u32[]{:S(2)}, u32[]{:S(2)}) %all-to-all-start) | async-done | bytes 2162720 | tf_op jit(solution)/shard_map/all_to_all | solution.py:1777
  186.8 173.3 %gather_feed.1 = (bf16[8,4,128,2048]{3,2,1,0:T(8,128)(2,1)}, bf16[8,4,128,2048]{3,2,1,0:T(8,128)(2,1)}, f32[8,4,24,128]{3,2,1,0:T(8,128)}, bf16[8,512,2048]{2,1,...) custom-call(bf16[128,2048]{1,0:T(8,128)(2,1)} %fusion.8.rows, ...), custom_call_target="tpu_custom_call" | custom-call | tf_op jit(solution)/shard_map/gather_feed/pallas_call | solution.py:625
  360.1 153.2 %scatter_rows.1 = (f32[128,2048]{1,0:T(8,128)}, f32[128,2048]{1,0:T(8,128)}, f32[24,128]{1,0:T(8,128)}, bf16[2,3,352,2048]{3,2,1,0:T(8,128)(2,1)}, bf16[8,3,176,256]{3,2,1,0:T(8,128)(2,1)}) custom-call(bf16[8,4,128,2048]{3,2,1,0:T(8,128)(2,1)} %bitcast.72, bf16[8,4,128,2048]{3,2,1,0:T(8,128)(2,1)} %bitcast.71, f32[8,4,24,128]{3,2,1,0:T(8,128)} %get-tuple-element.57.scalars, ...), custom_call_target="tpu_custom_call" | custom-call | tf_op jit(solution)/shard_map/scatter_rows/pallas_call | solution.py:986
  513.4 0.8 fusion.28
  514.1 0.7 multiply_reduce_fusion.4
  514.9 0.7 multiply_reduce_fusion.3
  515.6 0.7 fusion.6
  516.3 1.4 fusion.5
  517.8 1.4 multiply_reduce_fusion
  519.2 4.4 all-to-all-start.1
  523.7 0.7 pad_maximum_fusion.2
  524.5 3.1 fusion.32
  527.6 68.3 %back_attention.1 = (bf16[4,128,2048]{2,1,0:T(8,128)(2,1)}, bf16[3,512,512]{2,1,0:T(8,128)(2,1)}) custom-call(bf16[128,2048]{1,0:T(8,128)(2,1)} %get-tuple-element.87.rows, bf16[512,2048]{1,0:T(8,128)(2,1)} %get-tuple-element.52.weights, f32[512,1]{1,0:T(8,128)} %copy-done.6, bf16[512,512]{1,0:T(8,128)(2,1)} %copy-done.8, ...), custom_call_target="tpu_custom_call" | custom-call | tf_op jit(solution)/shard_map/back_attention/pallas_call | solution.py:1628
  595.9 2.2 convert_reduce_fusion.tail
  598.2 102.6 %finish.1 = (f32[3,256,512]{2,1,0:T(8,128)}, f32[512,256]{1,0:T(8,128)}, f32[4,8,512]{2,1,0:T(8,128)}, bf16[4,128,2048]{2,1,0:T(8,128)(2,1)}) custom-call(bf16[512,2048]{1,0:T(8,128)(2,1)} %get-tuple-element.69.normed, bf16[3,512,512]{2,1,0:T(8,128)(2,1)} %get-tuple-element.73.grad_raw, bf16[512,512]{1,0:T(8,128)(2,1)} %copy-done.7, ...), custom_call_target="tpu_custom_call" | custom-call | tf_op jit(solution)/shard_map/finish/pallas_call | solution.py:1380
  700.8 0.9 slice_reduce_fusion
  701.6 0.6 copy.32
  702.3 1.3 dynamic-slice_bitcast_fusion
  703.6 1.5 fusion.33
  705.1 1.6 slice_bitcast_fusion
  706.7 14.3 %widen.1 = (f32[2,2,352,2048]{3,2,1,0:T(8,128)}, f32[2,352,2048]{2,1,0:T(8,128)}, f32[2,256,1408]{2,1,0:T(8,128)}, f32[1408,256]{1,0:T(8,128)}, bf16[512,2048]{1,0:T(8,128)(2,1)}) custom-call(bf16[2,3,352,2048]{3,2,1,0:T(8,128)(2,1)} %get-tuple-element.67.experts, bf16[8,3,176,256]{3,2,1,0:T(8,128)(2,1)} %all-to-all-done.1.shared, ...), custom_call_target="tpu_custom_call" | custom-call | tf_op jit(solution)/shard_map/widen/pallas_call | solution.py:1437
  721.0 1.3 copy.37
  722.3 0.8 copy-done.21
  723.1 1.1 copy.38
  724.3 0.3 copy-done.23
  724.5 0.8 copy.39
  (74 shorter events, 1.1 us)
Async XLA Ops:
  8.0 164.8 %copy-start = (f32[2048,16]{0,1:T(8,128)S(1)}, f32[2048,16]{0,1:T(8,128)}, u32[]{:S(2)}) copy-start(f32[2048,16]{0,1:T(8,128)} %param.24) | copy-start | bytes 393220
  8.0 5.2 copy-start.9
  8.0 5.2 copy-start.17
  8.0 5.2 copy-start.16
  10.3 3.0 copy-start.12
  13.2 120.1 %copy-start.3 = (f32[512,128]{1,0:T(8,128)}, f32[512,128]{1,0:T(8,128)S(1)}, u32[]{:S(2)}) copy-start(f32[512,128]{1,0:T(8,128)S(1)} %get-tuple-element.101.cosine) | copy-start | bytes 786436
  13.2 120.1 %copy-start.4 = (f32[512,128]{1,0:T(8,128)}, f32[512,128]{1,0:T(8,128)S(1)}, u32[]{:S(2)}) copy-start(f32[512,128]{1,0:T(8,128)S(1)} %get-tuple-element.102.sine) | copy-start | bytes 786436
  13.2 1.3 copy-start.11
  14.5 0.9 copy-start.13
  133.2 0.7 copy-start.14
  133.3 6.9 copy-start.8
  133.9 52.9 %all-to-all-start = ((bf16[8,3,176,256]{3,2,1,0:T(8,128)(2,1)}), bf16[8,3,176,256]{3,2,1,0:T(8,128)(2,1)}, u32[]{:S(2)}, u32[]{:S(2)}) async-start(bf16[8,3,176,256]{3,2,1,0:T(8,128)(2,1)} %get-tuple-element.54), calls=%async_computation | async-start | bytes 4325376 | tf_op jit(solution)/shard_map/all_to_all | solution.py:1777
  140.0 12.0 %copy-start.6 = (f32[512,1]{1,0:T(8,128)}, f32[512,1]{1,0:T(8,128)S(1)}, u32[]{:S(2)}) copy-start(f32[512,1]{1,0:T(8,128)S(1)} %fusion.20.valid) | copy-start | bytes 6148
  140.1 12.0 %copy-start.15 = (s32[1,1536]{1,0:T(1,128)}, s32[1,1536]{1,0:T(1,128)S(1)}, u32[]{:S(2)}) copy-start(s32[1,1536]{1,0:T(1,128)S(1)} %compare_select_fusion.key_doc) | copy-start | bytes 18436
  140.1 12.0 %copy-start.5 = (s32[512,1]{1,0:T(8,128)}, s32[512,1]{1,0:T(8,128)S(1)}, u32[]{:S(2)}) copy-start(s32[512,1]{1,0:T(8,128)S(1)} %fusion.19.query_doc) | copy-start | bytes 6148
  140.1 2.0 copy-start.1
  142.1 10.9 %copy-start.2 = (bf16[512,2048]{1,0:T(8,128)(2,1)S(1)}, bf16[512,2048]{1,0:T(8,128)(2,1)}, u32[]{:S(2)}) copy-start(bf16[512,2048]{1,0:T(8,128)(2,1)} %get-tuple-element.52.weights) | copy-start | bytes 6291460
  152.1 1.0 copy-start.10
  153.1 19.8 %copy-start.7 = (bf16[512,512]{1,0:T(8,128)(2,1)}, bf16[512,512]{1,0:T(8,128)(2,1)S(1)}, u32[]{:S(2)}) copy-start(bf16[512,512]{1,0:T(8,128)(2,1)S(1)} %get-tuple-element.51.heads) | copy-start | bytes 1572868
  170.1 2.7 copy-start.24
  170.8 3.1 copy-start.26
  172.8 2.9 copy-start.18
  360.1 155.5 %copy-start.19 = (f32[128,2048]{1,0:T(8,128)S(1)}, f32[128,2048]{1,0:T(8,128)}, u32[]{:S(2)}) copy-start(f32[128,2048]{1,0:T(8,128)} %copy-done.18) | copy-start | bytes 3145732
  513.4 4.4 copy-start.22
  513.4 4.4 copy-start.25
  519.2 187.5 %all-to-all-start.1 = ((bf16[8,3,176,256]{3,2,1,0:T(8,128)(2,1)}), bf16[8,3,176,256]{3,2,1,0:T(8,128)(2,1)}, u32[]{:S(2)}, u32[]{:S(2)}) async-start(bf16[8,3,176,256]{3,2,1,0:T(8,128)(2,1)} %get-tuple-element.68), calls=%async_computation.1 | async-start | bytes 4325376 | tf_op jit(solution)/shard_map/all_to_all | solution.py:1837
  523.6 179.9 %all-reduce.3.cloned.1.call-start = ((), (), s32[]{:S(2)}) async-start(), calls=%async_computation.3 | async-start | bytes 393216 | tf_op jit(solution)/shard_map/psum | solution.py:1859
  524.4 182.3 %all-gather.2.cloned.1.call-start = ((), (), s32[]{:S(2)}) async-start(), calls=%async_computation.2 | async-start | bytes 2621440 | tf_op jit(solution)/shard_map/all_gather | solution.py:1836
  706.7 14.3 %copy-start.20 = (bf16[512,2048]{1,0:T(8,128)(2,1)S(1)}, bf16[512,2048]{1,0:T(8,128)(2,1)}, u32[]{:S(2)}) copy-start(bf16[512,2048]{1,0:T(8,128)(2,1)} %all-gather.2.cloned.1.call-done) | copy-start | bytes 6291460
  721.0 2.2 copy-start.21
  723.1 1.4 copy-start.23
Sparse Core Ops, SparseCore 0:
  530.0 143.3 all-reduce.2
Sparse Core Ops, SparseCore 1:
  527.7 30.5 all-gather.1
